TPU v7x, 256 devices: a whole 4x4x8 slice. The times are simulated.
256 devices in a mesh: dp: 32 (over z, x_lo, core), tensor: 8 (over y, x_hi).
Axes of the slice: x: 4 (x_hi: 2, x_lo: 2; x = x_hi * 2 + x_lo), y: 4, z: 8, core: 2. Of those that a mesh axis runs over, the one named last changes fastest.
Arguments:
- grad_out: bfloat16 [16384, 4096], P(('dp', 'tensor')), may hold values from -4 to 4
- x_act: bfloat16 [16384, 8192], P('dp', 'tensor'), may hold values from -6 to 6
- z_act: bfloat16 [16384, 8192], P('dp', 'tensor'), may hold values from -6 to 6
- b_act: bfloat16 [16384, 8, 128], P('dp', 'tensor'), may hold values from -2 to 2
- c_act: bfloat16 [16384, 8, 128], P('dp', 'tensor'), may hold values from -2 to 2
- step_size: float32 [16384, 128], P('dp', 'tensor'), may hold values from 0.001 to 0.3
- log_rate: float32 [128], P('tensor'), may hold values from -0.7 to 2.5
- skip_gain: float32 [128], P('tensor'), may hold values from 0.5 to 1.5
- norm_gain: float32 [8192], P('tensor'), may hold values from 0.5 to 1.5
- w_out: bfloat16 [4096, 8192], P('dp', 'tensor'), may hold values from -0.0625 to 0.0625
Outputs:
- grad_x: bfloat16 [16384, 8192], P('dp', 'tensor')
- grad_z: bfloat16 [16384, 8192], P('dp', 'tensor')
- grad_b: bfloat16 [16384, 8, 128], P('dp', 'tensor')
- grad_c: bfloat16 [16384, 8, 128], P('dp', 'tensor')
- grad_step: float32 [16384, 128], P('dp', 'tensor')
- grad_log_rate: float32 [128], P('tensor')
- grad_skip: float32 [128], P('tensor')
- grad_norm_gain: float32 [8192], P('tensor')
- grad_w_out: float32 [4096, 8192], P('dp', 'tensor')
All inputs are finite; a program needn't handle non-finite values.
Results may differ from a plain program's by a relative error of at most 0.0029.
Values may be sent and summed in bfloat16 or wider, within the bound.
No kernel may reach another device: no remote copies, remote signals or barrier semaphores. Data moves between devices by JAX's collectives and lax.ppermute only.
A program may use at most 192 MiB of HBM per device.

v0:
```python
import jax
import jax.numpy as jnp
from jax import lax
from jax.experimental import pallas as pl
from jax.experimental.pallas import tpu as pltpu
from jax.sharding import PartitionSpec as P

F32, BF16 = jnp.float32, jnp.bfloat16
HEADS = 16
SPAN = 256
TOK = 512
CH = 1024
HALF = 128
LOG2E = 1.4426950408889634
BIG = 126.0
VMEM_LIMIT = 48 * 1024 * 1024
SMALL = pl.CostEstimate(flops=1000, bytes_accessed=1000, transcendentals=0)


def dot(a, b):
    return jnp.dot(a, b, preferred_element_type=F32)


def dot_nt(a, b):
    return lax.dot_general(a, b, (((1,), (1,)), ((), ())), preferred_element_type=F32)


def split2(v):
    hi = v.astype(BF16)
    return hi, (v - hi.astype(F32)).astype(BF16)


def dot3(a, b, fn):
    ah, al = split2(a)
    bh, bl = split2(b)
    return fn(ah, bh) + (fn(ah, bl) + fn(al, bh))


def spread_matrix(width):
    row = lax.broadcasted_iota(jnp.int32, (128, HEADS * width), 0)
    col = lax.broadcasted_iota(jnp.int32, (128, HEADS * width), 1)
    return jnp.where((row < 48) & ((row & 15) == col // width), 1.0, 0.0).astype(BF16)


def parts3(v):
    lane = lax.broadcasted_iota(jnp.int32, v.shape, 1)
    v = jnp.where(lane < HEADS, v, 0.0)
    one = v.astype(BF16).astype(F32)
    rest = v - one
    two = rest.astype(BF16).astype(F32)
    three = rest - two
    return (one + pltpu.roll(two, 16, 1) + pltpu.roll(three, 32, 1)).astype(BF16)


def cumulate(tri, v):
    one = v.astype(BF16)
    rest = v - one.astype(F32)
    two = rest.astype(BF16)
    three = (rest - two.astype(F32)).astype(BF16)
    return dot(tri, one) + (dot(tri, two) + dot(tri, three))


def triangle(n, lower):
    row = lax.broadcasted_iota(jnp.int32, (n, n), 0)
    col = lax.broadcasted_iota(jnp.int32, (n, n), 1)
    return jnp.where(row >= col if lower else row <= col, 1.0, 0.0).astype(BF16)


def prepare(dt_ref, rate_ref, pad_ref, ratepad_ref):
    pad_ref[...] = jnp.ones((TOK, 128), F32)
    pad_ref[:, :HEADS] = dt_ref[...]
    ratepad_ref[...] = jnp.zeros((8, 128), F32)
    ratepad_ref[0:1, :HEADS] = rate_ref[...]
    rate = -jnp.exp(ratepad_ref[0:1, :])
    tri = triangle(SPAN, True)
    cums, rs = [], []
    for k in range(2):
        dt = pad_ref[k * SPAN:(k + 1) * SPAN, :]
        cum = cumulate(tri, dt * (rate * LOG2E))
        cums.append(cum)
        rs.append(jnp.log2(dt) - cum)
    return rate, cums, rs


def fwd_kernel(x_ref, z_ref, b_ref, c_ref, dt_ref, rate_ref, skip_ref, gain_ref,
               ys_ref, n_ref, pad_ref, ratepad_ref, cexp_ref, rt_ref, s_ref, coef_ref):
    rate, cums, rs = prepare(dt_ref, rate_ref, pad_ref, ratepad_ref)
    wide = spread_matrix(HALF)
    narrow = spread_matrix(64)
    row = lax.broadcasted_iota(jnp.int32, (SPAN, SPAN), 0)
    col = lax.broadcasted_iota(jnp.int32, (SPAN, SPAN), 1)
    ratepad_ref[0:1, :HEADS] = skip_ref[...]
    skip = ratepad_ref[0:1, :]
    for k in range(2):
        rows = slice(k * SPAN, (k + 1) * SPAN)
        cexp_ref[rows, :] = dot(parts3(cums[k]), wide)
        rt_ref[k] = rs[k].T
        bk, ck = b_ref[rows, :], c_ref[rows, :]
        s_ref[k] = jnp.where(row > col, dot_nt(ck, bk), 0.0)
        diag = jnp.sum(bk.astype(F32) * ck.astype(F32), axis=1, keepdims=True)
        coef_ref[rows, :] = dot(parts3(diag * pad_ref[rows, :] + skip), narrow)
    lane = lax.broadcasted_iota(jnp.int32, (SPAN, 128), 1)

    def pair(hp, _):
        cols = pl.ds(pl.multiple_of(hp * 128, 128), 128)
        for k in range(2):
            rows = slice(k * SPAN, (k + 1) * SPAN)
            xp = x_ref[rows, cols]
            tops, bots = [], []
            for half in range(2):
                h = hp * 2 + half
                rrow = rt_ref[k, pl.ds(h, 1), :]
                hcols = pl.ds(pl.multiple_of(h * 128, 128), 128)
                top = cexp_ref[k * SPAN:k * SPAN + HALF, hcols]
                bot = cexp_ref[k * SPAN + HALF:(k + 1) * SPAN, hcols]
                wt = s_ref[k, :HALF, :HALF] * jnp.exp2(jnp.minimum(top + rrow[:, :HALF], BIG))
                wb = s_ref[k, HALF:, :] * jnp.exp2(
                    jnp.minimum(jnp.concatenate([bot, bot], axis=1) + rrow, BIG))
                tops += split2(wt)
                bots += split2(wb)
            yt = dot(jnp.concatenate(tops, axis=0), xp[:HALF])
            yb = dot(jnp.concatenate(bots, axis=0), xp)
            ys = [jnp.concatenate([v[256 * h:256 * h + 128] + v[256 * h + 128:256 * h + 256] for v in (yt, yb)], axis=0)
                  for h in range(2)]
            ys_ref[rows, cols] = jnp.where(lane < 64, ys[0], ys[1])
        return 0

    lax.fori_loop(0, 8, pair, 0)

    s10 = dot_nt(c_ref[SPAN:, :], b_ref[:SPAN, :])
    qdt = parts3(jnp.exp2(cums[0][SPAN - 1:SPAN, :] + rs[0]))
    p = parts3(jnp.exp2(cums[1]))
    for j in range(4):
        cols = slice(j * 256, (j + 1) * 256)
        xq = dot(qdt, narrow[:, cols]) * x_ref[:SPAN, cols].astype(F32)
        ys_ref[SPAN:, cols] += dot(p, narrow[:, cols]) * dot3(s10, xq, dot)

    gain = gain_ref[...]

    def norm(i, _):
        rows = pl.ds(pl.multiple_of(i * 32, 32), 32)
        z = z_ref[rows, :].astype(F32)
        y = ys_ref[rows, :] + coef_ref[rows, :] * x_ref[rows, :].astype(F32)
        gated = y * (z / (1.0 + jnp.exp(-z)))
        inv = lax.rsqrt(jnp.mean(gated * gated, axis=1, keepdims=True) + 1e-05)
        n_ref[rows, :] = (gated * inv * gain).astype(BF16)
        return 0

    lax.fori_loop(0, TOK // 32, norm, 0)


def bwd_kernel(u_ref, ys_ref, x_ref, z_ref, b_ref, c_ref, dt_ref, rate_ref, skip_ref, gain_ref,
               dx_ref, dz_ref, db_ref, dc_ref, ddt_ref, small_ref,
               pad_ref, ratepad_ref, rexp_ref, ct_ref, s_ref, coef_ref, dy_ref, dxs_ref, ds_ref, dg_ref):
    rate, cums, rs = prepare(dt_ref, rate_ref, pad_ref, ratepad_ref)
    wide = spread_matrix(HALF)
    narrow = spread_matrix(64)
    row = lax.broadcasted_iota(jnp.int32, (SPAN, SPAN), 0)
    col = lax.broadcasted_iota(jnp.int32, (SPAN, SPAN), 1)
    ratepad_ref[0:1, :HEADS] = skip_ref[...]
    skip = ratepad_ref[0:1, :]
    diags = []
    for k in range(2):
        rows = slice(k * SPAN, (k + 1) * SPAN)
        rexp_ref[rows, :] = dot(parts3(rs[k]), wide)
        ct_ref[k] = cums[k].T
        bk, ck = b_ref[rows, :], c_ref[rows, :]
        s_ref[k] = jnp.where(row < col, dot_nt(bk, ck), 0.0)
        diag = jnp.sum(bk.astype(F32) * ck.astype(F32), axis=1, keepdims=True)
        diags.append(diag)
        coef_ref[rows, :] = dot(parts3(diag * pad_ref[rows, :] + skip), narrow)

    gain = gain_ref[...]
    dg_ref[...] = jnp.zeros((8, CH), F32)

    def gate(i, _):
        rows = pl.ds(pl.multiple_of(i * 32, 32), 32)
        z = z_ref[rows, :].astype(F32)
        y = ys_ref[rows, :] + coef_ref[rows, :] * x_ref[rows, :].astype(F32)
        sig = 1.0 / (1.0 + jnp.exp(-z))
        sz = z * sig
        gated = y * sz
        inv = lax.rsqrt(jnp.mean(gated * gated, axis=1, keepdims=True) + 1e-05)
        unit = gated * inv
        u = u_ref[rows, :]
        ug = u * unit
        dg_ref[...] += (ug[0:8] + ug[8:16]) + (ug[16:24] + ug[24:32])
        v = u * gain
        dgated = inv * (v - unit * jnp.mean(v * unit, axis=1, keepdims=True))
        dy_ref[rows, :] = dgated * sz
        dz_ref[rows, :] = (dgated * y * (sig * (1.0 + z * (1.0 - sig)))).astype(BF16)
        return 0

    lax.fori_loop(0, TOK // 32, gate, 0)

    ds_ref[...] = jnp.zeros((2, SPAN, SPAN), F32)
    lane = lax.broadcasted_iota(jnp.int32, (SPAN, 128), 1)

    def pair(hp, _):
        cols = pl.ds(pl.multiple_of(hp * 128, 128), 128)
        for k in range(2):
            rows = slice(k * SPAN, (k + 1) * SPAN)
            xp = x_ref[rows, cols].astype(F32)
            dh, dl = split2(dy_ref[rows, cols])
            dhl = jnp.concatenate([dh, dl], axis=1)
            xx = []
            for half in range(2):
                xm = jnp.where((lane < 64) if half == 0 else (lane >= 64), xp, 0.0).astype(BF16)
                xx.append(jnp.concatenate([xm, xm], axis=1))
            gts = dot_nt(jnp.concatenate([v[:HALF] for v in xx], axis=0), dhl)
            gbs = dot_nt(jnp.concatenate([v[HALF:] for v in xx], axis=0), dhl[HALF:])
            ths, tls, bhs, bls = [], [], [], []
            dst, dsb = ds_ref[k, :HALF, :], ds_ref[k, HALF:, HALF:]
            for half in range(2):
                h = hp * 2 + half
                part = slice(half * HALF, (half + 1) * HALF)
                crow = ct_ref[k, pl.ds(h, 1), :]
                hcols = pl.ds(pl.multiple_of(h * 128, 128), 128)
                top = rexp_ref[k * SPAN:k * SPAN + HALF, hcols]
                bot = rexp_ref[k * SPAN + HALF:(k + 1) * SPAN, hcols]
                et = jnp.exp2(jnp.minimum(jnp.concatenate([top, top], axis=1) + crow, BIG))
                eb = jnp.exp2(jnp.minimum(bot + crow[:, HALF:], BIG))
                dst = dst + et * gts[part]
                dsb = dsb + eb * gbs[part]
                hi, lo = split2(s_ref[k, :HALF, :] * et)
                ths.append(hi)
                tls.append(lo)
                hi, lo = split2(s_ref[k, HALF:, HALF:] * eb)
                bhs.append(hi)
                bls.append(lo)
            ds_ref[k, :HALF, :] = dst
            ds_ref[k, HALF:, HALF:] = dsb
            ot = dot(jnp.concatenate(ths, axis=0), dhl)
            ob = dot(jnp.concatenate(bhs, axis=0), dhl[HALF:])
            ot = (ot[:, :128] + ot[:, 128:]) + dot(jnp.concatenate(tls, axis=0), dh)
            ob = (ob[:, :128] + ob[:, 128:]) + dot(jnp.concatenate(bls, axis=0), dh[HALF:])
            outs = [jnp.concatenate([v[h * HALF:(h + 1) * HALF] for v in (ot, ob)], axis=0) for h in range(2)]
            dxs_ref[rows, cols] = jnp.where(lane < 64, outs[0], outs[1])
        return 0

    lax.fori_loop(0, 8, pair, 0)

    st = dot_nt(b_ref[:SPAN, :], c_ref[SPAN:, :])
    qdt = parts3(jnp.exp2(cums[0][SPAN - 1:SPAN, :] + rs[0]))
    p = parts3(jnp.exp2(cums[1]))
    dst = jnp.zeros((SPAN, SPAN), F32)
    for j in range(4):
        cols = slice(j * 256, (j + 1) * 256)
        qx = dot(qdt, narrow[:, cols])
        xq = qx * x_ref[:SPAN, cols].astype(F32)
        pdy = dot(p, narrow[:, cols]) * dy_ref[SPAN:, cols]
        dxs_ref[:SPAN, cols] += qx * dot3(st, pdy, dot)
        dst = dst + dot3(xq, pdy, dot_nt)

    seg_row = lax.broadcasted_iota(jnp.int32, (CH, 128), 0)
    seg_col = lax.broadcasted_iota(jnp.int32, (CH, 128), 1)
    seg = jnp.where(seg_row // 64 == seg_col, 1.0, 0.0).astype(BF16)

    def heads_sum(v):
        hi, lo = split2(v)
        return dot(hi, seg) + dot(lo, seg)

    tri = triangle(SPAN, False)
    later = jnp.zeros((1, 128), F32)
    rate_sum = jnp.zeros((1, 128), F32)
    skip_sum = jnp.zeros((1, 128), F32)
    for k in (1, 0):
        rows = slice(k * SPAN, (k + 1) * SPAN)
        xf = x_ref[rows, :].astype(F32)
        dy = dy_ref[rows, :]
        dxs = dxs_ref[rows, :]
        kx = heads_sum(dy * xf)
        r = heads_sum(dy * ys_ref[rows, :])
        q = heads_sum(xf * dxs)
        suffix = cumulate(tri, r - q) + later
        later = suffix[0:1, :]
        dt = pad_ref[rows, :]
        ddt = q / dt + kx * diags[k] + rate * suffix
        ddt_ref[rows, :] = ddt[:, :HEADS]
        rate_sum = rate_sum + rate * jnp.sum(dt * suffix, axis=0, keepdims=True)
        skip_sum = skip_sum + jnp.sum(kx, axis=0, keepdims=True)
        sd = jnp.sum(dt * kx, axis=1, keepdims=True)
        dsk = jnp.where(row < col, ds_ref[k], 0.0)
        bk, ck = b_ref[rows, :], c_ref[rows, :]
        sh, sl = split2(dsk)
        db = dot(sh, ck) + dot(sl, ck) + sd * ck.astype(F32)
        sh, sl = split2(dsk.T)
        dc = dot(sh, bk) + dot(sl, bk) + sd * bk.astype(F32)
        if k == 0:
            oh, ol = split2(dst)
            db = db + dot(oh, c_ref[SPAN:, :]) + dot(ol, c_ref[SPAN:, :])
        else:
            oh, ol = split2(dst.T)
            dc = dc + dot(oh, b_ref[:SPAN, :]) + dot(ol, b_ref[:SPAN, :])
        db_ref[rows, :] = db.astype(BF16)
        dc_ref[rows, :] = dc.astype(BF16)
        dx_ref[rows, :] = (dxs + coef_ref[rows, :] * dy).astype(BF16)

    dg = jnp.sum(dg_ref[...], axis=0, keepdims=True)
    for j in range(8):
        small_ref[j:j + 1, :] = dg[:, j * 128:(j + 1) * 128]
    small_ref[8:9, :] = rate_sum
    small_ref[9:10, :] = skip_sum
    small_ref[10:16, :] = jnp.zeros((6, 128), F32)


def scan_forward(x, z, b, c, dt, rate, skip, gain):
    return pl.pallas_call(
        fwd_kernel,
        out_shape=(jax.ShapeDtypeStruct((TOK, CH), F32), jax.ShapeDtypeStruct((TOK, CH), BF16)),
        scratch_shapes=[
            pltpu.VMEM((TOK, 128), F32),
            pltpu.VMEM((8, 128), F32),
            pltpu.VMEM((TOK, HEADS * HALF), F32),
            pltpu.VMEM((2, 128, SPAN), F32),
            pltpu.VMEM((2, SPAN, SPAN), F32),
            pltpu.VMEM((TOK, CH), F32),
        ],
        compiler_params=pltpu.CompilerParams(vmem_limit_bytes=VMEM_LIMIT),
        cost_estimate=SMALL,
        name="scan_forward",
    )(x, z, b, c, dt, rate, skip, gain)


def scan_backward(u, ys, x, z, b, c, dt, rate, skip, gain):
    return pl.pallas_call(
        bwd_kernel,
        out_shape=(
            jax.ShapeDtypeStruct((TOK, CH), BF16),
            jax.ShapeDtypeStruct((TOK, CH), BF16),
            jax.ShapeDtypeStruct((TOK, 128), BF16),
            jax.ShapeDtypeStruct((TOK, 128), BF16),
            jax.ShapeDtypeStruct((TOK, HEADS), F32),
            jax.ShapeDtypeStruct((16, 128), F32),
        ),
        scratch_shapes=[
            pltpu.VMEM((TOK, 128), F32),
            pltpu.VMEM((8, 128), F32),
            pltpu.VMEM((TOK, HEADS * HALF), F32),
            pltpu.VMEM((2, 128, SPAN), F32),
            pltpu.VMEM((2, SPAN, SPAN), F32),
            pltpu.VMEM((TOK, CH), F32),
            pltpu.VMEM((TOK, CH), F32),
            pltpu.VMEM((TOK, CH), F32),
            pltpu.VMEM((2, SPAN, SPAN), F32),
            pltpu.VMEM((8, CH), F32),
        ],
        compiler_params=pltpu.CompilerParams(vmem_limit_bytes=VMEM_LIMIT),
        cost_estimate=SMALL,
        name="scan_backward",
    )(u, ys, x, z, b, c, dt, rate, skip, gain)


AXES = {"z": 8, "xl": 2, "c": 2, "y": 4, "xh": 2}
DP = ("z", "xl", "c")
TP = ("y", "xh")


def send(v, axis, shift):
    n = AXES[axis]
    return lax.ppermute(v, axis, [(i, (i + shift) % n) for i in range(n)])


def swap(v, axis, mask):
    return lax.ppermute(v, axis, [(i, i ^ mask) for i in range(AXES[axis])])


def both_ways(up, down, axis):
    return send(up, axis, 1), send(down, axis, -1)


def tie(values, *first):
    return lax.optimization_barrier((tuple(values),) + tuple(first))[0]


def shuffle(name, shapes, plan, scalars, *arrays):
    count = len(plan([0] * len(scalars)))

    def kernel(s_ref, *refs):
        src, dst, sem = refs[:len(arrays)], refs[len(arrays):-1], refs[-1]
        copies = [
            pltpu.make_async_copy(src[i].at[a], dst[o].at[b], sem.at[k])
            for k, (i, a, o, b) in enumerate(plan([s_ref[j] for j in range(len(scalars))]))
        ]
        for copy in copies:
            copy.start()
        for copy in copies:
            copy.wait()

    return pl.pallas_call(
        kernel,
        out_shape=tuple(jax.ShapeDtypeStruct(s, BF16) for s in shapes),
        in_specs=[pl.BlockSpec(memory_space=pltpu.SMEM)] + [pl.BlockSpec(memory_space=pl.ANY)] * len(arrays),
        out_specs=tuple(pl.BlockSpec(memory_space=pltpu.VMEM) for _ in shapes),
        scratch_shapes=[pltpu.SemaphoreType.DMA((count,))],
        cost_estimate=SMALL,
        name=name,
    )(jnp.stack([s.astype(jnp.int32) for s in scalars]), *arrays)


def own_first(rows, core):
    def kernel(core_ref, in_ref, out_ref):
        for j in range(16):
            even = in_ref[:, 256 * j:256 * j + 128]
            odd = in_ref[:, 256 * j + 128:256 * j + 256]
            first = core_ref[0] == 0
            out_ref[:, 128 * j:128 * j + 128] = jnp.where(first, even, odd)
            out_ref[:, 2048 + 128 * j:2048 + 128 * j + 128] = jnp.where(first, odd, even)

    return pl.pallas_call(
        kernel,
        out_shape=jax.ShapeDtypeStruct(rows.shape, rows.dtype),
        in_specs=[pl.BlockSpec(memory_space=pltpu.SMEM), pl.BlockSpec(memory_space=pltpu.VMEM)],
        out_specs=pl.BlockSpec(memory_space=pltpu.VMEM),
        cost_estimate=SMALL,
        name="own_first",
    )(core.astype(jnp.int32).reshape(1), rows)


def at_rows(start, size):
    return (pl.ds(pl.multiple_of(start, 32), size), slice(None)) if not isinstance(start, int) else (slice(start, start + size), slice(None))


def place_tokens(yi, xh, first, *pieces):
    parts = ((0, 64, 0, 0, 0), (1, 64, 0, 1, 0), (2, 64, 3, 0, 0), (3, 64, 3, 1, 0), (4, 64, 1, 0, 0),
             (5, 64, 1, 1, 0), (6, 64, 2, 0, 0), (7, 32, 2, 1, 0), (8, 32, 2, 1, 32))

    def plan(s):
        moves = []
        for piece, size, turn, other, offset in parts:
            start = ((s[0] + turn) % 4) * 128 + (1 - s[1] if other else s[1]) * 64 + offset
            moves.append((piece, (slice(None), slice(first, first + 2048)), 0, at_rows(start, size)))
        return moves

    return shuffle("place_tokens", [(TOK, 2048)], plan, (yi, xh), *pieces)[0]


def weight_blocks(zi, shifts, keep, theirs, normed, normed_other):
    def kernel(at_ref, a_ref, b_ref, n_ref, m_ref, out_ref):
        def term(r, n):
            return lax.dot_general(r[...], n[...], (((0,), (0,)), ((), ())), preferred_element_type=F32)

        out_ref[0] = term(a_ref, n_ref) + term(b_ref, m_ref)

    columns = pl.BlockSpec((TOK, 256), lambda i, at: (0, at[i]))
    whole = pl.BlockSpec((TOK, CH), lambda i, at: (0, 0))
    return pl.pallas_call(
        kernel,
        grid_spec=pltpu.PrefetchScalarGridSpec(
            num_scalar_prefetch=1,
            grid=(len(shifts),),
            in_specs=[columns, columns, whole, whole],
            out_specs=pl.BlockSpec((1, 256, CH), lambda i, at: (i, 0, 0)),
        ),
        out_shape=jax.ShapeDtypeStruct((len(shifts), 256, CH), F32),
        compiler_params=pltpu.CompilerParams(vmem_limit_bytes=VMEM_LIMIT),
        cost_estimate=SMALL,
        name="weight_blocks",
    )(jnp.stack([(zi + k + 8) % 8 for k in shifts]).astype(jnp.int32), keep, theirs, normed, normed_other)


def back_project(core, keep, give, w):
    def kernel(core_ref, a_ref, b_ref, v_ref, w_ref, out_ref):
        out_ref[...] = dot(a_ref[...], v_ref[...].reshape(2048, 256)) + dot(b_ref[...], w_ref[...].reshape(2048, 256))

    rows = pl.BlockSpec((TOK, 2048), lambda i, core: (0, 0))
    return pl.pallas_call(
        kernel,
        grid_spec=pltpu.PrefetchScalarGridSpec(
            num_scalar_prefetch=1,
            grid=(4,),
            in_specs=[
                rows,
                rows,
                pl.BlockSpec((16, None, 128, 256), lambda i, core: (0, core[0], 0, i)),
                pl.BlockSpec((16, None, 128, 256), lambda i, core: (0, 1 - core[0], 0, i)),
            ],
            out_specs=pl.BlockSpec((TOK, 256), lambda i, core: (0, i)),
        ),
        out_shape=jax.ShapeDtypeStruct((TOK, CH), F32),
        compiler_params=pltpu.CompilerParams(vmem_limit_bytes=VMEM_LIMIT),
        cost_estimate=SMALL,
        name="back_project",
    )(core.astype(jnp.int32).reshape(1), keep, give, w, w)


def on_device(grad_out, x, z, b, c, dt, rate, skip, gain, w_out):
    zi, xl, core, yi, xh = (lax.axis_index(a) for a in ("z", "xl", "c", "y", "xh"))
    scan = (x, z, b.reshape(TOK, 128), c.reshape(TOK, 128), dt, rate[None], skip[None], gain[None])

    w = lax.all_gather(w_out, DP, axis=0, tiled=True).reshape(16, 2, 128, CH)

    own = own_first(grad_out, core)
    below, above = both_ways(own, own, "y")
    other = send(own, "xh", 1)
    below, above, other, late = tie((below, above, other, scan[6]))

    b_other = send(other, "y", 1)
    far_own = send(above, "y", -1)
    a_other = send(above, "xh", 1)
    ys, normed = scan_forward(*scan[:6], late, scan[7])
    b_other, far_own, a_other, normed = tie((b_other, far_own, a_other, normed))

    far_b, far_a = both_ways(b_other[:32], a_other[32:], "y")
    normed_other = send(normed, "c", 1)
    far_b, far_a, normed_other = tie((far_b, far_a, normed_other))
    pieces = (own, other, below, b_other, above, a_other, far_own, far_b, far_a)
    give = place_tokens(yi, xh, 2048, *pieces)
    theirs = send(give, "c", 1)
    keep = place_tokens(yi, xh, 0, *tie(pieces, give))
    theirs, keep = tie((theirs, keep))

    def blocks(*shifts):
        return weight_blocks(zi, shifts, keep, theirs, normed, normed_other)

    half = CH // 2
    far = blocks(4)[0].astype(BF16)
    up, down = both_ways(far[:, half:], far[:, :half], "z")
    v = blocks(3, -3)
    up, down, v = tie((up, down, v))

    up = jnp.concatenate([v[0, :, :half], v[0, :, half:] + up.astype(F32)], axis=1).astype(BF16)
    down = jnp.concatenate([v[1, :, :half] + down.astype(F32), v[1, :, half:]], axis=1).astype(BF16)
    up, down = both_ways(up, down, "z")
    upstream = back_project(core, keep, give, w)
    v = blocks(2, -2)
    up, down, v, upstream = tie((up, down, v, upstream))

    up, down = both_ways((v[0] + up.astype(F32)).astype(BF16), (v[1] + down.astype(F32)).astype(BF16), "z")
    dx, dz, db, dc, ddt, small = scan_backward(upstream, ys, *scan)
    v = blocks(1, -1)
    up, down, v, small = tie((up, down, v, small))

    up, down = both_ways((v[0] + up.astype(F32)).astype(BF16), (v[1] + down.astype(F32)).astype(BF16), "z")
    small = small + send(small, "c", 1)
    small = small + send(small, "xl", 1)
    total = blocks(0)[0]
    up, down, small, total = tie((up, down, small, total))
    total = (total + (up.astype(F32) + down.astype(F32))).reshape(2, 128, CH)
    stay = lax.dynamic_index_in_dim(total, xl, 0, keepdims=False)
    leave = lax.dynamic_index_in_dim(total, 1 - xl, 0, keepdims=False)
    small, leave = tie((small, leave))
    arrived = send(leave, "xl", 1)
    for mask in (1, 2, 4):
        small = small + swap(small, "z", mask)
    arrived, = tie((arrived,), small)
    grad_weight = stay + arrived
    return (dx, dz, db[:, None], dc[:, None], ddt, small[8, :HEADS], small[9, :HEADS],
            small[:8].reshape(CH), grad_weight)


def solution(mesh):
    fine = jax.sharding.Mesh(mesh.devices.reshape(tuple(AXES.values())), tuple(AXES))
    part = P(DP, TP)
    part3 = P(DP, TP, None)
    head = P(TP)
    return jax.shard_map(
        on_device,
        mesh=fine,
        in_specs=(P(DP + TP, None), part, part, part3, part3, part, head, head, head, part),
        out_specs=(part, part, part3, part3, part, head, head, head, part),
        check_vma=False,
    )
```

profile of v0, /device:TPU:2, one launch (start us, length us, event | category | flops | bytes accessed | tf_op | source)
XLA Modules:
  0.0 189.8 jit_solution(14878517375930797258)
XLA Ops:
  7.2 0.7 all-gather.2.cloned.1.call-update
  7.9 2.0 %own_first.1.refs_0_ = bf16[64,4096]{1,0:T(8,128)(2,1)} custom-call(s32[1]{0:T(128)} %bitcast.3.core_ref, bf16[64,4096]{1,0:T(8,128)(2,1)} %in_ref.1), custom_call_target="tpu_custom_call" | custom-call | flops 1000 | bytes 1000 | tf_op jit(solution)/shard_map/own_first/pallas_call | solution.py:410
  9.9 2.1 %collective-permute-start.2 = (bf16[64,4096]{1,0:T(8,128)(2,1)}, bf16[64,4096]{1,0:T(8,128)(2,1)}, u32[]{:S(2)}, u32[]{:S(2)}) collective-permute-start(bf16[64,4096]{1,0:T(8,128)(2,1)} %own_first.1.refs_0_), channel_id=1, source_target_pairs={{0,1},{1,0},{2,3},{3,2},{4,5},{5,4},{6,7},{7,6},{8,9},{9,8},{10,11... | collective-permute-start | bytes 1572872 | tf_op jit(solution)/shard_map/ppermute | solution.py:361
  12.0 3.0 %collective-permute-start.1 = (bf16[64,4096]{1,0:T(8,128)(2,1)}, bf16[64,4096]{1,0:T(8,128)(2,1)}, u32[]{:S(2)}, u32[]{:S(2)}) collective-permute-start(bf16[64,4096]{1,0:T(8,128)(2,1)} %own_first.1.refs_0_), channel_id=1, source_target_pairs={{0,6},{2,0},{4,2},{6,4},{1,7},{3,1},{5,3},{7,5},{8,14},{10,8},{12,... | collective-permute-start | bytes 1572872 | tf_op jit(solution)/shard_map/ppermute | solution.py:361
  15.0 10.3 %collective-permute-done.2.refs_1_ = bf16[64,4096]{1,0:T(8,128)(2,1)} collective-permute-done((bf16[64,4096]{1,0:T(8,128)(2,1)}, bf16[64,4096]{1,0:T(8,128)(2,1)}, u32[]{:S(2)}, u32[]{:S(2)}) %collective-permute-start.2) | collective-permute-done | bytes 524320 | tf_op jit(solution)/shard_map/ppermute | solution.py:361
  25.4 0.9 collective-permute-done.1.refs_4_
  26.3 3.3 %collective-permute-done.refs_2_ = bf16[64,4096]{1,0:T(8,128)(2,1)S(1)} collective-permute-done((bf16[64,4096]{1,0:T(8,128)(2,1)}, bf16[64,4096]{1,0:T(8,128)(2,1)S(1)}, u32[]{:S(2)}, u32[]{:S(2)}) %collective-permute-start) | collective-permute-done | bytes 524320 | tf_op jit(solution)/shard_map/ppermute | solution.py:361
  29.6 1.4 collective-permute-start.5
  31.0 3.2 %collective-permute-start.4 = (bf16[64,4096]{1,0:T(8,128)(2,1)}, bf16[64,4096]{1,0:T(8,128)(2,1)}, u32[]{:S(2)}, u32[]{:S(2)}) collective-permute-start(bf16[64,4096]{1,0:T(8,128)(2,1)} %collective-permute-done.1.refs_4_), channel_id=1, source_target_pairs={{0,6},{2,0},{4,2},{6,4},{1,7},{3,1},{5,3},{7,5},{8,14},{10,8},{12,... | collective-permute-start | bytes 1572872 | tf_op jit(solution)/shard_map/ppermute | solution.py:361
  34.2 0.9 copy.19.dt_ref
  35.1 1.2 copy-done.13
  36.3 0.9 copy-done.16
  37.2 0.9 copy-done.18
  38.2 0.7 copy-done.22
  38.8 0.7 copy-done.24
  39.5 0.7 copy-done.26
  40.2 8.4 %scan_forward.1 = (f32[512,1024]{1,0:T(8,128)S(1)}, bf16[512,1024]{1,0:T(8,128)(2,1)S(1)}) custom-call(bf16[512,1024]{1,0:T(8,128)(2,1)S(1)} %copy-done.11, bf16[512,1024]{1,0:T(8,128)(2,1)S(1)} %copy-done.13, bf16[512,128]{1,0:T(8,128)(2,1)S(1)} %bitcast.62, bf16[512,128]{1,0:T(8,128)(2,1)S(1)} %bitcast.64, f32[512,16]{1,0:T(8,128)S(1)} %copy.19.dt_ref, ...), custom_call_target="tpu_custom_call" | custom-call | flops 1000 | bytes 1000 | tf_op jit(solution)/shard_map/scan_forward/pallas_call | solution.py:308
  48.6 1.3 copy-done.15
  49.9 6.4 %collective-permute-done.5.refs_5_ = bf16[64,4096]{1,0:T(8,128)(2,1)S(1)} collective-permute-done((bf16[64,4096]{1,0:T(8,128)(2,1)}, bf16[64,4096]{1,0:T(8,128)(2,1)S(1)}, u32[]{:S(2)}, u32[]{:S(2)}) %collective-permute-start.5) | collective-permute-done | bytes 524320 | tf_op jit(solution)/shard_map/ppermute | solution.py:361
  56.3 0.8 slice.47
  57.1 0.7 slice.48
  57.8 3.1 %collective-permute-start.7 = (bf16[32,4096]{1,0:T(8,128)(2,1)}, bf16[32,4096]{1,0:T(8,128)(2,1)}, u32[]{:S(2)}, u32[]{:S(2)}) collective-permute-start(bf16[32,4096]{1,0:T(8,128)(2,1)} %slice.48), channel_id=1, source_target_pairs={{0,6},{2,0},{4,2},{6,4},{1,7},{3,1},{5,3},{7,5},{8,14},{10,8},{12,... | collective-permute-start | bytes 786440 | tf_op jit(solution)/shard_map/ppermute | solution.py:361
  60.9 0.6 pad_add_fusion.s_ref
  61.5 5.9 %collective-permute-done.7.refs_8_ = bf16[32,4096]{1,0:T(8,128)(2,1)} collective-permute-done((bf16[32,4096]{1,0:T(8,128)(2,1)}, bf16[32,4096]{1,0:T(8,128)(2,1)}, u32[]{:S(2)}, u32[]{:S(2)}) %collective-permute-start.7) | collective-permute-done | bytes 262176 | tf_op jit(solution)/shard_map/ppermute | solution.py:361
  67.4 3.4 %collective-permute-done.6.refs_7_ = bf16[32,4096]{1,0:T(8,128)(2,1)} collective-permute-done((bf16[32,4096]{1,0:T(8,128)(2,1)}, bf16[32,4096]{1,0:T(8,128)(2,1)}, u32[]{:S(2)}, u32[]{:S(2)}) %collective-permute-start.6) | collective-permute-done | bytes 262176 | tf_op jit(solution)/shard_map/ppermute | solution.py:361
  70.8 3.6 %place_tokens.2.b_ref = bf16[512,2048]{1,0:T(8,128)(2,1)} custom-call(s32[2]{0:T(128)} %pad_add_fusion.s_ref, bf16[64,4096]{1,0:T(8,128)(2,1)} %own_first.1.refs_0_, bf16[64,4096]{1,0:T(8,128)(2,1)} %collective-permute-done.2.refs_1_, bf16[64,4096]{1,0:T(8,128)(2,1)} %copy-done.30, bf16[64,4096]{1,0:T(8,128)(2,1)} %copy-done.28, ...), custom_call_target="tpu_custom_call" | custom-call | flops 1000 | bytes 1000 | tf_op jit(solution)/shard_map/place_tokens/pallas_call | solution.py:390
  74.5 3.6 %place_tokens.3.a_ref = bf16[512,2048]{1,0:T(8,128)(2,1)} custom-call(s32[2]{0:T(128)} %pad_add_fusion.s_ref, bf16[64,4096]{1,0:T(8,128)(2,1)} %own_first.1.refs_0_, bf16[64,4096]{1,0:T(8,128)(2,1)} %collective-permute-done.2.refs_1_, bf16[64,4096]{1,0:T(8,128)(2,1)} %copy-done.30, bf16[64,4096]{1,0:T(8,128)(2,1)} %copy-done.28, ...), custom_call_target="tpu_custom_call" | custom-call | flops 1000 | bytes 1000 | tf_op jit(solution)/shard_map/place_tokens/pallas_call | solution.py:390
  78.1 0.9 collective-permute-done.9.b_ref
  79.0 1.6 copy-done
  80.6 1.7 weight_blocks.5
  82.4 6.1 %collective-permute-start.11 = (bf16[256,512]{1,0:T(8,128)(2,1)S(1)}, bf16[256,512]{1,0:T(8,128)(2,1)S(1)}, u32[]{:S(2)}, u32[]{:S(2)}) collective-permute-start(bf16[256,512]{1,0:T(8,128)(2,1)S(1)} %get-tuple-element.122), channel_id=1, source_target_pairs={{0,224},{32,0},{64,32},{96,64},{128,96},{160,128},{192,160},{224,1... | collective-permute-start | bytes 786440 | tf_op jit(solution)/shard_map/ppermute | solution.py:361
  88.6 3.1 %weight_blocks.6 = f32[2,256,1024]{2,1,0:T(8,128)S(1)} custom-call(s32[2]{0:T(128)S(1)} %pad_add_fusion.1.at_ref, bf16[512,2048]{1,0:T(8,128)(2,1)} %place_tokens.3.a_ref, bf16[512,2048]{1,0:T(8,128)(2,1)} %collective-permute-done.9.b_ref, bf16[512,1024]{1,0:T(8,128)(2,1)S(1)} %get-tuple-element.65.n_ref, bf16[512,1024]{1,0:T(8,128)(2,1)S(1)} %collective-permute-done.8.m_ref), custom_call_target="tpu_custom_call" | custom-call | flops 1000 | bytes 1000 | tf_op jit(solution)/shard_map/weight_blocks/pallas_call | solution.py:447
  91.7 2.6 %collective-permute-done.11 = bf16[256,512]{1,0:T(8,128)(2,1)S(1)} collective-permute-done((bf16[256,512]{1,0:T(8,128)(2,1)S(1)}, bf16[256,512]{1,0:T(8,128)(2,1)S(1)}, u32[]{:S(2)}, u32[]{:S(2)}) %collective-permute-start.11) | collective-permute-done | bytes 262176 | tf_op jit(solution)/shard_map/ppermute | solution.py:361
  94.4 3.4 %collective-permute-done.10 = bf16[256,512]{1,0:T(8,128)(2,1)S(1)} collective-permute-done((bf16[256,512]{1,0:T(8,128)(2,1)S(1)}, bf16[256,512]{1,0:T(8,128)(2,1)S(1)}, u32[]{:S(2)}, u32[]{:S(2)}) %collective-permute-start.10) | collective-permute-done | bytes 262176 | tf_op jit(solution)/shard_map/ppermute | solution.py:361
  98.1 0.9 pad_maximum_fusion
  99.0 0.9 pad_maximum_fusion.1
  99.9 3.2 %collective-permute-start.13 = (bf16[256,1024]{1,0:T(8,128)(2,1)}, bf16[256,1024]{1,0:T(8,128)(2,1)}, u32[]{:S(2)}, u32[]{:S(2)}) collective-permute-start(bf16[256,1024]{1,0:T(8,128)(2,1)} %pad_maximum_fusion.1), channel_id=1, source_target_pairs={{0,224},{32,0},{64,32},{96,64},{128,96},{160,128},{192,160},{224,1... | collective-permute-start | bytes 1572872 | tf_op jit(solution)/shard_map/ppermute | solution.py:361
  103.2 1.2 copy-done.4
  104.4 3.2 %weight_blocks.7 = f32[2,256,1024]{2,1,0:T(8,128)S(1)} custom-call(s32[2]{0:T(128)S(1)} %pad_add_fusion.2.at_ref, bf16[512,2048]{1,0:T(8,128)(2,1)} %place_tokens.3.a_ref, bf16[512,2048]{1,0:T(8,128)(2,1)} %collective-permute-done.9.b_ref, bf16[512,1024]{1,0:T(8,128)(2,1)S(1)} %get-tuple-element.65.n_ref, bf16[512,1024]{1,0:T(8,128)(2,1)S(1)} %copy-done.4), custom_call_target="tpu_custom_call" | custom-call | flops 1000 | bytes 1000 | tf_op jit(solution)/shard_map/weight_blocks/pallas_call | solution.py:447
  107.6 1.3 copy-done.9
  109.0 8.0 %back_project.1.u_ref = f32[512,1024]{1,0:T(8,128)S(1)} custom-call(s32[1]{0:T(128)} %bitcast.3.core_ref, bf16[512,2048]{1,0:T(8,128)(2,1)S(1)} %copy-done.1, bf16[512,2048]{1,0:T(8,128)(2,1)} %place_tokens.2.b_ref, bf16[16,2,128,1024]{3,2,1,0:T(8,128)(2,1)} %bitcast.72, bf16[16,2,128,1024]{3,2,1,0:T(8,128)(2,1)} %bitcast.73), custom_call_target="tpu_custom_call" | custom-call | flops 1000 | bytes 1000 | tf_op jit(solution)/shard_map/back_project/pallas_call | solution.py:467
  117.0 3.1 %fusion.2 = (bf16[256,1024]{1,0:T(8,128)(2,1)}, bf16[256,1024]{1,0:T(8,128)(2,1)S(1)}) fusion(bf16[256,1024]{1,0:T(8,128)(2,1)} %collective-permute-done.13, f32[2,256,1024]{2,1,0:T(8,128)S(1)} %copy-done.10, bf16[256,1024]{1,0:T(8,128)(2,1)} %collective-permute-done.12), kind=kLoop, calls=%fused_computation.5 | loop fusion | flops 1572864 | bytes 4194304 | tf_op jit(solution)/shard_map/convert_element_type | solution.py:529
  120.3 1.9 collective-permute-start.14
  122.3 3.4 %weight_blocks.8 = f32[2,256,1024]{2,1,0:T(8,128)S(1)} custom-call(s32[2]{0:T(128)S(1)} %pad_add_fusion.3.at_ref, bf16[512,2048]{1,0:T(8,128)(2,1)} %place_tokens.3.a_ref, bf16[512,2048]{1,0:T(8,128)(2,1)} %collective-permute-done.9.b_ref, bf16[512,1024]{1,0:T(8,128)(2,1)S(1)} %get-tuple-element.65.n_ref, bf16[512,1024]{1,0:T(8,128)(2,1)S(1)} %copy-done.5), custom_call_target="tpu_custom_call" | custom-call | flops 1000 | bytes 1000 | tf_op jit(solution)/shard_map/weight_blocks/pallas_call | solution.py:447
  125.8 18.1 %scan_backward.1 = (bf16[512,1024]{1,0:T(8,128)(2,1)}, bf16[512,1024]{1,0:T(8,128)(2,1)}, bf16[512,128]{1,0:T(8,128)(2,1)}, bf16[512,128]{1,0:T(8,128)(2,1)}, f3...) custom-call(f32[512,1024]{1,0:T(8,128)S(1)} %copy-done.8, f32[512,1024]{1,0:T(8,128)} %copy-done.15, ...), custom_call_target="tpu_custom_call" | custom-call | flops 1000 | bytes 1000 | tf_op jit(solution)/shard_map/scan_backward/pallas_call | solution.py:326
  143.9 0.8 copy-done.31
  144.7 2.7 %fusion = (bf16[256,1024]{1,0:T(8,128)(2,1)}, bf16[256,1024]{1,0:T(8,128)(2,1)}) fusion(bf16[256,1024]{1,0:T(8,128)(2,1)} %copy-done.31, f32[2,256,1024]{2,1,0:T(8,128)S(1)} %weight_blocks.8, bf16[256,1024]{1,0:T(8,128)(2,1)} %collective-permute-done.14), kind=kLoop, calls=%fused_computation.1 | loop fusion | flops 1572864 | bytes 4194304 | tf_op jit(solution)/shard_map/convert_element_type | solution.py:534
  147.4 1.4 collective-permute-start.17
  148.8 0.7 collective-permute-start.16
  149.4 1.2 collective-permute-done.18
  150.6 1.8 collective-permute-start.19
  152.4 1.2 copy-done.6
  153.6 1.7 weight_blocks.9
  155.4 4.0 %collective-permute-done.17 = bf16[256,1024]{1,0:T(8,128)(2,1)} collective-permute-done((bf16[256,1024]{1,0:T(8,128)(2,1)}, bf16[256,1024]{1,0:T(8,128)(2,1)}, u32[]{:S(2)}, u32[]{:S(2)}) %collective-permute-start.17) | collective-permute-done | bytes 524320 | tf_op jit(solution)/shard_map/ppermute | solution.py:361
  159.3 2.4 %collective-permute-done.16 = bf16[256,1024]{1,0:T(8,128)(2,1)} collective-permute-done((bf16[256,1024]{1,0:T(8,128)(2,1)}, bf16[256,1024]{1,0:T(8,128)(2,1)}, u32[]{:S(2)}, u32[]{:S(2)}) %collective-permute-start.16) | collective-permute-done | bytes 524320 | tf_op jit(solution)/shard_map/ppermute | solution.py:361
  161.8 1.5 add_add_fusion
  163.3 1.9 %collective-permute-start.23 = (f32[128,1024]{1,0:T(8,128)S(1)}, f32[128,1024]{1,0:T(8,128)S(1)}, u32[]{:S(2)}, u32[]{:S(2)}) collective-permute-start(f32[128,1024]{1,0:T(8,128)S(1)} %dynamic-slice_bitcast_fusion), channel_id=1, source_target_pairs={{0,16},{16,0},{1,17},{17,1},{2,18},{18,2},{3,19},{19,3},{4,20},{20... | collective-permute-start | bytes 1572872 | tf_op jit(solution)/shard_map/ppermute | solution.py:361
  165.2 3.6 %collective-permute-done.20 = f32[16,128]{1,0:T(8,128)S(1)} collective-permute-done((f32[16,128]{1,0:T(8,128)S(1)}, f32[16,128]{1,0:T(8,128)S(1)}, u32[]{:S(2)}, u32[]{:S(2)}) %collective-permute-start.20) | collective-permute-done | bytes 8224 | tf_op jit(solution)/shard_map/ppermute | solution.py:365
  168.9 4.5 %collective-permute-done.21 = f32[16,128]{1,0:T(8,128)S(1)} collective-permute-done((f32[16,128]{1,0:T(8,128)S(1)}, f32[16,128]{1,0:T(8,128)S(1)}, u32[]{:S(2)}, u32[]{:S(2)}) %collective-permute-start.21) | collective-permute-done | bytes 8224 | tf_op jit(solution)/shard_map/ppermute | solution.py:365
  173.5 0.7 copy.21
  174.2 6.8 %collective-permute-done.22 = f32[16,128]{1,0:T(8,128)S(1)} collective-permute-done((f32[16,128]{1,0:T(8,128)S(1)}, f32[16,128]{1,0:T(8,128)S(1)}, u32[]{:S(2)}, u32[]{:S(2)}) %collective-permute-start.22) | collective-permute-done | bytes 8224 | tf_op jit(solution)/shard_map/ppermute | solution.py:365
  181.0 0.5 slice_bitcast_fusion.3
  181.5 0.6 slice_bitcast_fusion.2
  182.1 0.9 bitcast_add_fusion.4
  (89 shorter events, 1.2 us)
Async XLA Ops:
  7.2 27.9 %copy-start.11 = (bf16[512,1024]{1,0:T(8,128)(2,1)S(1)}, bf16[512,1024]{1,0:T(8,128)(2,1)}, u32[]{:S(2)}) copy-start(bf16[512,1024]{1,0:T(8,128)(2,1)} %x_ref.3) | copy-start | bytes 3145732
  7.2 101.8 %all-gather.2.cloned.1.call-start = ((), (), s32[]{:S(2)}) async-start(), calls=%async_computation | async-start | bytes 8650752 | tf_op jit(solution)/shard_map/all_gather | solution.py:491
  9.9 15.5 %collective-permute-start.2 = (bf16[64,4096]{1,0:T(8,128)(2,1)}, bf16[64,4096]{1,0:T(8,128)(2,1)}, u32[]{:S(2)}, u32[]{:S(2)}) collective-permute-start(bf16[64,4096]{1,0:T(8,128)(2,1)} %own_first.1.refs_0_), channel_id=1, source_target_pairs={{0,1},{1,0},{2,3},{3,2},{4,5},{5,4},{6,7},{7,6},{8,9},{9,8},{10,11... | collective-permute-start | bytes 1572872 | tf_op jit(solution)/shard_map/ppermute | solution.py:361
  12.0 14.2 %collective-permute-start.1 = (bf16[64,4096]{1,0:T(8,128)(2,1)}, bf16[64,4096]{1,0:T(8,128)(2,1)}, u32[]{:S(2)}, u32[]{:S(2)}) collective-permute-start(bf16[64,4096]{1,0:T(8,128)(2,1)} %own_first.1.refs_0_), channel_id=1, source_target_pairs={{0,6},{2,0},{4,2},{6,4},{1,7},{3,1},{5,3},{7,5},{8,14},{10,8},{12,... | collective-permute-start | bytes 1572872 | tf_op jit(solution)/shard_map/ppermute | solution.py:361
  15.0 14.5 %collective-permute-start = (bf16[64,4096]{1,0:T(8,128)(2,1)}, bf16[64,4096]{1,0:T(8,128)(2,1)S(1)}, u32[]{:S(2)}, u32[]{:S(2)}) collective-permute-start(bf16[64,4096]{1,0:T(8,128)(2,1)} %own_first.1.refs_0_), channel_id=1, source_target_pairs={{0,2},{2,4},{4,6},{6,0},{1,3},{3,5},{5,7},{7,1},{8,10},{10,12},{12... | collective-permute-start | bytes 1572872 | tf_op jit(solution)/shard_map/ppermute | solution.py:361
  29.6 5.5 %copy-start.30 = (bf16[64,4096]{1,0:T(8,128)(2,1)}, bf16[64,4096]{1,0:T(8,128)(2,1)S(1)}, u32[]{:S(2)}) copy-start(bf16[64,4096]{1,0:T(8,128)(2,1)S(1)} %collective-permute-done.refs_2_) | copy-start | bytes 1572868
  29.6 20.4 %collective-permute-start.3 = (bf16[64,4096]{1,0:T(8,128)(2,1)}, bf16[64,4096]{1,0:T(8,128)(2,1)S(1)}, u32[]{:S(2)}, u32[]{:S(2)}) collective-permute-start(bf16[64,4096]{1,0:T(8,128)(2,1)} %collective-permute-done.2.refs_1_), channel_id=1, source_target_pairs={{0,2},{2,4},{4,6},{6,0},{1,3},{3,5},{5,7},{7,1},{8,10},{10,12},{12... | collective-permute-start | bytes 1572872 | tf_op jit(solution)/shard_map/ppermute | solution.py:361
  29.6 26.7 %collective-permute-start.5 = (bf16[64,4096]{1,0:T(8,128)(2,1)}, bf16[64,4096]{1,0:T(8,128)(2,1)S(1)}, u32[]{:S(2)}, u32[]{:S(2)}) collective-permute-start(bf16[64,4096]{1,0:T(8,128)(2,1)} %collective-permute-done.1.refs_4_), channel_id=1, source_target_pairs={{0,1},{1,0},{2,3},{3,2},{4,5},{5,4},{6,7},{7,6},{8,9},{9,8},{10,11... | collective-permute-start | bytes 1572872 | tf_op jit(solution)/shard_map/ppermute | solution.py:361
  31.0 25.3 %collective-permute-start.4 = (bf16[64,4096]{1,0:T(8,128)(2,1)}, bf16[64,4096]{1,0:T(8,128)(2,1)}, u32[]{:S(2)}, u32[]{:S(2)}) collective-permute-start(bf16[64,4096]{1,0:T(8,128)(2,1)} %collective-permute-done.1.refs_4_), channel_id=1, source_target_pairs={{0,6},{2,0},{4,2},{6,4},{1,7},{3,1},{5,3},{7,5},{8,14},{10,8},{12,... | collective-permute-start | bytes 1572872 | tf_op jit(solution)/shard_map/ppermute | solution.py:361
  35.1 1.2 copy-start.13
  36.3 0.9 copy-start.16
  37.2 0.9 copy-start.18
  38.2 0.7 copy-start.22
  38.8 0.7 copy-start.24
  39.5 0.7 copy-start.26
  48.6 1.3 copy-start.15
  49.9 20.9 %copy-start.28 = (bf16[64,4096]{1,0:T(8,128)(2,1)}, bf16[64,4096]{1,0:T(8,128)(2,1)S(1)}, u32[]{:S(2)}) copy-start(bf16[64,4096]{1,0:T(8,128)(2,1)S(1)} %collective-permute-done.3.refs_3_) | copy-start | bytes 1572868
  56.3 14.5 %copy-start.29 = (bf16[64,4096]{1,0:T(8,128)(2,1)}, bf16[64,4096]{1,0:T(8,128)(2,1)S(1)}, u32[]{:S(2)}) copy-start(bf16[64,4096]{1,0:T(8,128)(2,1)S(1)} %collective-permute-done.5.refs_5_) | copy-start | bytes 1572868
  56.3 14.5 %collective-permute-start.8 = (bf16[512,1024]{1,0:T(8,128)(2,1)S(1)}, bf16[512,1024]{1,0:T(8,128)(2,1)S(1)}, u32[]{:S(2)}, u32[]{:S(2)}) collective-permute-start(bf16[512,1024]{1,0:T(8,128)(2,1)S(1)} %get-tuple-element.65.n_ref), channel_id=1, source_target_pairs={{0,8},{8,0},{1,9},{9,1},{2,10},{10,2},{3,11},{11,3},{4,12},{12,4},... | collective-permute-start | bytes 3145736 | tf_op jit(solution)/shard_map/ppermute | solution.py:361
  57.8 9.6 %collective-permute-start.7 = (bf16[32,4096]{1,0:T(8,128)(2,1)}, bf16[32,4096]{1,0:T(8,128)(2,1)}, u32[]{:S(2)}, u32[]{:S(2)}) collective-permute-start(bf16[32,4096]{1,0:T(8,128)(2,1)} %slice.48), channel_id=1, source_target_pairs={{0,6},{2,0},{4,2},{6,4},{1,7},{3,1},{5,3},{7,5},{8,14},{10,8},{12,... | collective-permute-start | bytes 786440 | tf_op jit(solution)/shard_map/ppermute | solution.py:361
  60.9 9.9 %collective-permute-start.6 = (bf16[32,4096]{1,0:T(8,128)(2,1)}, bf16[32,4096]{1,0:T(8,128)(2,1)}, u32[]{:S(2)}, u32[]{:S(2)}) collective-permute-start(bf16[32,4096]{1,0:T(8,128)(2,1)} %slice.47), channel_id=1, source_target_pairs={{0,2},{2,4},{4,6},{6,0},{1,3},{3,5},{5,7},{7,1},{8,10},{10,12},{12... | collective-permute-start | bytes 786440 | tf_op jit(solution)/shard_map/ppermute | solution.py:361
  70.8 17.8 %copy-start.3 = (bf16[512,1024]{1,0:T(8,128)(2,1)}, bf16[512,1024]{1,0:T(8,128)(2,1)S(1)}, u32[]{:S(2)}) copy-start(bf16[512,1024]{1,0:T(8,128)(2,1)S(1)} %collective-permute-done.8.m_ref) | copy-start | bytes 3145732
  74.4 4.6 %collective-permute-start.9 = (bf16[512,2048]{1,0:T(8,128)(2,1)}, bf16[512,2048]{1,0:T(8,128)(2,1)}, u32[]{:S(2)}, u32[]{:S(2)}) collective-permute-start(bf16[512,2048]{1,0:T(8,128)(2,1)} %place_tokens.2.b_ref), channel_id=1, source_target_pairs={{0,8},{8,0},{1,9},{9,1},{2,10},{10,2},{3,11},{11,3},{4,12},{12,4},... | collective-permute-start | bytes 6291464 | tf_op jit(solution)/shard_map/ppermute | solution.py:361
  79.0 1.6 copy-start
  82.4 11.9 %collective-permute-start.11 = (bf16[256,512]{1,0:T(8,128)(2,1)S(1)}, bf16[256,512]{1,0:T(8,128)(2,1)S(1)}, u32[]{:S(2)}, u32[]{:S(2)}) collective-permute-start(bf16[256,512]{1,0:T(8,128)(2,1)S(1)} %get-tuple-element.122), channel_id=1, source_target_pairs={{0,224},{32,0},{64,32},{96,64},{128,96},{160,128},{192,160},{224,1... | collective-permute-start | bytes 786440 | tf_op jit(solution)/shard_map/ppermute | solution.py:361
  88.5 9.2 %collective-permute-start.10 = (bf16[256,512]{1,0:T(8,128)(2,1)S(1)}, bf16[256,512]{1,0:T(8,128)(2,1)S(1)}, u32[]{:S(2)}, u32[]{:S(2)}) collective-permute-start(bf16[256,512]{1,0:T(8,128)(2,1)S(1)} %get-tuple-element.123), channel_id=1, source_target_pairs={{0,32},{32,64},{64,96},{96,128},{128,160},{160,192},{192,224},{224... | collective-permute-start | bytes 786440 | tf_op jit(solution)/shard_map/ppermute | solution.py:361
  99.0 18.0 %collective-permute-start.12 = (bf16[256,1024]{1,0:T(8,128)(2,1)}, bf16[256,1024]{1,0:T(8,128)(2,1)}, u32[]{:S(2)}, u32[]{:S(2)}) collective-permute-start(bf16[256,1024]{1,0:T(8,128)(2,1)} %pad_maximum_fusion), channel_id=1, source_target_pairs={{0,32},{32,64},{64,96},{96,128},{128,160},{160,192},{192,224},{224... | collective-permute-start | bytes 1572872 | tf_op jit(solution)/shard_map/ppermute | solution.py:361
  99.9 17.1 %collective-permute-start.13 = (bf16[256,1024]{1,0:T(8,128)(2,1)}, bf16[256,1024]{1,0:T(8,128)(2,1)}, u32[]{:S(2)}, u32[]{:S(2)}) collective-permute-start(bf16[256,1024]{1,0:T(8,128)(2,1)} %pad_maximum_fusion.1), channel_id=1, source_target_pairs={{0,224},{32,0},{64,32},{96,64},{128,96},{160,128},{192,160},{224,1... | collective-permute-start | bytes 1572872 | tf_op jit(solution)/shard_map/ppermute | solution.py:361
  103.2 1.2 copy-start.4
  104.4 4.5 %copy-start.1 = (bf16[512,2048]{1,0:T(8,128)(2,1)S(1)}, bf16[512,2048]{1,0:T(8,128)(2,1)}, u32[]{:S(2)}) copy-start(bf16[512,2048]{1,0:T(8,128)(2,1)} %place_tokens.3.a_ref) | copy-start | bytes 6291460
  107.6 1.3 copy-start.9
  108.9 8.1 %copy-start.10 = (f32[2,256,1024]{2,1,0:T(8,128)S(1)}, f32[2,256,1024]{2,1,0:T(8,128)}, u32[]{:S(2)}) copy-start(f32[2,256,1024]{2,1,0:T(8,128)} %copy-done.9) | copy-start | bytes 6291460
  117.0 3.2 %copy-start.7 = (f32[512,1024]{1,0:T(8,128)}, f32[512,1024]{1,0:T(8,128)S(1)}, u32[]{:S(2)}) copy-start(f32[512,1024]{1,0:T(8,128)S(1)} %back_project.1.u_ref) | copy-start | bytes 6291460
  117.0 5.3 %copy-start.5 = (bf16[512,1024]{1,0:T(8,128)(2,1)S(1)}, bf16[512,1024]{1,0:T(8,128)(2,1)}, u32[]{:S(2)}) copy-start(bf16[512,1024]{1,0:T(8,128)(2,1)} %copy-done.3) | copy-start | bytes 3145732
  120.1 23.7 %collective-permute-start.15 = (bf16[256,1024]{1,0:T(8,128)(2,1)}, bf16[256,1024]{1,0:T(8,128)(2,1)S(1)}, u32[]{:S(2)}, u32[]{:S(2)}) collective-permute-start(bf16[256,1024]{1,0:T(8,128)(2,1)} %get-tuple-element.116), channel_id=1, source_target_pairs={{0,224},{32,0},{64,32},{96,64},{128,96},{160,128},{192,160},{224,1... | collective-permute-start | bytes 1572872 | tf_op jit(solution)/shard_map/ppermute | solution.py:361
  120.3 23.6 %collective-permute-start.14 = (bf16[256,1024]{1,0:T(8,128)(2,1)S(1)}, bf16[256,1024]{1,0:T(8,128)(2,1)}, u32[]{:S(2)}, u32[]{:S(2)}) collective-permute-start(bf16[256,1024]{1,0:T(8,128)(2,1)S(1)} %get-tuple-element.117), channel_id=1, source_target_pairs={{0,32},{32,64},{64,96},{96,128},{128,160},{160,192},{192,224},{224... | collective-permute-start | bytes 1572872 | tf_op jit(solution)/shard_map/ppermute | solution.py:361
  122.2 3.5 %copy-start.8 = (f32[512,1024]{1,0:T(8,128)S(1)}, f32[512,1024]{1,0:T(8,128)}, u32[]{:S(2)}) copy-start(f32[512,1024]{1,0:T(8,128)} %copy-done.7) | copy-start | bytes 6291460
  122.2 3.5 %copy-start.12 = (bf16[512,1024]{1,0:T(8,128)(2,1)S(1)}, bf16[512,1024]{1,0:T(8,128)(2,1)}, u32[]{:S(2)}) copy-start(bf16[512,1024]{1,0:T(8,128)(2,1)} %x_ref.3) | copy-start | bytes 3145732
  122.2 3.5 %copy-start.14 = (bf16[512,1024]{1,0:T(8,128)(2,1)S(1)}, bf16[512,1024]{1,0:T(8,128)(2,1)}, u32[]{:S(2)}) copy-start(bf16[512,1024]{1,0:T(8,128)(2,1)} %z_ref.3) | copy-start | bytes 3145732
  122.2 3.5 %copy-start.17 = (bf16[512,1,128]{2,0,1:T(8,128)(2,1)S(1)}, bf16[512,1,128]{2,0,1:T(8,128)(2,1)}, u32[]{:S(2)}) copy-start(bf16[512,1,128]{2,0,1:T(8,128)(2,1)} %param.13) | copy-start | bytes 393220
  122.3 3.5 %copy-start.19 = (bf16[512,1,128]{2,0,1:T(8,128)(2,1)S(1)}, bf16[512,1,128]{2,0,1:T(8,128)(2,1)}, u32[]{:S(2)}) copy-start(bf16[512,1,128]{2,0,1:T(8,128)(2,1)} %param.14) | copy-start | bytes 393220
  122.3 3.5 %copy-start.23 = (f32[1024]{0:T(1024)S(1)}, f32[1024]{0:T(1024)}, u32[]{:S(2)}) copy-start(f32[1024]{0:T(1024)} %param.18) | copy-start | bytes 12292
  122.3 3.5 %copy-start.25 = (f32[16]{0:T(128)S(1)}, f32[16]{0:T(128)}, u32[]{:S(2)}) copy-start(f32[16]{0:T(128)} %param.16) | copy-start | bytes 196
  122.3 3.5 %copy-start.27 = (f32[16]{0:T(128)S(1)}, f32[16]{0:T(128)}, u32[]{:S(2)}) copy-start(f32[16]{0:T(128)} %param.17) | copy-start | bytes 196
  143.9 3.5 %copy-start.20 = (f32[512,16]{1,0:T(8,128)}, f32[512,16]{1,0:T(8,128)S(1)}, u32[]{:S(2)}) copy-start(f32[512,16]{1,0:T(8,128)S(1)} %get-tuple-element.109) | copy-start | bytes 98308
  143.9 0.8 copy-start.31
  144.7 7.7 %copy-start.2 = (bf16[512,2048]{1,0:T(8,128)(2,1)S(1)}, bf16[512,2048]{1,0:T(8,128)(2,1)}, u32[]{:S(2)}) copy-start(bf16[512,2048]{1,0:T(8,128)(2,1)} %place_tokens.3.a_ref) | copy-start | bytes 6291460
  147.4 11.9 %collective-permute-start.17 = (bf16[256,1024]{1,0:T(8,128)(2,1)}, bf16[256,1024]{1,0:T(8,128)(2,1)}, u32[]{:S(2)}, u32[]{:S(2)}) collective-permute-start(bf16[256,1024]{1,0:T(8,128)(2,1)} %get-tuple-element.114), channel_id=1, source_target_pairs={{0,224},{32,0},{64,32},{96,64},{128,96},{160,128},{192,160},{224,1... | collective-permute-start | bytes 1572872 | tf_op jit(solution)/shard_map/ppermute | solution.py:361
  148.8 13.0 %collective-permute-start.16 = (bf16[256,1024]{1,0:T(8,128)(2,1)}, bf16[256,1024]{1,0:T(8,128)(2,1)}, u32[]{:S(2)}, u32[]{:S(2)}) collective-permute-start(bf16[256,1024]{1,0:T(8,128)(2,1)} %get-tuple-element.115), channel_id=1, source_target_pairs={{0,32},{32,64},{64,96},{96,128},{128,160},{160,192},{192,224},{224... | collective-permute-start | bytes 1572872 | tf_op jit(solution)/shard_map/ppermute | solution.py:361
  149.4 1.2 collective-permute-start.18
  150.6 4.7 %collective-permute-start.19 = (f32[16,128]{1,0:T(8,128)S(1)}, f32[16,128]{1,0:T(8,128)S(1)}, u32[]{:S(2)}, u32[]{:S(2)}) collective-permute-start(f32[16,128]{1,0:T(8,128)S(1)} %add.140), channel_id=1, source_target_pairs={{0,16},{16,0},{1,17},{17,1},{2,18},{18,2},{3,19},{19,3},{4,20},{20... | collective-permute-start | bytes 24584 | tf_op jit(solution)/shard_map/ppermute | solution.py:361
  152.4 1.2 copy-start.6
  161.8 11.7 %copy-start.21 = (f32[512,16]{1,0:T(8,128)S(1)}, f32[512,16]{1,0:T(8,128)}, u32[]{:S(2)}) copy-start(f32[512,16]{1,0:T(8,128)} %copy-done.20) | copy-start | bytes 98308
  163.3 18.8 %collective-permute-start.23 = (f32[128,1024]{1,0:T(8,128)S(1)}, f32[128,1024]{1,0:T(8,128)S(1)}, u32[]{:S(2)}, u32[]{:S(2)}) collective-permute-start(f32[128,1024]{1,0:T(8,128)S(1)} %dynamic-slice_bitcast_fusion), channel_id=1, source_target_pairs={{0,16},{16,0},{1,17},{17,1},{2,18},{18,2},{3,19},{19,3},{4,20},{20... | collective-permute-start | bytes 1572872 | tf_op jit(solution)/shard_map/ppermute | solution.py:361
  165.2 3.7 %collective-permute-start.20 = (f32[16,128]{1,0:T(8,128)S(1)}, f32[16,128]{1,0:T(8,128)S(1)}, u32[]{:S(2)}, u32[]{:S(2)}) collective-permute-start(f32[16,128]{1,0:T(8,128)S(1)} %add.141), channel_id=1, source_target_pairs={{0,32},{32,0},{64,96},{96,64},{128,160},{160,128},{192,224},{224,1... | collective-permute-start | bytes 24584 | tf_op jit(solution)/shard_map/ppermute | solution.py:365
  168.9 4.5 %collective-permute-start.21 = (f32[16,128]{1,0:T(8,128)S(1)}, f32[16,128]{1,0:T(8,128)S(1)}, u32[]{:S(2)}, u32[]{:S(2)}) collective-permute-start(f32[16,128]{1,0:T(8,128)S(1)} %add.147), channel_id=1, source_target_pairs={{0,64},{32,96},{64,0},{96,32},{128,192},{160,224},{192,128},{224,1... | collective-permute-start | bytes 24584 | tf_op jit(solution)/shard_map/ppermute | solution.py:365
  173.4 7.6 %collective-permute-start.22 = (f32[16,128]{1,0:T(8,128)S(1)}, f32[16,128]{1,0:T(8,128)S(1)}, u32[]{:S(2)}, u32[]{:S(2)}) collective-permute-start(f32[16,128]{1,0:T(8,128)S(1)} %add.148), channel_id=1, source_target_pairs={{0,128},{32,160},{64,192},{96,224},{128,0},{160,32},{192,64},{224,... | collective-permute-start | bytes 24584 | tf_op jit(solution)/shard_map/ppermute | solution.py:365
Sparse Core Ops, SparseCore 0:
  9.9 84.7 all-gather.1
where the time goes:
time: 191 us; the launch traced here: 190 us
  waiting for transfers between devices  60.4 us (32%)
  Pallas kernels  56.7 us (30%)
  starting transfers between devices  30.1 us (16%)
  local copies, waits for them, and re-layouts  16.9 us (9%)
  between operations  14.5 us (8%)
  other arithmetic  11.1 us (6%)
    ppermute x21, waiting for transfers between devices, send(): return lax.ppermute(v, axis, [(i, (i + shift) % n) for i in range(n)])  44.7 us
    ppermute x21, starting transfers between devices, send(): return lax.ppermute(v, axis, [(i, (i + shift) % n) for i in range(n)])  30.1 us
    pallas_call x1, Pallas kernels, scan_backward(): pl.pallas_call(bwd_kernel, out_shape=(jax.ShapeDtypeStruct((TOK, CH), BF1...  18.1 us
    ppermute x3, waiting for transfers between devices, swap(): return lax.ppermute(v, axis, [(i, i ^ mask) for i in range(AXES[axis])])  15 us
    unnamed x66, local copies, waits for them, and re-layouts  14.2 us
    pallas_call x5, Pallas kernels, weight_blocks(): pl.pallas_call(kernel, grid_spec=pltpu.PrefetchScalarGridSpec(num_scalar_...  13.1 us
    pallas_call x1, Pallas kernels, scan_forward(): pl.pallas_call(fwd_kernel, out_shape=(jax.ShapeDtypeStruct((TOK, CH), F32...  8.43 us
    pallas_call x1, Pallas kernels, back_project(): pl.pallas_call(kernel, grid_spec=pltpu.PrefetchScalarGridSpec(num_scalar_...  8 us
  transfers between devices with their start and end apart: 25, of which 15 were waited for; matrix products, arithmetic and copies ran while one was open for 4% of the time, Pallas kernels for 30%

commit v1 on v0

--- a/solution.py
+++ b/solution.py
@@ -13,7 +13,7 @@
 HALF = 128
 LOG2E = 1.4426950408889634
 BIG = 126.0
-VMEM_LIMIT = 48 * 1024 * 1024
+MIB = 1024 * 1024
 SMALL = pl.CostEstimate(flops=1000, bytes_accessed=1000, transcendentals=0)
 
 
@@ -316,7 +316,7 @@
             pltpu.VMEM((2, SPAN, SPAN), F32),
             pltpu.VMEM((TOK, CH), F32),
         ],
-        compiler_params=pltpu.CompilerParams(vmem_limit_bytes=VMEM_LIMIT),
+        compiler_params=pltpu.CompilerParams(vmem_limit_bytes=28 * MIB),
         cost_estimate=SMALL,
         name="scan_forward",
     )(x, z, b, c, dt, rate, skip, gain)
@@ -345,7 +345,7 @@
             pltpu.VMEM((2, SPAN, SPAN), F32),
             pltpu.VMEM((8, CH), F32),
         ],
-        compiler_params=pltpu.CompilerParams(vmem_limit_bytes=VMEM_LIMIT),
+        compiler_params=pltpu.CompilerParams(vmem_limit_bytes=36 * MIB),
         cost_estimate=SMALL,
         name="scan_backward",
     )(u, ys, x, z, b, c, dt, rate, skip, gain)
@@ -423,7 +423,7 @@
 
 def place_tokens(yi, xh, first, *pieces):
     parts = ((0, 64, 0, 0, 0), (1, 64, 0, 1, 0), (2, 64, 3, 0, 0), (3, 64, 3, 1, 0), (4, 64, 1, 0, 0),
-             (5, 64, 1, 1, 0), (6, 64, 2, 0, 0), (7, 32, 2, 1, 0), (8, 32, 2, 1, 32))
+             (5, 64, 1, 1, 0), (6, 32, 2, 0, 0), (7, 32, 2, 0, 32), (8, 32, 2, 1, 0), (9, 32, 2, 1, 32))
 
     def plan(s):
         moves = []
@@ -453,7 +453,7 @@
             out_specs=pl.BlockSpec((1, 256, CH), lambda i, at: (i, 0, 0)),
         ),
         out_shape=jax.ShapeDtypeStruct((len(shifts), 256, CH), F32),
-        compiler_params=pltpu.CompilerParams(vmem_limit_bytes=VMEM_LIMIT),
+        compiler_params=pltpu.CompilerParams(vmem_limit_bytes=16 * MIB),
         cost_estimate=SMALL,
         name="weight_blocks",
     )(jnp.stack([(zi + k + 8) % 8 for k in shifts]).astype(jnp.int32), keep, theirs, normed, normed_other)
@@ -478,7 +478,7 @@
             out_specs=pl.BlockSpec((TOK, 256), lambda i, core: (0, i)),
         ),
         out_shape=jax.ShapeDtypeStruct((TOK, CH), F32),
-        compiler_params=pltpu.CompilerParams(vmem_limit_bytes=VMEM_LIMIT),
+        compiler_params=pltpu.CompilerParams(vmem_limit_bytes=24 * MIB),
         cost_estimate=SMALL,
         name="back_project",
     )(core.astype(jnp.int32).reshape(1), keep, give, w, w)
@@ -495,16 +495,15 @@
     other = send(own, "xh", 1)
     below, above, other, late = tie((below, above, other, scan[6]))
 
-    b_other = send(other, "y", 1)
-    far_own = send(above, "y", -1)
-    a_other = send(above, "xh", 1)
+    b_other, a_other = both_ways(other, other, "y")
+    far_b, far_a = both_ways(below[:32], above[32:], "y")
     ys, normed = scan_forward(*scan[:6], late, scan[7])
-    b_other, far_own, a_other, normed = tie((b_other, far_own, a_other, normed))
-
-    far_b, far_a = both_ways(b_other[:32], a_other[32:], "y")
+    b_other, a_other, far_b, far_a, normed = tie((b_other, a_other, far_b, far_a, normed))
+
+    far_other = both_ways(b_other[:32], a_other[32:], "y")
     normed_other = send(normed, "c", 1)
-    far_b, far_a, normed_other = tie((far_b, far_a, normed_other))
-    pieces = (own, other, below, b_other, above, a_other, far_own, far_b, far_a)
+    far_other, normed_other = tie((far_other, normed_other))
+    pieces = (own, other, below, b_other, above, a_other, far_b, far_a) + far_other
     give = place_tokens(yi, xh, 2048, *pieces)
     theirs = send(give, "c", 1)
     keep = place_tokens(yi, xh, 0, *tie(pieces, give))
@@ -516,35 +515,36 @@
     half = CH // 2
     far = blocks(4)[0].astype(BF16)
     up, down = both_ways(far[:, half:], far[:, :half], "z")
-    v = blocks(3, -3)
+    v = blocks(3, -3, 2, -2)
     up, down, v = tie((up, down, v))
 
     up = jnp.concatenate([v[0, :, :half], v[0, :, half:] + up.astype(F32)], axis=1).astype(BF16)
     down = jnp.concatenate([v[1, :, :half] + down.astype(F32), v[1, :, half:]], axis=1).astype(BF16)
     up, down = both_ways(up, down, "z")
+    last = blocks(1, -1, 0)
     upstream = back_project(core, keep, give, w)
-    v = blocks(2, -2)
-    up, down, v, upstream = tie((up, down, v, upstream))
-
-    up, down = both_ways((v[0] + up.astype(F32)).astype(BF16), (v[1] + down.astype(F32)).astype(BF16), "z")
+    up, down, last, upstream = tie((up, down, last, upstream))
+
+    up, down = both_ways((v[2] + up.astype(F32)).astype(BF16), (v[3] + down.astype(F32)).astype(BF16), "z")
     dx, dz, db, dc, ddt, small = scan_backward(upstream, ys, *scan)
-    v = blocks(1, -1)
-    up, down, v, small = tie((up, down, v, small))
-
-    up, down = both_ways((v[0] + up.astype(F32)).astype(BF16), (v[1] + down.astype(F32)).astype(BF16), "z")
+    up, down, small = tie((up, down, small))
+
+    def halves(r):
+        return lax.dynamic_slice_in_dim(r, (1 - xl) * 128, 128, 0), lax.dynamic_slice_in_dim(r, xl * 128, 128, 0)
+
+    up_leave, up_stay = halves((last[0] + up.astype(F32)).astype(BF16))
+    down_leave, down_stay = halves((last[1] + down.astype(F32)).astype(BF16))
+    up_leave, down_leave = both_ways(up_leave, down_leave, "z")
+    up_stay, down_stay = both_ways(up_stay, down_stay, "z")
     small = small + send(small, "c", 1)
     small = small + send(small, "xl", 1)
-    total = blocks(0)[0]
-    up, down, small, total = tie((up, down, small, total))
-    total = (total + (up.astype(F32) + down.astype(F32))).reshape(2, 128, CH)
-    stay = lax.dynamic_index_in_dim(total, xl, 0, keepdims=False)
-    leave = lax.dynamic_index_in_dim(total, 1 - xl, 0, keepdims=False)
-    small, leave = tie((small, leave))
-    arrived = send(leave, "xl", 1)
+    leave, stay = halves(last[2])
+    up_leave, down_leave, small = tie((up_leave, down_leave, small))
+    leave = send(leave + (up_leave.astype(F32) + down_leave.astype(F32)), "xl", 1)
     for mask in (1, 2, 4):
         small = small + swap(small, "z", mask)
-    arrived, = tie((arrived,), small)
-    grad_weight = stay + arrived
+    up_stay, down_stay, leave, stay = tie((up_stay, down_stay, leave, stay), small)
+    grad_weight = (stay + leave) + (up_stay.astype(F32) + down_stay.astype(F32))
     return (dx, dz, db[:, None], dc[:, None], ddt, small[8, :HEADS], small[9, :HEADS],
             small[:8].reshape(CH), grad_weight)
 

time: 191 us -> 183 us (0.958)
  waiting for transfers between devices: 60.4 us -> 46.4 us
  local copies, waits for them, and re-layouts: 16.9 us -> 29.9 us
  Pallas kernels: 56.7 us -> 48.2 us
  starting transfers between devices: 30.1 us -> 32.3 us
    unnamed x66 -> x70, local copies, waits for them, and re-layouts: 14.2 us -> 24.3 us
    ppermute x21 -> x24, waiting for transfers between devices: 44.7 us -> 36.5 us  [send(): return lax.ppermute(v, axis, [(i, (i + shift) % n) for i in range(n)])]
    ppermute x3, waiting for transfers between devices: 15 us -> 9.24 us  [swap(): return lax.ppermute(v, axis, [(i, i ^ mask) for i in range(AXES[axis])])]
    pallas_call x5 -> x3, Pallas kernels: 13.1 us -> 7.61 us  [weight_blocks(): pl.pallas_call(kernel, grid_spec=pltpu.PrefetchScalarGridSpec(num_scalar_...]
    slice x2 -> x5, local copies, waits for them, and re-layouts: 1.49 us -> 3.47 us  [the longest x2 1.94 us: on_device(): far_other = both_ways(b_other[:32], a_other[32:], 'y')]
    ppermute x21 -> x24, starting transfers between devices: 30.1 us -> 30.5 us  [send(): return lax.ppermute(v, axis, [(i, (i + shift) % n) for i in range(n)])]
  transfers between devices with their start and end apart: 25 -> 28, of which waited for: 15 -> 17; matrix products, arithmetic and copies ran while one was open for 4% -> 6% of each run, Pallas kernels for 30% -> 27%
where the time goes in v1:
time: 183 us; the launch traced here: 181 us
  Pallas kernels  48.2 us (26%)
  waiting for transfers between devices  46.4 us (25%)
  starting transfers between devices  32.3 us (18%)
  local copies, waits for them, and re-layouts  29.9 us (16%)
  between operations  14.5 us (8%)
  other arithmetic  9.86 us (5%)
    ppermute x24, waiting for transfers between devices, send(): return lax.ppermute(v, axis, [(i, (i + shift) % n) for i in range(n)])  36.5 us
    ppermute x24, starting transfers between devices, send(): return lax.ppermute(v, axis, [(i, (i + shift) % n) for i in range(n)])  30.5 us
    unnamed x70, local copies, waits for them, and re-layouts  24.3 us
    pallas_call x1, Pallas kernels, scan_backward(): pl.pallas_call(bwd_kernel, out_shape=(jax.ShapeDtypeStruct((TOK, CH), BF1...  16.5 us
    ppermute x3, waiting for transfers between devices, swap(): return lax.ppermute(v, axis, [(i, i ^ mask) for i in range(AXES[axis])])  9.24 us
    pallas_call x1, Pallas kernels, scan_forward(): pl.pallas_call(fwd_kernel, out_shape=(jax.ShapeDtypeStruct((TOK, CH), F32...  8.57 us
    pallas_call x3, Pallas kernels, weight_blocks(): pl.pallas_call(kernel, grid_spec=pltpu.PrefetchScalarGridSpec(num_scalar_...  7.61 us
    pallas_call x2, Pallas kernels, shuffle(): pl.pallas_call(kernel, out_shape=tuple((jax.ShapeDtypeStruct(s, BF16) for...  7.21 us
  transfers between devices with their start and end apart: 28, of which 17 were waited for; matrix products, arithmetic and copies ran while one was open for 6% of the time, Pallas kernels for 27%

profile of v1, /device:TPU:2, one launch (start us, length us, event | category | flops | bytes accessed | tf_op | source)
XLA Modules:
  0.0 181.2 jit_solution(15329932111119211657)
XLA Ops:
  8.0 2.0 %own_first.1.refs_0_ = bf16[64,4096]{1,0:T(8,128)(2,1)} custom-call(s32[1]{0:T(128)} %bitcast.3.core_ref, bf16[64,4096]{1,0:T(8,128)(2,1)} %in_ref.1), custom_call_target="tpu_custom_call" | custom-call | flops 1000 | bytes 1000 | tf_op jit(solution)/shard_map/own_first/pallas_call | solution.py:410
  10.0 2.1 %collective-permute-start.2 = (bf16[64,4096]{1,0:T(8,128)(2,1)}, bf16[64,4096]{1,0:T(8,128)(2,1)}, u32[]{:S(2)}, u32[]{:S(2)}) collective-permute-start(bf16[64,4096]{1,0:T(8,128)(2,1)} %own_first.1.refs_0_), channel_id=1, source_target_pairs={{0,1},{1,0},{2,3},{3,2},{4,5},{5,4},{6,7},{7,6},{8,9},{9,8},{10,11... | collective-permute-start | bytes 1572872 | tf_op jit(solution)/shard_map/ppermute | solution.py:361
  12.1 3.0 %collective-permute-start.1 = (bf16[64,4096]{1,0:T(8,128)(2,1)}, bf16[64,4096]{1,0:T(8,128)(2,1)S(1)}, u32[]{:S(2)}, u32[]{:S(2)}) collective-permute-start(bf16[64,4096]{1,0:T(8,128)(2,1)} %own_first.1.refs_0_), channel_id=1, source_target_pairs={{0,6},{2,0},{4,2},{6,4},{1,7},{3,1},{5,3},{7,5},{8,14},{10,8},{12,... | collective-permute-start | bytes 1572872 | tf_op jit(solution)/shard_map/ppermute | solution.py:361
  15.1 10.3 %collective-permute-done.2.refs_1_ = bf16[64,4096]{1,0:T(8,128)(2,1)} collective-permute-done((bf16[64,4096]{1,0:T(8,128)(2,1)}, bf16[64,4096]{1,0:T(8,128)(2,1)}, u32[]{:S(2)}, u32[]{:S(2)}) %collective-permute-start.2) | collective-permute-done | bytes 524320 | tf_op jit(solution)/shard_map/ppermute | solution.py:361
  25.4 0.9 collective-permute-done.1.refs_4_
  26.3 3.3 %collective-permute-done.refs_2_ = bf16[64,4096]{1,0:T(8,128)(2,1)S(1)} collective-permute-done((bf16[64,4096]{1,0:T(8,128)(2,1)}, bf16[64,4096]{1,0:T(8,128)(2,1)S(1)}, u32[]{:S(2)}, u32[]{:S(2)}) %collective-permute-start) | collective-permute-done | bytes 524320 | tf_op jit(solution)/shard_map/ppermute | solution.py:361
  30.0 1.7 collective-permute-start.3
  33.1 1.6 collective-permute-start.6
  35.3 0.9 copy-done.24
  36.2 8.6 %scan_forward.1 = (f32[512,1024]{1,0:T(8,128)S(1)}, bf16[512,1024]{1,0:T(8,128)(2,1)S(1)}) custom-call(bf16[512,1024]{1,0:T(8,128)(2,1)S(1)} %copy-done.17, bf16[512,1024]{1,0:T(8,128)(2,1)S(1)} %copy-done.19, bf16[512,128]{1,0:T(8,128)(2,1)S(1)} %bitcast.61, bf16[512,128]{1,0:T(8,128)(2,1)S(1)} %bitcast.63, f32[512,16]{1,0:T(8,128)S(1)} %copy.19.dt_ref, ...), custom_call_target="tpu_custom_call" | custom-call | flops 1000 | bytes 1000 | tf_op jit(solution)/shard_map/scan_forward/pallas_call | solution.py:308
  44.8 1.3 copy-done.21
  46.2 1.6 collective-permute-done.6.refs_7_
  47.7 1.6 collective-permute-done.5.refs_6_
  49.3 1.0 slice.58
  50.3 1.0 slice.59
  51.7 1.6 collective-permute-start.7
  54.0 6.1 %collective-permute-done.8.refs_9_ = bf16[32,4096]{1,0:T(8,128)(2,1)S(1)} collective-permute-done((bf16[32,4096]{1,0:T(8,128)(2,1)S(1)}, bf16[32,4096]{1,0:T(8,128)(2,1)S(1)}, u32[]{:S(2)}, u32[]{:S(2)}) %collective-permute-start.8) | collective-permute-done | bytes 262176 | tf_op jit(solution)/shard_map/ppermute | solution.py:361
  60.1 1.3 collective-permute-done.7.refs_8_
  62.1 1.0 copy-done.10
  63.1 3.6 %place_tokens.2.b_ref = bf16[512,2048]{1,0:T(8,128)(2,1)} custom-call(s32[2]{0:T(128)} %pad_add_fusion.s_ref, bf16[64,4096]{1,0:T(8,128)(2,1)} %own_first.1.refs_0_, bf16[64,4096]{1,0:T(8,128)(2,1)} %collective-permute-done.2.refs_1_, bf16[64,4096]{1,0:T(8,128)(2,1)} %copy-done.30, bf16[64,4096]{1,0:T(8,128)(2,1)} %collective-permute-done.3.refs_3_, ...), custom_call_target="tpu_custom_call" | custom-call | flops 1000 | bytes 1000 | tf_op jit(solution)/shard_map/place_tokens/pallas_call | solution.py:390
  66.8 3.6 %place_tokens.3.a_ref = bf16[512,2048]{1,0:T(8,128)(2,1)} custom-call(s32[2]{0:T(128)} %pad_add_fusion.s_ref, bf16[64,4096]{1,0:T(8,128)(2,1)} %own_first.1.refs_0_, bf16[64,4096]{1,0:T(8,128)(2,1)} %collective-permute-done.2.refs_1_, bf16[64,4096]{1,0:T(8,128)(2,1)} %copy-done.30, bf16[64,4096]{1,0:T(8,128)(2,1)} %collective-permute-done.3.refs_3_, ...), custom_call_target="tpu_custom_call" | custom-call | flops 1000 | bytes 1000 | tf_op jit(solution)/shard_map/place_tokens/pallas_call | solution.py:390
  70.4 0.8 collective-permute-done.10.b_ref
  71.2 1.6 copy-done
  72.8 1.2 copy-done.11
  74.1 0.7 weight_blocks.3
  74.8 1.3 copy-done.5
  76.2 0.8 fusion.6
  77.0 5.9 %collective-permute-start.12 = (bf16[256,512]{1,0:T(8,128)(2,1)}, bf16[256,512]{1,0:T(8,128)(2,1)}, u32[]{:S(2)}, u32[]{:S(2)}) collective-permute-start(bf16[256,512]{1,0:T(8,128)(2,1)} %get-tuple-element.128), channel_id=1, source_target_pairs={{0,224},{32,0},{64,32},{96,64},{128,96},{160,128},{192,160},{224,1... | collective-permute-start | bytes 786440 | tf_op jit(solution)/shard_map/ppermute | solution.py:361
  83.0 1.6 copy-done.6
  84.6 1.2 copy-done.12
  85.8 3.8 %weight_blocks.4 = f32[4,256,1024]{2,1,0:T(8,128)S(1)} custom-call(s32[4]{0:T(128)S(1)} %pad_add_fusion.1.at_ref, bf16[512,2048]{1,0:T(8,128)(2,1)S(1)} %copy-done.1, bf16[512,2048]{1,0:T(8,128)(2,1)S(1)} %copy-done.6, bf16[512,1024]{1,0:T(8,128)(2,1)S(1)} %get-tuple-element.67.n_ref, bf16[512,1024]{1,0:T(8,128)(2,1)S(1)} %copy-done.12), custom_call_target="tpu_custom_call" | custom-call | flops 1000 | bytes 1000 | tf_op jit(solution)/shard_map/weight_blocks/pallas_call | solution.py:447
  89.7 2.7 %collective-permute-done.11 = bf16[256,512]{1,0:T(8,128)(2,1)} collective-permute-done((bf16[256,512]{1,0:T(8,128)(2,1)}, bf16[256,512]{1,0:T(8,128)(2,1)}, u32[]{:S(2)}, u32[]{:S(2)}) %collective-permute-start.11) | collective-permute-done | bytes 262176 | tf_op jit(solution)/shard_map/ppermute | solution.py:361
  92.8 1.2 fusion.4
  94.1 0.9 pad_maximum_fusion
  94.9 0.9 pad_maximum_fusion.1
  95.8 3.2 %collective-permute-start.14 = (bf16[256,1024]{1,0:T(8,128)(2,1)}, bf16[256,1024]{1,0:T(8,128)(2,1)}, u32[]{:S(2)}, u32[]{:S(2)}) collective-permute-start(bf16[256,1024]{1,0:T(8,128)(2,1)} %pad_maximum_fusion.1), channel_id=1, source_target_pairs={{0,224},{32,0},{64,32},{96,64},{128,96},{160,128},{192,160},{224,1... | collective-permute-start | bytes 1572872 | tf_op jit(solution)/shard_map/ppermute | solution.py:361
  99.1 1.6 copy-done.7
  100.7 1.2 copy-done.13
  101.9 3.0 %weight_blocks.5 = f32[3,256,1024]{2,1,0:T(8,128)S(1)} custom-call(s32[3]{0:T(128)S(1)} %pad_add_fusion.2.at_ref, bf16[512,2048]{1,0:T(8,128)(2,1)S(1)} %copy-done.1, bf16[512,2048]{1,0:T(8,128)(2,1)S(1)} %copy-done.7, bf16[512,1024]{1,0:T(8,128)(2,1)S(1)} %get-tuple-element.67.n_ref, bf16[512,1024]{1,0:T(8,128)(2,1)S(1)} %copy-done.13), custom_call_target="tpu_custom_call" | custom-call | flops 1000 | bytes 1000 | tf_op jit(solution)/shard_map/weight_blocks/pallas_call | solution.py:447
  105.0 1.6 copy-done.8
  106.6 3.4 %copy-done.2 = bf16[4096,1024]{1,0:T(8,128)(2,1)S(1)} copy-done((bf16[4096,1024]{1,0:T(8,128)(2,1)S(1)}, bf16[4096,1024]{1,0:T(8,128)(2,1)}, u32[]{:S(2)}) %copy-start.2) | copy-done | bytes 8388632
  110.0 1.6 copy-done.14
  111.6 6.4 %back_project.1.u_ref = f32[512,1024]{1,0:T(8,128)S(1)} custom-call(s32[1]{0:T(128)} %bitcast.3.core_ref, bf16[512,2048]{1,0:T(8,128)(2,1)S(1)} %copy-done.1, bf16[512,2048]{1,0:T(8,128)(2,1)S(1)} %copy-done.14, bf16[16,2,128,1024]{3,2,1,0:T(8,128)(2,1)S(1)} %bitcast.59, bf16[16,2,128,1024]{3,2,1,0:T(8,128)(2,1)S(1)} %bitcast.60), custom_call_target="tpu_custom_call" | custom-call | flops 1000 | bytes 1000 | tf_op jit(solution)/shard_map/back_project/pallas_call | solution.py:467
  118.0 3.2 %fusion.1 = (bf16[256,1024]{1,0:T(8,128)(2,1)}, bf16[256,1024]{1,0:T(8,128)(2,1)S(1)}) fusion(bf16[256,1024]{1,0:T(8,128)(2,1)} %collective-permute-done.14, f32[4,256,1024]{2,1,0:T(8,128)S(1)} %copy-done.4, bf16[256,1024]{1,0:T(8,128)(2,1)} %collective-permute-done.13), kind=kLoop, calls=%fused_computation.3 | loop fusion | flops 1572864 | bytes 4194304 | tf_op jit(solution)/shard_map/convert_element_type | solution.py:528
  121.2 0.9 collective-permute-start.16
  122.1 1.1 collective-permute-start.15
  123.2 1.6 copy-done.16
  124.8 1.6 copy-done.22
  126.4 16.5 %scan_backward.1 = (bf16[512,1024]{1,0:T(8,128)(2,1)}, bf16[512,1024]{1,0:T(8,128)(2,1)}, bf16[512,128]{1,0:T(8,128)(2,1)}, bf16[512,128]{1,0:T(8,128)(2,1)}, f3...) custom-call(f32[512,1024]{1,0:T(8,128)S(1)} %copy-done.16, f32[512,1024]{1,0:T(8,128)S(1)} %copy-done.22, ...), custom_call_target="tpu_custom_call" | custom-call | flops 1000 | bytes 1000 | tf_op jit(solution)/shard_map/scan_backward/pallas_call | solution.py:326
  142.9 1.6 fusion
  144.5 2.2 %collective-permute-start.18 = (bf16[128,1024]{1,0:T(8,128)(2,1)S(1)}, bf16[128,1024]{1,0:T(8,128)(2,1)S(1)}, u32[]{:S(2)}, u32[]{:S(2)}) collective-permute-start(bf16[128,1024]{1,0:T(8,128)(2,1)S(1)} %get-tuple-element.125), channel_id=1, source_target_pairs={{0,224},{32,0},{64,32},{96,64},{128,96},{160,128},{192,160},{224,1... | collective-permute-start | bytes 786440 | tf_op jit(solution)/shard_map/ppermute | solution.py:361
  147.0 1.2 collective-permute-done.19
  148.1 1.7 collective-permute-start.20
  149.9 1.9 %collective-permute-done.20 = f32[16,128]{1,0:T(8,128)S(1)} collective-permute-done((f32[16,128]{1,0:T(8,128)S(1)}, f32[16,128]{1,0:T(8,128)S(1)}, u32[]{:S(2)}, u32[]{:S(2)}) %collective-permute-start.20) | collective-permute-done | bytes 8224 | tf_op jit(solution)/shard_map/ppermute | solution.py:361
  151.8 2.6 %collective-permute-done.17 = bf16[128,1024]{1,0:T(8,128)(2,1)S(1)} collective-permute-done((bf16[128,1024]{1,0:T(8,128)(2,1)S(1)}, bf16[128,1024]{1,0:T(8,128)(2,1)S(1)}, u32[]{:S(2)}, u32[]{:S(2)}) %collective-permute-start.17) | collective-permute-done | bytes 262176 | tf_op jit(solution)/shard_map/ppermute | solution.py:361
  154.6 3.5 %collective-permute-done.21 = f32[16,128]{1,0:T(8,128)S(1)} collective-permute-done((f32[16,128]{1,0:T(8,128)S(1)}, f32[16,128]{1,0:T(8,128)S(1)}, u32[]{:S(2)}, u32[]{:S(2)}) %collective-permute-start.21) | collective-permute-done | bytes 8224 | tf_op jit(solution)/shard_map/ppermute | solution.py:365
  158.2 1.8 %collective-permute-start.26 = (f32[128,1024]{1,0:T(8,128)S(1)}, f32[128,1024]{1,0:T(8,128)S(1)}, u32[]{:S(2)}, u32[]{:S(2)}) collective-permute-start(f32[128,1024]{1,0:T(8,128)S(1)} %bitcast_add_fusion.4), channel_id=1, source_target_pairs={{0,16},{16,0},{1,17},{17,1},{2,18},{18,2},{3,19},{19,3},{4,20},{20... | collective-permute-start | bytes 1572872 | tf_op jit(solution)/shard_map/ppermute | solution.py:361
  160.0 2.6 %collective-permute-done.22 = f32[16,128]{1,0:T(8,128)S(1)} collective-permute-done((f32[16,128]{1,0:T(8,128)S(1)}, f32[16,128]{1,0:T(8,128)S(1)}, u32[]{:S(2)}, u32[]{:S(2)}) %collective-permute-start.22) | collective-permute-done | bytes 8224 | tf_op jit(solution)/shard_map/ppermute | solution.py:365
  162.7 1.7 collective-permute-start.23
  164.4 0.7 copy.21
  165.8 1.3 collective-permute-start.24
  167.2 3.1 %collective-permute-done.23 = f32[16,128]{1,0:T(8,128)S(1)} collective-permute-done((f32[16,128]{1,0:T(8,128)S(1)}, f32[16,128]{1,0:T(8,128)S(1)}, u32[]{:S(2)}, u32[]{:S(2)}) %collective-permute-start.23) | collective-permute-done | bytes 8224 | tf_op jit(solution)/shard_map/ppermute | solution.py:365
  171.5 1.9 %collective-permute-done.24 = bf16[128,1024]{1,0:T(8,128)(2,1)S(1)} collective-permute-done((bf16[128,1024]{1,0:T(8,128)(2,1)S(1)}, bf16[128,1024]{1,0:T(8,128)(2,1)S(1)}, u32[]{:S(2)}, u32[]{:S(2)}) %collective-permute-start.24) | collective-permute-done | bytes 262176 | tf_op jit(solution)/shard_map/ppermute | solution.py:361
  173.4 0.9 add_add_fusion
  (101 shorter events, 8.1 us)
Async XLA Ops:
  7.2 28.1 %copy-start.28 = (f32[16]{0:T(128)S(1)}, f32[16]{0:T(128)}, u32[]{:S(2)}) copy-start(f32[16]{0:T(128)} %param.17) | copy-start | bytes 196
  7.2 27.9 %copy-start.33 = (f32[512,16]{0,1:T(8,128)S(1)}, f32[512,16]{0,1:T(8,128)}, u32[]{:S(2)}) copy-start(f32[512,16]{0,1:T(8,128)} %param.15) | copy-start | bytes 98308
  7.2 28.1 %copy-start.19 = (bf16[512,1024]{1,0:T(8,128)(2,1)S(1)}, bf16[512,1024]{1,0:T(8,128)(2,1)}, u32[]{:S(2)}) copy-start(bf16[512,1024]{1,0:T(8,128)(2,1)} %z_ref.3) | copy-start | bytes 3145732
  7.2 28.1 %copy-start.17 = (bf16[512,1024]{1,0:T(8,128)(2,1)S(1)}, bf16[512,1024]{1,0:T(8,128)(2,1)}, u32[]{:S(2)}) copy-start(bf16[512,1024]{1,0:T(8,128)(2,1)} %x_ref.3) | copy-start | bytes 3145732
  7.2 28.1 %copy-start.26 = (f32[1024]{0:T(1024)S(1)}, f32[1024]{0:T(1024)}, u32[]{:S(2)}) copy-start(f32[1024]{0:T(1024)} %param.18) | copy-start | bytes 12292
  7.2 28.1 %copy-start.27 = (f32[16]{0:T(128)S(1)}, f32[16]{0:T(128)}, u32[]{:S(2)}) copy-start(f32[16]{0:T(128)} %param.16) | copy-start | bytes 196
  7.2 28.1 %copy-start.23 = (bf16[512,1,128]{2,0,1:T(8,128)(2,1)S(1)}, bf16[512,1,128]{2,0,1:T(8,128)(2,1)}, u32[]{:S(2)}) copy-start(bf16[512,1,128]{2,0,1:T(8,128)(2,1)} %param.13) | copy-start | bytes 393220
  7.3 99.3 %all-gather.2.cloned.1.call-start = ((), (), s32[]{:S(2)}) async-start(), calls=%async_computation | async-start | bytes 8650752 | tf_op jit(solution)/shard_map/all_gather | solution.py:491
  10.0 15.5 %collective-permute-start.2 = (bf16[64,4096]{1,0:T(8,128)(2,1)}, bf16[64,4096]{1,0:T(8,128)(2,1)}, u32[]{:S(2)}, u32[]{:S(2)}) collective-permute-start(bf16[64,4096]{1,0:T(8,128)(2,1)} %own_first.1.refs_0_), channel_id=1, source_target_pairs={{0,1},{1,0},{2,3},{3,2},{4,5},{5,4},{6,7},{7,6},{8,9},{9,8},{10,11... | collective-permute-start | bytes 1572872 | tf_op jit(solution)/shard_map/ppermute | solution.py:361
  12.1 14.2 %collective-permute-start.1 = (bf16[64,4096]{1,0:T(8,128)(2,1)}, bf16[64,4096]{1,0:T(8,128)(2,1)S(1)}, u32[]{:S(2)}, u32[]{:S(2)}) collective-permute-start(bf16[64,4096]{1,0:T(8,128)(2,1)} %own_first.1.refs_0_), channel_id=1, source_target_pairs={{0,6},{2,0},{4,2},{6,4},{1,7},{3,1},{5,3},{7,5},{8,14},{10,8},{12,... | collective-permute-start | bytes 1572872 | tf_op jit(solution)/shard_map/ppermute | solution.py:361
  15.1 14.5 %collective-permute-start = (bf16[64,4096]{1,0:T(8,128)(2,1)}, bf16[64,4096]{1,0:T(8,128)(2,1)S(1)}, u32[]{:S(2)}, u32[]{:S(2)}) collective-permute-start(bf16[64,4096]{1,0:T(8,128)(2,1)} %own_first.1.refs_0_), channel_id=1, source_target_pairs={{0,2},{2,4},{4,6},{6,0},{1,3},{3,5},{5,7},{7,1},{8,10},{10,12},{12... | collective-permute-start | bytes 1572872 | tf_op jit(solution)/shard_map/ppermute | solution.py:361
  26.3 8.3 %copy-start.29 = (bf16[64,4096]{1,0:T(8,128)(2,1)}, bf16[64,4096]{1,0:T(8,128)(2,1)S(1)}, u32[]{:S(2)}) copy-start(bf16[64,4096]{1,0:T(8,128)(2,1)S(1)} %collective-permute-done.1.refs_4_) | copy-start | bytes 1572868
  29.6 5.6 %copy-start.30 = (bf16[64,4096]{1,0:T(8,128)(2,1)}, bf16[64,4096]{1,0:T(8,128)(2,1)S(1)}, u32[]{:S(2)}) copy-start(bf16[64,4096]{1,0:T(8,128)(2,1)S(1)} %collective-permute-done.refs_2_) | copy-start | bytes 1572868
  29.6 19.7 %collective-permute-start.4 = (bf16[64,4096]{1,0:T(8,128)(2,1)}, bf16[64,4096]{1,0:T(8,128)(2,1)}, u32[]{:S(2)}, u32[]{:S(2)}) collective-permute-start(bf16[64,4096]{1,0:T(8,128)(2,1)} %collective-permute-done.2.refs_1_), channel_id=1, source_target_pairs={{0,6},{2,0},{4,2},{6,4},{1,7},{3,1},{5,3},{7,5},{8,14},{10,8},{12,... | collective-permute-start | bytes 1572872 | tf_op jit(solution)/shard_map/ppermute | solution.py:361
  30.0 19.3 %collective-permute-start.3 = (bf16[64,4096]{1,0:T(8,128)(2,1)}, bf16[64,4096]{1,0:T(8,128)(2,1)}, u32[]{:S(2)}, u32[]{:S(2)}) collective-permute-start(bf16[64,4096]{1,0:T(8,128)(2,1)} %collective-permute-done.2.refs_1_), channel_id=1, source_target_pairs={{0,2},{2,4},{4,6},{6,0},{1,3},{3,5},{5,7},{7,1},{8,10},{10,12},{12... | collective-permute-start | bytes 1572872 | tf_op jit(solution)/shard_map/ppermute | solution.py:361
  33.1 14.6 %collective-permute-start.6 = (bf16[32,4096]{1,0:T(8,128)(2,1)}, bf16[32,4096]{1,0:T(8,128)(2,1)}, u32[]{:S(2)}, u32[]{:S(2)}) collective-permute-start(bf16[32,4096]{1,0:T(8,128)(2,1)} %slice.57), channel_id=1, source_target_pairs={{0,6},{2,0},{4,2},{6,4},{1,7},{3,1},{5,3},{7,5},{8,14},{10,8},{12,... | collective-permute-start | bytes 786440 | tf_op jit(solution)/shard_map/ppermute | solution.py:361
  34.7 14.7 %collective-permute-start.5 = (bf16[32,4096]{1,0:T(8,128)(2,1)}, bf16[32,4096]{1,0:T(8,128)(2,1)}, u32[]{:S(2)}, u32[]{:S(2)}) collective-permute-start(bf16[32,4096]{1,0:T(8,128)(2,1)} %slice.56), channel_id=1, source_target_pairs={{0,2},{2,4},{4,6},{6,0},{1,3},{3,5},{5,7},{7,1},{8,10},{10,12},{12... | collective-permute-start | bytes 786440 | tf_op jit(solution)/shard_map/ppermute | solution.py:361
  35.3 0.9 copy-start.24
  44.8 1.3 copy-start.21
  49.3 12.1 %collective-permute-start.9 = (bf16[512,1024]{1,0:T(8,128)(2,1)S(1)}, bf16[512,1024]{1,0:T(8,128)(2,1)S(1)}, u32[]{:S(2)}, u32[]{:S(2)}) collective-permute-start(bf16[512,1024]{1,0:T(8,128)(2,1)S(1)} %get-tuple-element.67.n_ref), channel_id=1, source_target_pairs={{0,8},{8,0},{1,9},{9,1},{2,10},{10,2},{3,11},{11,3},{4,12},{12,4},... | collective-permute-start | bytes 3145736 | tf_op jit(solution)/shard_map/ppermute | solution.py:361
  51.3 8.8 %collective-permute-start.8 = (bf16[32,4096]{1,0:T(8,128)(2,1)S(1)}, bf16[32,4096]{1,0:T(8,128)(2,1)S(1)}, u32[]{:S(2)}, u32[]{:S(2)}) collective-permute-start(bf16[32,4096]{1,0:T(8,128)(2,1)S(1)} %slice.59), channel_id=1, source_target_pairs={{0,6},{2,0},{4,2},{6,4},{1,7},{3,1},{5,3},{7,5},{8,14},{10,8},{12,... | collective-permute-start | bytes 786440 | tf_op jit(solution)/shard_map/ppermute | solution.py:361
  51.7 9.6 %collective-permute-start.7 = (bf16[32,4096]{1,0:T(8,128)(2,1)S(1)}, bf16[32,4096]{1,0:T(8,128)(2,1)S(1)}, u32[]{:S(2)}, u32[]{:S(2)}) collective-permute-start(bf16[32,4096]{1,0:T(8,128)(2,1)S(1)} %slice.58), channel_id=1, source_target_pairs={{0,2},{2,4},{4,6},{6,0},{1,3},{3,5},{5,7},{7,1},{8,10},{10,12},{12... | collective-permute-start | bytes 786440 | tf_op jit(solution)/shard_map/ppermute | solution.py:361
  60.1 1.3 copy-start.31
  61.4 0.7 copy-start.32
  62.1 1.0 copy-start.10
  66.7 4.6 %collective-permute-start.10 = (bf16[512,2048]{1,0:T(8,128)(2,1)}, bf16[512,2048]{1,0:T(8,128)(2,1)S(1)}, u32[]{:S(2)}, u32[]{:S(2)}) collective-permute-start(bf16[512,2048]{1,0:T(8,128)(2,1)} %place_tokens.2.b_ref), channel_id=1, source_target_pairs={{0,8},{8,0},{1,9},{9,1},{2,10},{10,2},{3,11},{11,3},{4,12},{12,4},... | collective-permute-start | bytes 6291464 | tf_op jit(solution)/shard_map/ppermute | solution.py:361
  71.2 1.6 copy-start
  72.8 1.2 copy-start.11
  74.8 1.3 copy-start.5
  76.1 6.9 %copy-start.1 = (bf16[512,2048]{1,0:T(8,128)(2,1)S(1)}, bf16[512,2048]{1,0:T(8,128)(2,1)}, u32[]{:S(2)}) copy-start(bf16[512,2048]{1,0:T(8,128)(2,1)} %place_tokens.3.a_ref) | copy-start | bytes 6291460
  77.0 12.7 %collective-permute-start.12 = (bf16[256,512]{1,0:T(8,128)(2,1)}, bf16[256,512]{1,0:T(8,128)(2,1)}, u32[]{:S(2)}, u32[]{:S(2)}) collective-permute-start(bf16[256,512]{1,0:T(8,128)(2,1)} %get-tuple-element.128), channel_id=1, source_target_pairs={{0,224},{32,0},{64,32},{96,64},{128,96},{160,128},{192,160},{224,1... | collective-permute-start | bytes 786440 | tf_op jit(solution)/shard_map/ppermute | solution.py:361
  82.9 9.5 %collective-permute-start.11 = (bf16[256,512]{1,0:T(8,128)(2,1)}, bf16[256,512]{1,0:T(8,128)(2,1)}, u32[]{:S(2)}, u32[]{:S(2)}) collective-permute-start(bf16[256,512]{1,0:T(8,128)(2,1)} %get-tuple-element.129), channel_id=1, source_target_pairs={{0,32},{32,64},{64,96},{96,128},{128,160},{160,192},{192,224},{224... | collective-permute-start | bytes 786440 | tf_op jit(solution)/shard_map/ppermute | solution.py:361
  83.0 1.6 copy-start.6
  84.6 1.2 copy-start.12
  89.7 3.1 %copy-start.3 = (f32[4,256,1024]{2,1,0:T(8,128)}, f32[4,256,1024]{2,1,0:T(8,128)S(1)}, u32[]{:S(2)}) copy-start(f32[4,256,1024]{2,1,0:T(8,128)S(1)} %weight_blocks.4) | copy-start | bytes 12582916
  94.9 23.0 %collective-permute-start.13 = (bf16[256,1024]{1,0:T(8,128)(2,1)}, bf16[256,1024]{1,0:T(8,128)(2,1)}, u32[]{:S(2)}, u32[]{:S(2)}) collective-permute-start(bf16[256,1024]{1,0:T(8,128)(2,1)} %pad_maximum_fusion), channel_id=1, source_target_pairs={{0,32},{32,64},{64,96},{96,128},{128,160},{160,192},{192,224},{224... | collective-permute-start | bytes 1572872 | tf_op jit(solution)/shard_map/ppermute | solution.py:361
  95.8 22.2 %collective-permute-start.14 = (bf16[256,1024]{1,0:T(8,128)(2,1)}, bf16[256,1024]{1,0:T(8,128)(2,1)}, u32[]{:S(2)}, u32[]{:S(2)}) collective-permute-start(bf16[256,1024]{1,0:T(8,128)(2,1)} %pad_maximum_fusion.1), channel_id=1, source_target_pairs={{0,224},{32,0},{64,32},{96,64},{128,96},{160,128},{192,160},{224,1... | collective-permute-start | bytes 1572872 | tf_op jit(solution)/shard_map/ppermute | solution.py:361
  99.1 1.6 copy-start.7
  100.7 1.2 copy-start.13
  105.0 1.6 copy-start.8
  106.6 3.4 %copy-start.2 = (bf16[4096,1024]{1,0:T(8,128)(2,1)S(1)}, bf16[4096,1024]{1,0:T(8,128)(2,1)}, u32[]{:S(2)}) copy-start(bf16[4096,1024]{1,0:T(8,128)(2,1)} %all-gather.2.cloned.1.call-done) | copy-start | bytes 25165828
  110.0 1.6 copy-start.14
  111.6 6.4 %copy-start.4 = (f32[4,256,1024]{2,1,0:T(8,128)S(1)}, f32[4,256,1024]{2,1,0:T(8,128)}, u32[]{:S(2)}) copy-start(f32[4,256,1024]{2,1,0:T(8,128)} %copy-done.3) | copy-start | bytes 12582916
  117.9 3.2 %copy-start.15 = (f32[512,1024]{1,0:T(8,128)}, f32[512,1024]{1,0:T(8,128)S(1)}, u32[]{:S(2)}) copy-start(f32[512,1024]{1,0:T(8,128)S(1)} %back_project.1.u_ref) | copy-start | bytes 6291460
  117.9 5.3 %copy-start.18 = (bf16[512,1024]{1,0:T(8,128)(2,1)S(1)}, bf16[512,1024]{1,0:T(8,128)(2,1)}, u32[]{:S(2)}) copy-start(bf16[512,1024]{1,0:T(8,128)(2,1)} %x_ref.3) | copy-start | bytes 3145732
  117.9 5.3 %copy-start.20 = (bf16[512,1024]{1,0:T(8,128)(2,1)S(1)}, bf16[512,1024]{1,0:T(8,128)(2,1)}, u32[]{:S(2)}) copy-start(bf16[512,1024]{1,0:T(8,128)(2,1)} %z_ref.3) | copy-start | bytes 3145732
  118.0 5.3 %copy-start.25 = (bf16[512,1,128]{2,0,1:T(8,128)(2,1)S(1)}, bf16[512,1,128]{2,0,1:T(8,128)(2,1)}, u32[]{:S(2)}) copy-start(bf16[512,1,128]{2,0,1:T(8,128)(2,1)} %param.14) | copy-start | bytes 393220
  121.2 21.7 %collective-permute-start.16 = (bf16[256,1024]{1,0:T(8,128)(2,1)}, bf16[256,1024]{1,0:T(8,128)(2,1)}, u32[]{:S(2)}, u32[]{:S(2)}) collective-permute-start(bf16[256,1024]{1,0:T(8,128)(2,1)} %get-tuple-element.116), channel_id=1, source_target_pairs={{0,224},{32,0},{64,32},{96,64},{128,96},{160,128},{192,160},{224,1... | collective-permute-start | bytes 1572872 | tf_op jit(solution)/shard_map/ppermute | solution.py:361
  122.1 20.8 %collective-permute-start.15 = (bf16[256,1024]{1,0:T(8,128)(2,1)S(1)}, bf16[256,1024]{1,0:T(8,128)(2,1)}, u32[]{:S(2)}, u32[]{:S(2)}) collective-permute-start(bf16[256,1024]{1,0:T(8,128)(2,1)S(1)} %get-tuple-element.117), channel_id=1, source_target_pairs={{0,32},{32,64},{64,96},{96,128},{128,160},{160,192},{192,224},{224... | collective-permute-start | bytes 1572872 | tf_op jit(solution)/shard_map/ppermute | solution.py:361
  123.2 1.6 copy-start.16
  124.8 1.6 copy-start.22
  126.4 16.5 %copy-start.9 = (f32[3,256,1024]{2,1,0:T(8,128)S(1)}, f32[3,256,1024]{2,1,0:T(8,128)}, u32[]{:S(2)}) copy-start(f32[3,256,1024]{2,1,0:T(8,128)} %copy-done.8) | copy-start | bytes 9437188
  144.5 7.3 %collective-permute-start.18 = (bf16[128,1024]{1,0:T(8,128)(2,1)S(1)}, bf16[128,1024]{1,0:T(8,128)(2,1)S(1)}, u32[]{:S(2)}, u32[]{:S(2)}) collective-permute-start(bf16[128,1024]{1,0:T(8,128)(2,1)S(1)} %get-tuple-element.125), channel_id=1, source_target_pairs={{0,224},{32,0},{64,32},{96,64},{128,96},{160,128},{192,160},{224,1... | collective-permute-start | bytes 786440 | tf_op jit(solution)/shard_map/ppermute | solution.py:361
  146.8 7.7 %collective-permute-start.17 = (bf16[128,1024]{1,0:T(8,128)(2,1)S(1)}, bf16[128,1024]{1,0:T(8,128)(2,1)S(1)}, u32[]{:S(2)}, u32[]{:S(2)}) collective-permute-start(bf16[128,1024]{1,0:T(8,128)(2,1)S(1)} %get-tuple-element.127), channel_id=1, source_target_pairs={{0,32},{32,64},{64,96},{96,128},{128,160},{160,192},{192,224},{224... | collective-permute-start | bytes 786440 | tf_op jit(solution)/shard_map/ppermute | solution.py:361
  146.9 1.3 collective-permute-start.19
  148.1 3.7 %collective-permute-start.20 = (f32[16,128]{1,0:T(8,128)S(1)}, f32[16,128]{1,0:T(8,128)S(1)}, u32[]{:S(2)}, u32[]{:S(2)}) collective-permute-start(f32[16,128]{1,0:T(8,128)S(1)} %add.151), channel_id=1, source_target_pairs={{0,16},{16,0},{1,17},{17,1},{2,18},{18,2},{3,19},{19,3},{4,20},{20... | collective-permute-start | bytes 24584 | tf_op jit(solution)/shard_map/ppermute | solution.py:361
  154.5 3.7 %collective-permute-start.21 = (f32[16,128]{1,0:T(8,128)S(1)}, f32[16,128]{1,0:T(8,128)S(1)}, u32[]{:S(2)}, u32[]{:S(2)}) collective-permute-start(f32[16,128]{1,0:T(8,128)S(1)} %add.152), channel_id=1, source_target_pairs={{0,32},{32,0},{64,96},{96,64},{128,160},{160,128},{192,224},{224,1... | collective-permute-start | bytes 24584 | tf_op jit(solution)/shard_map/ppermute | solution.py:365
  158.1 4.6 %collective-permute-start.22 = (f32[16,128]{1,0:T(8,128)S(1)}, f32[16,128]{1,0:T(8,128)S(1)}, u32[]{:S(2)}, u32[]{:S(2)}) collective-permute-start(f32[16,128]{1,0:T(8,128)S(1)} %add.153), channel_id=1, source_target_pairs={{0,64},{32,96},{64,0},{96,32},{128,192},{160,224},{192,128},{224,1... | collective-permute-start | bytes 24584 | tf_op jit(solution)/shard_map/ppermute | solution.py:365
  158.2 15.2 %collective-permute-start.26 = (f32[128,1024]{1,0:T(8,128)S(1)}, f32[128,1024]{1,0:T(8,128)S(1)}, u32[]{:S(2)}, u32[]{:S(2)}) collective-permute-start(f32[128,1024]{1,0:T(8,128)S(1)} %bitcast_add_fusion.4), channel_id=1, source_target_pairs={{0,16},{16,0},{1,17},{17,1},{2,18},{18,2},{3,19},{19,3},{4,20},{20... | collective-permute-start | bytes 1572872 | tf_op jit(solution)/shard_map/ppermute | solution.py:361
  162.7 7.6 %collective-permute-start.23 = (f32[16,128]{1,0:T(8,128)S(1)}, f32[16,128]{1,0:T(8,128)S(1)}, u32[]{:S(2)}, u32[]{:S(2)}) collective-permute-start(f32[16,128]{1,0:T(8,128)S(1)} %add.154), channel_id=1, source_target_pairs={{0,128},{32,160},{64,192},{96,224},{128,0},{160,32},{192,64},{224,... | collective-permute-start | bytes 24584 | tf_op jit(solution)/shard_map/ppermute | solution.py:365
  165.1 6.4 %collective-permute-start.25 = (bf16[128,1024]{1,0:T(8,128)(2,1)S(1)}, bf16[128,1024]{1,0:T(8,128)(2,1)S(1)}, u32[]{:S(2)}, u32[]{:S(2)}) collective-permute-start(bf16[128,1024]{1,0:T(8,128)(2,1)S(1)} %get-tuple-element.124), channel_id=1, source_target_pairs={{0,224},{32,0},{64,32},{96,64},{128,96},{160,128},{192,160},{224,1... | collective-permute-start | bytes 786440 | tf_op jit(solution)/shard_map/ppermute | solution.py:361
  165.8 7.6 %collective-permute-start.24 = (bf16[128,1024]{1,0:T(8,128)(2,1)S(1)}, bf16[128,1024]{1,0:T(8,128)(2,1)S(1)}, u32[]{:S(2)}, u32[]{:S(2)}) collective-permute-start(bf16[128,1024]{1,0:T(8,128)(2,1)S(1)} %get-tuple-element.126), channel_id=1, source_target_pairs={{0,32},{32,64},{64,96},{96,128},{128,160},{160,192},{192,224},{224... | collective-permute-start | bytes 786440 | tf_op jit(solution)/shard_map/ppermute | solution.py:361
Sparse Core Ops, SparseCore 0:
  9.9 76.7 all-gather.1

commit v2 on v1

--- a/solution.py
+++ b/solution.py
@@ -13,7 +13,7 @@
 HALF = 128
 LOG2E = 1.4426950408889634
 BIG = 126.0
-MIB = 1024 * 1024
+VMEM_LIMIT = 48 * 1024 * 1024
 SMALL = pl.CostEstimate(flops=1000, bytes_accessed=1000, transcendentals=0)
 
 
@@ -316,7 +316,7 @@
             pltpu.VMEM((2, SPAN, SPAN), F32),
             pltpu.VMEM((TOK, CH), F32),
         ],
-        compiler_params=pltpu.CompilerParams(vmem_limit_bytes=28 * MIB),
+        compiler_params=pltpu.CompilerParams(vmem_limit_bytes=VMEM_LIMIT),
         cost_estimate=SMALL,
         name="scan_forward",
     )(x, z, b, c, dt, rate, skip, gain)
@@ -345,7 +345,7 @@
             pltpu.VMEM((2, SPAN, SPAN), F32),
             pltpu.VMEM((8, CH), F32),
         ],
-        compiler_params=pltpu.CompilerParams(vmem_limit_bytes=36 * MIB),
+        compiler_params=pltpu.CompilerParams(vmem_limit_bytes=VMEM_LIMIT),
         cost_estimate=SMALL,
         name="scan_backward",
     )(u, ys, x, z, b, c, dt, rate, skip, gain)
@@ -453,10 +453,51 @@
             out_specs=pl.BlockSpec((1, 256, CH), lambda i, at: (i, 0, 0)),
         ),
         out_shape=jax.ShapeDtypeStruct((len(shifts), 256, CH), F32),
-        compiler_params=pltpu.CompilerParams(vmem_limit_bytes=16 * MIB),
+        compiler_params=pltpu.CompilerParams(vmem_limit_bytes=VMEM_LIMIT),
         cost_estimate=SMALL,
         name="weight_blocks",
     )(jnp.stack([(zi + k + 8) % 8 for k in shifts]).astype(jnp.int32), keep, theirs, normed, normed_other)
+
+
+def ring_step(zi, shift, keep, theirs, normed, normed_other, up, down):
+    width = up.shape[1]
+    at = CH - width
+
+    def kernel(at_ref, a_ref, b_ref, n_ref, m_ref, up_ref, down_ref, up_out, down_out):
+        def term(r, n):
+            return lax.dot_general(r[...], n[...], (((0,), (0,)), ((), ())), preferred_element_type=F32)
+
+        total = term(a_ref, n_ref) + term(b_ref, m_ref)
+
+        @pl.when(pl.program_id(0) == 0)
+        def _():
+            if at:
+                up_out[:, :at] = total[:, :at].astype(BF16)
+            up_out[:, at:] = (total[:, at:] + up_ref[...].astype(F32)).astype(BF16)
+
+        @pl.when(pl.program_id(0) == 1)
+        def _():
+            if at:
+                down_out[:, width:] = total[:, width:].astype(BF16)
+            down_out[:, :width] = (total[:, :width] + down_ref[...].astype(F32)).astype(BF16)
+
+    columns = pl.BlockSpec((TOK, 256), lambda i, at: (0, at[i]))
+    whole = pl.BlockSpec((TOK, CH), lambda i, at: (0, 0))
+    part = pl.BlockSpec((256, width), lambda i, at: (0, 0))
+    full = pl.BlockSpec((256, CH), lambda i, at: (0, 0))
+    return pl.pallas_call(
+        kernel,
+        grid_spec=pltpu.PrefetchScalarGridSpec(
+            num_scalar_prefetch=1,
+            grid=(2,),
+            in_specs=[columns, columns, whole, whole, part, part],
+            out_specs=(full, full),
+        ),
+        out_shape=(jax.ShapeDtypeStruct((256, CH), BF16),) * 2,
+        compiler_params=pltpu.CompilerParams(vmem_limit_bytes=VMEM_LIMIT),
+        cost_estimate=SMALL,
+        name="ring_step",
+    )(jnp.stack([(zi + k + 8) % 8 for k in (shift, -shift)]).astype(jnp.int32), keep, theirs, normed, normed_other, up, down)
 
 
 def back_project(core, keep, give, w):
@@ -478,7 +519,7 @@
             out_specs=pl.BlockSpec((TOK, 256), lambda i, core: (0, i)),
         ),
         out_shape=jax.ShapeDtypeStruct((TOK, CH), F32),
-        compiler_params=pltpu.CompilerParams(vmem_limit_bytes=24 * MIB),
+        compiler_params=pltpu.CompilerParams(vmem_limit_bytes=VMEM_LIMIT),
         cost_estimate=SMALL,
         name="back_project",
     )(core.astype(jnp.int32).reshape(1), keep, give, w, w)
@@ -515,19 +556,19 @@
     half = CH // 2
     far = blocks(4)[0].astype(BF16)
     up, down = both_ways(far[:, half:], far[:, :half], "z")
-    v = blocks(3, -3, 2, -2)
-    up, down, v = tie((up, down, v))
-
-    up = jnp.concatenate([v[0, :, :half], v[0, :, half:] + up.astype(F32)], axis=1).astype(BF16)
-    down = jnp.concatenate([v[1, :, :half] + down.astype(F32), v[1, :, half:]], axis=1).astype(BF16)
-    up, down = both_ways(up, down, "z")
-    last = blocks(1, -1, 0)
     upstream = back_project(core, keep, give, w)
-    up, down, last, upstream = tie((up, down, last, upstream))
-
-    up, down = both_ways((v[2] + up.astype(F32)).astype(BF16), (v[3] + down.astype(F32)).astype(BF16), "z")
+    up, down, upstream = tie((up, down, upstream))
+
+    up, down = both_ways(*ring_step(zi, 3, keep, theirs, normed, normed_other, up, down), "z")
     dx, dz, db, dc, ddt, small = scan_backward(upstream, ys, *scan)
     up, down, small = tie((up, down, small))
+
+    up, down = both_ways(*ring_step(zi, 2, keep, theirs, normed, normed_other, up, down), "z")
+    last = blocks(1, -1, 0)
+    small = small + send(small, "c", 1)
+    small = small + send(small, "xl", 1)
+    small = small + swap(small, "z", 1)
+    up, down, last, small = tie((up, down, last, small))
 
     def halves(r):
         return lax.dynamic_slice_in_dim(r, (1 - xl) * 128, 128, 0), lax.dynamic_slice_in_dim(r, xl * 128, 128, 0)
@@ -536,13 +577,11 @@
     down_leave, down_stay = halves((last[1] + down.astype(F32)).astype(BF16))
     up_leave, down_leave = both_ways(up_leave, down_leave, "z")
     up_stay, down_stay = both_ways(up_stay, down_stay, "z")
-    small = small + send(small, "c", 1)
-    small = small + send(small, "xl", 1)
+    small = small + swap(small, "z", 2)
     leave, stay = halves(last[2])
     up_leave, down_leave, small = tie((up_leave, down_leave, small))
     leave = send(leave + (up_leave.astype(F32) + down_leave.astype(F32)), "xl", 1)
-    for mask in (1, 2, 4):
-        small = small + swap(small, "z", mask)
+    small = small + swap(small, "z", 4)
     up_stay, down_stay, leave, stay = tie((up_stay, down_stay, leave, stay), small)
     grad_weight = (stay + leave) + (up_stay.astype(F32) + down_stay.astype(F32))
     return (dx, dz, db[:, None], dc[:, None], ddt, small[8, :HEADS], small[9, :HEADS],

time: 183 us -> 174 us (0.951)
  local copies, waits for them, and re-layouts: 29.9 us -> 14.3 us
  starting transfers between devices: 32.3 us -> 44.1 us
  Pallas kernels: 48.2 us -> 58.6 us
  waiting for transfers between devices: 46.4 us -> 37.6 us
  other arithmetic: 9.86 us -> 4.58 us
    unnamed x70 -> x50, local copies, waits for them, and re-layouts: 24.3 us -> 7.54 us
    ppermute x24, starting transfers between devices: 30.5 us -> 38.9 us  [send(): return lax.ppermute(v, axis, [(i, (i + shift) % n) for i in range(n)])]
    pallas_call x0 -> x2, Pallas kernels: none -> 7.84 us  [ring_step(): pl.pallas_call(kernel, grid_spec=pltpu.PrefetchScalarGridSpec(num_scalar_...]
    ppermute x24, waiting for transfers between devices: 36.5 us -> 30.1 us  [send(): return lax.ppermute(v, axis, [(i, (i + shift) % n) for i in range(n)])]
    ppermute x3, waiting for transfers between devices: 9.24 us -> 3.89 us  [swap(): return lax.ppermute(v, axis, [(i, i ^ mask) for i in range(AXES[axis])])]
    ppermute x3, starting transfers between devices: 1.72 us -> 5.17 us  [swap(): return lax.ppermute(v, axis, [(i, i ^ mask) for i in range(AXES[axis])])]
    convert_element_type x1 -> x0, other arithmetic: 3.17 us -> none  [on_device(): (v[3] + down.astype(F32)).astype(BF16)]
    all_gather x1, waiting for transfers between devices: 0.01 us -> 3.02 us  [on_device(): w = lax.all_gather(w_out, DP, axis=0, tiled=True).reshape(16, 2, 128, CH)]
  transfers between devices with their start and end apart: 28 -> 28, of which waited for: 17 -> 14; matrix products, arithmetic and copies ran while one was open for 6% -> 6% of each run, Pallas kernels for 27% -> 29%
where the time goes in v2:
time: 174 us
  Pallas kernels  58.6 us (34%)
  starting transfers between devices  44.1 us (25%)
  waiting for transfers between devices  37.6 us (22%)
  between operations  14.5 us (8%)
  local copies, waits for them, and re-layouts  14.3 us (8%)
  other arithmetic  4.58 us (3%)
    ppermute x24, starting transfers between devices, send(): return lax.ppermute(v, axis, [(i, (i + shift) % n) for i in range(n)])  38.9 us
    ppermute x24, waiting for transfers between devices, send(): return lax.ppermute(v, axis, [(i, (i + shift) % n) for i in range(n)])  30.1 us
    pallas_call x1, Pallas kernels, scan_backward(): pl.pallas_call(bwd_kernel, out_shape=(jax.ShapeDtypeStruct((TOK, CH), BF1...  18 us
    pallas_call x1, Pallas kernels, scan_forward(): pl.pallas_call(fwd_kernel, out_shape=(jax.ShapeDtypeStruct((TOK, CH), F32...  8.59 us
    pallas_call x1, Pallas kernels, back_project(): pl.pallas_call(kernel, grid_spec=pltpu.PrefetchScalarGridSpec(num_scalar_...  8.06 us
    pallas_call x2, Pallas kernels, ring_step(): pl.pallas_call(kernel, grid_spec=pltpu.PrefetchScalarGridSpec(num_scalar_...  7.84 us
    unnamed x50, local copies, waits for them, and re-layouts  7.54 us
    pallas_call x2, Pallas kernels, shuffle(): pl.pallas_call(kernel, out_shape=tuple((jax.ShapeDtypeStruct(s, BF16) for...  7.21 us
  transfers between devices with their start and end apart: 28, of which 14 were waited for; matrix products, arithmetic and copies ran while one was open for 6% of the time, Pallas kernels for 29%

profile of v2, /device:TPU:2, one launch (start us, length us, event | category | flops | bytes accessed | tf_op | source)
XLA Modules:
  0.0 173.8 jit_solution(16248192119301056612)
XLA Ops:
  7.3 0.7 all-gather.2.cloned.1.call-update
  8.0 2.0 %own_first.1.refs_0_ = bf16[64,4096]{1,0:T(8,128)(2,1)} custom-call(s32[1]{0:T(128)} %bitcast.3.core_ref, bf16[64,4096]{1,0:T(8,128)(2,1)} %in_ref.1), custom_call_target="tpu_custom_call" | custom-call | flops 1000 | bytes 1000 | tf_op jit(solution)/shard_map/own_first/pallas_call | solution.py:410
  10.0 1.6 collective-permute-start
  11.5 1.7 collective-permute-start.1
  13.2 2.1 %collective-permute-start.2 = (bf16[64,4096]{1,0:T(8,128)(2,1)}, bf16[64,4096]{1,0:T(8,128)(2,1)}, u32[]{:S(2)}, u32[]{:S(2)}) collective-permute-start(bf16[64,4096]{1,0:T(8,128)(2,1)} %own_first.1.refs_0_), channel_id=1, source_target_pairs={{0,1},{1,0},{2,3},{3,2},{4,5},{5,4},{6,7},{7,6},{8,9},{9,8},{10,11... | collective-permute-start | bytes 1572872 | tf_op jit(solution)/shard_map/ppermute | solution.py:361
  15.3 9.8 %collective-permute-done.refs_2_ = bf16[64,4096]{1,0:T(8,128)(2,1)S(1)} collective-permute-done((bf16[64,4096]{1,0:T(8,128)(2,1)}, bf16[64,4096]{1,0:T(8,128)(2,1)S(1)}, u32[]{:S(2)}, u32[]{:S(2)}) %collective-permute-start) | collective-permute-done | bytes 524320 | tf_op jit(solution)/shard_map/ppermute | solution.py:361
  25.1 4.8 %collective-permute-done.2.refs_1_ = bf16[64,4096]{1,0:T(8,128)(2,1)} collective-permute-done((bf16[64,4096]{1,0:T(8,128)(2,1)}, bf16[64,4096]{1,0:T(8,128)(2,1)}, u32[]{:S(2)}, u32[]{:S(2)}) %collective-permute-start.2) | collective-permute-done | bytes 524320 | tf_op jit(solution)/shard_map/ppermute | solution.py:361
  29.9 3.2 %collective-permute-start.4 = (bf16[64,4096]{1,0:T(8,128)(2,1)}, bf16[64,4096]{1,0:T(8,128)(2,1)}, u32[]{:S(2)}, u32[]{:S(2)}) collective-permute-start(bf16[64,4096]{1,0:T(8,128)(2,1)} %collective-permute-done.2.refs_1_), channel_id=1, source_target_pairs={{0,6},{2,0},{4,2},{6,4},{1,7},{3,1},{5,3},{7,5},{8,14},{10,8},{12,... | collective-permute-start | bytes 1572872 | tf_op jit(solution)/shard_map/ppermute | solution.py:361
  33.1 0.7 slice.36
  33.9 0.7 slice.37
  34.6 3.2 %collective-permute-start.6 = (bf16[32,4096]{1,0:T(8,128)(2,1)}, bf16[32,4096]{1,0:T(8,128)(2,1)}, u32[]{:S(2)}, u32[]{:S(2)}) collective-permute-start(bf16[32,4096]{1,0:T(8,128)(2,1)} %slice.37), channel_id=1, source_target_pairs={{0,6},{2,0},{4,2},{6,4},{1,7},{3,1},{5,3},{7,5},{8,14},{10,8},{12,... | collective-permute-start | bytes 786440 | tf_op jit(solution)/shard_map/ppermute | solution.py:361
  37.8 0.9 copy.19.dt_ref
  38.8 0.9 copy-done.12
  39.7 8.6 %scan_forward.1 = (f32[512,1024]{1,0:T(8,128)S(1)}, bf16[512,1024]{1,0:T(8,128)(2,1)S(1)}) custom-call(bf16[512,1024]{1,0:T(8,128)(2,1)S(1)} %copy-done.6, bf16[512,1024]{1,0:T(8,128)(2,1)S(1)} %copy-done.8, bf16[512,128]{1,0:T(8,128)(2,1)S(1)} %bitcast.39, bf16[512,128]{1,0:T(8,128)(2,1)S(1)} %bitcast.41, f32[512,16]{1,0:T(8,128)S(1)} %copy.19.dt_ref, ...), custom_call_target="tpu_custom_call" | custom-call | flops 1000 | bytes 1000 | tf_op jit(solution)/shard_map/scan_forward/pallas_call | solution.py:308
  48.3 1.4 copy-done.10
  49.8 1.0 slice.38
  50.9 1.0 slice.39
  51.9 3.3 %collective-permute-start.8 = (bf16[32,4096]{1,0:T(8,128)(2,1)S(1)}, bf16[32,4096]{1,0:T(8,128)(2,1)S(1)}, u32[]{:S(2)}, u32[]{:S(2)}) collective-permute-start(bf16[32,4096]{1,0:T(8,128)(2,1)S(1)} %slice.39), channel_id=1, source_target_pairs={{0,6},{2,0},{4,2},{6,4},{1,7},{3,1},{5,3},{7,5},{8,14},{10,8},{12,... | collective-permute-start | bytes 786440 | tf_op jit(solution)/shard_map/ppermute | solution.py:361
  55.2 0.6 pad_add_fusion.s_ref
  55.8 5.0 %collective-permute-done.7.refs_8_ = bf16[32,4096]{1,0:T(8,128)(2,1)S(1)} collective-permute-done((bf16[32,4096]{1,0:T(8,128)(2,1)S(1)}, bf16[32,4096]{1,0:T(8,128)(2,1)S(1)}, u32[]{:S(2)}, u32[]{:S(2)}) %collective-permute-start.7) | collective-permute-done | bytes 262176 | tf_op jit(solution)/shard_map/ppermute | solution.py:361
  60.8 0.3 collective-permute-done.8.refs_9_
  61.1 0.4 copy-done.22
  61.5 0.3 copy-done.23
  61.8 3.6 %place_tokens.2.b_ref = bf16[512,2048]{1,0:T(8,128)(2,1)} custom-call(s32[2]{0:T(128)} %pad_add_fusion.s_ref, bf16[64,4096]{1,0:T(8,128)(2,1)} %own_first.1.refs_0_, bf16[64,4096]{1,0:T(8,128)(2,1)} %collective-permute-done.2.refs_1_, bf16[64,4096]{1,0:T(8,128)(2,1)} %copy-done.20, bf16[64,4096]{1,0:T(8,128)(2,1)} %collective-permute-done.3.refs_3_, ...), custom_call_target="tpu_custom_call" | custom-call | flops 1000 | bytes 1000 | tf_op jit(solution)/shard_map/place_tokens/pallas_call | solution.py:390
  65.4 0.1 collective-permute-start.10
  65.6 3.6 %place_tokens.3.a_ref = bf16[512,2048]{1,0:T(8,128)(2,1)} custom-call(s32[2]{0:T(128)} %pad_add_fusion.s_ref, bf16[64,4096]{1,0:T(8,128)(2,1)} %own_first.1.refs_0_, bf16[64,4096]{1,0:T(8,128)(2,1)} %collective-permute-done.2.refs_1_, bf16[64,4096]{1,0:T(8,128)(2,1)} %copy-done.20, bf16[64,4096]{1,0:T(8,128)(2,1)} %collective-permute-done.3.refs_3_, ...), custom_call_target="tpu_custom_call" | custom-call | flops 1000 | bytes 1000 | tf_op jit(solution)/shard_map/place_tokens/pallas_call | solution.py:390
  69.2 1.0 collective-permute-done.10.b_ref
  70.2 1.6 copy-done
  71.8 1.7 weight_blocks.2
  73.7 0.8 fusion.2
  74.5 9.4 %collective-permute-start.12 = (bf16[256,512]{1,0:T(8,128)(2,1)}, bf16[256,512]{1,0:T(8,128)(2,1)}, u32[]{:S(2)}, u32[]{:S(2)}) collective-permute-start(bf16[256,512]{1,0:T(8,128)(2,1)} %get-tuple-element.130), channel_id=1, source_target_pairs={{0,224},{32,0},{64,32},{96,64},{128,96},{160,128},{192,160},{224,1... | collective-permute-start | bytes 786440 | tf_op jit(solution)/shard_map/ppermute | solution.py:361
  83.9 0.7 pad_add_fusion.1
  84.5 3.0 %all-gather.2.cloned.1.call-done = bf16[4096,1024]{1,0:T(8,128)(2,1)} async-done(((bf16[128,1024]{1,0:T(8,128)(2,1)}), bf16[4096,1024]{1,0:T(8,128)(2,1)}) %all-gather.2.cloned.1.call-update) | async-done | bytes 8388624 | tf_op jit(solution)/shard_map/all_gather | solution.py:532
  87.5 8.1 %back_project.1.u_ref = f32[512,1024]{1,0:T(8,128)S(1)} custom-call(s32[1]{0:T(128)} %bitcast.3.core_ref, bf16[512,2048]{1,0:T(8,128)(2,1)S(1)} %copy-done.1, bf16[512,2048]{1,0:T(8,128)(2,1)} %place_tokens.2.b_ref, bf16[16,2,128,1024]{3,2,1,0:T(8,128)(2,1)} %bitcast.49, bf16[16,2,128,1024]{3,2,1,0:T(8,128)(2,1)} %bitcast.50), custom_call_target="tpu_custom_call" | custom-call | flops 1000 | bytes 1000 | tf_op jit(solution)/shard_map/back_project/pallas_call | solution.py:508
  95.7 3.4 %ring_step.2 = (bf16[256,1024]{1,0:T(8,128)(2,1)S(1)}, bf16[256,1024]{1,0:T(8,128)(2,1)S(1)}) custom-call(s32[2]{0:T(128)S(1)} %get-tuple-element.135.at_ref, bf16[512,2048]{1,0:T(8,128)(2,1)S(1)} %copy-done.1, bf16[512,2048]{1,0:T(8,128)(2,1)} %collective-permute-done.10.b_ref, bf16[512,1024]{1,0:T(8,128)(2,1)S(1)} %get-tuple-element.71.n_ref, ...), custom_call_target="tpu_custom_call" | custom-call | flops 1000 | bytes 1000 | tf_op jit(solution)/shard_map/ring_step/pallas_call | solution.py:488
  99.1 1.7 collective-permute-start.13
  100.8 1.6 collective-permute-start.14
  102.4 18.0 %scan_backward.1 = (bf16[512,1024]{1,0:T(8,128)(2,1)}, bf16[512,1024]{1,0:T(8,128)(2,1)}, bf16[512,128]{1,0:T(8,128)(2,1)}, bf16[512,128]{1,0:T(8,128)(2,1)}, f3...) custom-call(f32[512,1024]{1,0:T(8,128)S(1)} %back_project.1.u_ref, f32[512,1024]{1,0:T(8,128)} %copy-done.10, ...), custom_call_target="tpu_custom_call" | custom-call | flops 1000 | bytes 1000 | tf_op jit(solution)/shard_map/scan_backward/pallas_call | solution.py:326
  120.5 4.4 %ring_step.3 = (bf16[256,1024]{1,0:T(8,128)(2,1)}, bf16[256,1024]{1,0:T(8,128)(2,1)}) custom-call(s32[2]{0:T(128)S(1)} %copy-done.19, bf16[512,2048]{1,0:T(8,128)(2,1)} %place_tokens.3.a_ref, bf16[512,2048]{1,0:T(8,128)(2,1)} %collective-permute-done.10.b_ref, bf16[512,1024]{1,0:T(8,128)(2,1)S(1)} %get-tuple-element.71.n_ref, ...), custom_call_target="tpu_custom_call" | custom-call | flops 1000 | bytes 1000 | tf_op jit(solution)/shard_map/ring_step/pallas_call | solution.py:488
  124.9 0.4 collective-permute-start.15
  125.3 2.8 %collective-permute-start.16 = (bf16[256,1024]{1,0:T(8,128)(2,1)}, bf16[256,1024]{1,0:T(8,128)(2,1)}, u32[]{:S(2)}, u32[]{:S(2)}) collective-permute-start(bf16[256,1024]{1,0:T(8,128)(2,1)} %get-tuple-element.102), channel_id=1, source_target_pairs={{0,224},{32,0},{64,32},{96,64},{128,96},{160,128},{192,160},{224,1... | collective-permute-start | bytes 1572872 | tf_op jit(solution)/shard_map/ppermute | solution.py:361
  128.1 1.2 collective-permute-done.17
  129.3 1.1 collective-permute-start.18
  130.4 2.5 %collective-permute-done.18 = f32[16,128]{1,0:T(8,128)S(1)} collective-permute-done((f32[16,128]{1,0:T(8,128)S(1)}, f32[16,128]{1,0:T(8,128)S(1)}, u32[]{:S(2)}, u32[]{:S(2)}) %collective-permute-start.18) | collective-permute-done | bytes 8224 | tf_op jit(solution)/shard_map/ppermute | solution.py:361
  133.0 1.2 copy-done.5
  134.3 5.2 %weight_blocks.3 = f32[3,256,1024]{2,1,0:T(8,128)} custom-call(s32[3]{0:T(128)S(1)} %pad_add_fusion.3.at_ref, bf16[512,2048]{1,0:T(8,128)(2,1)S(1)} %copy-done.2, bf16[512,2048]{1,0:T(8,128)(2,1)} %collective-permute-done.10.b_ref, bf16[512,1024]{1,0:T(8,128)(2,1)S(1)} %get-tuple-element.71.n_ref, bf16[512,1024]{1,0:T(8,128)(2,1)S(1)} %copy-done.5), custom_call_target="tpu_custom_call" | custom-call | flops 1000 | bytes 1000 | tf_op jit(solution)/shard_map/weight_blocks/pallas_call | solution.py:447
  139.5 0.4 collective-permute-done.15
  139.9 2.2 %fusion = (bf16[256,1024]{1,0:T(8,128)(2,1)S(1)}, bf16[256,1024]{1,0:T(8,128)(2,1)S(1)}) fusion(bf16[256,1024]{1,0:T(8,128)(2,1)} %collective-permute-done.16, f32[3,256,1024]{2,1,0:T(8,128)} %weight_blocks.3, bf16[256,1024]{1,0:T(8,128)(2,1)} %collective-permute-done.15), kind=kLoop, calls=%fused_computation.1 | loop fusion | flops 1572864 | bytes 4194304 | tf_op jit(solution)/shard_map/convert_element_type | solution.py:577
  142.2 3.0 %collective-permute-start.21 = (bf16[128,1024]{1,0:T(8,128)(2,1)S(1)}, bf16[128,1024]{1,0:T(8,128)(2,1)S(1)}, u32[]{:S(2)}, u32[]{:S(2)}) collective-permute-start(bf16[128,1024]{1,0:T(8,128)(2,1)S(1)} %get-tuple-element.127), channel_id=1, source_target_pairs={{0,224},{32,0},{64,32},{96,64},{128,96},{160,128},{192,160},{224,1... | collective-permute-start | bytes 786440 | tf_op jit(solution)/shard_map/ppermute | solution.py:361
  145.3 1.4 collective-permute-start.22
  146.7 0.7 copy.21
  147.4 1.3 slice.47
  148.7 2.2 %collective-permute-done.22 = f32[16,128]{1,0:T(8,128)S(1)} collective-permute-done((f32[16,128]{1,0:T(8,128)S(1)}, f32[16,128]{1,0:T(8,128)S(1)}, u32[]{:S(2)}, u32[]{:S(2)}) %collective-permute-start.22) | collective-permute-done | bytes 8224 | tf_op jit(solution)/shard_map/ppermute | solution.py:365
  150.9 2.0 %collective-permute-done.20 = bf16[128,1024]{1,0:T(8,128)(2,1)S(1)} collective-permute-done((bf16[128,1024]{1,0:T(8,128)(2,1)S(1)}, bf16[128,1024]{1,0:T(8,128)(2,1)S(1)}, u32[]{:S(2)}, u32[]{:S(2)}) %collective-permute-start.20) | collective-permute-done | bytes 262176 | tf_op jit(solution)/shard_map/ppermute | solution.py:361
  153.0 1.2 collective-permute-start.26
  154.3 3.8 %collective-permute-start.23 = (f32[16,128]{1,0:T(8,128)S(1)}, f32[16,128]{1,0:T(8,128)S(1)}, u32[]{:S(2)}, u32[]{:S(2)}) collective-permute-start(f32[16,128]{1,0:T(8,128)S(1)} %add.138), channel_id=1, source_target_pairs={{0,128},{32,160},{64,192},{96,224},{128,0},{160,32},{192,64},{224,... | collective-permute-start | bytes 24584 | tf_op jit(solution)/shard_map/ppermute | solution.py:365
  158.1 0.3 collective-permute-start.25
  158.4 1.8 %collective-permute-start.24 = (bf16[128,1024]{1,0:T(8,128)(2,1)S(1)}, bf16[128,1024]{1,0:T(8,128)(2,1)S(1)}, u32[]{:S(2)}, u32[]{:S(2)}) collective-permute-start(bf16[128,1024]{1,0:T(8,128)(2,1)S(1)} %get-tuple-element.128), channel_id=1, source_target_pairs={{0,32},{32,64},{64,96},{96,128},{128,160},{160,192},{192,224},{224... | collective-permute-start | bytes 786440 | tf_op jit(solution)/shard_map/ppermute | solution.py:361
  160.2 1.7 %collective-permute-done.23 = f32[16,128]{1,0:T(8,128)S(1)} collective-permute-done((f32[16,128]{1,0:T(8,128)S(1)}, f32[16,128]{1,0:T(8,128)S(1)}, u32[]{:S(2)}, u32[]{:S(2)}) %collective-permute-start.23) | collective-permute-done | bytes 8224 | tf_op jit(solution)/shard_map/ppermute | solution.py:365
  162.0 0.5 slice_bitcast_fusion.1
  162.5 0.6 slice_bitcast_fusion
  163.1 1.5 collective-permute-done.25
  164.6 1.4 collective-permute-done.24
  166.0 0.9 add_add_fusion
  (76 shorter events, 0.8 us)
Async XLA Ops:
  7.2 31.6 %copy-start.18 = (f32[16]{0:T(128)S(1)}, f32[16]{0:T(128)}, u32[]{:S(2)}) copy-start(f32[16]{0:T(128)} %param.17) | copy-start | bytes 196
  7.2 31.6 %copy-start.11 = (bf16[512,1,128]{2,0,1:T(8,128)(2,1)S(1)}, bf16[512,1,128]{2,0,1:T(8,128)(2,1)}, u32[]{:S(2)}) copy-start(bf16[512,1,128]{2,0,1:T(8,128)(2,1)} %param.13) | copy-start | bytes 393220
  7.2 31.6 %copy-start.17 = (f32[16]{0:T(128)S(1)}, f32[16]{0:T(128)}, u32[]{:S(2)}) copy-start(f32[16]{0:T(128)} %param.16) | copy-start | bytes 196
  7.2 31.6 %copy-start.16 = (f32[1024]{0:T(1024)S(1)}, f32[1024]{0:T(1024)}, u32[]{:S(2)}) copy-start(f32[1024]{0:T(1024)} %param.18) | copy-start | bytes 12292
  7.2 31.6 %copy-start.6 = (bf16[512,1024]{1,0:T(8,128)(2,1)S(1)}, bf16[512,1024]{1,0:T(8,128)(2,1)}, u32[]{:S(2)}) copy-start(bf16[512,1024]{1,0:T(8,128)(2,1)} %x_ref.3) | copy-start | bytes 3145732
  7.2 31.6 %copy-start.8 = (bf16[512,1024]{1,0:T(8,128)(2,1)S(1)}, bf16[512,1024]{1,0:T(8,128)(2,1)}, u32[]{:S(2)}) copy-start(bf16[512,1024]{1,0:T(8,128)(2,1)} %z_ref.3) | copy-start | bytes 3145732
  7.2 80.3 %all-gather.2.cloned.1.call-start = ((), (), s32[]{:S(2)}) async-start(), calls=%async_computation | async-start | bytes 8650752 | tf_op jit(solution)/shard_map/all_gather | solution.py:532
  10.0 15.1 %collective-permute-start = (bf16[64,4096]{1,0:T(8,128)(2,1)}, bf16[64,4096]{1,0:T(8,128)(2,1)S(1)}, u32[]{:S(2)}, u32[]{:S(2)}) collective-permute-start(bf16[64,4096]{1,0:T(8,128)(2,1)} %own_first.1.refs_0_), channel_id=1, source_target_pairs={{0,2},{2,4},{4,6},{6,0},{1,3},{3,5},{5,7},{7,1},{8,10},{10,12},{12... | collective-permute-start | bytes 1572872 | tf_op jit(solution)/shard_map/ppermute | solution.py:361
  11.5 13.6 %collective-permute-start.1 = (bf16[64,4096]{1,0:T(8,128)(2,1)}, bf16[64,4096]{1,0:T(8,128)(2,1)S(1)}, u32[]{:S(2)}, u32[]{:S(2)}) collective-permute-start(bf16[64,4096]{1,0:T(8,128)(2,1)} %own_first.1.refs_0_), channel_id=1, source_target_pairs={{0,6},{2,0},{4,2},{6,4},{1,7},{3,1},{5,3},{7,5},{8,14},{10,8},{12,... | collective-permute-start | bytes 1572872 | tf_op jit(solution)/shard_map/ppermute | solution.py:361
  13.2 16.7 %collective-permute-start.2 = (bf16[64,4096]{1,0:T(8,128)(2,1)}, bf16[64,4096]{1,0:T(8,128)(2,1)}, u32[]{:S(2)}, u32[]{:S(2)}) collective-permute-start(bf16[64,4096]{1,0:T(8,128)(2,1)} %own_first.1.refs_0_), channel_id=1, source_target_pairs={{0,1},{1,0},{2,3},{3,2},{4,5},{5,4},{6,7},{7,6},{8,9},{9,8},{10,11... | collective-permute-start | bytes 1572872 | tf_op jit(solution)/shard_map/ppermute | solution.py:361
  25.1 13.6 %copy-start.20 = (bf16[64,4096]{1,0:T(8,128)(2,1)}, bf16[64,4096]{1,0:T(8,128)(2,1)S(1)}, u32[]{:S(2)}) copy-start(bf16[64,4096]{1,0:T(8,128)(2,1)S(1)} %collective-permute-done.refs_2_) | copy-start | bytes 1572868
  25.1 13.6 %copy-start.21 = (bf16[64,4096]{1,0:T(8,128)(2,1)}, bf16[64,4096]{1,0:T(8,128)(2,1)S(1)}, u32[]{:S(2)}) copy-start(bf16[64,4096]{1,0:T(8,128)(2,1)S(1)} %collective-permute-done.1.refs_4_) | copy-start | bytes 1572868
  29.9 19.8 %collective-permute-start.3 = (bf16[64,4096]{1,0:T(8,128)(2,1)}, bf16[64,4096]{1,0:T(8,128)(2,1)}, u32[]{:S(2)}, u32[]{:S(2)}) collective-permute-start(bf16[64,4096]{1,0:T(8,128)(2,1)} %collective-permute-done.2.refs_1_), channel_id=1, source_target_pairs={{0,2},{2,4},{4,6},{6,0},{1,3},{3,5},{5,7},{7,1},{8,10},{10,12},{12... | collective-permute-start | bytes 1572872 | tf_op jit(solution)/shard_map/ppermute | solution.py:361
  29.9 19.8 %collective-permute-start.4 = (bf16[64,4096]{1,0:T(8,128)(2,1)}, bf16[64,4096]{1,0:T(8,128)(2,1)}, u32[]{:S(2)}, u32[]{:S(2)}) collective-permute-start(bf16[64,4096]{1,0:T(8,128)(2,1)} %collective-permute-done.2.refs_1_), channel_id=1, source_target_pairs={{0,6},{2,0},{4,2},{6,4},{1,7},{3,1},{5,3},{7,5},{8,14},{10,8},{12,... | collective-permute-start | bytes 1572872 | tf_op jit(solution)/shard_map/ppermute | solution.py:361
  33.9 15.9 %collective-permute-start.5 = (bf16[32,4096]{1,0:T(8,128)(2,1)}, bf16[32,4096]{1,0:T(8,128)(2,1)}, u32[]{:S(2)}, u32[]{:S(2)}) collective-permute-start(bf16[32,4096]{1,0:T(8,128)(2,1)} %slice.36), channel_id=1, source_target_pairs={{0,2},{2,4},{4,6},{6,0},{1,3},{3,5},{5,7},{7,1},{8,10},{10,12},{12... | collective-permute-start | bytes 786440 | tf_op jit(solution)/shard_map/ppermute | solution.py:361
  34.6 15.1 %collective-permute-start.6 = (bf16[32,4096]{1,0:T(8,128)(2,1)}, bf16[32,4096]{1,0:T(8,128)(2,1)}, u32[]{:S(2)}, u32[]{:S(2)}) collective-permute-start(bf16[32,4096]{1,0:T(8,128)(2,1)} %slice.37), channel_id=1, source_target_pairs={{0,6},{2,0},{4,2},{6,4},{1,7},{3,1},{5,3},{7,5},{8,14},{10,8},{12,... | collective-permute-start | bytes 786440 | tf_op jit(solution)/shard_map/ppermute | solution.py:361
  38.8 0.9 copy-start.12
  48.3 1.4 copy-start.10
  49.7 11.4 %collective-permute-start.9 = (bf16[512,1024]{1,0:T(8,128)(2,1)S(1)}, bf16[512,1024]{1,0:T(8,128)(2,1)S(1)}, u32[]{:S(2)}, u32[]{:S(2)}) collective-permute-start(bf16[512,1024]{1,0:T(8,128)(2,1)S(1)} %get-tuple-element.71.n_ref), channel_id=1, source_target_pairs={{0,8},{8,0},{1,9},{9,1},{2,10},{10,2},{3,11},{11,3},{4,12},{12,4},... | collective-permute-start | bytes 3145736 | tf_op jit(solution)/shard_map/ppermute | solution.py:361
  50.8 10.0 %collective-permute-start.7 = (bf16[32,4096]{1,0:T(8,128)(2,1)S(1)}, bf16[32,4096]{1,0:T(8,128)(2,1)S(1)}, u32[]{:S(2)}, u32[]{:S(2)}) collective-permute-start(bf16[32,4096]{1,0:T(8,128)(2,1)S(1)} %slice.38), channel_id=1, source_target_pairs={{0,2},{2,4},{4,6},{6,0},{1,3},{3,5},{5,7},{7,1},{8,10},{10,12},{12... | collective-permute-start | bytes 786440 | tf_op jit(solution)/shard_map/ppermute | solution.py:361
  51.9 9.2 %collective-permute-start.8 = (bf16[32,4096]{1,0:T(8,128)(2,1)S(1)}, bf16[32,4096]{1,0:T(8,128)(2,1)S(1)}, u32[]{:S(2)}, u32[]{:S(2)}) collective-permute-start(bf16[32,4096]{1,0:T(8,128)(2,1)S(1)} %slice.39), channel_id=1, source_target_pairs={{0,6},{2,0},{4,2},{6,4},{1,7},{3,1},{5,3},{7,5},{8,14},{10,8},{12,... | collective-permute-start | bytes 786440 | tf_op jit(solution)/shard_map/ppermute | solution.py:361
  60.8 0.7 copy-start.22
  61.1 0.7 copy-start.23
  61.8 8.4 %copy-start.3 = (bf16[512,1024]{1,0:T(8,128)(2,1)}, bf16[512,1024]{1,0:T(8,128)(2,1)S(1)}, u32[]{:S(2)}) copy-start(bf16[512,1024]{1,0:T(8,128)(2,1)S(1)} %collective-permute-done.9.m_ref) | copy-start | bytes 3145732
  65.4 4.8 %collective-permute-start.10 = (bf16[512,2048]{1,0:T(8,128)(2,1)}, bf16[512,2048]{1,0:T(8,128)(2,1)}, u32[]{:S(2)}, u32[]{:S(2)}) collective-permute-start(bf16[512,2048]{1,0:T(8,128)(2,1)} %place_tokens.2.b_ref), channel_id=1, source_target_pairs={{0,8},{8,0},{1,9},{9,1},{2,10},{10,2},{3,11},{11,3},{4,12},{12,4},... | collective-permute-start | bytes 6291464 | tf_op jit(solution)/shard_map/ppermute | solution.py:361
  70.2 1.6 copy-start
  73.6 14.0 %copy-start.1 = (bf16[512,2048]{1,0:T(8,128)(2,1)S(1)}, bf16[512,2048]{1,0:T(8,128)(2,1)}, u32[]{:S(2)}) copy-start(bf16[512,2048]{1,0:T(8,128)(2,1)} %place_tokens.3.a_ref) | copy-start | bytes 6291460
  74.5 21.1 %collective-permute-start.11 = (bf16[256,512]{1,0:T(8,128)(2,1)}, bf16[256,512]{1,0:T(8,128)(2,1)}, u32[]{:S(2)}, u32[]{:S(2)}) collective-permute-start(bf16[256,512]{1,0:T(8,128)(2,1)} %get-tuple-element.131), channel_id=1, source_target_pairs={{0,32},{32,64},{64,96},{96,128},{128,160},{160,192},{192,224},{224... | collective-permute-start | bytes 786440 | tf_op jit(solution)/shard_map/ppermute | solution.py:361
  74.5 21.1 %collective-permute-start.12 = (bf16[256,512]{1,0:T(8,128)(2,1)}, bf16[256,512]{1,0:T(8,128)(2,1)}, u32[]{:S(2)}, u32[]{:S(2)}) collective-permute-start(bf16[256,512]{1,0:T(8,128)(2,1)} %get-tuple-element.130), channel_id=1, source_target_pairs={{0,224},{32,0},{64,32},{96,64},{128,96},{160,128},{192,160},{224,1... | collective-permute-start | bytes 786440 | tf_op jit(solution)/shard_map/ppermute | solution.py:361
  87.5 8.1 %copy-start.4 = (bf16[512,1024]{1,0:T(8,128)(2,1)S(1)}, bf16[512,1024]{1,0:T(8,128)(2,1)}, u32[]{:S(2)}) copy-start(bf16[512,1024]{1,0:T(8,128)(2,1)} %copy-done.3) | copy-start | bytes 3145732
  95.6 6.8 %copy-start.7 = (bf16[512,1024]{1,0:T(8,128)(2,1)S(1)}, bf16[512,1024]{1,0:T(8,128)(2,1)}, u32[]{:S(2)}) copy-start(bf16[512,1024]{1,0:T(8,128)(2,1)} %x_ref.3) | copy-start | bytes 3145732
  95.6 6.8 %copy-start.9 = (bf16[512,1024]{1,0:T(8,128)(2,1)S(1)}, bf16[512,1024]{1,0:T(8,128)(2,1)}, u32[]{:S(2)}) copy-start(bf16[512,1024]{1,0:T(8,128)(2,1)} %z_ref.3) | copy-start | bytes 3145732
  95.7 6.7 %copy-start.13 = (bf16[512,1,128]{2,0,1:T(8,128)(2,1)S(1)}, bf16[512,1,128]{2,0,1:T(8,128)(2,1)}, u32[]{:S(2)}) copy-start(bf16[512,1,128]{2,0,1:T(8,128)(2,1)} %param.14) | copy-start | bytes 393220
  99.1 21.4 %collective-permute-start.13 = (bf16[256,1024]{1,0:T(8,128)(2,1)S(1)}, bf16[256,1024]{1,0:T(8,128)(2,1)S(1)}, u32[]{:S(2)}, u32[]{:S(2)}) collective-permute-start(bf16[256,1024]{1,0:T(8,128)(2,1)S(1)} %get-tuple-element.96), channel_id=1, source_target_pairs={{0,32},{32,64},{64,96},{96,128},{128,160},{160,192},{192,224},{224... | collective-permute-start | bytes 1572872 | tf_op jit(solution)/shard_map/ppermute | solution.py:361
  100.8 19.7 %collective-permute-start.14 = (bf16[256,1024]{1,0:T(8,128)(2,1)S(1)}, bf16[256,1024]{1,0:T(8,128)(2,1)S(1)}, u32[]{:S(2)}, u32[]{:S(2)}) collective-permute-start(bf16[256,1024]{1,0:T(8,128)(2,1)S(1)} %get-tuple-element.97), channel_id=1, source_target_pairs={{0,224},{32,0},{64,32},{96,64},{128,96},{160,128},{192,160},{224,1... | collective-permute-start | bytes 1572872 | tf_op jit(solution)/shard_map/ppermute | solution.py:361
  102.4 18.0 %copy-start.19 = (s32[2]{0:T(128)S(1)}, s32[2]{0:T(128)}, u32[]{:S(2)}) copy-start(s32[2]{0:T(128)} %get-tuple-element.134.at_ref) | copy-start | bytes 28
  120.4 4.5 %copy-start.14 = (f32[512,16]{1,0:T(8,128)}, f32[512,16]{1,0:T(8,128)S(1)}, u32[]{:S(2)}) copy-start(f32[512,16]{1,0:T(8,128)S(1)} %get-tuple-element.119) | copy-start | bytes 98308
  120.4 12.6 %copy-start.2 = (bf16[512,2048]{1,0:T(8,128)(2,1)S(1)}, bf16[512,2048]{1,0:T(8,128)(2,1)}, u32[]{:S(2)}) copy-start(bf16[512,2048]{1,0:T(8,128)(2,1)} %place_tokens.3.a_ref) | copy-start | bytes 6291460
  124.9 15.0 %collective-permute-start.15 = (bf16[256,1024]{1,0:T(8,128)(2,1)}, bf16[256,1024]{1,0:T(8,128)(2,1)}, u32[]{:S(2)}, u32[]{:S(2)}) collective-permute-start(bf16[256,1024]{1,0:T(8,128)(2,1)} %get-tuple-element.101), channel_id=1, source_target_pairs={{0,32},{32,64},{64,96},{96,128},{128,160},{160,192},{192,224},{224... | collective-permute-start | bytes 1572872 | tf_op jit(solution)/shard_map/ppermute | solution.py:361
  125.3 14.6 %collective-permute-start.16 = (bf16[256,1024]{1,0:T(8,128)(2,1)}, bf16[256,1024]{1,0:T(8,128)(2,1)}, u32[]{:S(2)}, u32[]{:S(2)}) collective-permute-start(bf16[256,1024]{1,0:T(8,128)(2,1)} %get-tuple-element.102), channel_id=1, source_target_pairs={{0,224},{32,0},{64,32},{96,64},{128,96},{160,128},{192,160},{224,1... | collective-permute-start | bytes 1572872 | tf_op jit(solution)/shard_map/ppermute | solution.py:361
  128.1 1.2 collective-permute-start.17
  129.3 3.7 %collective-permute-start.18 = (f32[16,128]{1,0:T(8,128)S(1)}, f32[16,128]{1,0:T(8,128)S(1)}, u32[]{:S(2)}, u32[]{:S(2)}) collective-permute-start(f32[16,128]{1,0:T(8,128)S(1)} %add.132), channel_id=1, source_target_pairs={{0,16},{16,0},{1,17},{17,1},{2,18},{18,2},{3,19},{19,3},{4,20},{20... | collective-permute-start | bytes 24584 | tf_op jit(solution)/shard_map/ppermute | solution.py:361
  133.0 6.5 %collective-permute-start.19 = (f32[16,128]{1,0:T(8,128)S(1)}, f32[16,128]{1,0:T(8,128)S(1)}, u32[]{:S(2)}, u32[]{:S(2)}) collective-permute-start(f32[16,128]{1,0:T(8,128)S(1)} %add.133), channel_id=1, source_target_pairs={{0,32},{32,0},{64,96},{96,64},{128,160},{160,128},{192,224},{224,1... | collective-permute-start | bytes 24584 | tf_op jit(solution)/shard_map/ppermute | solution.py:365
  133.0 1.2 copy-start.5
  142.1 4.6 %copy-start.15 = (f32[512,16]{1,0:T(8,128)S(1)}, f32[512,16]{1,0:T(8,128)}, u32[]{:S(2)}) copy-start(f32[512,16]{1,0:T(8,128)} %copy-done.14) | copy-start | bytes 98308
  142.2 8.7 %collective-permute-start.21 = (bf16[128,1024]{1,0:T(8,128)(2,1)S(1)}, bf16[128,1024]{1,0:T(8,128)(2,1)S(1)}, u32[]{:S(2)}, u32[]{:S(2)}) collective-permute-start(bf16[128,1024]{1,0:T(8,128)(2,1)S(1)} %get-tuple-element.127), channel_id=1, source_target_pairs={{0,224},{32,0},{64,32},{96,64},{128,96},{160,128},{192,160},{224,1... | collective-permute-start | bytes 786440 | tf_op jit(solution)/shard_map/ppermute | solution.py:361
  145.2 7.7 %collective-permute-start.20 = (bf16[128,1024]{1,0:T(8,128)(2,1)S(1)}, bf16[128,1024]{1,0:T(8,128)(2,1)S(1)}, u32[]{:S(2)}, u32[]{:S(2)}) collective-permute-start(bf16[128,1024]{1,0:T(8,128)(2,1)S(1)} %get-tuple-element.129), channel_id=1, source_target_pairs={{0,32},{32,64},{64,96},{96,128},{128,160},{160,192},{192,224},{224... | collective-permute-start | bytes 786440 | tf_op jit(solution)/shard_map/ppermute | solution.py:361
  145.3 5.6 %collective-permute-start.22 = (f32[16,128]{1,0:T(8,128)S(1)}, f32[16,128]{1,0:T(8,128)S(1)}, u32[]{:S(2)}, u32[]{:S(2)}) collective-permute-start(f32[16,128]{1,0:T(8,128)S(1)} %add.134), channel_id=1, source_target_pairs={{0,64},{32,96},{64,0},{96,32},{128,192},{160,224},{192,128},{224,1... | collective-permute-start | bytes 24584 | tf_op jit(solution)/shard_map/ppermute | solution.py:365
  153.0 13.0 %collective-permute-start.26 = (f32[128,1024]{1,0:T(8,128)S(1)}, f32[128,1024]{1,0:T(8,128)S(1)}, u32[]{:S(2)}, u32[]{:S(2)}) collective-permute-start(f32[128,1024]{1,0:T(8,128)S(1)} %bitcast_add_fusion.2), channel_id=1, source_target_pairs={{0,16},{16,0},{1,17},{17,1},{2,18},{18,2},{3,19},{19,3},{4,20},{20... | collective-permute-start | bytes 1572872 | tf_op jit(solution)/shard_map/ppermute | solution.py:361
  154.3 7.7 %collective-permute-start.23 = (f32[16,128]{1,0:T(8,128)S(1)}, f32[16,128]{1,0:T(8,128)S(1)}, u32[]{:S(2)}, u32[]{:S(2)}) collective-permute-start(f32[16,128]{1,0:T(8,128)S(1)} %add.138), channel_id=1, source_target_pairs={{0,128},{32,160},{64,192},{96,224},{128,0},{160,32},{192,64},{224,... | collective-permute-start | bytes 24584 | tf_op jit(solution)/shard_map/ppermute | solution.py:365
  158.1 6.5 %collective-permute-start.25 = (bf16[128,1024]{1,0:T(8,128)(2,1)S(1)}, bf16[128,1024]{1,0:T(8,128)(2,1)S(1)}, u32[]{:S(2)}, u32[]{:S(2)}) collective-permute-start(bf16[128,1024]{1,0:T(8,128)(2,1)S(1)} %get-tuple-element.126), channel_id=1, source_target_pairs={{0,224},{32,0},{64,32},{96,64},{128,96},{160,128},{192,160},{224,1... | collective-permute-start | bytes 786440 | tf_op jit(solution)/shard_map/ppermute | solution.py:361
  158.4 7.6 %collective-permute-start.24 = (bf16[128,1024]{1,0:T(8,128)(2,1)S(1)}, bf16[128,1024]{1,0:T(8,128)(2,1)S(1)}, u32[]{:S(2)}, u32[]{:S(2)}) collective-permute-start(bf16[128,1024]{1,0:T(8,128)(2,1)S(1)} %get-tuple-element.128), channel_id=1, source_target_pairs={{0,32},{32,64},{64,96},{96,128},{128,160},{160,192},{192,224},{224... | collective-permute-start | bytes 786440 | tf_op jit(solution)/shard_map/ppermute | solution.py:361
Sparse Core Ops, SparseCore 0:
  9.9 77.5 all-gather.1

commit v3 on v2

--- a/solution.py
+++ b/solution.py
@@ -373,66 +373,45 @@
     return lax.optimization_barrier((tuple(values),) + tuple(first))[0]
 
 
-def shuffle(name, shapes, plan, scalars, *arrays):
-    count = len(plan([0] * len(scalars)))
+def place_tokens(yi, xh, core, *pieces):
+    parts = ((0, 64, 0, 0, 0), (1, 64, 0, 1, 0), (2, 64, 3, 0, 0), (3, 64, 3, 1, 0), (4, 64, 1, 0, 0), (5, 64, 1, 1, 0),
+             (6, 32, 2, 0, 0), (7, 32, 2, 0, 32), (8, 32, 2, 1, 0), (9, 32, 2, 1, 32))
 
     def kernel(s_ref, *refs):
-        src, dst, sem = refs[:len(arrays)], refs[len(arrays):-1], refs[-1]
-        copies = [
-            pltpu.make_async_copy(src[i].at[a], dst[o].at[b], sem.at[k])
-            for k, (i, a, o, b) in enumerate(plan([s_ref[j] for j in range(len(scalars))]))
-        ]
+        src, (keep, give, land, sem) = refs[:len(pieces)], refs[len(pieces):]
+        copies = []
+        for piece, size, turn, other, offset in parts:
+            start = ((s_ref[0] + turn) % 4) * 128 + (1 - s_ref[1] if other else s_ref[1]) * 64 + offset
+            rows = pl.ds(pl.multiple_of(start, 32), size)
+            copies.append(pltpu.make_async_copy(src[piece], land.at[rows, :], sem.at[piece]))
         for copy in copies:
             copy.start()
         for copy in copies:
             copy.wait()
 
+        def split(even, odd):
+            def step(i, _):
+                rows = pl.ds(pl.multiple_of(i * 64, 64), 64)
+                for j in range(16):
+                    even[rows, 128 * j:128 * j + 128] = land[rows, 256 * j:256 * j + 128]
+                    odd[rows, 128 * j:128 * j + 128] = land[rows, 256 * j + 128:256 * j + 256]
+                return 0
+
+            lax.fori_loop(0, TOK // 64, step, 0)
+
+        pl.when(s_ref[2] == 0)(lambda: split(keep, give))
+        pl.when(s_ref[2] == 1)(lambda: split(give, keep))
+
     return pl.pallas_call(
         kernel,
-        out_shape=tuple(jax.ShapeDtypeStruct(s, BF16) for s in shapes),
-        in_specs=[pl.BlockSpec(memory_space=pltpu.SMEM)] + [pl.BlockSpec(memory_space=pl.ANY)] * len(arrays),
-        out_specs=tuple(pl.BlockSpec(memory_space=pltpu.VMEM) for _ in shapes),
-        scratch_shapes=[pltpu.SemaphoreType.DMA((count,))],
-        cost_estimate=SMALL,
-        name=name,
-    )(jnp.stack([s.astype(jnp.int32) for s in scalars]), *arrays)
-
-
-def own_first(rows, core):
-    def kernel(core_ref, in_ref, out_ref):
-        for j in range(16):
-            even = in_ref[:, 256 * j:256 * j + 128]
-            odd = in_ref[:, 256 * j + 128:256 * j + 256]
-            first = core_ref[0] == 0
-            out_ref[:, 128 * j:128 * j + 128] = jnp.where(first, even, odd)
-            out_ref[:, 2048 + 128 * j:2048 + 128 * j + 128] = jnp.where(first, odd, even)
-
-    return pl.pallas_call(
-        kernel,
-        out_shape=jax.ShapeDtypeStruct(rows.shape, rows.dtype),
-        in_specs=[pl.BlockSpec(memory_space=pltpu.SMEM), pl.BlockSpec(memory_space=pltpu.VMEM)],
-        out_specs=pl.BlockSpec(memory_space=pltpu.VMEM),
-        cost_estimate=SMALL,
-        name="own_first",
-    )(core.astype(jnp.int32).reshape(1), rows)
-
-
-def at_rows(start, size):
-    return (pl.ds(pl.multiple_of(start, 32), size), slice(None)) if not isinstance(start, int) else (slice(start, start + size), slice(None))
-
-
-def place_tokens(yi, xh, first, *pieces):
-    parts = ((0, 64, 0, 0, 0), (1, 64, 0, 1, 0), (2, 64, 3, 0, 0), (3, 64, 3, 1, 0), (4, 64, 1, 0, 0),
-             (5, 64, 1, 1, 0), (6, 32, 2, 0, 0), (7, 32, 2, 0, 32), (8, 32, 2, 1, 0), (9, 32, 2, 1, 32))
-
-    def plan(s):
-        moves = []
-        for piece, size, turn, other, offset in parts:
-            start = ((s[0] + turn) % 4) * 128 + (1 - s[1] if other else s[1]) * 64 + offset
-            moves.append((piece, (slice(None), slice(first, first + 2048)), 0, at_rows(start, size)))
-        return moves
-
-    return shuffle("place_tokens", [(TOK, 2048)], plan, (yi, xh), *pieces)[0]
+        out_shape=(jax.ShapeDtypeStruct((TOK, 2048), BF16),) * 2,
+        in_specs=[pl.BlockSpec(memory_space=pltpu.SMEM)] + [pl.BlockSpec(memory_space=pl.ANY)] * len(pieces),
+        out_specs=(pl.BlockSpec(memory_space=pltpu.VMEM),) * 2,
+        scratch_shapes=[pltpu.VMEM((TOK, 4096), BF16), pltpu.SemaphoreType.DMA((len(parts),))],
+        compiler_params=pltpu.CompilerParams(vmem_limit_bytes=VMEM_LIMIT),
+        cost_estimate=SMALL,
+        name="place_tokens",
+    )(jnp.stack([yi, xh, core]).astype(jnp.int32), *pieces)
 
 
 def weight_blocks(zi, shifts, keep, theirs, normed, normed_other):
@@ -500,40 +479,55 @@
     )(jnp.stack([(zi + k + 8) % 8 for k in (shift, -shift)]).astype(jnp.int32), keep, theirs, normed, normed_other, up, down)
 
 
-def back_project(core, keep, give, w):
-    def kernel(core_ref, a_ref, b_ref, v_ref, w_ref, out_ref):
-        out_ref[...] = dot(a_ref[...], v_ref[...].reshape(2048, 256)) + dot(b_ref[...], w_ref[...].reshape(2048, 256))
-
-    rows = pl.BlockSpec((TOK, 2048), lambda i, core: (0, 0))
+def first_step(zi, keep, theirs, normed, normed_other):
+    def kernel(at_ref, a_ref, b_ref, n_ref, m_ref, up_out, down_out):
+        def term(r, n):
+            return lax.dot_general(r[...], n[...], (((0,), (0,)), ((), ())), preferred_element_type=F32)
+
+        total = term(a_ref, n_ref) + term(b_ref, m_ref)
+        up_out[...] = total[:, CH // 2:].astype(BF16)
+        down_out[...] = total[:, :CH // 2].astype(BF16)
+
+    columns = pl.BlockSpec((TOK, 256), lambda i, at: (0, at[0]))
+    whole = pl.BlockSpec((TOK, CH), lambda i, at: (0, 0))
+    part = pl.BlockSpec((256, CH // 2), lambda i, at: (0, 0))
     return pl.pallas_call(
         kernel,
         grid_spec=pltpu.PrefetchScalarGridSpec(
-            num_scalar_prefetch=1,
-            grid=(4,),
-            in_specs=[
-                rows,
-                rows,
-                pl.BlockSpec((16, None, 128, 256), lambda i, core: (0, core[0], 0, i)),
-                pl.BlockSpec((16, None, 128, 256), lambda i, core: (0, 1 - core[0], 0, i)),
-            ],
-            out_specs=pl.BlockSpec((TOK, 256), lambda i, core: (0, i)),
-        ),
+            num_scalar_prefetch=1, grid=(1,), in_specs=[columns, columns, whole, whole], out_specs=(part, part)),
+        out_shape=(jax.ShapeDtypeStruct((256, CH // 2), BF16),) * 2,
+        compiler_params=pltpu.CompilerParams(vmem_limit_bytes=VMEM_LIMIT),
+        cost_estimate=SMALL,
+        name="first_step",
+    )(((zi + 4) % 8).astype(jnp.int32).reshape(1), keep, theirs, normed, normed_other)
+
+
+def back_project(keep, give, w_keep, w_give):
+    def kernel(a_ref, b_ref, v_ref, w_ref, out_ref):
+        out_ref[...] = dot(a_ref[...], v_ref[...]) + dot(b_ref[...], w_ref[...])
+
+    rows = pl.BlockSpec((TOK, 2048), lambda i: (0, 0))
+    columns = pl.BlockSpec((2048, 256), lambda i: (0, i))
+    return pl.pallas_call(
+        kernel,
+        grid=(4,),
+        in_specs=[rows, rows, columns, columns],
+        out_specs=pl.BlockSpec((TOK, 256), lambda i: (0, i)),
         out_shape=jax.ShapeDtypeStruct((TOK, CH), F32),
         compiler_params=pltpu.CompilerParams(vmem_limit_bytes=VMEM_LIMIT),
         cost_estimate=SMALL,
         name="back_project",
-    )(core.astype(jnp.int32).reshape(1), keep, give, w, w)
+    )(keep, give, w_keep, w_give)
 
 
 def on_device(grad_out, x, z, b, c, dt, rate, skip, gain, w_out):
     zi, xl, core, yi, xh = (lax.axis_index(a) for a in ("z", "xl", "c", "y", "xh"))
     scan = (x, z, b.reshape(TOK, 128), c.reshape(TOK, 128), dt, rate[None], skip[None], gain[None])
 
-    w = lax.all_gather(w_out, DP, axis=0, tiled=True).reshape(16, 2, 128, CH)
-
-    own = own_first(grad_out, core)
-    below, above = both_ways(own, own, "y")
-    other = send(own, "xh", 1)
+    w_keep = lax.all_gather(w_out, ("z", "xl"), axis=0, tiled=True)
+
+    other = send(grad_out, "xh", 1)
+    below, above = both_ways(grad_out, grad_out, "y")
     below, above, other, late = tie((below, above, other, scan[6]))
 
     b_other, a_other = both_ways(other, other, "y")
@@ -544,19 +538,18 @@
     far_other = both_ways(b_other[:32], a_other[32:], "y")
     normed_other = send(normed, "c", 1)
     far_other, normed_other = tie((far_other, normed_other))
-    pieces = (own, other, below, b_other, above, a_other, far_b, far_a) + far_other
-    give = place_tokens(yi, xh, 2048, *pieces)
+    pieces = (grad_out, other, below, b_other, above, a_other, far_b, far_a) + far_other
+    keep, give = place_tokens(yi, xh, core, *pieces)
     theirs = send(give, "c", 1)
-    keep = place_tokens(yi, xh, 0, *tie(pieces, give))
     theirs, keep = tie((theirs, keep))
+    w_keep, = tie((w_keep,), theirs)
+    w_give = send(w_keep, "c", 1)
 
     def blocks(*shifts):
         return weight_blocks(zi, shifts, keep, theirs, normed, normed_other)
 
-    half = CH // 2
-    far = blocks(4)[0].astype(BF16)
-    up, down = both_ways(far[:, half:], far[:, :half], "z")
-    upstream = back_project(core, keep, give, w)
+    up, down = both_ways(*first_step(zi, keep, theirs, normed, normed_other), "z")
+    upstream = back_project(keep, give, w_keep, w_give)
     up, down, upstream = tie((up, down, upstream))
 
     up, down = both_ways(*ring_step(zi, 3, keep, theirs, normed, normed_other, up, down), "z")

time: 174 us -> 211 us (1.21)
  waiting for transfers between devices: 37.6 us -> 76.5 us
  local copies, waits for them, and re-layouts: 14.3 us -> 19.8 us
  Pallas kernels: 58.6 us -> 55.2 us
  starting transfers between devices: 44.1 us -> 40.8 us
    all_gather x1, waiting for transfers between devices: 3.02 us -> 41.4 us  [on_device(): w_keep = lax.all_gather(w_out, ('z', 'xl'), axis=0, tiled=True)]
    unnamed x50 -> x60, local copies, waits for them, and re-layouts: 7.54 us -> 15.3 us
    ppermute x24 -> x25, starting transfers between devices: 38.9 us -> 34.7 us  [send(): return lax.ppermute(v, axis, [(i, (i + shift) % n) for i in range(n)])]
    pallas_call x2 -> x1, Pallas kernels: 6.92 us -> 5.2 us  [weight_blocks(): pl.pallas_call(kernel, grid_spec=pltpu.PrefetchScalarGridSpec(num_scalar_...]
    pallas_call x4 -> x3, Pallas kernels: 17.2 us -> 15.5 us  [the longest x1 7.86 us: back_project(): pl.pallas_call(kernel, grid=(4,), in_specs=[rows, rows, columns, columns]...]
    ppermute x24 -> x25, waiting for transfers between devices: 30.1 us -> 31.3 us  [send(): return lax.ppermute(v, axis, [(i, (i + shift) % n) for i in range(n)])]
  transfers between devices with their start and end apart: 28 -> 29, of which waited for: 14 -> 14; matrix products, arithmetic and copies ran while one was open for 6% -> 3% of each run, Pallas kernels for 29% -> 22%
where the time goes in v3:
time: 211 us; the launch traced here: 210 us
  waiting for transfers between devices  76.5 us (36%)
  Pallas kernels  55.2 us (26%)
  starting transfers between devices  40.8 us (19%)
  local copies, waits for them, and re-layouts  19.8 us (9%)
  between operations  14.4 us (7%)
  other arithmetic  3.41 us (2%)
    all_gather x1, waiting for transfers between devices, on_device(): w_keep = lax.all_gather(w_out, ('z', 'xl'), axis=0, tiled=True)  41.4 us
    ppermute x25, starting transfers between devices, send(): return lax.ppermute(v, axis, [(i, (i + shift) % n) for i in range(n)])  34.7 us
    ppermute x25, waiting for transfers between devices, send(): return lax.ppermute(v, axis, [(i, (i + shift) % n) for i in range(n)])  31.3 us
    pallas_call x1, Pallas kernels, scan_backward(): pl.pallas_call(bwd_kernel, out_shape=(jax.ShapeDtypeStruct((TOK, CH), BF1...  18.1 us
    unnamed x60, local copies, waits for them, and re-layouts  15.3 us
    pallas_call x1, Pallas kernels, scan_forward(): pl.pallas_call(fwd_kernel, out_shape=(jax.ShapeDtypeStruct((TOK, CH), F32...  8.43 us
    pallas_call x2, Pallas kernels, ring_step(): pl.pallas_call(kernel, grid_spec=pltpu.PrefetchScalarGridSpec(num_scalar_...  7.88 us
    pallas_call x1, Pallas kernels, back_project(): pl.pallas_call(kernel, grid=(4,), in_specs=[rows, rows, columns, columns]...  7.86 us
  transfers between devices with their start and end apart: 29, of which 14 were waited for; matrix products, arithmetic and copies ran while one was open for 3% of the time, Pallas kernels for 22%

profile of v3, /device:TPU:2, one launch (start us, length us, event | category | flops | bytes accessed | tf_op | source)
XLA Modules:
  0.0 210.2 jit_solution(17785591828550113870)
XLA Ops:
  7.2 0.7 all-gather.2.cloned.1.call-update
  7.9 1.7 collective-permute-start
  9.6 1.7 collective-permute-start.1
  11.2 2.1 %collective-permute-start.2 = (bf16[64,4096]{1,0:T(8,128)(2,1)}, bf16[64,4096]{1,0:T(8,128)(2,1)}, u32[]{:S(2)}, u32[]{:S(2)}) collective-permute-start(bf16[64,4096]{1,0:T(8,128)(2,1)} %refs_0_.1), channel_id=1, source_target_pairs={{0,1},{1,0},{2,3},{3,2},{4,5},{5,4},{6,7},{7,6},{8,9},{9,8},{10,11... | collective-permute-start | bytes 1572872 | tf_op jit(solution)/shard_map/ppermute | solution.py:361
  13.4 9.8 %collective-permute-done.refs_2_ = bf16[64,4096]{1,0:T(8,128)(2,1)S(1)} collective-permute-done((bf16[64,4096]{1,0:T(8,128)(2,1)}, bf16[64,4096]{1,0:T(8,128)(2,1)S(1)}, u32[]{:S(2)}, u32[]{:S(2)}) %collective-permute-start) | collective-permute-done | bytes 524320 | tf_op jit(solution)/shard_map/ppermute | solution.py:361
  23.2 3.1 %collective-permute-done.2.refs_1_ = bf16[64,4096]{1,0:T(8,128)(2,1)} collective-permute-done((bf16[64,4096]{1,0:T(8,128)(2,1)}, bf16[64,4096]{1,0:T(8,128)(2,1)}, u32[]{:S(2)}, u32[]{:S(2)}) %collective-permute-start.2) | collective-permute-done | bytes 524320 | tf_op jit(solution)/shard_map/ppermute | solution.py:361
  26.3 0.2 collective-permute-start.3
  26.5 3.0 %collective-permute-start.4 = (bf16[64,4096]{1,0:T(8,128)(2,1)}, bf16[64,4096]{1,0:T(8,128)(2,1)}, u32[]{:S(2)}, u32[]{:S(2)}) collective-permute-start(bf16[64,4096]{1,0:T(8,128)(2,1)} %collective-permute-done.2.refs_1_), channel_id=1, source_target_pairs={{0,6},{2,0},{4,2},{6,4},{1,7},{3,1},{5,3},{7,5},{8,14},{10,8},{12,... | collective-permute-start | bytes 1572872 | tf_op jit(solution)/shard_map/ppermute | solution.py:361
  29.7 3.3 %collective-permute-start.6 = (bf16[32,4096]{1,0:T(8,128)(2,1)S(1)}, bf16[32,4096]{1,0:T(8,128)(2,1)}, u32[]{:S(2)}, u32[]{:S(2)}) collective-permute-start(bf16[32,4096]{1,0:T(8,128)(2,1)S(1)} %slice.31), channel_id=1, source_target_pairs={{0,6},{2,0},{4,2},{6,4},{1,7},{3,1},{5,3},{7,5},{8,14},{10,8},{12,... | collective-permute-start | bytes 786440 | tf_op jit(solution)/shard_map/ppermute | solution.py:361
  33.0 0.9 copy.19.dt_ref
  33.9 1.2 copy-done.9
  35.1 0.9 copy-done.17
  36.0 0.9 copy-done.19
  36.9 0.7 copy-done.23
  37.6 0.7 copy-done.25
  38.3 0.7 copy-done.27
  38.9 8.4 %scan_forward.1 = (f32[512,1024]{1,0:T(8,128)S(1)}, bf16[512,1024]{1,0:T(8,128)(2,1)S(1)}) custom-call(bf16[512,1024]{1,0:T(8,128)(2,1)S(1)} %copy-done.7, bf16[512,1024]{1,0:T(8,128)(2,1)S(1)} %copy-done.9, bf16[512,128]{1,0:T(8,128)(2,1)S(1)} %bitcast.36, bf16[512,128]{1,0:T(8,128)(2,1)S(1)} %bitcast.38, f32[512,16]{1,0:T(8,128)S(1)} %copy.19.dt_ref, ...), custom_call_target="tpu_custom_call" | custom-call | flops 1000 | bytes 1000 | tf_op jit(solution)/shard_map/scan_forward/pallas_call | solution.py:308
  47.4 1.4 copy-done.11
  48.9 1.0 slice.32
  50.0 1.0 slice.33
  51.0 3.3 %collective-permute-start.8 = (bf16[32,4096]{1,0:T(8,128)(2,1)S(1)}, bf16[32,4096]{1,0:T(8,128)(2,1)S(1)}, u32[]{:S(2)}, u32[]{:S(2)}) collective-permute-start(bf16[32,4096]{1,0:T(8,128)(2,1)S(1)} %slice.33), channel_id=1, source_target_pairs={{0,6},{2,0},{4,2},{6,4},{1,7},{3,1},{5,3},{7,5},{8,14},{10,8},{12,... | collective-permute-start | bytes 786440 | tf_op jit(solution)/shard_map/ppermute | solution.py:361
  54.3 5.6 %collective-permute-done.7.refs_8_ = bf16[32,4096]{1,0:T(8,128)(2,1)S(1)} collective-permute-done((bf16[32,4096]{1,0:T(8,128)(2,1)S(1)}, bf16[32,4096]{1,0:T(8,128)(2,1)S(1)}, u32[]{:S(2)}, u32[]{:S(2)}) %collective-permute-start.7) | collective-permute-done | bytes 262176 | tf_op jit(solution)/shard_map/ppermute | solution.py:361
  59.9 0.3 collective-permute-done.8.refs_9_
  60.2 1.0 copy-done.13
  61.3 1.0 copy-done.15
  62.3 1.0 copy-done.16
  63.3 5.1 %place_tokens.1 = (bf16[512,2048]{1,0:T(8,128)(2,1)}, bf16[512,2048]{1,0:T(8,128)(2,1)}) custom-call(s32[3]{0:T(128)S(1)} %pad_add_fusion.s_ref, bf16[64,4096]{1,0:T(8,128)(2,1)S(1)} %copy-done.16, bf16[64,4096]{1,0:T(8,128)(2,1)} %collective-permute-done.2.refs_1_, bf16[64,4096]{1,0:T(8,128)(2,1)S(1)} %copy-done.13, ...), custom_call_target="tpu_custom_call" | custom-call | flops 1000 | bytes 1000 | tf_op jit(solution)/shard_map/place_tokens/pallas_call | solution.py:405
  68.5 0.1 collective-permute-start.10
  68.6 4.5 %collective-permute-done.10.b_ref = bf16[512,2048]{1,0:T(8,128)(2,1)} collective-permute-done((bf16[512,2048]{1,0:T(8,128)(2,1)}, bf16[512,2048]{1,0:T(8,128)(2,1)}, u32[]{:S(2)}, u32[]{:S(2)}) %collective-permute-start.10) | collective-permute-done | bytes 2097184 | tf_op jit(solution)/shard_map/ppermute | solution.py:361
  73.1 41.4 %all-gather.2.cloned.1.call-done.v_ref = bf16[2048,1024]{1,0:T(8,128)(2,1)} async-done(((bf16[128,1024]{1,0:T(8,128)(2,1)}), bf16[2048,1024]{1,0:T(8,128)(2,1)}) %all-gather.2.cloned.1.call-update) | async-done | bytes 4194320 | tf_op jit(solution)/shard_map/all_gather | solution.py:527
  114.5 1.6 copy-done
  116.1 1.2 copy-done.4
  117.3 2.6 %first_step.1 = (bf16[256,512]{1,0:T(8,128)(2,1)}, bf16[256,512]{1,0:T(8,128)(2,1)}) custom-call(s32[1]{0:T(128)} %bitcast.at_ref, bf16[512,2048]{1,0:T(8,128)(2,1)S(1)} %copy-done, bf16[512,2048]{1,0:T(8,128)(2,1)} %collective-permute-done.10.b_ref, bf16[512,1024]{1,0:T(8,128)(2,1)S(1)} %get-tuple-element.66.n_ref, bf16[512,1024]{1,0:T(8,128)(2,1)S(1)} %copy-done.4), custom_call_target="tpu_custom_call" | custom-call | flops 1000 | bytes 1000 | tf_op jit(solution)/shard_map/first_step/pallas_call | solution.py:494
  119.8 1.2 collective-permute-start.11
  121.1 2.4 %collective-permute-start.12 = (bf16[256,512]{1,0:T(8,128)(2,1)}, bf16[256,512]{1,0:T(8,128)(2,1)}, u32[]{:S(2)}, u32[]{:S(2)}) collective-permute-start(bf16[256,512]{1,0:T(8,128)(2,1)} %get-tuple-element.75), channel_id=1, source_target_pairs={{0,224},{32,0},{64,32},{96,64},{128,96},{160,128},{192,160},{224,1... | collective-permute-start | bytes 786440 | tf_op jit(solution)/shard_map/ppermute | solution.py:361
  123.6 7.9 %back_project.1.u_ref = f32[512,1024]{1,0:T(8,128)S(1)} custom-call(bf16[512,2048]{1,0:T(8,128)(2,1)S(1)} %copy-done.1, bf16[512,2048]{1,0:T(8,128)(2,1)} %get-tuple-element.69.b_ref, bf16[2048,1024]{1,0:T(8,128)(2,1)} %all-gather.2.cloned.1.call-done.v_ref, bf16[2048,1024]{1,0:T(8,128)(2,1)} %collective-permute-done.13.w_ref), custom_call_target="tpu_custom_call" | custom-call | flops 1000 | bytes 1000 | tf_op jit(solution)/shard_map/back_project/pallas_call | solution.py:511
  131.6 3.4 %ring_step.2 = (bf16[256,1024]{1,0:T(8,128)(2,1)S(1)}, bf16[256,1024]{1,0:T(8,128)(2,1)S(1)}) custom-call(s32[2]{0:T(128)S(1)} %get-tuple-element.123.at_ref, bf16[512,2048]{1,0:T(8,128)(2,1)S(1)} %copy-done.1, bf16[512,2048]{1,0:T(8,128)(2,1)} %collective-permute-done.10.b_ref, bf16[512,1024]{1,0:T(8,128)(2,1)S(1)} %get-tuple-element.66.n_ref, ...), custom_call_target="tpu_custom_call" | custom-call | flops 1000 | bytes 1000 | tf_op jit(solution)/shard_map/ring_step/pallas_call | solution.py:467
  135.1 3.2 %collective-permute-start.15 = (bf16[256,1024]{1,0:T(8,128)(2,1)S(1)}, bf16[256,1024]{1,0:T(8,128)(2,1)S(1)}, u32[]{:S(2)}, u32[]{:S(2)}) collective-permute-start(bf16[256,1024]{1,0:T(8,128)(2,1)S(1)} %get-tuple-element.87), channel_id=1, source_target_pairs={{0,224},{32,0},{64,32},{96,64},{128,96},{160,128},{192,160},{224,1... | collective-permute-start | bytes 1572872 | tf_op jit(solution)/shard_map/ppermute | solution.py:361
  138.4 18.1 %scan_backward.1 = (bf16[512,1024]{1,0:T(8,128)(2,1)}, bf16[512,1024]{1,0:T(8,128)(2,1)}, bf16[512,128]{1,0:T(8,128)(2,1)}, bf16[512,128]{1,0:T(8,128)(2,1)}, f3...) custom-call(f32[512,1024]{1,0:T(8,128)S(1)} %back_project.1.u_ref, f32[512,1024]{1,0:T(8,128)} %copy-done.11, ...), custom_call_target="tpu_custom_call" | custom-call | flops 1000 | bytes 1000 | tf_op jit(solution)/shard_map/scan_backward/pallas_call | solution.py:326
  156.5 4.4 %ring_step.3 = (bf16[256,1024]{1,0:T(8,128)(2,1)}, bf16[256,1024]{1,0:T(8,128)(2,1)}) custom-call(s32[2]{0:T(128)S(1)} %get-tuple-element.122.at_ref, bf16[512,2048]{1,0:T(8,128)(2,1)} %get-tuple-element.71.a_ref, bf16[512,2048]{1,0:T(8,128)(2,1)} %collective-permute-done.10.b_ref, bf16[512,1024]{1,0:T(8,128)(2,1)S(1)} %get-tuple-element.66.n_ref, ...), custom_call_target="tpu_custom_call" | custom-call | flops 1000 | bytes 1000 | tf_op jit(solution)/shard_map/ring_step/pallas_call | solution.py:467
  160.9 3.2 %collective-permute-start.17 = (bf16[256,1024]{1,0:T(8,128)(2,1)}, bf16[256,1024]{1,0:T(8,128)(2,1)}, u32[]{:S(2)}, u32[]{:S(2)}) collective-permute-start(bf16[256,1024]{1,0:T(8,128)(2,1)} %get-tuple-element.92), channel_id=1, source_target_pairs={{0,224},{32,0},{64,32},{96,64},{128,96},{160,128},{192,160},{224,1... | collective-permute-start | bytes 1572872 | tf_op jit(solution)/shard_map/ppermute | solution.py:361
  164.2 1.2 collective-permute-done.18
  165.4 1.8 collective-permute-start.19
  167.2 1.8 collective-permute-done.19
  169.1 1.2 copy-done.6
  170.3 5.2 %weight_blocks.1 = f32[3,256,1024]{2,1,0:T(8,128)} custom-call(s32[3]{0:T(128)S(1)} %pad_add_fusion.3.at_ref, bf16[512,2048]{1,0:T(8,128)(2,1)S(1)} %copy-done.2, bf16[512,2048]{1,0:T(8,128)(2,1)} %collective-permute-done.10.b_ref, bf16[512,1024]{1,0:T(8,128)(2,1)S(1)} %get-tuple-element.66.n_ref, bf16[512,1024]{1,0:T(8,128)(2,1)S(1)} %copy-done.6), custom_call_target="tpu_custom_call" | custom-call | flops 1000 | bytes 1000 | tf_op jit(solution)/shard_map/weight_blocks/pallas_call | solution.py:426
  175.5 0.4 collective-permute-done.16
  176.0 2.2 %fusion = (bf16[256,1024]{1,0:T(8,128)(2,1)S(1)}, bf16[256,1024]{1,0:T(8,128)(2,1)S(1)}) fusion(bf16[256,1024]{1,0:T(8,128)(2,1)} %collective-permute-done.17, f32[3,256,1024]{2,1,0:T(8,128)} %weight_blocks.1, bf16[256,1024]{1,0:T(8,128)(2,1)} %collective-permute-done.16), kind=kLoop, calls=%fused_computation.1 | loop fusion | flops 1572864 | bytes 4194304 | tf_op jit(solution)/shard_map/convert_element_type | solution.py:570
  178.2 3.2 %collective-permute-start.22 = (bf16[128,1024]{1,0:T(8,128)(2,1)S(1)}, bf16[128,1024]{1,0:T(8,128)(2,1)S(1)}, u32[]{:S(2)}, u32[]{:S(2)}) collective-permute-start(bf16[128,1024]{1,0:T(8,128)(2,1)S(1)} %get-tuple-element.117), channel_id=1, source_target_pairs={{0,224},{32,0},{64,32},{96,64},{128,96},{160,128},{192,160},{224,1... | collective-permute-start | bytes 786440 | tf_op jit(solution)/shard_map/ppermute | solution.py:361
  181.6 2.7 %collective-permute-start.23 = (f32[16,128]{1,0:T(8,128)S(1)}, f32[16,128]{1,0:T(8,128)S(1)}, u32[]{:S(2)}, u32[]{:S(2)}) collective-permute-start(f32[16,128]{1,0:T(8,128)S(1)} %add.131), channel_id=1, source_target_pairs={{0,64},{32,96},{64,0},{96,32},{128,192},{160,224},{192,128},{224,1... | collective-permute-start | bytes 24584 | tf_op jit(solution)/shard_map/ppermute | solution.py:365
  184.3 0.7 copy.21
  185.0 1.3 slice.39
  186.4 0.9 collective-permute-done.23
  187.3 1.9 collective-permute-done.21
  189.3 1.6 collective-permute-start.27
  190.9 3.3 %collective-permute-start.24 = (f32[16,128]{1,0:T(8,128)S(1)}, f32[16,128]{1,0:T(8,128)S(1)}, u32[]{:S(2)}, u32[]{:S(2)}) collective-permute-start(f32[16,128]{1,0:T(8,128)S(1)} %add.135), channel_id=1, source_target_pairs={{0,128},{32,160},{64,192},{96,224},{128,0},{160,32},{192,64},{224,... | collective-permute-start | bytes 24584 | tf_op jit(solution)/shard_map/ppermute | solution.py:365
  194.3 0.5 collective-permute-start.26
  194.8 1.6 collective-permute-start.25
  196.4 2.2 %collective-permute-done.24 = f32[16,128]{1,0:T(8,128)S(1)} collective-permute-done((f32[16,128]{1,0:T(8,128)S(1)}, f32[16,128]{1,0:T(8,128)S(1)}, u32[]{:S(2)}, u32[]{:S(2)}) %collective-permute-start.24) | collective-permute-done | bytes 8224 | tf_op jit(solution)/shard_map/ppermute | solution.py:365
  198.6 0.5 slice_bitcast_fusion.1
  199.1 0.6 slice_bitcast_fusion
  199.7 1.0 collective-permute-done.26
  200.7 1.7 collective-permute-done.25
  202.4 0.9 add_add_fusion
  (84 shorter events, 1.1 us)
Async XLA Ops:
  7.2 26.7 %copy-start.7 = (bf16[512,1024]{1,0:T(8,128)(2,1)S(1)}, bf16[512,1024]{1,0:T(8,128)(2,1)}, u32[]{:S(2)}) copy-start(bf16[512,1024]{1,0:T(8,128)(2,1)} %x_ref.3) | copy-start | bytes 3145732
  7.2 107.3 %all-gather.2.cloned.1.call-start = ((), (), s32[]{:S(2)}) async-start(), calls=%async_computation | async-start | bytes 4456448 | tf_op jit(solution)/shard_map/all_gather | solution.py:527
  7.9 15.2 %collective-permute-start = (bf16[64,4096]{1,0:T(8,128)(2,1)}, bf16[64,4096]{1,0:T(8,128)(2,1)S(1)}, u32[]{:S(2)}, u32[]{:S(2)}) collective-permute-start(bf16[64,4096]{1,0:T(8,128)(2,1)} %refs_0_.1), channel_id=1, source_target_pairs={{0,2},{2,4},{4,6},{6,0},{1,3},{3,5},{5,7},{7,1},{8,10},{10,12},{12... | collective-permute-start | bytes 1572872 | tf_op jit(solution)/shard_map/ppermute | solution.py:361
  9.6 13.6 %collective-permute-start.1 = (bf16[64,4096]{1,0:T(8,128)(2,1)}, bf16[64,4096]{1,0:T(8,128)(2,1)S(1)}, u32[]{:S(2)}, u32[]{:S(2)}) collective-permute-start(bf16[64,4096]{1,0:T(8,128)(2,1)} %refs_0_.1), channel_id=1, source_target_pairs={{0,6},{2,0},{4,2},{6,4},{1,7},{3,1},{5,3},{7,5},{8,14},{10,8},{12,... | collective-permute-start | bytes 1572872 | tf_op jit(solution)/shard_map/ppermute | solution.py:361
  11.2 15.1 %collective-permute-start.2 = (bf16[64,4096]{1,0:T(8,128)(2,1)}, bf16[64,4096]{1,0:T(8,128)(2,1)}, u32[]{:S(2)}, u32[]{:S(2)}) collective-permute-start(bf16[64,4096]{1,0:T(8,128)(2,1)} %refs_0_.1), channel_id=1, source_target_pairs={{0,1},{1,0},{2,3},{3,2},{4,5},{5,4},{6,7},{7,6},{8,9},{9,8},{10,11... | collective-permute-start | bytes 1572872 | tf_op jit(solution)/shard_map/ppermute | solution.py:361
  23.1 6.5 %copy-start.12 = (bf16[64,4096]{1,0:T(8,128)(2,1)}, bf16[64,4096]{1,0:T(8,128)(2,1)S(1)}, u32[]{:S(2)}) copy-start(bf16[64,4096]{1,0:T(8,128)(2,1)S(1)} %collective-permute-done.refs_2_) | copy-start | bytes 1572868
  23.2 6.5 %copy-start.14 = (bf16[64,4096]{1,0:T(8,128)(2,1)}, bf16[64,4096]{1,0:T(8,128)(2,1)S(1)}, u32[]{:S(2)}) copy-start(bf16[64,4096]{1,0:T(8,128)(2,1)S(1)} %collective-permute-done.1.refs_4_) | copy-start | bytes 1572868
  26.3 22.5 %collective-permute-start.3 = (bf16[64,4096]{1,0:T(8,128)(2,1)}, bf16[64,4096]{1,0:T(8,128)(2,1)}, u32[]{:S(2)}, u32[]{:S(2)}) collective-permute-start(bf16[64,4096]{1,0:T(8,128)(2,1)} %collective-permute-done.2.refs_1_), channel_id=1, source_target_pairs={{0,2},{2,4},{4,6},{6,0},{1,3},{3,5},{5,7},{7,1},{8,10},{10,12},{12... | collective-permute-start | bytes 1572872 | tf_op jit(solution)/shard_map/ppermute | solution.py:361
  26.5 22.3 %collective-permute-start.4 = (bf16[64,4096]{1,0:T(8,128)(2,1)}, bf16[64,4096]{1,0:T(8,128)(2,1)}, u32[]{:S(2)}, u32[]{:S(2)}) collective-permute-start(bf16[64,4096]{1,0:T(8,128)(2,1)} %collective-permute-done.2.refs_1_), channel_id=1, source_target_pairs={{0,6},{2,0},{4,2},{6,4},{1,7},{3,1},{5,3},{7,5},{8,14},{10,8},{12,... | collective-permute-start | bytes 1572872 | tf_op jit(solution)/shard_map/ppermute | solution.py:361
  29.6 19.2 %collective-permute-start.5 = (bf16[32,4096]{1,0:T(8,128)(2,1)S(1)}, bf16[32,4096]{1,0:T(8,128)(2,1)}, u32[]{:S(2)}, u32[]{:S(2)}) collective-permute-start(bf16[32,4096]{1,0:T(8,128)(2,1)S(1)} %slice.30), channel_id=1, source_target_pairs={{0,2},{2,4},{4,6},{6,0},{1,3},{3,5},{5,7},{7,1},{8,10},{10,12},{12... | collective-permute-start | bytes 786440 | tf_op jit(solution)/shard_map/ppermute | solution.py:361
  29.7 19.1 %collective-permute-start.6 = (bf16[32,4096]{1,0:T(8,128)(2,1)S(1)}, bf16[32,4096]{1,0:T(8,128)(2,1)}, u32[]{:S(2)}, u32[]{:S(2)}) collective-permute-start(bf16[32,4096]{1,0:T(8,128)(2,1)S(1)} %slice.31), channel_id=1, source_target_pairs={{0,6},{2,0},{4,2},{6,4},{1,7},{3,1},{5,3},{7,5},{8,14},{10,8},{12,... | collective-permute-start | bytes 786440 | tf_op jit(solution)/shard_map/ppermute | solution.py:361
  33.9 1.2 copy-start.9
  35.1 0.9 copy-start.17
  36.0 0.9 copy-start.19
  36.9 0.7 copy-start.23
  37.6 0.7 copy-start.25
  38.3 0.7 copy-start.27
  47.4 1.4 copy-start.11
  48.8 11.4 %collective-permute-start.9 = (bf16[512,1024]{1,0:T(8,128)(2,1)S(1)}, bf16[512,1024]{1,0:T(8,128)(2,1)S(1)}, u32[]{:S(2)}, u32[]{:S(2)}) collective-permute-start(bf16[512,1024]{1,0:T(8,128)(2,1)S(1)} %get-tuple-element.66.n_ref), channel_id=1, source_target_pairs={{0,8},{8,0},{1,9},{9,1},{2,10},{10,2},{3,11},{11,3},{4,12},{12,4},... | collective-permute-start | bytes 3145736 | tf_op jit(solution)/shard_map/ppermute | solution.py:361
  49.9 10.0 %collective-permute-start.7 = (bf16[32,4096]{1,0:T(8,128)(2,1)S(1)}, bf16[32,4096]{1,0:T(8,128)(2,1)S(1)}, u32[]{:S(2)}, u32[]{:S(2)}) collective-permute-start(bf16[32,4096]{1,0:T(8,128)(2,1)S(1)} %slice.32), channel_id=1, source_target_pairs={{0,2},{2,4},{4,6},{6,0},{1,3},{3,5},{5,7},{7,1},{8,10},{10,12},{12... | collective-permute-start | bytes 786440 | tf_op jit(solution)/shard_map/ppermute | solution.py:361
  51.0 9.2 %collective-permute-start.8 = (bf16[32,4096]{1,0:T(8,128)(2,1)S(1)}, bf16[32,4096]{1,0:T(8,128)(2,1)S(1)}, u32[]{:S(2)}, u32[]{:S(2)}) collective-permute-start(bf16[32,4096]{1,0:T(8,128)(2,1)S(1)} %slice.33), channel_id=1, source_target_pairs={{0,6},{2,0},{4,2},{6,4},{1,7},{3,1},{5,3},{7,5},{8,14},{10,8},{12,... | collective-permute-start | bytes 786440 | tf_op jit(solution)/shard_map/ppermute | solution.py:361
  60.2 1.0 copy-start.13
  61.3 1.0 copy-start.15
  62.3 1.0 copy-start.16
  63.3 5.1 %copy-start.3 = (bf16[512,1024]{1,0:T(8,128)(2,1)}, bf16[512,1024]{1,0:T(8,128)(2,1)S(1)}, u32[]{:S(2)}) copy-start(bf16[512,1024]{1,0:T(8,128)(2,1)S(1)} %collective-permute-done.9.m_ref) | copy-start | bytes 3145732
  68.5 4.6 %collective-permute-start.10 = (bf16[512,2048]{1,0:T(8,128)(2,1)}, bf16[512,2048]{1,0:T(8,128)(2,1)}, u32[]{:S(2)}, u32[]{:S(2)}) collective-permute-start(bf16[512,2048]{1,0:T(8,128)(2,1)} %get-tuple-element.69.b_ref), channel_id=1, source_target_pairs={{0,8},{8,0},{1,9},{9,1},{2,10},{10,2},{3,11},{11,3},{4,12},{12,4},... | collective-permute-start | bytes 6291464 | tf_op jit(solution)/shard_map/ppermute | solution.py:361
  114.5 9.1 %collective-permute-start.13 = (bf16[2048,1024]{1,0:T(8,128)(2,1)}, bf16[2048,1024]{1,0:T(8,128)(2,1)}, u32[]{:S(2)}, u32[]{:S(2)}) collective-permute-start(bf16[2048,1024]{1,0:T(8,128)(2,1)} %all-gather.2.cloned.1.call-done.v_ref), channel_id=1, source_target_pairs={{0,8},{8,0},{1,9},{9,1},{2,10},{10,2},{3,11},{11,3},{4,12},{12,4},... | collective-permute-start | bytes 12582920 | tf_op jit(solution)/shard_map/ppermute | solution.py:361
  114.5 1.6 copy-start
  116.1 1.2 copy-start.4
  117.3 6.3 %copy-start.1 = (bf16[512,2048]{1,0:T(8,128)(2,1)S(1)}, bf16[512,2048]{1,0:T(8,128)(2,1)}, u32[]{:S(2)}) copy-start(bf16[512,2048]{1,0:T(8,128)(2,1)} %get-tuple-element.71.a_ref) | copy-start | bytes 6291460
  119.8 11.6 %collective-permute-start.11 = (bf16[256,512]{1,0:T(8,128)(2,1)}, bf16[256,512]{1,0:T(8,128)(2,1)}, u32[]{:S(2)}, u32[]{:S(2)}) collective-permute-start(bf16[256,512]{1,0:T(8,128)(2,1)} %get-tuple-element.74), channel_id=1, source_target_pairs={{0,32},{32,64},{64,96},{96,128},{128,160},{160,192},{192,224},{224... | collective-permute-start | bytes 786440 | tf_op jit(solution)/shard_map/ppermute | solution.py:361
  121.1 10.4 %collective-permute-start.12 = (bf16[256,512]{1,0:T(8,128)(2,1)}, bf16[256,512]{1,0:T(8,128)(2,1)}, u32[]{:S(2)}, u32[]{:S(2)}) collective-permute-start(bf16[256,512]{1,0:T(8,128)(2,1)} %get-tuple-element.75), channel_id=1, source_target_pairs={{0,224},{32,0},{64,32},{96,64},{128,96},{160,128},{192,160},{224,1... | collective-permute-start | bytes 786440 | tf_op jit(solution)/shard_map/ppermute | solution.py:361
  123.6 7.9 %copy-start.5 = (bf16[512,1024]{1,0:T(8,128)(2,1)S(1)}, bf16[512,1024]{1,0:T(8,128)(2,1)}, u32[]{:S(2)}) copy-start(bf16[512,1024]{1,0:T(8,128)(2,1)} %copy-done.3) | copy-start | bytes 3145732
  131.5 6.9 %copy-start.8 = (bf16[512,1024]{1,0:T(8,128)(2,1)S(1)}, bf16[512,1024]{1,0:T(8,128)(2,1)}, u32[]{:S(2)}) copy-start(bf16[512,1024]{1,0:T(8,128)(2,1)} %x_ref.3) | copy-start | bytes 3145732
  131.5 6.8 %copy-start.10 = (bf16[512,1024]{1,0:T(8,128)(2,1)S(1)}, bf16[512,1024]{1,0:T(8,128)(2,1)}, u32[]{:S(2)}) copy-start(bf16[512,1024]{1,0:T(8,128)(2,1)} %z_ref.3) | copy-start | bytes 3145732
  131.5 6.8 %copy-start.18 = (bf16[512,1,128]{2,0,1:T(8,128)(2,1)S(1)}, bf16[512,1,128]{2,0,1:T(8,128)(2,1)}, u32[]{:S(2)}) copy-start(bf16[512,1,128]{2,0,1:T(8,128)(2,1)} %param.13) | copy-start | bytes 393220
  131.5 6.8 %copy-start.20 = (bf16[512,1,128]{2,0,1:T(8,128)(2,1)S(1)}, bf16[512,1,128]{2,0,1:T(8,128)(2,1)}, u32[]{:S(2)}) copy-start(bf16[512,1,128]{2,0,1:T(8,128)(2,1)} %param.14) | copy-start | bytes 393220
  131.5 6.8 %copy-start.24 = (f32[1024]{0:T(1024)S(1)}, f32[1024]{0:T(1024)}, u32[]{:S(2)}) copy-start(f32[1024]{0:T(1024)} %param.18) | copy-start | bytes 12292
  131.5 6.8 %copy-start.26 = (f32[16]{0:T(128)S(1)}, f32[16]{0:T(128)}, u32[]{:S(2)}) copy-start(f32[16]{0:T(128)} %param.16) | copy-start | bytes 196
  131.6 6.8 %copy-start.28 = (f32[16]{0:T(128)S(1)}, f32[16]{0:T(128)}, u32[]{:S(2)}) copy-start(f32[16]{0:T(128)} %param.17) | copy-start | bytes 196
  135.0 21.5 %collective-permute-start.14 = (bf16[256,1024]{1,0:T(8,128)(2,1)S(1)}, bf16[256,1024]{1,0:T(8,128)(2,1)S(1)}, u32[]{:S(2)}, u32[]{:S(2)}) collective-permute-start(bf16[256,1024]{1,0:T(8,128)(2,1)S(1)} %get-tuple-element.86), channel_id=1, source_target_pairs={{0,32},{32,64},{64,96},{96,128},{128,160},{160,192},{192,224},{224... | collective-permute-start | bytes 1572872 | tf_op jit(solution)/shard_map/ppermute | solution.py:361
  135.1 21.4 %collective-permute-start.15 = (bf16[256,1024]{1,0:T(8,128)(2,1)S(1)}, bf16[256,1024]{1,0:T(8,128)(2,1)S(1)}, u32[]{:S(2)}, u32[]{:S(2)}) collective-permute-start(bf16[256,1024]{1,0:T(8,128)(2,1)S(1)} %get-tuple-element.87), channel_id=1, source_target_pairs={{0,224},{32,0},{64,32},{96,64},{128,96},{160,128},{192,160},{224,1... | collective-permute-start | bytes 1572872 | tf_op jit(solution)/shard_map/ppermute | solution.py:361
  156.5 4.5 %copy-start.21 = (f32[512,16]{1,0:T(8,128)}, f32[512,16]{1,0:T(8,128)S(1)}, u32[]{:S(2)}) copy-start(f32[512,16]{1,0:T(8,128)S(1)} %get-tuple-element.109) | copy-start | bytes 98308
  156.5 12.6 %copy-start.2 = (bf16[512,2048]{1,0:T(8,128)(2,1)S(1)}, bf16[512,2048]{1,0:T(8,128)(2,1)}, u32[]{:S(2)}) copy-start(bf16[512,2048]{1,0:T(8,128)(2,1)} %get-tuple-element.71.a_ref) | copy-start | bytes 6291460
  160.9 15.0 %collective-permute-start.16 = (bf16[256,1024]{1,0:T(8,128)(2,1)}, bf16[256,1024]{1,0:T(8,128)(2,1)}, u32[]{:S(2)}, u32[]{:S(2)}) collective-permute-start(bf16[256,1024]{1,0:T(8,128)(2,1)} %get-tuple-element.91), channel_id=1, source_target_pairs={{0,32},{32,64},{64,96},{96,128},{128,160},{160,192},{192,224},{224... | collective-permute-start | bytes 1572872 | tf_op jit(solution)/shard_map/ppermute | solution.py:361
  160.9 15.0 %collective-permute-start.17 = (bf16[256,1024]{1,0:T(8,128)(2,1)}, bf16[256,1024]{1,0:T(8,128)(2,1)}, u32[]{:S(2)}, u32[]{:S(2)}) collective-permute-start(bf16[256,1024]{1,0:T(8,128)(2,1)} %get-tuple-element.92), channel_id=1, source_target_pairs={{0,224},{32,0},{64,32},{96,64},{128,96},{160,128},{192,160},{224,1... | collective-permute-start | bytes 1572872 | tf_op jit(solution)/shard_map/ppermute | solution.py:361
  164.2 1.2 collective-permute-start.18
  165.4 3.7 %collective-permute-start.19 = (f32[16,128]{1,0:T(8,128)S(1)}, f32[16,128]{1,0:T(8,128)S(1)}, u32[]{:S(2)}, u32[]{:S(2)}) collective-permute-start(f32[16,128]{1,0:T(8,128)S(1)} %add.129), channel_id=1, source_target_pairs={{0,16},{16,0},{1,17},{17,1},{2,18},{18,2},{3,19},{19,3},{4,20},{20... | collective-permute-start | bytes 24584 | tf_op jit(solution)/shard_map/ppermute | solution.py:361
  169.0 6.5 %collective-permute-start.20 = (f32[16,128]{1,0:T(8,128)S(1)}, f32[16,128]{1,0:T(8,128)S(1)}, u32[]{:S(2)}, u32[]{:S(2)}) collective-permute-start(f32[16,128]{1,0:T(8,128)S(1)} %add.130), channel_id=1, source_target_pairs={{0,32},{32,0},{64,96},{96,64},{128,160},{160,128},{192,224},{224,1... | collective-permute-start | bytes 24584 | tf_op jit(solution)/shard_map/ppermute | solution.py:365
  169.1 1.2 copy-start.6
  178.1 6.2 %copy-start.22 = (f32[512,16]{1,0:T(8,128)S(1)}, f32[512,16]{1,0:T(8,128)}, u32[]{:S(2)}) copy-start(f32[512,16]{1,0:T(8,128)} %copy-done.21) | copy-start | bytes 98308
  178.2 9.1 %collective-permute-start.22 = (bf16[128,1024]{1,0:T(8,128)(2,1)S(1)}, bf16[128,1024]{1,0:T(8,128)(2,1)S(1)}, u32[]{:S(2)}, u32[]{:S(2)}) collective-permute-start(bf16[128,1024]{1,0:T(8,128)(2,1)S(1)} %get-tuple-element.117), channel_id=1, source_target_pairs={{0,224},{32,0},{64,32},{96,64},{128,96},{160,128},{192,160},{224,1... | collective-permute-start | bytes 786440 | tf_op jit(solution)/shard_map/ppermute | solution.py:361
  181.5 7.7 %collective-permute-start.21 = (bf16[128,1024]{1,0:T(8,128)(2,1)S(1)}, bf16[128,1024]{1,0:T(8,128)(2,1)S(1)}, u32[]{:S(2)}, u32[]{:S(2)}) collective-permute-start(bf16[128,1024]{1,0:T(8,128)(2,1)S(1)} %get-tuple-element.119), channel_id=1, source_target_pairs={{0,32},{32,64},{64,96},{96,128},{128,160},{160,192},{192,224},{224... | collective-permute-start | bytes 786440 | tf_op jit(solution)/shard_map/ppermute | solution.py:361
  181.6 5.7 %collective-permute-start.23 = (f32[16,128]{1,0:T(8,128)S(1)}, f32[16,128]{1,0:T(8,128)S(1)}, u32[]{:S(2)}, u32[]{:S(2)}) collective-permute-start(f32[16,128]{1,0:T(8,128)S(1)} %add.131), channel_id=1, source_target_pairs={{0,64},{32,96},{64,0},{96,32},{128,192},{160,224},{192,128},{224,1... | collective-permute-start | bytes 24584 | tf_op jit(solution)/shard_map/ppermute | solution.py:365
  189.3 13.1 %collective-permute-start.27 = (f32[128,1024]{1,0:T(8,128)S(1)}, f32[128,1024]{1,0:T(8,128)S(1)}, u32[]{:S(2)}, u32[]{:S(2)}) collective-permute-start(f32[128,1024]{1,0:T(8,128)S(1)} %bitcast_add_fusion.2), channel_id=1, source_target_pairs={{0,16},{16,0},{1,17},{17,1},{2,18},{18,2},{3,19},{19,3},{4,20},{20... | collective-permute-start | bytes 1572872 | tf_op jit(solution)/shard_map/ppermute | solution.py:361
  190.9 7.7 %collective-permute-start.24 = (f32[16,128]{1,0:T(8,128)S(1)}, f32[16,128]{1,0:T(8,128)S(1)}, u32[]{:S(2)}, u32[]{:S(2)}) collective-permute-start(f32[16,128]{1,0:T(8,128)S(1)} %add.135), channel_id=1, source_target_pairs={{0,128},{32,160},{64,192},{96,224},{128,0},{160,32},{192,64},{224,... | collective-permute-start | bytes 24584 | tf_op jit(solution)/shard_map/ppermute | solution.py:365
  194.3 6.5 %collective-permute-start.26 = (bf16[128,1024]{1,0:T(8,128)(2,1)S(1)}, bf16[128,1024]{1,0:T(8,128)(2,1)S(1)}, u32[]{:S(2)}, u32[]{:S(2)}) collective-permute-start(bf16[128,1024]{1,0:T(8,128)(2,1)S(1)} %get-tuple-element.116), channel_id=1, source_target_pairs={{0,224},{32,0},{64,32},{96,64},{128,96},{160,128},{192,160},{224,1... | collective-permute-start | bytes 786440 | tf_op jit(solution)/shard_map/ppermute | solution.py:361
  194.8 7.6 %collective-permute-start.25 = (bf16[128,1024]{1,0:T(8,128)(2,1)S(1)}, bf16[128,1024]{1,0:T(8,128)(2,1)S(1)}, u32[]{:S(2)}, u32[]{:S(2)}) collective-permute-start(bf16[128,1024]{1,0:T(8,128)(2,1)S(1)} %get-tuple-element.118), channel_id=1, source_target_pairs={{0,32},{32,64},{64,96},{96,128},{128,160},{160,192},{192,224},{224... | collective-permute-start | bytes 786440 | tf_op jit(solution)/shard_map/ppermute | solution.py:361
Sparse Core Ops, SparseCore 0:
  9.8 104.6 all-gather.1

commit v4 on v2

--- a/solution.py
+++ b/solution.py
@@ -149,9 +149,16 @@
     lax.fori_loop(0, TOK // 32, norm, 0)
 
 
-def bwd_kernel(u_ref, ys_ref, x_ref, z_ref, b_ref, c_ref, dt_ref, rate_ref, skip_ref, gain_ref,
-               dx_ref, dz_ref, db_ref, dc_ref, ddt_ref, small_ref,
-               pad_ref, ratepad_ref, rexp_ref, ct_ref, s_ref, coef_ref, dy_ref, dxs_ref, ds_ref, dg_ref):
+def bwd_kernel(u_hbm, ys_hbm, x_hbm, z_hbm, b_ref, c_ref, dt_ref, rate_ref, skip_ref, gain_ref,
+               dx_ref, dz_hbm, db_ref, dc_ref, ddt_ref, small_ref,
+               pad_ref, ratepad_ref, rexp_ref, ct_ref, s_ref, coef_ref, dy_ref, dxs_ref, ds_ref, dg_ref,
+               u_ref, ys_ref, x_ref, z_ref, dz_ref, sem):
+    loads = [
+        pltpu.make_async_copy(src, dst, sem.at[j])
+        for j, (src, dst) in enumerate(((z_hbm, z_ref), (ys_hbm, ys_ref), (x_hbm, x_ref), (u_hbm, u_ref)))
+    ]
+    for load in loads:
+        load.start()
     rate, cums, rs = prepare(dt_ref, rate_ref, pad_ref, ratepad_ref)
     wide = spread_matrix(HALF)
     narrow = spread_matrix(64)
@@ -191,7 +198,11 @@
         dz_ref[rows, :] = (dgated * y * (sig * (1.0 + z * (1.0 - sig)))).astype(BF16)
         return 0
 
+    for load in loads:
+        load.wait()
     lax.fori_loop(0, TOK // 32, gate, 0)
+    store = pltpu.make_async_copy(dz_ref, dz_hbm, sem.at[4])
+    store.start()
 
     ds_ref[...] = jnp.zeros((2, SPAN, SPAN), F32)
     lane = lax.broadcasted_iota(jnp.int32, (SPAN, 128), 1)
@@ -302,6 +313,7 @@
     small_ref[8:9, :] = rate_sum
     small_ref[9:10, :] = skip_sum
     small_ref[10:16, :] = jnp.zeros((6, 128), F32)
+    store.wait()
 
 
 def scan_forward(x, z, b, c, dt, rate, skip, gain):
@@ -344,7 +356,15 @@
             pltpu.VMEM((TOK, CH), F32),
             pltpu.VMEM((2, SPAN, SPAN), F32),
             pltpu.VMEM((8, CH), F32),
+            pltpu.VMEM((TOK, CH), F32),
+            pltpu.VMEM((TOK, CH), F32),
+            pltpu.VMEM((TOK, CH), BF16),
+            pltpu.VMEM((TOK, CH), BF16),
+            pltpu.VMEM((TOK, CH), BF16),
+            pltpu.SemaphoreType.DMA((5,)),
         ],
+        in_specs=[pl.BlockSpec(memory_space=pltpu.HBM)] * 4 + [pl.BlockSpec(memory_space=pltpu.VMEM)] * 6,
+        out_specs=tuple(pl.BlockSpec(memory_space=pltpu.HBM if j == 1 else pltpu.VMEM) for j in range(6)),
         compiler_params=pltpu.CompilerParams(vmem_limit_bytes=VMEM_LIMIT),
         cost_estimate=SMALL,
         name="scan_backward",
@@ -556,19 +576,20 @@
     half = CH // 2
     far = blocks(4)[0].astype(BF16)
     up, down = both_ways(far[:, half:], far[:, :half], "z")
+    last = blocks(1, -1, 0)
+    w, = tie((w,), last)
     upstream = back_project(core, keep, give, w)
-    up, down, upstream = tie((up, down, upstream))
+    up, down, last, upstream = tie((up, down, last, upstream))
 
     up, down = both_ways(*ring_step(zi, 3, keep, theirs, normed, normed_other, up, down), "z")
     dx, dz, db, dc, ddt, small = scan_backward(upstream, ys, *scan)
     up, down, small = tie((up, down, small))
 
     up, down = both_ways(*ring_step(zi, 2, keep, theirs, normed, normed_other, up, down), "z")
-    last = blocks(1, -1, 0)
     small = small + send(small, "c", 1)
     small = small + send(small, "xl", 1)
     small = small + swap(small, "z", 1)
-    up, down, last, small = tie((up, down, last, small))
+    up, down, small = tie((up, down, small))
 
     def halves(r):
         return lax.dynamic_slice_in_dim(r, (1 - xl) * 128, 128, 0), lax.dynamic_slice_in_dim(r, xl * 128, 128, 0)

time: 174 us -> 174 us (level); the launches traced: 174 us -> 172 us
  waiting for transfers between devices: 37.6 us -> 42.1 us
  starting transfers between devices: 44.1 us -> 40.6 us
  Pallas kernels: 58.6 us -> 56 us
    ppermute x3, waiting for transfers between devices: 3.89 us -> 12.4 us  [swap(): return lax.ppermute(v, axis, [(i, i ^ mask) for i in range(AXES[axis])])]
    ppermute x3, starting transfers between devices: 5.17 us -> 1.11 us  [swap(): return lax.ppermute(v, axis, [(i, i ^ mask) for i in range(AXES[axis])])]
    all_gather x1, waiting for transfers between devices: 3.02 us -> 0.01 us  [on_device(): w = lax.all_gather(w_out, DP, axis=0, tiled=True).reshape(16, 2, 128, CH)]
    unnamed x50 -> x44, local copies, waits for them, and re-layouts: 7.54 us -> 7.48 us
  transfers between devices with their start and end apart: 28 -> 28, of which waited for: 14 -> 13; matrix products, arithmetic and copies ran while one was open for 6% -> 6% of each run, Pallas kernels for 29% -> 29%
where the time goes in v4:
time: 174 us; the launch traced here: 172 us
  Pallas kernels  56 us (32%)
  waiting for transfers between devices  42.1 us (24%)
  starting transfers between devices  40.6 us (23%)
  between operations  14.5 us (8%)
  local copies, waits for them, and re-layouts  14.3 us (8%)
  other arithmetic  4.36 us (3%)
    ppermute x24, starting transfers between devices, send(): return lax.ppermute(v, axis, [(i, (i + shift) % n) for i in range(n)])  39.5 us
    ppermute x24, waiting for transfers between devices, send(): return lax.ppermute(v, axis, [(i, (i + shift) % n) for i in range(n)])  29 us
    pallas_call x1, Pallas kernels, scan_backward(): pl.pallas_call(bwd_kernel, out_shape=(jax.ShapeDtypeStruct((TOK, CH), BF1...  16.6 us
    ppermute x3, waiting for transfers between devices, swap(): return lax.ppermute(v, axis, [(i, i ^ mask) for i in range(AXES[axis])])  12.4 us
    pallas_call x1, Pallas kernels, scan_forward(): pl.pallas_call(fwd_kernel, out_shape=(jax.ShapeDtypeStruct((TOK, CH), F32...  8.58 us
    pallas_call x1, Pallas kernels, back_project(): pl.pallas_call(kernel, grid_spec=pltpu.PrefetchScalarGridSpec(num_scalar_...  7.92 us
    unnamed x44, local copies, waits for them, and re-layouts  7.48 us
    pallas_call x2, Pallas kernels, shuffle(): pl.pallas_call(kernel, out_shape=tuple((jax.ShapeDtypeStruct(s, BF16) for...  7.24 us
  transfers between devices with their start and end apart: 28, of which 13 were waited for; matrix products, arithmetic and copies ran while one was open for 6% of the time, Pallas kernels for 29%

profile of v4, /device:TPU:2, one launch (start us, length us, event | category | flops | bytes accessed | tf_op | source)
XLA Modules:
  0.0 171.7 jit_solution(3619701961730950935)
XLA Ops:
  7.3 0.7 all-gather.2.cloned.1.call-update
  8.0 2.0 %own_first.1.refs_0_ = bf16[64,4096]{1,0:T(8,128)(2,1)} custom-call(s32[1]{0:T(128)} %bitcast.3.core_ref, bf16[64,4096]{1,0:T(8,128)(2,1)} %in_ref.1), custom_call_target="tpu_custom_call" | custom-call | flops 1000 | bytes 1000 | tf_op jit(solution)/shard_map/own_first/pallas_call | solution.py:430
  10.0 1.6 collective-permute-start
  11.5 1.7 collective-permute-start.1
  13.2 2.1 %collective-permute-start.2 = (bf16[64,4096]{1,0:T(8,128)(2,1)}, bf16[64,4096]{1,0:T(8,128)(2,1)}, u32[]{:S(2)}, u32[]{:S(2)}) collective-permute-start(bf16[64,4096]{1,0:T(8,128)(2,1)} %own_first.1.refs_0_), channel_id=1, source_target_pairs={{0,1},{1,0},{2,3},{3,2},{4,5},{5,4},{6,7},{7,6},{8,9},{9,8},{10,11... | collective-permute-start | bytes 1572872 | tf_op jit(solution)/shard_map/ppermute | solution.py:381
  15.3 9.8 %collective-permute-done.refs_2_ = bf16[64,4096]{1,0:T(8,128)(2,1)S(1)} collective-permute-done((bf16[64,4096]{1,0:T(8,128)(2,1)}, bf16[64,4096]{1,0:T(8,128)(2,1)S(1)}, u32[]{:S(2)}, u32[]{:S(2)}) %collective-permute-start) | collective-permute-done | bytes 524320 | tf_op jit(solution)/shard_map/ppermute | solution.py:381
  25.1 4.8 %collective-permute-done.2.refs_1_ = bf16[64,4096]{1,0:T(8,128)(2,1)} collective-permute-done((bf16[64,4096]{1,0:T(8,128)(2,1)}, bf16[64,4096]{1,0:T(8,128)(2,1)}, u32[]{:S(2)}, u32[]{:S(2)}) %collective-permute-start.2) | collective-permute-done | bytes 524320 | tf_op jit(solution)/shard_map/ppermute | solution.py:381
  29.9 3.2 %collective-permute-start.4 = (bf16[64,4096]{1,0:T(8,128)(2,1)}, bf16[64,4096]{1,0:T(8,128)(2,1)}, u32[]{:S(2)}, u32[]{:S(2)}) collective-permute-start(bf16[64,4096]{1,0:T(8,128)(2,1)} %collective-permute-done.2.refs_1_), channel_id=1, source_target_pairs={{0,6},{2,0},{4,2},{6,4},{1,7},{3,1},{5,3},{7,5},{8,14},{10,8},{12,... | collective-permute-start | bytes 1572872 | tf_op jit(solution)/shard_map/ppermute | solution.py:381
  33.1 0.7 slice.36
  33.9 0.7 slice.37
  34.6 3.2 %collective-permute-start.6 = (bf16[32,4096]{1,0:T(8,128)(2,1)}, bf16[32,4096]{1,0:T(8,128)(2,1)}, u32[]{:S(2)}, u32[]{:S(2)}) collective-permute-start(bf16[32,4096]{1,0:T(8,128)(2,1)} %slice.37), channel_id=1, source_target_pairs={{0,6},{2,0},{4,2},{6,4},{1,7},{3,1},{5,3},{7,5},{8,14},{10,8},{12,... | collective-permute-start | bytes 786440 | tf_op jit(solution)/shard_map/ppermute | solution.py:381
  37.8 0.9 copy.19.dt_ref
  38.8 0.9 copy-done.11
  39.7 8.6 %scan_forward.1 = (f32[512,1024]{1,0:T(8,128)S(1)}, bf16[512,1024]{1,0:T(8,128)(2,1)S(1)}) custom-call(bf16[512,1024]{1,0:T(8,128)(2,1)S(1)} %copy-done.5, bf16[512,1024]{1,0:T(8,128)(2,1)S(1)} %copy-done.7, bf16[512,128]{1,0:T(8,128)(2,1)S(1)} %bitcast.39, bf16[512,128]{1,0:T(8,128)(2,1)S(1)} %bitcast.41, f32[512,16]{1,0:T(8,128)S(1)} %copy.19.dt_ref, ...), custom_call_target="tpu_custom_call" | custom-call | flops 1000 | bytes 1000 | tf_op jit(solution)/shard_map/scan_forward/pallas_call | solution.py:320
  48.3 1.3 copy-done.9
  49.7 0.1 collective-permute-start.9
  49.8 1.0 slice.38
  50.8 1.0 slice.39
  51.8 3.3 %collective-permute-start.8 = (bf16[32,4096]{1,0:T(8,128)(2,1)S(1)}, bf16[32,4096]{1,0:T(8,128)(2,1)S(1)}, u32[]{:S(2)}, u32[]{:S(2)}) collective-permute-start(bf16[32,4096]{1,0:T(8,128)(2,1)S(1)} %slice.39), channel_id=1, source_target_pairs={{0,6},{2,0},{4,2},{6,4},{1,7},{3,1},{5,3},{7,5},{8,14},{10,8},{12,... | collective-permute-start | bytes 786440 | tf_op jit(solution)/shard_map/ppermute | solution.py:381
  55.1 0.6 pad_add_fusion
  55.7 5.0 %collective-permute-done.7.refs_8_ = bf16[32,4096]{1,0:T(8,128)(2,1)S(1)} collective-permute-done((bf16[32,4096]{1,0:T(8,128)(2,1)S(1)}, bf16[32,4096]{1,0:T(8,128)(2,1)S(1)}, u32[]{:S(2)}, u32[]{:S(2)}) %collective-permute-start.7) | collective-permute-done | bytes 262176 | tf_op jit(solution)/shard_map/ppermute | solution.py:381
  60.7 0.3 collective-permute-done.8.refs_9_
  61.1 0.4 copy-done.19
  61.4 0.3 copy-done.20
  61.8 3.6 %place_tokens.2.b_ref = bf16[512,2048]{1,0:T(8,128)(2,1)} custom-call(s32[2]{0:T(128)} %get-tuple-element.136.s_ref, bf16[64,4096]{1,0:T(8,128)(2,1)} %own_first.1.refs_0_, bf16[64,4096]{1,0:T(8,128)(2,1)} %collective-permute-done.2.refs_1_, bf16[64,4096]{1,0:T(8,128)(2,1)} %copy-done.17, bf16[64,4096]{1,0:T(8,128)(2,1)} %collective-permute-done.3.refs_3_, ...), custom_call_target="tpu_custom_call" | custom-call | flops 1000 | bytes 1000 | tf_op jit(solution)/shard_map/place_tokens/pallas_call | solution.py:410
  65.4 0.1 collective-permute-start.10
  65.5 3.7 %place_tokens.3.a_ref = bf16[512,2048]{1,0:T(8,128)(2,1)} custom-call(s32[2]{0:T(128)} %get-tuple-element.136.s_ref, bf16[64,4096]{1,0:T(8,128)(2,1)} %own_first.1.refs_0_, bf16[64,4096]{1,0:T(8,128)(2,1)} %collective-permute-done.2.refs_1_, bf16[64,4096]{1,0:T(8,128)(2,1)} %copy-done.17, bf16[64,4096]{1,0:T(8,128)(2,1)} %collective-permute-done.3.refs_3_, ...), custom_call_target="tpu_custom_call" | custom-call | flops 1000 | bytes 1000 | tf_op jit(solution)/shard_map/place_tokens/pallas_call | solution.py:410
  69.1 0.8 collective-permute-done.10.b_ref
  69.9 1.6 copy-done
  71.6 1.7 weight_blocks.2
  73.4 0.8 fusion.2
  74.2 0.2 collective-permute-start.11
  74.4 9.1 %collective-permute-start.12 = (bf16[256,512]{1,0:T(8,128)(2,1)}, bf16[256,512]{1,0:T(8,128)(2,1)}, u32[]{:S(2)}, u32[]{:S(2)}) collective-permute-start(bf16[256,512]{1,0:T(8,128)(2,1)} %get-tuple-element.132), channel_id=1, source_target_pairs={{0,224},{32,0},{64,32},{96,64},{128,96},{160,128},{192,160},{224,1... | collective-permute-start | bytes 786440 | tf_op jit(solution)/shard_map/ppermute | solution.py:381
  83.6 0.6 pad_add_fusion.3.at_ref
  84.2 1.2 copy-done.3
  85.5 5.2 %weight_blocks.3 = f32[3,256,1024]{2,1,0:T(8,128)} custom-call(s32[3]{0:T(128)S(1)} %pad_add_fusion.1.at_ref, bf16[512,2048]{1,0:T(8,128)(2,1)S(1)} %copy-done.1, bf16[512,2048]{1,0:T(8,128)(2,1)} %collective-permute-done.10.b_ref, bf16[512,1024]{1,0:T(8,128)(2,1)S(1)} %get-tuple-element.72.n_ref, bf16[512,1024]{1,0:T(8,128)(2,1)S(1)} %copy-done.3), custom_call_target="tpu_custom_call" | custom-call | flops 1000 | bytes 1000 | tf_op jit(solution)/shard_map/weight_blocks/pallas_call | solution.py:467
  90.6 7.9 %back_project.1.u_hbm = f32[512,1024]{1,0:T(8,128)S(1)} custom-call(s32[1]{0:T(128)} %bitcast.3.core_ref, bf16[512,2048]{1,0:T(8,128)(2,1)S(1)} %copy-done.1, bf16[512,2048]{1,0:T(8,128)(2,1)} %place_tokens.2.b_ref, bf16[16,2,128,1024]{3,2,1,0:T(8,128)(2,1)} %bitcast.49, bf16[16,2,128,1024]{3,2,1,0:T(8,128)(2,1)} %bitcast.50), custom_call_target="tpu_custom_call" | custom-call | flops 1000 | bytes 1000 | tf_op jit(solution)/shard_map/back_project/pallas_call | solution.py:528
  98.7 3.4 %ring_step.2 = (bf16[256,1024]{1,0:T(8,128)(2,1)S(1)}, bf16[256,1024]{1,0:T(8,128)(2,1)S(1)}) custom-call(s32[2]{0:T(128)S(1)} %copy-done.16, bf16[512,2048]{1,0:T(8,128)(2,1)S(1)} %copy-done.1, bf16[512,2048]{1,0:T(8,128)(2,1)} %collective-permute-done.10.b_ref, bf16[512,1024]{1,0:T(8,128)(2,1)S(1)} %get-tuple-element.72.n_ref, ...), custom_call_target="tpu_custom_call" | custom-call | flops 1000 | bytes 1000 | tf_op jit(solution)/shard_map/ring_step/pallas_call | solution.py:508
  102.1 3.2 %collective-permute-start.14 = (bf16[256,1024]{1,0:T(8,128)(2,1)S(1)}, bf16[256,1024]{1,0:T(8,128)(2,1)S(1)}, u32[]{:S(2)}, u32[]{:S(2)}) collective-permute-start(bf16[256,1024]{1,0:T(8,128)(2,1)S(1)} %get-tuple-element.100), channel_id=1, source_target_pairs={{0,224},{32,0},{64,32},{96,64},{128,96},{160,128},{192,160},{224,1... | collective-permute-start | bytes 1572872 | tf_op jit(solution)/shard_map/ppermute | solution.py:381
  105.4 16.6 %scan_backward.1 = (bf16[512,1024]{1,0:T(8,128)(2,1)}, bf16[512,1024]{1,0:T(8,128)(2,1)}, bf16[512,128]{1,0:T(8,128)(2,1)}, bf16[512,128]{1,0:T(8,128)(2,1)}, f3...) custom-call(f32[512,1024]{1,0:T(8,128)S(1)} %back_project.1.u_hbm, f32[512,1024]{1,0:T(8,128)} %copy-done.9, ...), custom_call_target="tpu_custom_call" | custom-call | flops 1000 | bytes 1000 | tf_op jit(solution)/shard_map/scan_backward/pallas_call | solution.py:338
  122.0 3.3 %ring_step.3 = (bf16[256,1024]{1,0:T(8,128)(2,1)S(1)}, bf16[256,1024]{1,0:T(8,128)(2,1)S(1)}) custom-call(s32[2]{0:T(128)S(1)} %get-tuple-element.137.at_ref, bf16[512,2048]{1,0:T(8,128)(2,1)} %place_tokens.3.a_ref, bf16[512,2048]{1,0:T(8,128)(2,1)} %collective-permute-done.10.b_ref, bf16[512,1024]{1,0:T(8,128)(2,1)S(1)} %get-tuple-element.72.n_ref, ...), custom_call_target="tpu_custom_call" | custom-call | flops 1000 | bytes 1000 | tf_op jit(solution)/shard_map/ring_step/pallas_call | solution.py:508
  125.5 3.2 %collective-permute-start.16 = (bf16[256,1024]{1,0:T(8,128)(2,1)S(1)}, bf16[256,1024]{1,0:T(8,128)(2,1)}, u32[]{:S(2)}, u32[]{:S(2)}) collective-permute-start(bf16[256,1024]{1,0:T(8,128)(2,1)S(1)} %get-tuple-element.105), channel_id=1, source_target_pairs={{0,224},{32,0},{64,32},{96,64},{128,96},{160,128},{192,160},{224,1... | collective-permute-start | bytes 1572872 | tf_op jit(solution)/shard_map/ppermute | solution.py:381
  128.7 1.2 collective-permute-done.17
  129.9 1.3 collective-permute-start.18
  131.1 2.4 %collective-permute-done.18 = f32[16,128]{1,0:T(8,128)S(1)} collective-permute-done((f32[16,128]{1,0:T(8,128)S(1)}, f32[16,128]{1,0:T(8,128)S(1)}, u32[]{:S(2)}, u32[]{:S(2)}) %collective-permute-start.18) | collective-permute-done | bytes 8224 | tf_op jit(solution)/shard_map/ppermute | solution.py:381
  133.5 5.3 %collective-permute-done.19 = f32[16,128]{1,0:T(8,128)S(1)} collective-permute-done((f32[16,128]{1,0:T(8,128)S(1)}, f32[16,128]{1,0:T(8,128)S(1)}, u32[]{:S(2)}, u32[]{:S(2)}) %collective-permute-start.19) | collective-permute-done | bytes 8224 | tf_op jit(solution)/shard_map/ppermute | solution.py:385
  138.8 0.9 collective-permute-done.15
  139.7 2.0 %fusion = (bf16[256,1024]{1,0:T(8,128)(2,1)S(1)}, bf16[256,1024]{1,0:T(8,128)(2,1)S(1)}) fusion(bf16[256,1024]{1,0:T(8,128)(2,1)} %collective-permute-done.16, f32[3,256,1024]{2,1,0:T(8,128)} %weight_blocks.3, bf16[256,1024]{1,0:T(8,128)(2,1)S(1)} %collective-permute-done.15), kind=kLoop, calls=%fused_computation.1 | loop fusion | flops 1572864 | bytes 4194304 | tf_op jit(solution)/shard_map/convert_element_type | solution.py:598
  141.8 3.1 %collective-permute-start.21 = (bf16[128,1024]{1,0:T(8,128)(2,1)S(1)}, bf16[128,1024]{1,0:T(8,128)(2,1)S(1)}, u32[]{:S(2)}, u32[]{:S(2)}) collective-permute-start(bf16[128,1024]{1,0:T(8,128)(2,1)S(1)} %get-tuple-element.129), channel_id=1, source_target_pairs={{0,224},{32,0},{64,32},{96,64},{128,96},{160,128},{192,160},{224,1... | collective-permute-start | bytes 786440 | tf_op jit(solution)/shard_map/ppermute | solution.py:381
  145.0 0.3 collective-permute-start.20
  145.3 0.1 collective-permute-start.22
  145.4 1.3 slice.47
  146.8 3.2 %collective-permute-done.22 = f32[16,128]{1,0:T(8,128)S(1)} collective-permute-done((f32[16,128]{1,0:T(8,128)S(1)}, f32[16,128]{1,0:T(8,128)S(1)}, u32[]{:S(2)}, u32[]{:S(2)}) %collective-permute-start.22) | collective-permute-done | bytes 8224 | tf_op jit(solution)/shard_map/ppermute | solution.py:385
  150.0 2.9 %collective-permute-done.20 = bf16[128,1024]{1,0:T(8,128)(2,1)S(1)} collective-permute-done((bf16[128,1024]{1,0:T(8,128)(2,1)S(1)}, bf16[128,1024]{1,0:T(8,128)(2,1)S(1)}, u32[]{:S(2)}, u32[]{:S(2)}) %collective-permute-start.20) | collective-permute-done | bytes 262176 | tf_op jit(solution)/shard_map/ppermute | solution.py:381
  153.0 1.3 collective-permute-start.26
  154.3 1.0 collective-permute-start.23
  155.4 0.7 copy.21
  156.1 0.2 collective-permute-start.25
  156.3 1.8 %collective-permute-start.24 = (bf16[128,1024]{1,0:T(8,128)(2,1)S(1)}, bf16[128,1024]{1,0:T(8,128)(2,1)S(1)}, u32[]{:S(2)}, u32[]{:S(2)}) collective-permute-start(bf16[128,1024]{1,0:T(8,128)(2,1)S(1)} %get-tuple-element.130), channel_id=1, source_target_pairs={{0,32},{32,64},{64,96},{96,128},{128,160},{160,192},{192,224},{224... | collective-permute-start | bytes 786440 | tf_op jit(solution)/shard_map/ppermute | solution.py:381
  158.1 3.9 %collective-permute-done.23 = f32[16,128]{1,0:T(8,128)S(1)} collective-permute-done((f32[16,128]{1,0:T(8,128)S(1)}, f32[16,128]{1,0:T(8,128)S(1)}, u32[]{:S(2)}, u32[]{:S(2)}) %collective-permute-start.23) | collective-permute-done | bytes 8224 | tf_op jit(solution)/shard_map/ppermute | solution.py:385
  162.0 0.5 slice_bitcast_fusion.1
  162.6 0.6 slice_bitcast_fusion
  163.2 0.8 collective-permute-done.24
  164.0 0.9 add_add_fusion
  (70 shorter events, 0.8 us)
Async XLA Ops:
  7.2 31.5 %copy-start.15 = (f32[16]{0:T(128)S(1)}, f32[16]{0:T(128)}, u32[]{:S(2)}) copy-start(f32[16]{0:T(128)} %param.17) | copy-start | bytes 196
  7.2 31.5 %copy-start.10 = (bf16[512,1,128]{2,0,1:T(8,128)(2,1)S(1)}, bf16[512,1,128]{2,0,1:T(8,128)(2,1)}, u32[]{:S(2)}) copy-start(bf16[512,1,128]{2,0,1:T(8,128)(2,1)} %param.13) | copy-start | bytes 393220
  7.2 31.5 %copy-start.14 = (f32[16]{0:T(128)S(1)}, f32[16]{0:T(128)}, u32[]{:S(2)}) copy-start(f32[16]{0:T(128)} %param.16) | copy-start | bytes 196
  7.2 31.5 %copy-start.13 = (f32[1024]{0:T(1024)S(1)}, f32[1024]{0:T(1024)}, u32[]{:S(2)}) copy-start(f32[1024]{0:T(1024)} %param.18) | copy-start | bytes 12292
  7.2 31.5 %copy-start.5 = (bf16[512,1024]{1,0:T(8,128)(2,1)S(1)}, bf16[512,1024]{1,0:T(8,128)(2,1)}, u32[]{:S(2)}) copy-start(bf16[512,1024]{1,0:T(8,128)(2,1)} %x_hbm.1) | copy-start | bytes 3145732
  7.2 31.5 %copy-start.7 = (bf16[512,1024]{1,0:T(8,128)(2,1)S(1)}, bf16[512,1024]{1,0:T(8,128)(2,1)}, u32[]{:S(2)}) copy-start(bf16[512,1024]{1,0:T(8,128)(2,1)} %z_hbm.1) | copy-start | bytes 3145732
  7.2 83.4 %all-gather.2.cloned.1.call-start = ((), (), s32[]{:S(2)}) async-start(), calls=%async_computation | async-start | bytes 8650752 | tf_op jit(solution)/shard_map/all_gather | solution.py:552
  10.0 15.1 %collective-permute-start = (bf16[64,4096]{1,0:T(8,128)(2,1)}, bf16[64,4096]{1,0:T(8,128)(2,1)S(1)}, u32[]{:S(2)}, u32[]{:S(2)}) collective-permute-start(bf16[64,4096]{1,0:T(8,128)(2,1)} %own_first.1.refs_0_), channel_id=1, source_target_pairs={{0,2},{2,4},{4,6},{6,0},{1,3},{3,5},{5,7},{7,1},{8,10},{10,12},{12... | collective-permute-start | bytes 1572872 | tf_op jit(solution)/shard_map/ppermute | solution.py:381
  11.5 13.6 %collective-permute-start.1 = (bf16[64,4096]{1,0:T(8,128)(2,1)}, bf16[64,4096]{1,0:T(8,128)(2,1)S(1)}, u32[]{:S(2)}, u32[]{:S(2)}) collective-permute-start(bf16[64,4096]{1,0:T(8,128)(2,1)} %own_first.1.refs_0_), channel_id=1, source_target_pairs={{0,6},{2,0},{4,2},{6,4},{1,7},{3,1},{5,3},{7,5},{8,14},{10,8},{12,... | collective-permute-start | bytes 1572872 | tf_op jit(solution)/shard_map/ppermute | solution.py:381
  13.2 16.7 %collective-permute-start.2 = (bf16[64,4096]{1,0:T(8,128)(2,1)}, bf16[64,4096]{1,0:T(8,128)(2,1)}, u32[]{:S(2)}, u32[]{:S(2)}) collective-permute-start(bf16[64,4096]{1,0:T(8,128)(2,1)} %own_first.1.refs_0_), channel_id=1, source_target_pairs={{0,1},{1,0},{2,3},{3,2},{4,5},{5,4},{6,7},{7,6},{8,9},{9,8},{10,11... | collective-permute-start | bytes 1572872 | tf_op jit(solution)/shard_map/ppermute | solution.py:381
  25.1 13.6 %copy-start.17 = (bf16[64,4096]{1,0:T(8,128)(2,1)}, bf16[64,4096]{1,0:T(8,128)(2,1)S(1)}, u32[]{:S(2)}) copy-start(bf16[64,4096]{1,0:T(8,128)(2,1)S(1)} %collective-permute-done.refs_2_) | copy-start | bytes 1572868
  25.1 13.6 %copy-start.18 = (bf16[64,4096]{1,0:T(8,128)(2,1)}, bf16[64,4096]{1,0:T(8,128)(2,1)S(1)}, u32[]{:S(2)}) copy-start(bf16[64,4096]{1,0:T(8,128)(2,1)S(1)} %collective-permute-done.1.refs_4_) | copy-start | bytes 1572868
  29.9 19.7 %collective-permute-start.3 = (bf16[64,4096]{1,0:T(8,128)(2,1)}, bf16[64,4096]{1,0:T(8,128)(2,1)}, u32[]{:S(2)}, u32[]{:S(2)}) collective-permute-start(bf16[64,4096]{1,0:T(8,128)(2,1)} %collective-permute-done.2.refs_1_), channel_id=1, source_target_pairs={{0,2},{2,4},{4,6},{6,0},{1,3},{3,5},{5,7},{7,1},{8,10},{10,12},{12... | collective-permute-start | bytes 1572872 | tf_op jit(solution)/shard_map/ppermute | solution.py:381
  29.9 19.8 %collective-permute-start.4 = (bf16[64,4096]{1,0:T(8,128)(2,1)}, bf16[64,4096]{1,0:T(8,128)(2,1)}, u32[]{:S(2)}, u32[]{:S(2)}) collective-permute-start(bf16[64,4096]{1,0:T(8,128)(2,1)} %collective-permute-done.2.refs_1_), channel_id=1, source_target_pairs={{0,6},{2,0},{4,2},{6,4},{1,7},{3,1},{5,3},{7,5},{8,14},{10,8},{12,... | collective-permute-start | bytes 1572872 | tf_op jit(solution)/shard_map/ppermute | solution.py:381
  33.9 15.8 %collective-permute-start.5 = (bf16[32,4096]{1,0:T(8,128)(2,1)}, bf16[32,4096]{1,0:T(8,128)(2,1)}, u32[]{:S(2)}, u32[]{:S(2)}) collective-permute-start(bf16[32,4096]{1,0:T(8,128)(2,1)} %slice.36), channel_id=1, source_target_pairs={{0,2},{2,4},{4,6},{6,0},{1,3},{3,5},{5,7},{7,1},{8,10},{10,12},{12... | collective-permute-start | bytes 786440 | tf_op jit(solution)/shard_map/ppermute | solution.py:381
  34.6 15.1 %collective-permute-start.6 = (bf16[32,4096]{1,0:T(8,128)(2,1)}, bf16[32,4096]{1,0:T(8,128)(2,1)}, u32[]{:S(2)}, u32[]{:S(2)}) collective-permute-start(bf16[32,4096]{1,0:T(8,128)(2,1)} %slice.37), channel_id=1, source_target_pairs={{0,6},{2,0},{4,2},{6,4},{1,7},{3,1},{5,3},{7,5},{8,14},{10,8},{12,... | collective-permute-start | bytes 786440 | tf_op jit(solution)/shard_map/ppermute | solution.py:381
  38.8 0.9 copy-start.11
  48.3 1.4 copy-start.9
  49.7 11.4 %collective-permute-start.9 = (bf16[512,1024]{1,0:T(8,128)(2,1)S(1)}, bf16[512,1024]{1,0:T(8,128)(2,1)S(1)}, u32[]{:S(2)}, u32[]{:S(2)}) collective-permute-start(bf16[512,1024]{1,0:T(8,128)(2,1)S(1)} %get-tuple-element.72.n_ref), channel_id=1, source_target_pairs={{0,8},{8,0},{1,9},{9,1},{2,10},{10,2},{3,11},{11,3},{4,12},{12,4},... | collective-permute-start | bytes 3145736 | tf_op jit(solution)/shard_map/ppermute | solution.py:381
  50.7 10.0 %collective-permute-start.7 = (bf16[32,4096]{1,0:T(8,128)(2,1)S(1)}, bf16[32,4096]{1,0:T(8,128)(2,1)S(1)}, u32[]{:S(2)}, u32[]{:S(2)}) collective-permute-start(bf16[32,4096]{1,0:T(8,128)(2,1)S(1)} %slice.38), channel_id=1, source_target_pairs={{0,2},{2,4},{4,6},{6,0},{1,3},{3,5},{5,7},{7,1},{8,10},{10,12},{12... | collective-permute-start | bytes 786440 | tf_op jit(solution)/shard_map/ppermute | solution.py:381
  51.8 9.2 %collective-permute-start.8 = (bf16[32,4096]{1,0:T(8,128)(2,1)S(1)}, bf16[32,4096]{1,0:T(8,128)(2,1)S(1)}, u32[]{:S(2)}, u32[]{:S(2)}) collective-permute-start(bf16[32,4096]{1,0:T(8,128)(2,1)S(1)} %slice.39), channel_id=1, source_target_pairs={{0,6},{2,0},{4,2},{6,4},{1,7},{3,1},{5,3},{7,5},{8,14},{10,8},{12,... | collective-permute-start | bytes 786440 | tf_op jit(solution)/shard_map/ppermute | solution.py:381
  60.7 0.7 copy-start.19
  61.0 0.7 copy-start.20
  61.0 8.9 %copy-start.2 = (bf16[512,1024]{1,0:T(8,128)(2,1)}, bf16[512,1024]{1,0:T(8,128)(2,1)S(1)}, u32[]{:S(2)}) copy-start(bf16[512,1024]{1,0:T(8,128)(2,1)S(1)} %collective-permute-done.9.m_ref) | copy-start | bytes 3145732
  65.4 4.6 %collective-permute-start.10 = (bf16[512,2048]{1,0:T(8,128)(2,1)}, bf16[512,2048]{1,0:T(8,128)(2,1)}, u32[]{:S(2)}, u32[]{:S(2)}) collective-permute-start(bf16[512,2048]{1,0:T(8,128)(2,1)} %place_tokens.2.b_ref), channel_id=1, source_target_pairs={{0,8},{8,0},{1,9},{9,1},{2,10},{10,2},{3,11},{11,3},{4,12},{12,4},... | collective-permute-start | bytes 6291464 | tf_op jit(solution)/shard_map/ppermute | solution.py:381
  69.9 1.6 copy-start
  73.3 10.9 %copy-start.1 = (bf16[512,2048]{1,0:T(8,128)(2,1)S(1)}, bf16[512,2048]{1,0:T(8,128)(2,1)}, u32[]{:S(2)}) copy-start(bf16[512,2048]{1,0:T(8,128)(2,1)} %place_tokens.3.a_ref) | copy-start | bytes 6291460
  74.2 24.4 %collective-permute-start.11 = (bf16[256,512]{1,0:T(8,128)(2,1)}, bf16[256,512]{1,0:T(8,128)(2,1)}, u32[]{:S(2)}, u32[]{:S(2)}) collective-permute-start(bf16[256,512]{1,0:T(8,128)(2,1)} %get-tuple-element.133), channel_id=1, source_target_pairs={{0,32},{32,64},{64,96},{96,128},{128,160},{160,192},{192,224},{224... | collective-permute-start | bytes 786440 | tf_op jit(solution)/shard_map/ppermute | solution.py:381
  74.4 24.2 %collective-permute-start.12 = (bf16[256,512]{1,0:T(8,128)(2,1)}, bf16[256,512]{1,0:T(8,128)(2,1)}, u32[]{:S(2)}, u32[]{:S(2)}) collective-permute-start(bf16[256,512]{1,0:T(8,128)(2,1)} %get-tuple-element.132), channel_id=1, source_target_pairs={{0,224},{32,0},{64,32},{96,64},{128,96},{160,128},{192,160},{224,1... | collective-permute-start | bytes 786440 | tf_op jit(solution)/shard_map/ppermute | solution.py:381
  84.2 1.2 copy-start.3
  90.6 8.0 %copy-start.4 = (bf16[512,1024]{1,0:T(8,128)(2,1)S(1)}, bf16[512,1024]{1,0:T(8,128)(2,1)}, u32[]{:S(2)}) copy-start(bf16[512,1024]{1,0:T(8,128)(2,1)} %copy-done.2) | copy-start | bytes 3145732
  90.6 8.0 %copy-start.16 = (s32[2]{0:T(128)S(1)}, s32[2]{0:T(128)}, u32[]{:S(2)}) copy-start(s32[2]{0:T(128)} %pad_add_fusion.3.at_ref) | copy-start | bytes 28
  98.6 6.8 %copy-start.6 = (bf16[512,1024]{1,0:T(8,128)(2,1)S(1)}, bf16[512,1024]{1,0:T(8,128)(2,1)}, u32[]{:S(2)}) copy-start(bf16[512,1024]{1,0:T(8,128)(2,1)} %x_hbm.1) | copy-start | bytes 3145732
  98.6 6.8 %copy-start.8 = (bf16[512,1024]{1,0:T(8,128)(2,1)S(1)}, bf16[512,1024]{1,0:T(8,128)(2,1)}, u32[]{:S(2)}) copy-start(bf16[512,1024]{1,0:T(8,128)(2,1)} %z_hbm.1) | copy-start | bytes 3145732
  98.6 6.8 %copy-start.12 = (bf16[512,1,128]{2,0,1:T(8,128)(2,1)S(1)}, bf16[512,1,128]{2,0,1:T(8,128)(2,1)}, u32[]{:S(2)}) copy-start(bf16[512,1,128]{2,0,1:T(8,128)(2,1)} %param.14) | copy-start | bytes 393220
  102.0 20.0 %collective-permute-start.13 = (bf16[256,1024]{1,0:T(8,128)(2,1)S(1)}, bf16[256,1024]{1,0:T(8,128)(2,1)S(1)}, u32[]{:S(2)}, u32[]{:S(2)}) collective-permute-start(bf16[256,1024]{1,0:T(8,128)(2,1)S(1)} %get-tuple-element.99), channel_id=1, source_target_pairs={{0,32},{32,64},{64,96},{96,128},{128,160},{160,192},{192,224},{224... | collective-permute-start | bytes 1572872 | tf_op jit(solution)/shard_map/ppermute | solution.py:381
  102.1 19.9 %collective-permute-start.14 = (bf16[256,1024]{1,0:T(8,128)(2,1)S(1)}, bf16[256,1024]{1,0:T(8,128)(2,1)S(1)}, u32[]{:S(2)}, u32[]{:S(2)}) collective-permute-start(bf16[256,1024]{1,0:T(8,128)(2,1)S(1)} %get-tuple-element.100), channel_id=1, source_target_pairs={{0,224},{32,0},{64,32},{96,64},{128,96},{160,128},{192,160},{224,1... | collective-permute-start | bytes 1572872 | tf_op jit(solution)/shard_map/ppermute | solution.py:381
  125.4 14.3 %collective-permute-start.15 = (bf16[256,1024]{1,0:T(8,128)(2,1)S(1)}, bf16[256,1024]{1,0:T(8,128)(2,1)S(1)}, u32[]{:S(2)}, u32[]{:S(2)}) collective-permute-start(bf16[256,1024]{1,0:T(8,128)(2,1)S(1)} %get-tuple-element.104), channel_id=1, source_target_pairs={{0,32},{32,64},{64,96},{96,128},{128,160},{160,192},{192,224},{224... | collective-permute-start | bytes 1572872 | tf_op jit(solution)/shard_map/ppermute | solution.py:381
  125.5 14.3 %collective-permute-start.16 = (bf16[256,1024]{1,0:T(8,128)(2,1)S(1)}, bf16[256,1024]{1,0:T(8,128)(2,1)}, u32[]{:S(2)}, u32[]{:S(2)}) collective-permute-start(bf16[256,1024]{1,0:T(8,128)(2,1)S(1)} %get-tuple-element.105), channel_id=1, source_target_pairs={{0,224},{32,0},{64,32},{96,64},{128,96},{160,128},{192,160},{224,1... | collective-permute-start | bytes 1572872 | tf_op jit(solution)/shard_map/ppermute | solution.py:381
  128.7 1.2 collective-permute-start.17
  129.9 3.7 %collective-permute-start.18 = (f32[16,128]{1,0:T(8,128)S(1)}, f32[16,128]{1,0:T(8,128)S(1)}, u32[]{:S(2)}, u32[]{:S(2)}) collective-permute-start(f32[16,128]{1,0:T(8,128)S(1)} %add.132), channel_id=1, source_target_pairs={{0,16},{16,0},{1,17},{17,1},{2,18},{18,2},{3,19},{19,3},{4,20},{20... | collective-permute-start | bytes 24584 | tf_op jit(solution)/shard_map/ppermute | solution.py:381
  133.5 5.3 %collective-permute-start.19 = (f32[16,128]{1,0:T(8,128)S(1)}, f32[16,128]{1,0:T(8,128)S(1)}, u32[]{:S(2)}, u32[]{:S(2)}) collective-permute-start(f32[16,128]{1,0:T(8,128)S(1)} %add.133), channel_id=1, source_target_pairs={{0,32},{32,0},{64,96},{96,64},{128,160},{160,128},{192,224},{224,1... | collective-permute-start | bytes 24584 | tf_op jit(solution)/shard_map/ppermute | solution.py:385
  141.8 8.2 %collective-permute-start.21 = (bf16[128,1024]{1,0:T(8,128)(2,1)S(1)}, bf16[128,1024]{1,0:T(8,128)(2,1)S(1)}, u32[]{:S(2)}, u32[]{:S(2)}) collective-permute-start(bf16[128,1024]{1,0:T(8,128)(2,1)S(1)} %get-tuple-element.129), channel_id=1, source_target_pairs={{0,224},{32,0},{64,32},{96,64},{128,96},{160,128},{192,160},{224,1... | collective-permute-start | bytes 786440 | tf_op jit(solution)/shard_map/ppermute | solution.py:381
  145.0 7.9 %collective-permute-start.20 = (bf16[128,1024]{1,0:T(8,128)(2,1)S(1)}, bf16[128,1024]{1,0:T(8,128)(2,1)S(1)}, u32[]{:S(2)}, u32[]{:S(2)}) collective-permute-start(bf16[128,1024]{1,0:T(8,128)(2,1)S(1)} %get-tuple-element.131), channel_id=1, source_target_pairs={{0,32},{32,64},{64,96},{96,128},{128,160},{160,192},{192,224},{224... | collective-permute-start | bytes 786440 | tf_op jit(solution)/shard_map/ppermute | solution.py:381
  145.3 4.6 %collective-permute-start.22 = (f32[16,128]{1,0:T(8,128)S(1)}, f32[16,128]{1,0:T(8,128)S(1)}, u32[]{:S(2)}, u32[]{:S(2)}) collective-permute-start(f32[16,128]{1,0:T(8,128)S(1)} %add.134), channel_id=1, source_target_pairs={{0,64},{32,96},{64,0},{96,32},{128,192},{160,224},{192,128},{224,1... | collective-permute-start | bytes 24584 | tf_op jit(solution)/shard_map/ppermute | solution.py:385
  153.0 11.0 %collective-permute-start.26 = (f32[128,1024]{1,0:T(8,128)S(1)}, f32[128,1024]{1,0:T(8,128)S(1)}, u32[]{:S(2)}, u32[]{:S(2)}) collective-permute-start(f32[128,1024]{1,0:T(8,128)S(1)} %bitcast_add_fusion.2), channel_id=1, source_target_pairs={{0,16},{16,0},{1,17},{17,1},{2,18},{18,2},{3,19},{19,3},{4,20},{20... | collective-permute-start | bytes 1572872 | tf_op jit(solution)/shard_map/ppermute | solution.py:381
  154.3 7.7 %collective-permute-start.23 = (f32[16,128]{1,0:T(8,128)S(1)}, f32[16,128]{1,0:T(8,128)S(1)}, u32[]{:S(2)}, u32[]{:S(2)}) collective-permute-start(f32[16,128]{1,0:T(8,128)S(1)} %add.138), channel_id=1, source_target_pairs={{0,128},{32,160},{64,192},{96,224},{128,0},{160,32},{192,64},{224,... | collective-permute-start | bytes 24584 | tf_op jit(solution)/shard_map/ppermute | solution.py:385
  156.1 7.1 %collective-permute-start.25 = (bf16[128,1024]{1,0:T(8,128)(2,1)S(1)}, bf16[128,1024]{1,0:T(8,128)(2,1)S(1)}, u32[]{:S(2)}, u32[]{:S(2)}) collective-permute-start(bf16[128,1024]{1,0:T(8,128)(2,1)S(1)} %get-tuple-element.128), channel_id=1, source_target_pairs={{0,224},{32,0},{64,32},{96,64},{128,96},{160,128},{192,160},{224,1... | collective-permute-start | bytes 786440 | tf_op jit(solution)/shard_map/ppermute | solution.py:381
  156.3 7.7 %collective-permute-start.24 = (bf16[128,1024]{1,0:T(8,128)(2,1)S(1)}, bf16[128,1024]{1,0:T(8,128)(2,1)S(1)}, u32[]{:S(2)}, u32[]{:S(2)}) collective-permute-start(bf16[128,1024]{1,0:T(8,128)(2,1)S(1)} %get-tuple-element.130), channel_id=1, source_target_pairs={{0,32},{32,64},{64,96},{96,128},{128,160},{160,192},{192,224},{224... | collective-permute-start | bytes 786440 | tf_op jit(solution)/shard_map/ppermute | solution.py:381
Sparse Core Ops, SparseCore 0:
  9.9 77.4 all-gather.1

commit v5 on v4

--- a/solution.py
+++ b/solution.py
@@ -576,20 +576,21 @@
     half = CH // 2
     far = blocks(4)[0].astype(BF16)
     up, down = both_ways(far[:, half:], far[:, :half], "z")
-    last = blocks(1, -1, 0)
-    w, = tie((w,), last)
+    mine = blocks(0)[0]
+    w, = tie((w,), mine)
     upstream = back_project(core, keep, give, w)
-    up, down, last, upstream = tie((up, down, last, upstream))
+    up, down, mine, upstream = tie((up, down, mine, upstream))
 
     up, down = both_ways(*ring_step(zi, 3, keep, theirs, normed, normed_other, up, down), "z")
     dx, dz, db, dc, ddt, small = scan_backward(upstream, ys, *scan)
     up, down, small = tie((up, down, small))
 
     up, down = both_ways(*ring_step(zi, 2, keep, theirs, normed, normed_other, up, down), "z")
+    last = blocks(1, -1)
     small = small + send(small, "c", 1)
     small = small + send(small, "xl", 1)
     small = small + swap(small, "z", 1)
-    up, down, small = tie((up, down, small))
+    up, down, last, small = tie((up, down, last, small))
 
     def halves(r):
         return lax.dynamic_slice_in_dim(r, (1 - xl) * 128, 128, 0), lax.dynamic_slice_in_dim(r, xl * 128, 128, 0)
@@ -599,7 +600,7 @@
     up_leave, down_leave = both_ways(up_leave, down_leave, "z")
     up_stay, down_stay = both_ways(up_stay, down_stay, "z")
     small = small + swap(small, "z", 2)
-    leave, stay = halves(last[2])
+    leave, stay = halves(mine)
     up_leave, down_leave, small = tie((up_leave, down_leave, small))
     leave = send(leave + (up_leave.astype(F32) + down_leave.astype(F32)), "xl", 1)
     small = small + swap(small, "z", 4)

time: 174 us -> 173 us (level)
  starting transfers between devices: 40.6 us -> 44.1 us
  waiting for transfers between devices: 42.1 us -> 39.1 us
    ppermute x3, waiting for transfers between devices: 12.4 us -> 7.28 us  [swap(): return lax.ppermute(v, axis, [(i, i ^ mask) for i in range(AXES[axis])])]
    ppermute x3, starting transfers between devices: 1.11 us -> 4.57 us  [swap(): return lax.ppermute(v, axis, [(i, i ^ mask) for i in range(AXES[axis])])]
    ppermute x24, waiting for transfers between devices: 29 us -> 31.1 us  [send(): return lax.ppermute(v, axis, [(i, (i + shift) % n) for i in range(n)])]
    unnamed x44 -> x50, local copies, waits for them, and re-layouts: 7.48 us -> 8.44 us
    pallas_call x2 -> x3, Pallas kernels: 6.89 us -> 6.5 us  [weight_blocks(): pl.pallas_call(kernel, grid_spec=pltpu.PrefetchScalarGridSpec(num_scalar_...]
  transfers between devices with their start and end apart: 28 -> 28, of which waited for: 13 -> 14; matrix products, arithmetic and copies ran while one was open for 6% -> 5% of each run, Pallas kernels for 29% -> 28%
where the time goes in v5:
time: 173 us; the launch traced here: 172 us
  Pallas kernels  56.6 us (33%)
  starting transfers between devices  44.1 us (25%)
  waiting for transfers between devices  39.1 us (23%)
  between operations  14.5 us (8%)
  local copies, waits for them, and re-layouts  13.8 us (8%)
  other arithmetic  3.82 us (2%)
    ppermute x24, starting transfers between devices, send(): return lax.ppermute(v, axis, [(i, (i + shift) % n) for i in range(n)])  39.5 us
    ppermute x24, waiting for transfers between devices, send(): return lax.ppermute(v, axis, [(i, (i + shift) % n) for i in range(n)])  31.1 us
    pallas_call x1, Pallas kernels, scan_backward(): pl.pallas_call(bwd_kernel, out_shape=(jax.ShapeDtypeStruct((TOK, CH), BF1...  16.6 us
    pallas_call x1, Pallas kernels, scan_forward(): pl.pallas_call(fwd_kernel, out_shape=(jax.ShapeDtypeStruct((TOK, CH), F32...  8.59 us
    unnamed x50, local copies, waits for them, and re-layouts  8.44 us
    pallas_call x1, Pallas kernels, back_project(): pl.pallas_call(kernel, grid_spec=pltpu.PrefetchScalarGridSpec(num_scalar_...  7.92 us
    pallas_call x2, Pallas kernels, ring_step(): pl.pallas_call(kernel, grid_spec=pltpu.PrefetchScalarGridSpec(num_scalar_...  7.64 us
    pallas_call x2, Pallas kernels, shuffle(): pl.pallas_call(kernel, out_shape=tuple((jax.ShapeDtypeStruct(s, BF16) for...  7.32 us
  transfers between devices with their start and end apart: 28, of which 14 were waited for; matrix products, arithmetic and copies ran while one was open for 5% of the time, Pallas kernels for 28%

profile of v5, /device:TPU:2, one launch (start us, length us, event | category | flops | bytes accessed | tf_op | source)
XLA Modules:
  0.0 171.9 jit_solution(6556960674917434424)
XLA Ops:
  7.3 0.7 all-gather.2.cloned.1.call-update
  8.0 2.0 %own_first.1.refs_0_ = bf16[64,4096]{1,0:T(8,128)(2,1)} custom-call(s32[1]{0:T(128)} %bitcast.3.core_ref, bf16[64,4096]{1,0:T(8,128)(2,1)} %in_ref.1), custom_call_target="tpu_custom_call" | custom-call | flops 1000 | bytes 1000 | tf_op jit(solution)/shard_map/own_first/pallas_call | solution.py:430
  10.0 1.6 collective-permute-start
  11.5 1.7 collective-permute-start.1
  13.2 2.1 %collective-permute-start.2 = (bf16[64,4096]{1,0:T(8,128)(2,1)}, bf16[64,4096]{1,0:T(8,128)(2,1)}, u32[]{:S(2)}, u32[]{:S(2)}) collective-permute-start(bf16[64,4096]{1,0:T(8,128)(2,1)} %own_first.1.refs_0_), channel_id=1, source_target_pairs={{0,1},{1,0},{2,3},{3,2},{4,5},{5,4},{6,7},{7,6},{8,9},{9,8},{10,11... | collective-permute-start | bytes 1572872 | tf_op jit(solution)/shard_map/ppermute | solution.py:381
  15.3 9.8 %collective-permute-done.refs_2_ = bf16[64,4096]{1,0:T(8,128)(2,1)S(1)} collective-permute-done((bf16[64,4096]{1,0:T(8,128)(2,1)}, bf16[64,4096]{1,0:T(8,128)(2,1)S(1)}, u32[]{:S(2)}, u32[]{:S(2)}) %collective-permute-start) | collective-permute-done | bytes 524320 | tf_op jit(solution)/shard_map/ppermute | solution.py:381
  25.1 4.8 %collective-permute-done.2.refs_1_ = bf16[64,4096]{1,0:T(8,128)(2,1)} collective-permute-done((bf16[64,4096]{1,0:T(8,128)(2,1)}, bf16[64,4096]{1,0:T(8,128)(2,1)}, u32[]{:S(2)}, u32[]{:S(2)}) %collective-permute-start.2) | collective-permute-done | bytes 524320 | tf_op jit(solution)/shard_map/ppermute | solution.py:381
  29.9 3.2 %collective-permute-start.4 = (bf16[64,4096]{1,0:T(8,128)(2,1)}, bf16[64,4096]{1,0:T(8,128)(2,1)}, u32[]{:S(2)}, u32[]{:S(2)}) collective-permute-start(bf16[64,4096]{1,0:T(8,128)(2,1)} %collective-permute-done.2.refs_1_), channel_id=1, source_target_pairs={{0,6},{2,0},{4,2},{6,4},{1,7},{3,1},{5,3},{7,5},{8,14},{10,8},{12,... | collective-permute-start | bytes 1572872 | tf_op jit(solution)/shard_map/ppermute | solution.py:381
  33.1 0.7 slice.33
  33.9 0.7 slice.34
  34.6 3.2 %collective-permute-start.6 = (bf16[32,4096]{1,0:T(8,128)(2,1)}, bf16[32,4096]{1,0:T(8,128)(2,1)}, u32[]{:S(2)}, u32[]{:S(2)}) collective-permute-start(bf16[32,4096]{1,0:T(8,128)(2,1)} %slice.34), channel_id=1, source_target_pairs={{0,6},{2,0},{4,2},{6,4},{1,7},{3,1},{5,3},{7,5},{8,14},{10,8},{12,... | collective-permute-start | bytes 786440 | tf_op jit(solution)/shard_map/ppermute | solution.py:381
  37.8 0.9 copy.19.dt_ref
  38.8 0.9 copy-done.14
  39.7 8.6 %scan_forward.1 = (f32[512,1024]{1,0:T(8,128)S(1)}, bf16[512,1024]{1,0:T(8,128)(2,1)S(1)}) custom-call(bf16[512,1024]{1,0:T(8,128)(2,1)S(1)} %copy-done.6, bf16[512,1024]{1,0:T(8,128)(2,1)S(1)} %copy-done.8, bf16[512,128]{1,0:T(8,128)(2,1)S(1)} %bitcast.37, bf16[512,128]{1,0:T(8,128)(2,1)S(1)} %bitcast.39, f32[512,16]{1,0:T(8,128)S(1)} %copy.19.dt_ref, ...), custom_call_target="tpu_custom_call" | custom-call | flops 1000 | bytes 1000 | tf_op jit(solution)/shard_map/scan_forward/pallas_call | solution.py:320
  48.3 1.3 copy-done.12
  49.7 1.0 slice.35
  50.8 1.0 slice.36
  51.8 3.3 %collective-permute-start.8 = (bf16[32,4096]{1,0:T(8,128)(2,1)S(1)}, bf16[32,4096]{1,0:T(8,128)(2,1)S(1)}, u32[]{:S(2)}, u32[]{:S(2)}) collective-permute-start(bf16[32,4096]{1,0:T(8,128)(2,1)S(1)} %slice.36), channel_id=1, source_target_pairs={{0,6},{2,0},{4,2},{6,4},{1,7},{3,1},{5,3},{7,5},{8,14},{10,8},{12,... | collective-permute-start | bytes 786440 | tf_op jit(solution)/shard_map/ppermute | solution.py:381
  55.1 0.6 pad_add_fusion
  55.7 5.0 %collective-permute-done.7.refs_8_ = bf16[32,4096]{1,0:T(8,128)(2,1)S(1)} collective-permute-done((bf16[32,4096]{1,0:T(8,128)(2,1)S(1)}, bf16[32,4096]{1,0:T(8,128)(2,1)S(1)}, u32[]{:S(2)}, u32[]{:S(2)}) %collective-permute-start.7) | collective-permute-done | bytes 262176 | tf_op jit(solution)/shard_map/ppermute | solution.py:381
  60.7 0.3 collective-permute-done.8.refs_9_
  61.0 0.4 copy-done.22
  61.4 0.3 copy-done.23
  61.7 3.6 %place_tokens.2.b_ref = bf16[512,2048]{1,0:T(8,128)(2,1)} custom-call(s32[2]{0:T(128)} %get-tuple-element.140.s_ref, bf16[64,4096]{1,0:T(8,128)(2,1)} %own_first.1.refs_0_, bf16[64,4096]{1,0:T(8,128)(2,1)} %collective-permute-done.2.refs_1_, bf16[64,4096]{1,0:T(8,128)(2,1)} %copy-done.20, bf16[64,4096]{1,0:T(8,128)(2,1)} %collective-permute-done.3.refs_3_, ...), custom_call_target="tpu_custom_call" | custom-call | flops 1000 | bytes 1000 | tf_op jit(solution)/shard_map/place_tokens/pallas_call | solution.py:410
  65.4 3.7 %place_tokens.3.a_ref = bf16[512,2048]{1,0:T(8,128)(2,1)} custom-call(s32[2]{0:T(128)} %get-tuple-element.140.s_ref, bf16[64,4096]{1,0:T(8,128)(2,1)} %own_first.1.refs_0_, bf16[64,4096]{1,0:T(8,128)(2,1)} %collective-permute-done.2.refs_1_, bf16[64,4096]{1,0:T(8,128)(2,1)} %copy-done.20, bf16[64,4096]{1,0:T(8,128)(2,1)} %collective-permute-done.3.refs_3_, ...), custom_call_target="tpu_custom_call" | custom-call | flops 1000 | bytes 1000 | tf_op jit(solution)/shard_map/place_tokens/pallas_call | solution.py:410
  69.2 0.7 collective-permute-done.10.b_ref
  69.9 1.6 copy-done
  71.6 1.7 weight_blocks.3
  73.3 0.8 fusion.2
  74.2 0.2 collective-permute-start.11
  74.4 9.0 %collective-permute-start.12 = (bf16[256,512]{1,0:T(8,128)(2,1)}, bf16[256,512]{1,0:T(8,128)(2,1)}, u32[]{:S(2)}, u32[]{:S(2)}) collective-permute-start(bf16[256,512]{1,0:T(8,128)(2,1)} %get-tuple-element.136), channel_id=1, source_target_pairs={{0,224},{32,0},{64,32},{96,64},{128,96},{160,128},{192,160},{224,1... | collective-permute-start | bytes 786440 | tf_op jit(solution)/shard_map/ppermute | solution.py:381
  83.4 0.6 pad_add_fusion.2.at_ref
  84.0 1.2 copy-done.3
  85.2 1.7 weight_blocks.4
  86.9 1.0 copy-done.10
  87.9 7.9 %back_project.1.u_hbm = f32[512,1024]{1,0:T(8,128)S(1)} custom-call(s32[1]{0:T(128)} %bitcast.3.core_ref, bf16[512,2048]{1,0:T(8,128)(2,1)S(1)} %copy-done.1, bf16[512,2048]{1,0:T(8,128)(2,1)} %place_tokens.2.b_ref, bf16[16,2,128,1024]{3,2,1,0:T(8,128)(2,1)} %bitcast.47, bf16[16,2,128,1024]{3,2,1,0:T(8,128)(2,1)} %bitcast.48), custom_call_target="tpu_custom_call" | custom-call | flops 1000 | bytes 1000 | tf_op jit(solution)/shard_map/back_project/pallas_call | solution.py:528
  95.9 3.4 %ring_step.2 = (bf16[256,1024]{1,0:T(8,128)(2,1)S(1)}, bf16[256,1024]{1,0:T(8,128)(2,1)S(1)}) custom-call(s32[2]{0:T(128)S(1)} %copy-done.19, bf16[512,2048]{1,0:T(8,128)(2,1)S(1)} %copy-done.1, bf16[512,2048]{1,0:T(8,128)(2,1)} %collective-permute-done.10.b_ref, bf16[512,1024]{1,0:T(8,128)(2,1)S(1)} %get-tuple-element.73.n_ref, ...), custom_call_target="tpu_custom_call" | custom-call | flops 1000 | bytes 1000 | tf_op jit(solution)/shard_map/ring_step/pallas_call | solution.py:508
  99.3 0.9 collective-permute-start.13
  100.2 2.4 %collective-permute-start.14 = (bf16[256,1024]{1,0:T(8,128)(2,1)S(1)}, bf16[256,1024]{1,0:T(8,128)(2,1)S(1)}, u32[]{:S(2)}, u32[]{:S(2)}) collective-permute-start(bf16[256,1024]{1,0:T(8,128)(2,1)S(1)} %get-tuple-element.100), channel_id=1, source_target_pairs={{0,224},{32,0},{64,32},{96,64},{128,96},{160,128},{192,160},{224,1... | collective-permute-start | bytes 1572872 | tf_op jit(solution)/shard_map/ppermute | solution.py:381
  102.6 16.6 %scan_backward.1 = (bf16[512,1024]{1,0:T(8,128)(2,1)}, bf16[512,1024]{1,0:T(8,128)(2,1)}, bf16[512,128]{1,0:T(8,128)(2,1)}, bf16[512,128]{1,0:T(8,128)(2,1)}, f3...) custom-call(f32[512,1024]{1,0:T(8,128)S(1)} %back_project.1.u_hbm, f32[512,1024]{1,0:T(8,128)} %copy-done.12, ...), custom_call_target="tpu_custom_call" | custom-call | flops 1000 | bytes 1000 | tf_op jit(solution)/shard_map/scan_backward/pallas_call | solution.py:338
  119.3 4.3 %ring_step.3 = (bf16[256,1024]{1,0:T(8,128)(2,1)}, bf16[256,1024]{1,0:T(8,128)(2,1)}) custom-call(s32[2]{0:T(128)S(1)} %get-tuple-element.141.at_ref, bf16[512,2048]{1,0:T(8,128)(2,1)} %place_tokens.3.a_ref, bf16[512,2048]{1,0:T(8,128)(2,1)} %collective-permute-done.10.b_ref, bf16[512,1024]{1,0:T(8,128)(2,1)S(1)} %get-tuple-element.73.n_ref, ...), custom_call_target="tpu_custom_call" | custom-call | flops 1000 | bytes 1000 | tf_op jit(solution)/shard_map/ring_step/pallas_call | solution.py:508
  123.6 3.2 %collective-permute-start.16 = (bf16[256,1024]{1,0:T(8,128)(2,1)}, bf16[256,1024]{1,0:T(8,128)(2,1)}, u32[]{:S(2)}, u32[]{:S(2)}) collective-permute-start(bf16[256,1024]{1,0:T(8,128)(2,1)} %get-tuple-element.105), channel_id=1, source_target_pairs={{0,224},{32,0},{64,32},{96,64},{128,96},{160,128},{192,160},{224,1... | collective-permute-start | bytes 1572872 | tf_op jit(solution)/shard_map/ppermute | solution.py:381
  126.8 1.2 collective-permute-done.17
  128.0 1.4 collective-permute-start.18
  129.4 2.3 %collective-permute-done.18 = f32[16,128]{1,0:T(8,128)S(1)} collective-permute-done((f32[16,128]{1,0:T(8,128)S(1)}, f32[16,128]{1,0:T(8,128)S(1)}, u32[]{:S(2)}, u32[]{:S(2)}) %collective-permute-start.18) | collective-permute-done | bytes 8224 | tf_op jit(solution)/shard_map/ppermute | solution.py:381
  131.7 3.1 %weight_blocks.5 = f32[2,256,1024]{2,1,0:T(8,128)S(1)} custom-call(s32[2]{0:T(128)S(1)} %pad_add_fusion.3.at_ref, bf16[512,2048]{1,0:T(8,128)(2,1)} %place_tokens.3.a_ref, bf16[512,2048]{1,0:T(8,128)(2,1)} %collective-permute-done.10.b_ref, bf16[512,1024]{1,0:T(8,128)(2,1)S(1)} %get-tuple-element.73.n_ref, bf16[512,1024]{1,0:T(8,128)(2,1)S(1)} %copy-done.5), custom_call_target="tpu_custom_call" | custom-call | flops 1000 | bytes 1000 | tf_op jit(solution)/shard_map/weight_blocks/pallas_call | solution.py:467
  134.8 2.2 %collective-permute-done.19 = f32[16,128]{1,0:T(8,128)S(1)} collective-permute-done((f32[16,128]{1,0:T(8,128)S(1)}, f32[16,128]{1,0:T(8,128)S(1)}, u32[]{:S(2)}, u32[]{:S(2)}) %collective-permute-start.19) | collective-permute-done | bytes 8224 | tf_op jit(solution)/shard_map/ppermute | solution.py:385
  137.1 1.0 collective-permute-done.15
  138.1 1.4 fusion
  139.6 3.4 %collective-permute-start.21 = (bf16[128,1024]{1,0:T(8,128)(2,1)S(1)}, bf16[128,1024]{1,0:T(8,128)(2,1)S(1)}, u32[]{:S(2)}, u32[]{:S(2)}) collective-permute-start(bf16[128,1024]{1,0:T(8,128)(2,1)S(1)} %get-tuple-element.133), channel_id=1, source_target_pairs={{0,224},{32,0},{64,32},{96,64},{128,96},{160,128},{192,160},{224,1... | collective-permute-start | bytes 786440 | tf_op jit(solution)/shard_map/ppermute | solution.py:381
  143.1 1.2 collective-permute-start.22
  144.3 3.4 %collective-permute-done.22 = f32[16,128]{1,0:T(8,128)S(1)} collective-permute-done((f32[16,128]{1,0:T(8,128)S(1)}, f32[16,128]{1,0:T(8,128)S(1)}, u32[]{:S(2)}, u32[]{:S(2)}) %collective-permute-start.22) | collective-permute-done | bytes 8224 | tf_op jit(solution)/shard_map/ppermute | solution.py:385
  147.8 2.9 %collective-permute-done.20 = bf16[128,1024]{1,0:T(8,128)(2,1)S(1)} collective-permute-done((bf16[128,1024]{1,0:T(8,128)(2,1)S(1)}, bf16[128,1024]{1,0:T(8,128)(2,1)S(1)}, u32[]{:S(2)}, u32[]{:S(2)}) %collective-permute-start.20) | collective-permute-done | bytes 262176 | tf_op jit(solution)/shard_map/ppermute | solution.py:381
  150.8 1.4 collective-permute-start.26
  152.3 3.4 %collective-permute-start.23 = (f32[16,128]{1,0:T(8,128)S(1)}, f32[16,128]{1,0:T(8,128)S(1)}, u32[]{:S(2)}, u32[]{:S(2)}) collective-permute-start(f32[16,128]{1,0:T(8,128)S(1)} %add.138), channel_id=1, source_target_pairs={{0,128},{32,160},{64,192},{96,224},{128,0},{160,32},{192,64},{224,... | collective-permute-start | bytes 24584 | tf_op jit(solution)/shard_map/ppermute | solution.py:385
  155.6 0.7 copy.21
  156.4 0.2 collective-permute-start.25
  156.5 1.8 %collective-permute-start.24 = (bf16[128,1024]{1,0:T(8,128)(2,1)S(1)}, bf16[128,1024]{1,0:T(8,128)(2,1)S(1)}, u32[]{:S(2)}, u32[]{:S(2)}) collective-permute-start(bf16[128,1024]{1,0:T(8,128)(2,1)S(1)} %get-tuple-element.134), channel_id=1, source_target_pairs={{0,32},{32,64},{64,96},{96,128},{128,160},{160,192},{192,224},{224... | collective-permute-start | bytes 786440 | tf_op jit(solution)/shard_map/ppermute | solution.py:381
  158.4 1.6 collective-permute-done.23
  160.0 0.5 slice_bitcast_fusion.1
  160.5 0.6 slice_bitcast_fusion
  161.1 1.6 collective-permute-done.25
  162.7 1.4 collective-permute-done.24
  164.1 0.9 add_add_fusion
  (75 shorter events, 0.9 us)
Async XLA Ops:
  7.2 31.5 %copy-start.18 = (f32[16]{0:T(128)S(1)}, f32[16]{0:T(128)}, u32[]{:S(2)}) copy-start(f32[16]{0:T(128)} %param.17) | copy-start | bytes 196
  7.2 31.5 %copy-start.13 = (bf16[512,1,128]{2,0,1:T(8,128)(2,1)S(1)}, bf16[512,1,128]{2,0,1:T(8,128)(2,1)}, u32[]{:S(2)}) copy-start(bf16[512,1,128]{2,0,1:T(8,128)(2,1)} %param.13) | copy-start | bytes 393220
  7.2 31.5 %copy-start.17 = (f32[16]{0:T(128)S(1)}, f32[16]{0:T(128)}, u32[]{:S(2)}) copy-start(f32[16]{0:T(128)} %param.16) | copy-start | bytes 196
  7.2 31.5 %copy-start.16 = (f32[1024]{0:T(1024)S(1)}, f32[1024]{0:T(1024)}, u32[]{:S(2)}) copy-start(f32[1024]{0:T(1024)} %param.18) | copy-start | bytes 12292
  7.2 31.5 %copy-start.6 = (bf16[512,1024]{1,0:T(8,128)(2,1)S(1)}, bf16[512,1024]{1,0:T(8,128)(2,1)}, u32[]{:S(2)}) copy-start(bf16[512,1024]{1,0:T(8,128)(2,1)} %x_hbm.1) | copy-start | bytes 3145732
  7.2 31.5 %copy-start.8 = (bf16[512,1024]{1,0:T(8,128)(2,1)S(1)}, bf16[512,1024]{1,0:T(8,128)(2,1)}, u32[]{:S(2)}) copy-start(bf16[512,1024]{1,0:T(8,128)(2,1)} %z_hbm.1) | copy-start | bytes 3145732
  7.2 80.7 %all-gather.2.cloned.1.call-start = ((), (), s32[]{:S(2)}) async-start(), calls=%async_computation | async-start | bytes 8650752 | tf_op jit(solution)/shard_map/all_gather | solution.py:552
  10.0 15.1 %collective-permute-start = (bf16[64,4096]{1,0:T(8,128)(2,1)}, bf16[64,4096]{1,0:T(8,128)(2,1)S(1)}, u32[]{:S(2)}, u32[]{:S(2)}) collective-permute-start(bf16[64,4096]{1,0:T(8,128)(2,1)} %own_first.1.refs_0_), channel_id=1, source_target_pairs={{0,2},{2,4},{4,6},{6,0},{1,3},{3,5},{5,7},{7,1},{8,10},{10,12},{12... | collective-permute-start | bytes 1572872 | tf_op jit(solution)/shard_map/ppermute | solution.py:381
  11.5 13.6 %collective-permute-start.1 = (bf16[64,4096]{1,0:T(8,128)(2,1)}, bf16[64,4096]{1,0:T(8,128)(2,1)S(1)}, u32[]{:S(2)}, u32[]{:S(2)}) collective-permute-start(bf16[64,4096]{1,0:T(8,128)(2,1)} %own_first.1.refs_0_), channel_id=1, source_target_pairs={{0,6},{2,0},{4,2},{6,4},{1,7},{3,1},{5,3},{7,5},{8,14},{10,8},{12,... | collective-permute-start | bytes 1572872 | tf_op jit(solution)/shard_map/ppermute | solution.py:381
  13.2 16.7 %collective-permute-start.2 = (bf16[64,4096]{1,0:T(8,128)(2,1)}, bf16[64,4096]{1,0:T(8,128)(2,1)}, u32[]{:S(2)}, u32[]{:S(2)}) collective-permute-start(bf16[64,4096]{1,0:T(8,128)(2,1)} %own_first.1.refs_0_), channel_id=1, source_target_pairs={{0,1},{1,0},{2,3},{3,2},{4,5},{5,4},{6,7},{7,6},{8,9},{9,8},{10,11... | collective-permute-start | bytes 1572872 | tf_op jit(solution)/shard_map/ppermute | solution.py:381
  25.1 13.6 %copy-start.20 = (bf16[64,4096]{1,0:T(8,128)(2,1)}, bf16[64,4096]{1,0:T(8,128)(2,1)S(1)}, u32[]{:S(2)}) copy-start(bf16[64,4096]{1,0:T(8,128)(2,1)S(1)} %collective-permute-done.refs_2_) | copy-start | bytes 1572868
  25.1 13.6 %copy-start.21 = (bf16[64,4096]{1,0:T(8,128)(2,1)}, bf16[64,4096]{1,0:T(8,128)(2,1)S(1)}, u32[]{:S(2)}) copy-start(bf16[64,4096]{1,0:T(8,128)(2,1)S(1)} %collective-permute-done.1.refs_4_) | copy-start | bytes 1572868
  29.9 19.7 %collective-permute-start.3 = (bf16[64,4096]{1,0:T(8,128)(2,1)}, bf16[64,4096]{1,0:T(8,128)(2,1)}, u32[]{:S(2)}, u32[]{:S(2)}) collective-permute-start(bf16[64,4096]{1,0:T(8,128)(2,1)} %collective-permute-done.2.refs_1_), channel_id=1, source_target_pairs={{0,2},{2,4},{4,6},{6,0},{1,3},{3,5},{5,7},{7,1},{8,10},{10,12},{12... | collective-permute-start | bytes 1572872 | tf_op jit(solution)/shard_map/ppermute | solution.py:381
  29.9 19.7 %collective-permute-start.4 = (bf16[64,4096]{1,0:T(8,128)(2,1)}, bf16[64,4096]{1,0:T(8,128)(2,1)}, u32[]{:S(2)}, u32[]{:S(2)}) collective-permute-start(bf16[64,4096]{1,0:T(8,128)(2,1)} %collective-permute-done.2.refs_1_), channel_id=1, source_target_pairs={{0,6},{2,0},{4,2},{6,4},{1,7},{3,1},{5,3},{7,5},{8,14},{10,8},{12,... | collective-permute-start | bytes 1572872 | tf_op jit(solution)/shard_map/ppermute | solution.py:381
  33.8 15.8 %collective-permute-start.5 = (bf16[32,4096]{1,0:T(8,128)(2,1)}, bf16[32,4096]{1,0:T(8,128)(2,1)}, u32[]{:S(2)}, u32[]{:S(2)}) collective-permute-start(bf16[32,4096]{1,0:T(8,128)(2,1)} %slice.33), channel_id=1, source_target_pairs={{0,2},{2,4},{4,6},{6,0},{1,3},{3,5},{5,7},{7,1},{8,10},{10,12},{12... | collective-permute-start | bytes 786440 | tf_op jit(solution)/shard_map/ppermute | solution.py:381
  34.6 15.0 %collective-permute-start.6 = (bf16[32,4096]{1,0:T(8,128)(2,1)}, bf16[32,4096]{1,0:T(8,128)(2,1)}, u32[]{:S(2)}, u32[]{:S(2)}) collective-permute-start(bf16[32,4096]{1,0:T(8,128)(2,1)} %slice.34), channel_id=1, source_target_pairs={{0,6},{2,0},{4,2},{6,4},{1,7},{3,1},{5,3},{7,5},{8,14},{10,8},{12,... | collective-permute-start | bytes 786440 | tf_op jit(solution)/shard_map/ppermute | solution.py:381
  38.8 0.9 copy-start.14
  48.3 1.3 copy-start.12
  49.6 11.4 %collective-permute-start.9 = (bf16[512,1024]{1,0:T(8,128)(2,1)S(1)}, bf16[512,1024]{1,0:T(8,128)(2,1)S(1)}, u32[]{:S(2)}, u32[]{:S(2)}) collective-permute-start(bf16[512,1024]{1,0:T(8,128)(2,1)S(1)} %get-tuple-element.73.n_ref), channel_id=1, source_target_pairs={{0,8},{8,0},{1,9},{9,1},{2,10},{10,2},{3,11},{11,3},{4,12},{12,4},... | collective-permute-start | bytes 3145736 | tf_op jit(solution)/shard_map/ppermute | solution.py:381
  50.7 10.0 %collective-permute-start.7 = (bf16[32,4096]{1,0:T(8,128)(2,1)S(1)}, bf16[32,4096]{1,0:T(8,128)(2,1)S(1)}, u32[]{:S(2)}, u32[]{:S(2)}) collective-permute-start(bf16[32,4096]{1,0:T(8,128)(2,1)S(1)} %slice.35), channel_id=1, source_target_pairs={{0,2},{2,4},{4,6},{6,0},{1,3},{3,5},{5,7},{7,1},{8,10},{10,12},{12... | collective-permute-start | bytes 786440 | tf_op jit(solution)/shard_map/ppermute | solution.py:381
  51.8 9.2 %collective-permute-start.8 = (bf16[32,4096]{1,0:T(8,128)(2,1)S(1)}, bf16[32,4096]{1,0:T(8,128)(2,1)S(1)}, u32[]{:S(2)}, u32[]{:S(2)}) collective-permute-start(bf16[32,4096]{1,0:T(8,128)(2,1)S(1)} %slice.36), channel_id=1, source_target_pairs={{0,6},{2,0},{4,2},{6,4},{1,7},{3,1},{5,3},{7,5},{8,14},{10,8},{12,... | collective-permute-start | bytes 786440 | tf_op jit(solution)/shard_map/ppermute | solution.py:381
  60.7 0.7 copy-start.22
  61.0 0.7 copy-start.23
  61.0 8.9 %copy-start.2 = (bf16[512,1024]{1,0:T(8,128)(2,1)}, bf16[512,1024]{1,0:T(8,128)(2,1)S(1)}, u32[]{:S(2)}) copy-start(bf16[512,1024]{1,0:T(8,128)(2,1)S(1)} %collective-permute-done.9.m_ref) | copy-start | bytes 3145732
  65.3 4.6 %collective-permute-start.10 = (bf16[512,2048]{1,0:T(8,128)(2,1)}, bf16[512,2048]{1,0:T(8,128)(2,1)}, u32[]{:S(2)}, u32[]{:S(2)}) collective-permute-start(bf16[512,2048]{1,0:T(8,128)(2,1)} %place_tokens.2.b_ref), channel_id=1, source_target_pairs={{0,8},{8,0},{1,9},{9,1},{2,10},{10,2},{3,11},{11,3},{4,12},{12,4},... | collective-permute-start | bytes 6291464 | tf_op jit(solution)/shard_map/ppermute | solution.py:381
  69.9 1.6 copy-start
  73.3 10.7 %copy-start.1 = (bf16[512,2048]{1,0:T(8,128)(2,1)S(1)}, bf16[512,2048]{1,0:T(8,128)(2,1)}, u32[]{:S(2)}) copy-start(bf16[512,2048]{1,0:T(8,128)(2,1)} %place_tokens.3.a_ref) | copy-start | bytes 6291460
  74.2 21.7 %collective-permute-start.11 = (bf16[256,512]{1,0:T(8,128)(2,1)}, bf16[256,512]{1,0:T(8,128)(2,1)}, u32[]{:S(2)}, u32[]{:S(2)}) collective-permute-start(bf16[256,512]{1,0:T(8,128)(2,1)} %get-tuple-element.137), channel_id=1, source_target_pairs={{0,32},{32,64},{64,96},{96,128},{128,160},{160,192},{192,224},{224... | collective-permute-start | bytes 786440 | tf_op jit(solution)/shard_map/ppermute | solution.py:381
  74.4 21.5 %collective-permute-start.12 = (bf16[256,512]{1,0:T(8,128)(2,1)}, bf16[256,512]{1,0:T(8,128)(2,1)}, u32[]{:S(2)}, u32[]{:S(2)}) collective-permute-start(bf16[256,512]{1,0:T(8,128)(2,1)} %get-tuple-element.136), channel_id=1, source_target_pairs={{0,224},{32,0},{64,32},{96,64},{128,96},{160,128},{192,160},{224,1... | collective-permute-start | bytes 786440 | tf_op jit(solution)/shard_map/ppermute | solution.py:381
  84.0 1.2 copy-start.3
  86.9 1.0 copy-start.10
  87.9 8.0 %copy-start.4 = (bf16[512,1024]{1,0:T(8,128)(2,1)S(1)}, bf16[512,1024]{1,0:T(8,128)(2,1)}, u32[]{:S(2)}) copy-start(bf16[512,1024]{1,0:T(8,128)(2,1)} %copy-done.2) | copy-start | bytes 3145732
  87.9 8.0 %copy-start.19 = (s32[2]{0:T(128)S(1)}, s32[2]{0:T(128)}, u32[]{:S(2)}) copy-start(s32[2]{0:T(128)} %pad_add_fusion.2.at_ref) | copy-start | bytes 28
  95.9 6.8 %copy-start.7 = (bf16[512,1024]{1,0:T(8,128)(2,1)S(1)}, bf16[512,1024]{1,0:T(8,128)(2,1)}, u32[]{:S(2)}) copy-start(bf16[512,1024]{1,0:T(8,128)(2,1)} %x_hbm.1) | copy-start | bytes 3145732
  95.9 6.8 %copy-start.9 = (bf16[512,1024]{1,0:T(8,128)(2,1)S(1)}, bf16[512,1024]{1,0:T(8,128)(2,1)}, u32[]{:S(2)}) copy-start(bf16[512,1024]{1,0:T(8,128)(2,1)} %z_hbm.1) | copy-start | bytes 3145732
  95.9 6.8 %copy-start.15 = (bf16[512,1,128]{2,0,1:T(8,128)(2,1)S(1)}, bf16[512,1,128]{2,0,1:T(8,128)(2,1)}, u32[]{:S(2)}) copy-start(bf16[512,1,128]{2,0,1:T(8,128)(2,1)} %param.14) | copy-start | bytes 393220
  99.3 20.0 %collective-permute-start.13 = (bf16[256,1024]{1,0:T(8,128)(2,1)S(1)}, bf16[256,1024]{1,0:T(8,128)(2,1)S(1)}, u32[]{:S(2)}, u32[]{:S(2)}) collective-permute-start(bf16[256,1024]{1,0:T(8,128)(2,1)S(1)} %get-tuple-element.99), channel_id=1, source_target_pairs={{0,32},{32,64},{64,96},{96,128},{128,160},{160,192},{192,224},{224... | collective-permute-start | bytes 1572872 | tf_op jit(solution)/shard_map/ppermute | solution.py:381
  100.2 19.1 %collective-permute-start.14 = (bf16[256,1024]{1,0:T(8,128)(2,1)S(1)}, bf16[256,1024]{1,0:T(8,128)(2,1)S(1)}, u32[]{:S(2)}, u32[]{:S(2)}) collective-permute-start(bf16[256,1024]{1,0:T(8,128)(2,1)S(1)} %get-tuple-element.100), channel_id=1, source_target_pairs={{0,224},{32,0},{64,32},{96,64},{128,96},{160,128},{192,160},{224,1... | collective-permute-start | bytes 1572872 | tf_op jit(solution)/shard_map/ppermute | solution.py:381
  119.3 12.4 %copy-start.5 = (bf16[512,1024]{1,0:T(8,128)(2,1)S(1)}, bf16[512,1024]{1,0:T(8,128)(2,1)}, u32[]{:S(2)}) copy-start(bf16[512,1024]{1,0:T(8,128)(2,1)} %copy-done.2) | copy-start | bytes 3145732
  123.6 14.5 %collective-permute-start.15 = (bf16[256,1024]{1,0:T(8,128)(2,1)}, bf16[256,1024]{1,0:T(8,128)(2,1)S(1)}, u32[]{:S(2)}, u32[]{:S(2)}) collective-permute-start(bf16[256,1024]{1,0:T(8,128)(2,1)} %get-tuple-element.104), channel_id=1, source_target_pairs={{0,32},{32,64},{64,96},{96,128},{128,160},{160,192},{192,224},{224... | collective-permute-start | bytes 1572872 | tf_op jit(solution)/shard_map/ppermute | solution.py:381
  123.6 14.5 %collective-permute-start.16 = (bf16[256,1024]{1,0:T(8,128)(2,1)}, bf16[256,1024]{1,0:T(8,128)(2,1)}, u32[]{:S(2)}, u32[]{:S(2)}) collective-permute-start(bf16[256,1024]{1,0:T(8,128)(2,1)} %get-tuple-element.105), channel_id=1, source_target_pairs={{0,224},{32,0},{64,32},{96,64},{128,96},{160,128},{192,160},{224,1... | collective-permute-start | bytes 1572872 | tf_op jit(solution)/shard_map/ppermute | solution.py:381
  126.8 1.2 collective-permute-start.17
  128.0 3.7 %collective-permute-start.18 = (f32[16,128]{1,0:T(8,128)S(1)}, f32[16,128]{1,0:T(8,128)S(1)}, u32[]{:S(2)}, u32[]{:S(2)}) collective-permute-start(f32[16,128]{1,0:T(8,128)S(1)} %add.132), channel_id=1, source_target_pairs={{0,16},{16,0},{1,17},{17,1},{2,18},{18,2},{3,19},{19,3},{4,20},{20... | collective-permute-start | bytes 24584 | tf_op jit(solution)/shard_map/ppermute | solution.py:381
  131.7 5.4 %collective-permute-start.19 = (f32[16,128]{1,0:T(8,128)S(1)}, f32[16,128]{1,0:T(8,128)S(1)}, u32[]{:S(2)}, u32[]{:S(2)}) collective-permute-start(f32[16,128]{1,0:T(8,128)S(1)} %add.133), channel_id=1, source_target_pairs={{0,32},{32,0},{64,96},{96,64},{128,160},{160,128},{192,224},{224,1... | collective-permute-start | bytes 24584 | tf_op jit(solution)/shard_map/ppermute | solution.py:385
  139.5 11.2 %copy-start.11 = (f32[1,256,1024]{2,1,0:T(8,128)S(1)}, f32[1,256,1024]{2,1,0:T(8,128)}, u32[]{:S(2)}) copy-start(f32[1,256,1024]{2,1,0:T(8,128)} %copy-done.10) | copy-start | bytes 3145732
  139.6 8.2 %collective-permute-start.21 = (bf16[128,1024]{1,0:T(8,128)(2,1)S(1)}, bf16[128,1024]{1,0:T(8,128)(2,1)S(1)}, u32[]{:S(2)}, u32[]{:S(2)}) collective-permute-start(bf16[128,1024]{1,0:T(8,128)(2,1)S(1)} %get-tuple-element.133), channel_id=1, source_target_pairs={{0,224},{32,0},{64,32},{96,64},{128,96},{160,128},{192,160},{224,1... | collective-permute-start | bytes 786440 | tf_op jit(solution)/shard_map/ppermute | solution.py:381
  143.0 7.7 %collective-permute-start.20 = (bf16[128,1024]{1,0:T(8,128)(2,1)S(1)}, bf16[128,1024]{1,0:T(8,128)(2,1)S(1)}, u32[]{:S(2)}, u32[]{:S(2)}) collective-permute-start(bf16[128,1024]{1,0:T(8,128)(2,1)S(1)} %get-tuple-element.135), channel_id=1, source_target_pairs={{0,32},{32,64},{64,96},{96,128},{128,160},{160,192},{192,224},{224... | collective-permute-start | bytes 786440 | tf_op jit(solution)/shard_map/ppermute | solution.py:381
  143.1 4.6 %collective-permute-start.22 = (f32[16,128]{1,0:T(8,128)S(1)}, f32[16,128]{1,0:T(8,128)S(1)}, u32[]{:S(2)}, u32[]{:S(2)}) collective-permute-start(f32[16,128]{1,0:T(8,128)S(1)} %add.134), channel_id=1, source_target_pairs={{0,64},{32,96},{64,0},{96,32},{128,192},{160,224},{192,128},{224,1... | collective-permute-start | bytes 24584 | tf_op jit(solution)/shard_map/ppermute | solution.py:385
  150.8 13.3 %collective-permute-start.26 = (f32[128,1024]{1,0:T(8,128)S(1)}, f32[128,1024]{1,0:T(8,128)S(1)}, u32[]{:S(2)}, u32[]{:S(2)}) collective-permute-start(f32[128,1024]{1,0:T(8,128)S(1)} %get-tuple-element.131), channel_id=1, source_target_pairs={{0,16},{16,0},{1,17},{17,1},{2,18},{18,2},{3,19},{19,3},{4,20},{20... | collective-permute-start | bytes 1572872 | tf_op jit(solution)/shard_map/ppermute | solution.py:381
  152.3 7.7 %collective-permute-start.23 = (f32[16,128]{1,0:T(8,128)S(1)}, f32[16,128]{1,0:T(8,128)S(1)}, u32[]{:S(2)}, u32[]{:S(2)}) collective-permute-start(f32[16,128]{1,0:T(8,128)S(1)} %add.138), channel_id=1, source_target_pairs={{0,128},{32,160},{64,192},{96,224},{128,0},{160,32},{192,64},{224,... | collective-permute-start | bytes 24584 | tf_op jit(solution)/shard_map/ppermute | solution.py:385
  156.4 6.4 %collective-permute-start.25 = (bf16[128,1024]{1,0:T(8,128)(2,1)S(1)}, bf16[128,1024]{1,0:T(8,128)(2,1)S(1)}, u32[]{:S(2)}, u32[]{:S(2)}) collective-permute-start(bf16[128,1024]{1,0:T(8,128)(2,1)S(1)} %get-tuple-element.132), channel_id=1, source_target_pairs={{0,224},{32,0},{64,32},{96,64},{128,96},{160,128},{192,160},{224,1... | collective-permute-start | bytes 786440 | tf_op jit(solution)/shard_map/ppermute | solution.py:381
  156.5 7.6 %collective-permute-start.24 = (bf16[128,1024]{1,0:T(8,128)(2,1)S(1)}, bf16[128,1024]{1,0:T(8,128)(2,1)S(1)}, u32[]{:S(2)}, u32[]{:S(2)}) collective-permute-start(bf16[128,1024]{1,0:T(8,128)(2,1)S(1)} %get-tuple-element.134), channel_id=1, source_target_pairs={{0,32},{32,64},{64,96},{96,128},{128,160},{160,192},{192,224},{224... | collective-permute-start | bytes 786440 | tf_op jit(solution)/shard_map/ppermute | solution.py:381
Sparse Core Ops, SparseCore 0:
  9.9 77.3 all-gather.1

commit v6 on v5

--- a/solution.py
+++ b/solution.py
@@ -39,7 +39,7 @@
 def spread_matrix(width):
     row = lax.broadcasted_iota(jnp.int32, (128, HEADS * width), 0)
     col = lax.broadcasted_iota(jnp.int32, (128, HEADS * width), 1)
-    return jnp.where((row < 48) & ((row & 15) == col // width), 1.0, 0.0).astype(BF16)
+    return jnp.where((row < 48) & ((row & 15) == col >> (width.bit_length() - 1)), 1.0, 0.0).astype(BF16)
 
 
 def parts3(v):
@@ -125,7 +125,7 @@
             ys_ref[rows, cols] = jnp.where(lane < 64, ys[0], ys[1])
         return 0
 
-    lax.fori_loop(0, 8, pair, 0)
+    lax.fori_loop(0, 8, pair, 0, unroll=2)
 
     s10 = dot_nt(c_ref[SPAN:, :], b_ref[:SPAN, :])
     qdt = parts3(jnp.exp2(cums[0][SPAN - 1:SPAN, :] + rs[0]))
@@ -146,7 +146,7 @@
         n_ref[rows, :] = (gated * inv * gain).astype(BF16)
         return 0
 
-    lax.fori_loop(0, TOK // 32, norm, 0)
+    lax.fori_loop(0, TOK // 32, norm, 0, unroll=2)
 
 
 def bwd_kernel(u_hbm, ys_hbm, x_hbm, z_hbm, b_ref, c_ref, dt_ref, rate_ref, skip_ref, gain_ref,
@@ -200,7 +200,7 @@
 
     for load in loads:
         load.wait()
-    lax.fori_loop(0, TOK // 32, gate, 0)
+    lax.fori_loop(0, TOK // 32, gate, 0, unroll=4)
     store = pltpu.make_async_copy(dz_ref, dz_hbm, sem.at[4])
     store.start()
 
@@ -249,7 +249,7 @@
             dxs_ref[rows, cols] = jnp.where(lane < 64, outs[0], outs[1])
         return 0
 
-    lax.fori_loop(0, 8, pair, 0)
+    lax.fori_loop(0, 8, pair, 0, unroll=2)
 
     st = dot_nt(b_ref[:SPAN, :], c_ref[SPAN:, :])
     qdt = parts3(jnp.exp2(cums[0][SPAN - 1:SPAN, :] + rs[0]))
@@ -265,7 +265,7 @@
 
     seg_row = lax.broadcasted_iota(jnp.int32, (CH, 128), 0)
     seg_col = lax.broadcasted_iota(jnp.int32, (CH, 128), 1)
-    seg = jnp.where(seg_row // 64 == seg_col, 1.0, 0.0).astype(BF16)
+    seg = jnp.where(seg_row >> 6 == seg_col, 1.0, 0.0).astype(BF16)
 
     def heads_sum(v):
         hi, lo = split2(v)

time: 173 us -> 170 us (0.983)
  Pallas kernels: 56.6 us -> 52.7 us
    pallas_call x1, Pallas kernels: 16.6 us -> 14.3 us  [scan_backward(): pl.pallas_call(bwd_kernel, out_shape=(jax.ShapeDtypeStruct((TOK, CH), BF1...]
  transfers between devices with their start and end apart: 28 -> 28, of which waited for: 14 -> 15; matrix products, arithmetic and copies ran while one was open for 5% -> 5% of each run, Pallas kernels for 28% -> 27%
where the time goes in v6:
time: 170 us
  Pallas kernels  52.7 us (31%)
  starting transfers between devices  44.3 us (26%)
  waiting for transfers between devices  40.4 us (24%)
  between operations  14.5 us (9%)
  local copies, waits for them, and re-layouts  13.8 us (8%)
  other arithmetic  3.82 us (2%)
    ppermute x24, starting transfers between devices, send(): return lax.ppermute(v, axis, [(i, (i + shift) % n) for i in range(n)])  38.6 us
    ppermute x24, waiting for transfers between devices, send(): return lax.ppermute(v, axis, [(i, (i + shift) % n) for i in range(n)])  32.4 us
    pallas_call x1, Pallas kernels, scan_backward(): pl.pallas_call(bwd_kernel, out_shape=(jax.ShapeDtypeStruct((TOK, CH), BF1...  14.3 us
    unnamed x50, local copies, waits for them, and re-layouts  8.45 us
    pallas_call x1, Pallas kernels, back_project(): pl.pallas_call(kernel, grid_spec=pltpu.PrefetchScalarGridSpec(num_scalar_...  7.9 us
    pallas_call x2, Pallas kernels, ring_step(): pl.pallas_call(kernel, grid_spec=pltpu.PrefetchScalarGridSpec(num_scalar_...  7.64 us
    pallas_call x2, Pallas kernels, shuffle(): pl.pallas_call(kernel, out_shape=tuple((jax.ShapeDtypeStruct(s, BF16) for...  7.27 us
    pallas_call x1, Pallas kernels, scan_forward(): pl.pallas_call(fwd_kernel, out_shape=(jax.ShapeDtypeStruct((TOK, CH), F32...  7.16 us
  transfers between devices with their start and end apart: 28, of which 15 were waited for; matrix products, arithmetic and copies ran while one was open for 5% of the time, Pallas kernels for 27%

profile of v6, /device:TPU:2, one launch (start us, length us, event | category | flops | bytes accessed | tf_op | source)
XLA Modules:
  0.0 169.6 jit_solution(1716896183765339817)
XLA Ops:
  7.3 0.7 all-gather.2.cloned.1.call-update
  8.0 2.0 %own_first.1.refs_0_ = bf16[64,4096]{1,0:T(8,128)(2,1)} custom-call(s32[1]{0:T(128)} %bitcast.3.core_ref, bf16[64,4096]{1,0:T(8,128)(2,1)} %in_ref.1), custom_call_target="tpu_custom_call" | custom-call | flops 1000 | bytes 1000 | tf_op jit(solution)/shard_map/own_first/pallas_call | solution.py:430
  10.0 1.6 collective-permute-start
  11.5 1.7 collective-permute-start.1
  13.2 2.1 %collective-permute-start.2 = (bf16[64,4096]{1,0:T(8,128)(2,1)}, bf16[64,4096]{1,0:T(8,128)(2,1)}, u32[]{:S(2)}, u32[]{:S(2)}) collective-permute-start(bf16[64,4096]{1,0:T(8,128)(2,1)} %own_first.1.refs_0_), channel_id=1, source_target_pairs={{0,1},{1,0},{2,3},{3,2},{4,5},{5,4},{6,7},{7,6},{8,9},{9,8},{10,11... | collective-permute-start | bytes 1572872 | tf_op jit(solution)/shard_map/ppermute | solution.py:381
  15.3 9.8 %collective-permute-done.refs_2_ = bf16[64,4096]{1,0:T(8,128)(2,1)S(1)} collective-permute-done((bf16[64,4096]{1,0:T(8,128)(2,1)}, bf16[64,4096]{1,0:T(8,128)(2,1)S(1)}, u32[]{:S(2)}, u32[]{:S(2)}) %collective-permute-start) | collective-permute-done | bytes 524320 | tf_op jit(solution)/shard_map/ppermute | solution.py:381
  25.1 4.8 %collective-permute-done.2.refs_1_ = bf16[64,4096]{1,0:T(8,128)(2,1)} collective-permute-done((bf16[64,4096]{1,0:T(8,128)(2,1)}, bf16[64,4096]{1,0:T(8,128)(2,1)}, u32[]{:S(2)}, u32[]{:S(2)}) %collective-permute-start.2) | collective-permute-done | bytes 524320 | tf_op jit(solution)/shard_map/ppermute | solution.py:381
  29.9 3.2 %collective-permute-start.4 = (bf16[64,4096]{1,0:T(8,128)(2,1)}, bf16[64,4096]{1,0:T(8,128)(2,1)}, u32[]{:S(2)}, u32[]{:S(2)}) collective-permute-start(bf16[64,4096]{1,0:T(8,128)(2,1)} %collective-permute-done.2.refs_1_), channel_id=1, source_target_pairs={{0,6},{2,0},{4,2},{6,4},{1,7},{3,1},{5,3},{7,5},{8,14},{10,8},{12,... | collective-permute-start | bytes 1572872 | tf_op jit(solution)/shard_map/ppermute | solution.py:381
  33.1 0.7 slice.33
  33.9 0.7 slice.34
  34.6 3.2 %collective-permute-start.6 = (bf16[32,4096]{1,0:T(8,128)(2,1)}, bf16[32,4096]{1,0:T(8,128)(2,1)}, u32[]{:S(2)}, u32[]{:S(2)}) collective-permute-start(bf16[32,4096]{1,0:T(8,128)(2,1)} %slice.34), channel_id=1, source_target_pairs={{0,6},{2,0},{4,2},{6,4},{1,7},{3,1},{5,3},{7,5},{8,14},{10,8},{12,... | collective-permute-start | bytes 786440 | tf_op jit(solution)/shard_map/ppermute | solution.py:381
  37.8 0.9 copy.19.dt_ref
  38.8 0.9 copy-done.14
  39.7 7.2 %scan_forward.1 = (f32[512,1024]{1,0:T(8,128)S(1)}, bf16[512,1024]{1,0:T(8,128)(2,1)S(1)}) custom-call(bf16[512,1024]{1,0:T(8,128)(2,1)S(1)} %copy-done.6, bf16[512,1024]{1,0:T(8,128)(2,1)S(1)} %copy-done.8, bf16[512,128]{1,0:T(8,128)(2,1)S(1)} %bitcast.37, bf16[512,128]{1,0:T(8,128)(2,1)S(1)} %bitcast.39, f32[512,16]{1,0:T(8,128)S(1)} %copy.19.dt_ref, ...), custom_call_target="tpu_custom_call" | custom-call | flops 1000 | bytes 1000 | tf_op jit(solution)/shard_map/scan_forward/pallas_call | solution.py:320
  46.9 1.3 copy-done.12
  48.3 1.0 slice.35
  49.4 1.0 slice.36
  50.3 3.3 %collective-permute-start.8 = (bf16[32,4096]{1,0:T(8,128)(2,1)S(1)}, bf16[32,4096]{1,0:T(8,128)(2,1)S(1)}, u32[]{:S(2)}, u32[]{:S(2)}) collective-permute-start(bf16[32,4096]{1,0:T(8,128)(2,1)S(1)} %slice.36), channel_id=1, source_target_pairs={{0,6},{2,0},{4,2},{6,4},{1,7},{3,1},{5,3},{7,5},{8,14},{10,8},{12,... | collective-permute-start | bytes 786440 | tf_op jit(solution)/shard_map/ppermute | solution.py:381
  53.7 0.6 pad_add_fusion
  54.3 5.0 %collective-permute-done.7.refs_8_ = bf16[32,4096]{1,0:T(8,128)(2,1)S(1)} collective-permute-done((bf16[32,4096]{1,0:T(8,128)(2,1)S(1)}, bf16[32,4096]{1,0:T(8,128)(2,1)S(1)}, u32[]{:S(2)}, u32[]{:S(2)}) %collective-permute-start.7) | collective-permute-done | bytes 262176 | tf_op jit(solution)/shard_map/ppermute | solution.py:381
  59.3 0.3 collective-permute-done.8.refs_9_
  59.6 0.4 copy-done.22
  60.0 0.3 copy-done.23
  60.3 3.6 %place_tokens.2.b_ref = bf16[512,2048]{1,0:T(8,128)(2,1)} custom-call(s32[2]{0:T(128)} %get-tuple-element.140.s_ref, bf16[64,4096]{1,0:T(8,128)(2,1)} %own_first.1.refs_0_, bf16[64,4096]{1,0:T(8,128)(2,1)} %collective-permute-done.2.refs_1_, bf16[64,4096]{1,0:T(8,128)(2,1)} %copy-done.20, bf16[64,4096]{1,0:T(8,128)(2,1)} %collective-permute-done.3.refs_3_, ...), custom_call_target="tpu_custom_call" | custom-call | flops 1000 | bytes 1000 | tf_op jit(solution)/shard_map/place_tokens/pallas_call | solution.py:410
  64.2 3.7 %place_tokens.3.a_ref = bf16[512,2048]{1,0:T(8,128)(2,1)} custom-call(s32[2]{0:T(128)} %get-tuple-element.140.s_ref, bf16[64,4096]{1,0:T(8,128)(2,1)} %own_first.1.refs_0_, bf16[64,4096]{1,0:T(8,128)(2,1)} %collective-permute-done.2.refs_1_, bf16[64,4096]{1,0:T(8,128)(2,1)} %copy-done.20, bf16[64,4096]{1,0:T(8,128)(2,1)} %collective-permute-done.3.refs_3_, ...), custom_call_target="tpu_custom_call" | custom-call | flops 1000 | bytes 1000 | tf_op jit(solution)/shard_map/place_tokens/pallas_call | solution.py:410
  67.9 0.9 collective-permute-done.10.b_ref
  68.8 1.6 copy-done
  70.4 1.7 %weight_blocks.3 = f32[1,256,1024]{2,1,0:T(8,128)S(1)} custom-call(s32[1]{0:T(128)} %bitcast.at_ref, bf16[512,2048]{1,0:T(8,128)(2,1)S(1)} %copy-done, bf16[512,2048]{1,0:T(8,128)(2,1)} %collective-permute-done.10.b_ref, bf16[512,1024]{1,0:T(8,128)(2,1)S(1)} %get-tuple-element.73.n_ref, bf16[512,1024]{1,0:T(8,128)(2,1)S(1)} %collective-permute-done.9.m_ref), custom_call_target="tpu_custom_call" | custom-call | flops 1000 | bytes 1000 | tf_op jit(solution)/shard_map/weight_blocks/pallas_call | solution.py:467
  72.2 0.8 fusion.2
  73.0 1.3 collective-permute-start.11
  74.3 7.8 %collective-permute-start.12 = (bf16[256,512]{1,0:T(8,128)(2,1)}, bf16[256,512]{1,0:T(8,128)(2,1)}, u32[]{:S(2)}, u32[]{:S(2)}) collective-permute-start(bf16[256,512]{1,0:T(8,128)(2,1)} %get-tuple-element.136), channel_id=1, source_target_pairs={{0,224},{32,0},{64,32},{96,64},{128,96},{160,128},{192,160},{224,1... | collective-permute-start | bytes 786440 | tf_op jit(solution)/shard_map/ppermute | solution.py:381
  82.2 0.6 pad_add_fusion.2.at_ref
  82.8 1.3 copy-done.3
  84.0 1.7 %weight_blocks.4 = f32[1,256,1024]{2,1,0:T(8,128)S(1)} custom-call(s32[1]{0:T(128)} %bitcast.10.at_ref, bf16[512,2048]{1,0:T(8,128)(2,1)S(1)} %copy-done.1, bf16[512,2048]{1,0:T(8,128)(2,1)} %collective-permute-done.10.b_ref, bf16[512,1024]{1,0:T(8,128)(2,1)S(1)} %get-tuple-element.73.n_ref, bf16[512,1024]{1,0:T(8,128)(2,1)S(1)} %copy-done.3), custom_call_target="tpu_custom_call" | custom-call | flops 1000 | bytes 1000 | tf_op jit(solution)/shard_map/weight_blocks/pallas_call | solution.py:467
  85.7 1.0 copy-done.10
  86.7 0.7 all-gather.2.cloned.1.call-done
  87.4 7.9 %back_project.1.u_hbm = f32[512,1024]{1,0:T(8,128)S(1)} custom-call(s32[1]{0:T(128)} %bitcast.3.core_ref, bf16[512,2048]{1,0:T(8,128)(2,1)S(1)} %copy-done.1, bf16[512,2048]{1,0:T(8,128)(2,1)} %place_tokens.2.b_ref, bf16[16,2,128,1024]{3,2,1,0:T(8,128)(2,1)} %bitcast.47, bf16[16,2,128,1024]{3,2,1,0:T(8,128)(2,1)} %bitcast.48), custom_call_target="tpu_custom_call" | custom-call | flops 1000 | bytes 1000 | tf_op jit(solution)/shard_map/back_project/pallas_call | solution.py:528
  95.4 3.4 %ring_step.2 = (bf16[256,1024]{1,0:T(8,128)(2,1)S(1)}, bf16[256,1024]{1,0:T(8,128)(2,1)S(1)}) custom-call(s32[2]{0:T(128)S(1)} %copy-done.19, bf16[512,2048]{1,0:T(8,128)(2,1)S(1)} %copy-done.1, bf16[512,2048]{1,0:T(8,128)(2,1)} %collective-permute-done.10.b_ref, bf16[512,1024]{1,0:T(8,128)(2,1)S(1)} %get-tuple-element.73.n_ref, ...), custom_call_target="tpu_custom_call" | custom-call | flops 1000 | bytes 1000 | tf_op jit(solution)/shard_map/ring_step/pallas_call | solution.py:508
  98.8 1.6 collective-permute-start.13
  100.4 1.7 %collective-permute-start.14 = (bf16[256,1024]{1,0:T(8,128)(2,1)S(1)}, bf16[256,1024]{1,0:T(8,128)(2,1)S(1)}, u32[]{:S(2)}, u32[]{:S(2)}) collective-permute-start(bf16[256,1024]{1,0:T(8,128)(2,1)S(1)} %get-tuple-element.100), channel_id=1, source_target_pairs={{0,224},{32,0},{64,32},{96,64},{128,96},{160,128},{192,160},{224,1... | collective-permute-start | bytes 1572872 | tf_op jit(solution)/shard_map/ppermute | solution.py:381
  102.1 14.3 %scan_backward.1 = (bf16[512,1024]{1,0:T(8,128)(2,1)}, bf16[512,1024]{1,0:T(8,128)(2,1)}, bf16[512,128]{1,0:T(8,128)(2,1)}, bf16[512,128]{1,0:T(8,128)(2,1)}, f3...) custom-call(f32[512,1024]{1,0:T(8,128)S(1)} %back_project.1.u_hbm, f32[512,1024]{1,0:T(8,128)} %copy-done.12, ...), custom_call_target="tpu_custom_call" | custom-call | flops 1000 | bytes 1000 | tf_op jit(solution)/shard_map/scan_backward/pallas_call | solution.py:338
  116.5 4.3 %ring_step.3 = (bf16[256,1024]{1,0:T(8,128)(2,1)}, bf16[256,1024]{1,0:T(8,128)(2,1)}) custom-call(s32[2]{0:T(128)S(1)} %get-tuple-element.141.at_ref, bf16[512,2048]{1,0:T(8,128)(2,1)} %place_tokens.3.a_ref, bf16[512,2048]{1,0:T(8,128)(2,1)} %collective-permute-done.10.b_ref, bf16[512,1024]{1,0:T(8,128)(2,1)S(1)} %get-tuple-element.73.n_ref, ...), custom_call_target="tpu_custom_call" | custom-call | flops 1000 | bytes 1000 | tf_op jit(solution)/shard_map/ring_step/pallas_call | solution.py:508
  121.0 3.0 %collective-permute-start.16 = (bf16[256,1024]{1,0:T(8,128)(2,1)}, bf16[256,1024]{1,0:T(8,128)(2,1)}, u32[]{:S(2)}, u32[]{:S(2)}) collective-permute-start(bf16[256,1024]{1,0:T(8,128)(2,1)} %get-tuple-element.105), channel_id=1, source_target_pairs={{0,224},{32,0},{64,32},{96,64},{128,96},{160,128},{192,160},{224,1... | collective-permute-start | bytes 1572872 | tf_op jit(solution)/shard_map/ppermute | solution.py:381
  124.0 1.2 collective-permute-done.17
  125.1 1.0 collective-permute-start.18
  126.1 2.7 %collective-permute-done.18 = f32[16,128]{1,0:T(8,128)S(1)} collective-permute-done((f32[16,128]{1,0:T(8,128)S(1)}, f32[16,128]{1,0:T(8,128)S(1)}, u32[]{:S(2)}, u32[]{:S(2)}) %collective-permute-start.18) | collective-permute-done | bytes 8224 | tf_op jit(solution)/shard_map/ppermute | solution.py:381
  128.9 3.1 %weight_blocks.5 = f32[2,256,1024]{2,1,0:T(8,128)S(1)} custom-call(s32[2]{0:T(128)S(1)} %pad_add_fusion.3.at_ref, bf16[512,2048]{1,0:T(8,128)(2,1)} %place_tokens.3.a_ref, bf16[512,2048]{1,0:T(8,128)(2,1)} %collective-permute-done.10.b_ref, bf16[512,1024]{1,0:T(8,128)(2,1)S(1)} %get-tuple-element.73.n_ref, bf16[512,1024]{1,0:T(8,128)(2,1)S(1)} %copy-done.5), custom_call_target="tpu_custom_call" | custom-call | flops 1000 | bytes 1000 | tf_op jit(solution)/shard_map/weight_blocks/pallas_call | solution.py:467
  132.0 2.7 %collective-permute-done.19 = f32[16,128]{1,0:T(8,128)S(1)} collective-permute-done((f32[16,128]{1,0:T(8,128)S(1)}, f32[16,128]{1,0:T(8,128)S(1)}, u32[]{:S(2)}, u32[]{:S(2)}) %collective-permute-start.19) | collective-permute-done | bytes 8224 | tf_op jit(solution)/shard_map/ppermute | solution.py:385
  134.6 1.0 collective-permute-done.15
  135.6 1.4 fusion
  137.1 3.1 %collective-permute-start.21 = (bf16[128,1024]{1,0:T(8,128)(2,1)S(1)}, bf16[128,1024]{1,0:T(8,128)(2,1)S(1)}, u32[]{:S(2)}, u32[]{:S(2)}) collective-permute-start(bf16[128,1024]{1,0:T(8,128)(2,1)S(1)} %get-tuple-element.133), channel_id=1, source_target_pairs={{0,224},{32,0},{64,32},{96,64},{128,96},{160,128},{192,160},{224,1... | collective-permute-start | bytes 786440 | tf_op jit(solution)/shard_map/ppermute | solution.py:381
  140.4 1.5 collective-permute-start.22
  141.9 3.1 %collective-permute-done.22 = f32[16,128]{1,0:T(8,128)S(1)} collective-permute-done((f32[16,128]{1,0:T(8,128)S(1)}, f32[16,128]{1,0:T(8,128)S(1)}, u32[]{:S(2)}, u32[]{:S(2)}) %collective-permute-start.22) | collective-permute-done | bytes 8224 | tf_op jit(solution)/shard_map/ppermute | solution.py:385
  145.0 3.0 %collective-permute-done.20 = bf16[128,1024]{1,0:T(8,128)(2,1)S(1)} collective-permute-done((bf16[128,1024]{1,0:T(8,128)(2,1)S(1)}, bf16[128,1024]{1,0:T(8,128)(2,1)S(1)}, u32[]{:S(2)}, u32[]{:S(2)}) %collective-permute-start.20) | collective-permute-done | bytes 262176 | tf_op jit(solution)/shard_map/ppermute | solution.py:381
  148.2 1.1 collective-permute-start.26
  149.3 4.1 %collective-permute-start.23 = (f32[16,128]{1,0:T(8,128)S(1)}, f32[16,128]{1,0:T(8,128)S(1)}, u32[]{:S(2)}, u32[]{:S(2)}) collective-permute-start(f32[16,128]{1,0:T(8,128)S(1)} %add.138), channel_id=1, source_target_pairs={{0,128},{32,160},{64,192},{96,224},{128,0},{160,32},{192,64},{224,... | collective-permute-start | bytes 24584 | tf_op jit(solution)/shard_map/ppermute | solution.py:385
  153.3 0.7 copy.21
  154.2 1.8 %collective-permute-start.24 = (bf16[128,1024]{1,0:T(8,128)(2,1)S(1)}, bf16[128,1024]{1,0:T(8,128)(2,1)S(1)}, u32[]{:S(2)}, u32[]{:S(2)}) collective-permute-start(bf16[128,1024]{1,0:T(8,128)(2,1)S(1)} %get-tuple-element.134), channel_id=1, source_target_pairs={{0,32},{32,64},{64,96},{96,128},{128,160},{160,192},{192,224},{224... | collective-permute-start | bytes 786440 | tf_op jit(solution)/shard_map/ppermute | solution.py:381
  156.1 0.9 collective-permute-done.23
  157.0 0.5 slice_bitcast_fusion.1
  157.5 0.6 slice_bitcast_fusion
  158.1 2.3 %collective-permute-done.25 = bf16[128,1024]{1,0:T(8,128)(2,1)S(1)} collective-permute-done((bf16[128,1024]{1,0:T(8,128)(2,1)S(1)}, bf16[128,1024]{1,0:T(8,128)(2,1)S(1)}, u32[]{:S(2)}, u32[]{:S(2)}) %collective-permute-start.25) | collective-permute-done | bytes 262176 | tf_op jit(solution)/shard_map/ppermute | solution.py:381
  160.4 1.4 collective-permute-done.24
  161.8 0.9 add_add_fusion
  (75 shorter events, 1.6 us)
Async XLA Ops:
  7.2 31.5 %copy-start.18 = (f32[16]{0:T(128)S(1)}, f32[16]{0:T(128)}, u32[]{:S(2)}) copy-start(f32[16]{0:T(128)} %param.17) | copy-start | bytes 196
  7.2 31.5 %copy-start.13 = (bf16[512,1,128]{2,0,1:T(8,128)(2,1)S(1)}, bf16[512,1,128]{2,0,1:T(8,128)(2,1)}, u32[]{:S(2)}) copy-start(bf16[512,1,128]{2,0,1:T(8,128)(2,1)} %param.13) | copy-start | bytes 393220
  7.2 31.5 %copy-start.17 = (f32[16]{0:T(128)S(1)}, f32[16]{0:T(128)}, u32[]{:S(2)}) copy-start(f32[16]{0:T(128)} %param.16) | copy-start | bytes 196
  7.2 31.5 %copy-start.16 = (f32[1024]{0:T(1024)S(1)}, f32[1024]{0:T(1024)}, u32[]{:S(2)}) copy-start(f32[1024]{0:T(1024)} %param.18) | copy-start | bytes 12292
  7.2 31.5 %copy-start.6 = (bf16[512,1024]{1,0:T(8,128)(2,1)S(1)}, bf16[512,1024]{1,0:T(8,128)(2,1)}, u32[]{:S(2)}) copy-start(bf16[512,1024]{1,0:T(8,128)(2,1)} %x_hbm.1) | copy-start | bytes 3145732
  7.2 31.5 %copy-start.8 = (bf16[512,1024]{1,0:T(8,128)(2,1)S(1)}, bf16[512,1024]{1,0:T(8,128)(2,1)}, u32[]{:S(2)}) copy-start(bf16[512,1024]{1,0:T(8,128)(2,1)} %z_hbm.1) | copy-start | bytes 3145732
  7.2 80.2 %all-gather.2.cloned.1.call-start = ((), (), s32[]{:S(2)}) async-start(), calls=%async_computation | async-start | bytes 8650752 | tf_op jit(solution)/shard_map/all_gather | solution.py:552
  10.0 15.1 %collective-permute-start = (bf16[64,4096]{1,0:T(8,128)(2,1)}, bf16[64,4096]{1,0:T(8,128)(2,1)S(1)}, u32[]{:S(2)}, u32[]{:S(2)}) collective-permute-start(bf16[64,4096]{1,0:T(8,128)(2,1)} %own_first.1.refs_0_), channel_id=1, source_target_pairs={{0,2},{2,4},{4,6},{6,0},{1,3},{3,5},{5,7},{7,1},{8,10},{10,12},{12... | collective-permute-start | bytes 1572872 | tf_op jit(solution)/shard_map/ppermute | solution.py:381
  11.5 13.6 %collective-permute-start.1 = (bf16[64,4096]{1,0:T(8,128)(2,1)}, bf16[64,4096]{1,0:T(8,128)(2,1)S(1)}, u32[]{:S(2)}, u32[]{:S(2)}) collective-permute-start(bf16[64,4096]{1,0:T(8,128)(2,1)} %own_first.1.refs_0_), channel_id=1, source_target_pairs={{0,6},{2,0},{4,2},{6,4},{1,7},{3,1},{5,3},{7,5},{8,14},{10,8},{12,... | collective-permute-start | bytes 1572872 | tf_op jit(solution)/shard_map/ppermute | solution.py:381
  13.2 16.7 %collective-permute-start.2 = (bf16[64,4096]{1,0:T(8,128)(2,1)}, bf16[64,4096]{1,0:T(8,128)(2,1)}, u32[]{:S(2)}, u32[]{:S(2)}) collective-permute-start(bf16[64,4096]{1,0:T(8,128)(2,1)} %own_first.1.refs_0_), channel_id=1, source_target_pairs={{0,1},{1,0},{2,3},{3,2},{4,5},{5,4},{6,7},{7,6},{8,9},{9,8},{10,11... | collective-permute-start | bytes 1572872 | tf_op jit(solution)/shard_map/ppermute | solution.py:381
  25.1 13.6 %copy-start.20 = (bf16[64,4096]{1,0:T(8,128)(2,1)}, bf16[64,4096]{1,0:T(8,128)(2,1)S(1)}, u32[]{:S(2)}) copy-start(bf16[64,4096]{1,0:T(8,128)(2,1)S(1)} %collective-permute-done.refs_2_) | copy-start | bytes 1572868
  25.1 13.6 %copy-start.21 = (bf16[64,4096]{1,0:T(8,128)(2,1)}, bf16[64,4096]{1,0:T(8,128)(2,1)S(1)}, u32[]{:S(2)}) copy-start(bf16[64,4096]{1,0:T(8,128)(2,1)S(1)} %collective-permute-done.1.refs_4_) | copy-start | bytes 1572868
  29.9 18.3 %collective-permute-start.3 = (bf16[64,4096]{1,0:T(8,128)(2,1)}, bf16[64,4096]{1,0:T(8,128)(2,1)}, u32[]{:S(2)}, u32[]{:S(2)}) collective-permute-start(bf16[64,4096]{1,0:T(8,128)(2,1)} %collective-permute-done.2.refs_1_), channel_id=1, source_target_pairs={{0,2},{2,4},{4,6},{6,0},{1,3},{3,5},{5,7},{7,1},{8,10},{10,12},{12... | collective-permute-start | bytes 1572872 | tf_op jit(solution)/shard_map/ppermute | solution.py:381
  29.9 18.3 %collective-permute-start.4 = (bf16[64,4096]{1,0:T(8,128)(2,1)}, bf16[64,4096]{1,0:T(8,128)(2,1)}, u32[]{:S(2)}, u32[]{:S(2)}) collective-permute-start(bf16[64,4096]{1,0:T(8,128)(2,1)} %collective-permute-done.2.refs_1_), channel_id=1, source_target_pairs={{0,6},{2,0},{4,2},{6,4},{1,7},{3,1},{5,3},{7,5},{8,14},{10,8},{12,... | collective-permute-start | bytes 1572872 | tf_op jit(solution)/shard_map/ppermute | solution.py:381
  33.8 14.3 %collective-permute-start.5 = (bf16[32,4096]{1,0:T(8,128)(2,1)}, bf16[32,4096]{1,0:T(8,128)(2,1)}, u32[]{:S(2)}, u32[]{:S(2)}) collective-permute-start(bf16[32,4096]{1,0:T(8,128)(2,1)} %slice.33), channel_id=1, source_target_pairs={{0,2},{2,4},{4,6},{6,0},{1,3},{3,5},{5,7},{7,1},{8,10},{10,12},{12... | collective-permute-start | bytes 786440 | tf_op jit(solution)/shard_map/ppermute | solution.py:381
  34.6 13.6 %collective-permute-start.6 = (bf16[32,4096]{1,0:T(8,128)(2,1)}, bf16[32,4096]{1,0:T(8,128)(2,1)}, u32[]{:S(2)}, u32[]{:S(2)}) collective-permute-start(bf16[32,4096]{1,0:T(8,128)(2,1)} %slice.34), channel_id=1, source_target_pairs={{0,6},{2,0},{4,2},{6,4},{1,7},{3,1},{5,3},{7,5},{8,14},{10,8},{12,... | collective-permute-start | bytes 786440 | tf_op jit(solution)/shard_map/ppermute | solution.py:381
  38.8 0.9 copy-start.14
  46.9 1.3 copy-start.12
  48.2 11.4 %collective-permute-start.9 = (bf16[512,1024]{1,0:T(8,128)(2,1)S(1)}, bf16[512,1024]{1,0:T(8,128)(2,1)S(1)}, u32[]{:S(2)}, u32[]{:S(2)}) collective-permute-start(bf16[512,1024]{1,0:T(8,128)(2,1)S(1)} %get-tuple-element.73.n_ref), channel_id=1, source_target_pairs={{0,8},{8,0},{1,9},{9,1},{2,10},{10,2},{3,11},{11,3},{4,12},{12,4},... | collective-permute-start | bytes 3145736 | tf_op jit(solution)/shard_map/ppermute | solution.py:381
  49.3 10.0 %collective-permute-start.7 = (bf16[32,4096]{1,0:T(8,128)(2,1)S(1)}, bf16[32,4096]{1,0:T(8,128)(2,1)S(1)}, u32[]{:S(2)}, u32[]{:S(2)}) collective-permute-start(bf16[32,4096]{1,0:T(8,128)(2,1)S(1)} %slice.35), channel_id=1, source_target_pairs={{0,2},{2,4},{4,6},{6,0},{1,3},{3,5},{5,7},{7,1},{8,10},{10,12},{12... | collective-permute-start | bytes 786440 | tf_op jit(solution)/shard_map/ppermute | solution.py:381
  50.3 9.2 %collective-permute-start.8 = (bf16[32,4096]{1,0:T(8,128)(2,1)S(1)}, bf16[32,4096]{1,0:T(8,128)(2,1)S(1)}, u32[]{:S(2)}, u32[]{:S(2)}) collective-permute-start(bf16[32,4096]{1,0:T(8,128)(2,1)S(1)} %slice.36), channel_id=1, source_target_pairs={{0,6},{2,0},{4,2},{6,4},{1,7},{3,1},{5,3},{7,5},{8,14},{10,8},{12,... | collective-permute-start | bytes 786440 | tf_op jit(solution)/shard_map/ppermute | solution.py:381
  59.3 0.7 copy-start.22
  59.6 0.7 copy-start.23
  59.6 9.2 %copy-start.2 = (bf16[512,1024]{1,0:T(8,128)(2,1)}, bf16[512,1024]{1,0:T(8,128)(2,1)S(1)}, u32[]{:S(2)}) copy-start(bf16[512,1024]{1,0:T(8,128)(2,1)S(1)} %collective-permute-done.9.m_ref) | copy-start | bytes 3145732
  63.9 4.9 %collective-permute-start.10 = (bf16[512,2048]{1,0:T(8,128)(2,1)}, bf16[512,2048]{1,0:T(8,128)(2,1)}, u32[]{:S(2)}, u32[]{:S(2)}) collective-permute-start(bf16[512,2048]{1,0:T(8,128)(2,1)} %place_tokens.2.b_ref), channel_id=1, source_target_pairs={{0,8},{8,0},{1,9},{9,1},{2,10},{10,2},{3,11},{11,3},{4,12},{12,4},... | collective-permute-start | bytes 6291464 | tf_op jit(solution)/shard_map/ppermute | solution.py:381
  68.8 1.6 copy-start
  72.1 10.7 %copy-start.1 = (bf16[512,2048]{1,0:T(8,128)(2,1)S(1)}, bf16[512,2048]{1,0:T(8,128)(2,1)}, u32[]{:S(2)}) copy-start(bf16[512,2048]{1,0:T(8,128)(2,1)} %place_tokens.3.a_ref) | copy-start | bytes 6291460
  73.0 22.4 %collective-permute-start.11 = (bf16[256,512]{1,0:T(8,128)(2,1)}, bf16[256,512]{1,0:T(8,128)(2,1)}, u32[]{:S(2)}, u32[]{:S(2)}) collective-permute-start(bf16[256,512]{1,0:T(8,128)(2,1)} %get-tuple-element.137), channel_id=1, source_target_pairs={{0,32},{32,64},{64,96},{96,128},{128,160},{160,192},{192,224},{224... | collective-permute-start | bytes 786440 | tf_op jit(solution)/shard_map/ppermute | solution.py:381
  74.3 21.0 %collective-permute-start.12 = (bf16[256,512]{1,0:T(8,128)(2,1)}, bf16[256,512]{1,0:T(8,128)(2,1)}, u32[]{:S(2)}, u32[]{:S(2)}) collective-permute-start(bf16[256,512]{1,0:T(8,128)(2,1)} %get-tuple-element.136), channel_id=1, source_target_pairs={{0,224},{32,0},{64,32},{96,64},{128,96},{160,128},{192,160},{224,1... | collective-permute-start | bytes 786440 | tf_op jit(solution)/shard_map/ppermute | solution.py:381
  82.8 1.3 copy-start.3
  85.7 1.0 copy-start.10
  87.4 8.0 %copy-start.4 = (bf16[512,1024]{1,0:T(8,128)(2,1)S(1)}, bf16[512,1024]{1,0:T(8,128)(2,1)}, u32[]{:S(2)}) copy-start(bf16[512,1024]{1,0:T(8,128)(2,1)} %copy-done.2) | copy-start | bytes 3145732
  87.4 8.0 %copy-start.19 = (s32[2]{0:T(128)S(1)}, s32[2]{0:T(128)}, u32[]{:S(2)}) copy-start(s32[2]{0:T(128)} %pad_add_fusion.2.at_ref) | copy-start | bytes 28
  95.3 6.8 %copy-start.7 = (bf16[512,1024]{1,0:T(8,128)(2,1)S(1)}, bf16[512,1024]{1,0:T(8,128)(2,1)}, u32[]{:S(2)}) copy-start(bf16[512,1024]{1,0:T(8,128)(2,1)} %x_hbm.1) | copy-start | bytes 3145732
  95.4 6.8 %copy-start.9 = (bf16[512,1024]{1,0:T(8,128)(2,1)S(1)}, bf16[512,1024]{1,0:T(8,128)(2,1)}, u32[]{:S(2)}) copy-start(bf16[512,1024]{1,0:T(8,128)(2,1)} %z_hbm.1) | copy-start | bytes 3145732
  95.4 6.8 %copy-start.15 = (bf16[512,1,128]{2,0,1:T(8,128)(2,1)S(1)}, bf16[512,1,128]{2,0,1:T(8,128)(2,1)}, u32[]{:S(2)}) copy-start(bf16[512,1,128]{2,0,1:T(8,128)(2,1)} %param.14) | copy-start | bytes 393220
  98.8 17.6 %collective-permute-start.13 = (bf16[256,1024]{1,0:T(8,128)(2,1)S(1)}, bf16[256,1024]{1,0:T(8,128)(2,1)S(1)}, u32[]{:S(2)}, u32[]{:S(2)}) collective-permute-start(bf16[256,1024]{1,0:T(8,128)(2,1)S(1)} %get-tuple-element.99), channel_id=1, source_target_pairs={{0,32},{32,64},{64,96},{96,128},{128,160},{160,192},{192,224},{224... | collective-permute-start | bytes 1572872 | tf_op jit(solution)/shard_map/ppermute | solution.py:381
  100.4 16.1 %collective-permute-start.14 = (bf16[256,1024]{1,0:T(8,128)(2,1)S(1)}, bf16[256,1024]{1,0:T(8,128)(2,1)S(1)}, u32[]{:S(2)}, u32[]{:S(2)}) collective-permute-start(bf16[256,1024]{1,0:T(8,128)(2,1)S(1)} %get-tuple-element.100), channel_id=1, source_target_pairs={{0,224},{32,0},{64,32},{96,64},{128,96},{160,128},{192,160},{224,1... | collective-permute-start | bytes 1572872 | tf_op jit(solution)/shard_map/ppermute | solution.py:381
  116.4 12.4 %copy-start.5 = (bf16[512,1024]{1,0:T(8,128)(2,1)S(1)}, bf16[512,1024]{1,0:T(8,128)(2,1)}, u32[]{:S(2)}) copy-start(bf16[512,1024]{1,0:T(8,128)(2,1)} %copy-done.2) | copy-start | bytes 3145732
  120.7 14.9 %collective-permute-start.15 = (bf16[256,1024]{1,0:T(8,128)(2,1)}, bf16[256,1024]{1,0:T(8,128)(2,1)S(1)}, u32[]{:S(2)}, u32[]{:S(2)}) collective-permute-start(bf16[256,1024]{1,0:T(8,128)(2,1)} %get-tuple-element.104), channel_id=1, source_target_pairs={{0,32},{32,64},{64,96},{96,128},{128,160},{160,192},{192,224},{224... | collective-permute-start | bytes 1572872 | tf_op jit(solution)/shard_map/ppermute | solution.py:381
  121.0 14.6 %collective-permute-start.16 = (bf16[256,1024]{1,0:T(8,128)(2,1)}, bf16[256,1024]{1,0:T(8,128)(2,1)}, u32[]{:S(2)}, u32[]{:S(2)}) collective-permute-start(bf16[256,1024]{1,0:T(8,128)(2,1)} %get-tuple-element.105), channel_id=1, source_target_pairs={{0,224},{32,0},{64,32},{96,64},{128,96},{160,128},{192,160},{224,1... | collective-permute-start | bytes 1572872 | tf_op jit(solution)/shard_map/ppermute | solution.py:381
  124.0 1.2 collective-permute-start.17
  125.1 3.7 %collective-permute-start.18 = (f32[16,128]{1,0:T(8,128)S(1)}, f32[16,128]{1,0:T(8,128)S(1)}, u32[]{:S(2)}, u32[]{:S(2)}) collective-permute-start(f32[16,128]{1,0:T(8,128)S(1)} %add.132), channel_id=1, source_target_pairs={{0,16},{16,0},{1,17},{17,1},{2,18},{18,2},{3,19},{19,3},{4,20},{20... | collective-permute-start | bytes 24584 | tf_op jit(solution)/shard_map/ppermute | solution.py:381
  128.8 5.8 %collective-permute-start.19 = (f32[16,128]{1,0:T(8,128)S(1)}, f32[16,128]{1,0:T(8,128)S(1)}, u32[]{:S(2)}, u32[]{:S(2)}) collective-permute-start(f32[16,128]{1,0:T(8,128)S(1)} %add.133), channel_id=1, source_target_pairs={{0,32},{32,0},{64,96},{96,64},{128,160},{160,128},{192,224},{224,1... | collective-permute-start | bytes 24584 | tf_op jit(solution)/shard_map/ppermute | solution.py:385
  137.1 10.9 %copy-start.11 = (f32[1,256,1024]{2,1,0:T(8,128)S(1)}, f32[1,256,1024]{2,1,0:T(8,128)}, u32[]{:S(2)}) copy-start(f32[1,256,1024]{2,1,0:T(8,128)} %copy-done.10) | copy-start | bytes 3145732
  137.1 7.9 %collective-permute-start.21 = (bf16[128,1024]{1,0:T(8,128)(2,1)S(1)}, bf16[128,1024]{1,0:T(8,128)(2,1)S(1)}, u32[]{:S(2)}, u32[]{:S(2)}) collective-permute-start(bf16[128,1024]{1,0:T(8,128)(2,1)S(1)} %get-tuple-element.133), channel_id=1, source_target_pairs={{0,224},{32,0},{64,32},{96,64},{128,96},{160,128},{192,160},{224,1... | collective-permute-start | bytes 786440 | tf_op jit(solution)/shard_map/ppermute | solution.py:381
  140.3 7.7 %collective-permute-start.20 = (bf16[128,1024]{1,0:T(8,128)(2,1)S(1)}, bf16[128,1024]{1,0:T(8,128)(2,1)S(1)}, u32[]{:S(2)}, u32[]{:S(2)}) collective-permute-start(bf16[128,1024]{1,0:T(8,128)(2,1)S(1)} %get-tuple-element.135), channel_id=1, source_target_pairs={{0,32},{32,64},{64,96},{96,128},{128,160},{160,192},{192,224},{224... | collective-permute-start | bytes 786440 | tf_op jit(solution)/shard_map/ppermute | solution.py:381
  140.4 4.6 %collective-permute-start.22 = (f32[16,128]{1,0:T(8,128)S(1)}, f32[16,128]{1,0:T(8,128)S(1)}, u32[]{:S(2)}, u32[]{:S(2)}) collective-permute-start(f32[16,128]{1,0:T(8,128)S(1)} %add.134), channel_id=1, source_target_pairs={{0,64},{32,96},{64,0},{96,32},{128,192},{160,224},{192,128},{224,1... | collective-permute-start | bytes 24584 | tf_op jit(solution)/shard_map/ppermute | solution.py:385
  148.2 13.7 %collective-permute-start.26 = (f32[128,1024]{1,0:T(8,128)S(1)}, f32[128,1024]{1,0:T(8,128)S(1)}, u32[]{:S(2)}, u32[]{:S(2)}) collective-permute-start(f32[128,1024]{1,0:T(8,128)S(1)} %get-tuple-element.131), channel_id=1, source_target_pairs={{0,16},{16,0},{1,17},{17,1},{2,18},{18,2},{3,19},{19,3},{4,20},{20... | collective-permute-start | bytes 1572872 | tf_op jit(solution)/shard_map/ppermute | solution.py:381
  149.3 7.7 %collective-permute-start.23 = (f32[16,128]{1,0:T(8,128)S(1)}, f32[16,128]{1,0:T(8,128)S(1)}, u32[]{:S(2)}, u32[]{:S(2)}) collective-permute-start(f32[16,128]{1,0:T(8,128)S(1)} %add.138), channel_id=1, source_target_pairs={{0,128},{32,160},{64,192},{96,224},{128,0},{160,32},{192,64},{224,... | collective-permute-start | bytes 24584 | tf_op jit(solution)/shard_map/ppermute | solution.py:385
  154.0 6.4 %collective-permute-start.25 = (bf16[128,1024]{1,0:T(8,128)(2,1)S(1)}, bf16[128,1024]{1,0:T(8,128)(2,1)S(1)}, u32[]{:S(2)}, u32[]{:S(2)}) collective-permute-start(bf16[128,1024]{1,0:T(8,128)(2,1)S(1)} %get-tuple-element.132), channel_id=1, source_target_pairs={{0,224},{32,0},{64,32},{96,64},{128,96},{160,128},{192,160},{224,1... | collective-permute-start | bytes 786440 | tf_op jit(solution)/shard_map/ppermute | solution.py:381
  154.2 7.6 %collective-permute-start.24 = (bf16[128,1024]{1,0:T(8,128)(2,1)S(1)}, bf16[128,1024]{1,0:T(8,128)(2,1)S(1)}, u32[]{:S(2)}, u32[]{:S(2)}) collective-permute-start(bf16[128,1024]{1,0:T(8,128)(2,1)S(1)} %get-tuple-element.134), channel_id=1, source_target_pairs={{0,32},{32,64},{64,96},{96,128},{128,160},{160,192},{192,224},{224... | collective-permute-start | bytes 786440 | tf_op jit(solution)/shard_map/ppermute | solution.py:381
Sparse Core Ops, SparseCore 0:
  9.9 77.4 all-gather.1

commit v7 on v6

--- a/solution.py
+++ b/solution.py
@@ -577,20 +577,17 @@
     far = blocks(4)[0].astype(BF16)
     up, down = both_ways(far[:, half:], far[:, :half], "z")
     mine = blocks(0)[0]
-    w, = tie((w,), mine)
+    up, down, mine = tie((up, down, mine))
+
+    up, down = both_ways(*ring_step(zi, 3, keep, theirs, normed, normed_other, up, down), "z")
+    last = blocks(1, -1)
+    w, = tie((w,), last)
     upstream = back_project(core, keep, give, w)
-    up, down, mine, upstream = tie((up, down, mine, upstream))
-
-    up, down = both_ways(*ring_step(zi, 3, keep, theirs, normed, normed_other, up, down), "z")
+    up, down, last, upstream = tie((up, down, last, upstream))
+
+    up, down = both_ways(*ring_step(zi, 2, keep, theirs, normed, normed_other, up, down), "z")
     dx, dz, db, dc, ddt, small = scan_backward(upstream, ys, *scan)
     up, down, small = tie((up, down, small))
-
-    up, down = both_ways(*ring_step(zi, 2, keep, theirs, normed, normed_other, up, down), "z")
-    last = blocks(1, -1)
-    small = small + send(small, "c", 1)
-    small = small + send(small, "xl", 1)
-    small = small + swap(small, "z", 1)
-    up, down, last, small = tie((up, down, last, small))
 
     def halves(r):
         return lax.dynamic_slice_in_dim(r, (1 - xl) * 128, 128, 0), lax.dynamic_slice_in_dim(r, xl * 128, 128, 0)
@@ -599,6 +596,9 @@
     down_leave, down_stay = halves((last[1] + down.astype(F32)).astype(BF16))
     up_leave, down_leave = both_ways(up_leave, down_leave, "z")
     up_stay, down_stay = both_ways(up_stay, down_stay, "z")
+    small = small + send(small, "c", 1)
+    small = small + send(small, "xl", 1)
+    small = small + swap(small, "z", 1)
     small = small + swap(small, "z", 2)
     leave, stay = halves(mine)
     up_leave, down_leave, small = tie((up_leave, down_leave, small))

time: 170 us -> 177 us (1.041)
  local copies, waits for them, and re-layouts: 13.8 us -> 20 us
  starting transfers between devices: 44.3 us -> 40.1 us
  waiting for transfers between devices: 40.4 us -> 43.1 us
    unnamed x50 -> x58, local copies, waits for them, and re-layouts: 8.45 us -> 14.6 us
    ppermute x3, waiting for transfers between devices: 6.65 us -> 11 us  [swap(): return lax.ppermute(v, axis, [(i, i ^ mask) for i in range(AXES[axis])])]
    ppermute x3, starting transfers between devices: 5.62 us -> 2.18 us  [swap(): return lax.ppermute(v, axis, [(i, i ^ mask) for i in range(AXES[axis])])]
  transfers between devices with their start and end apart: 28 -> 28, of which waited for: 15 -> 13; matrix products, arithmetic and copies ran while one was open for 5% -> 4% of each run, Pallas kernels for 27% -> 28%
where the time goes in v7:
time: 177 us; the launch traced here: 175 us
  Pallas kernels  54.3 us (31%)
  waiting for transfers between devices  43.1 us (24%)
  starting transfers between devices  40.1 us (23%)
  local copies, waits for them, and re-layouts  20 us (11%)
  between operations  14.5 us (8%)
  other arithmetic  3.29 us (2%)
    ppermute x24, starting transfers between devices, send(): return lax.ppermute(v, axis, [(i, (i + shift) % n) for i in range(n)])  37.9 us
    ppermute x24, waiting for transfers between devices, send(): return lax.ppermute(v, axis, [(i, (i + shift) % n) for i in range(n)])  31.5 us
    unnamed x58, local copies, waits for them, and re-layouts  14.6 us
    pallas_call x1, Pallas kernels, scan_backward(): pl.pallas_call(bwd_kernel, out_shape=(jax.ShapeDtypeStruct((TOK, CH), BF1...  14.5 us
    ppermute x3, waiting for transfers between devices, swap(): return lax.ppermute(v, axis, [(i, i ^ mask) for i in range(AXES[axis])])  11 us
    pallas_call x2, Pallas kernels, ring_step(): pl.pallas_call(kernel, grid_spec=pltpu.PrefetchScalarGridSpec(num_scalar_...  8.96 us
    pallas_call x1, Pallas kernels, back_project(): pl.pallas_call(kernel, grid_spec=pltpu.PrefetchScalarGridSpec(num_scalar_...  7.93 us
    pallas_call x2, Pallas kernels, shuffle(): pl.pallas_call(kernel, out_shape=tuple((jax.ShapeDtypeStruct(s, BF16) for...  7.25 us
  transfers between devices with their start and end apart: 28, of which 13 were waited for; matrix products, arithmetic and copies ran while one was open for 4% of the time, Pallas kernels for 28%

profile of v7, /device:TPU:2, one launch (start us, length us, event | category | flops | bytes accessed | tf_op | source)
XLA Modules:
  0.0 175.2 jit_solution(16864216824162245269)
XLA Ops:
  7.3 0.7 all-gather.2.cloned.1.call-update
  8.0 2.0 %own_first.1.refs_0_ = bf16[64,4096]{1,0:T(8,128)(2,1)} custom-call(s32[1]{0:T(128)} %bitcast.4.core_ref, bf16[64,4096]{1,0:T(8,128)(2,1)} %in_ref.1), custom_call_target="tpu_custom_call" | custom-call | flops 1000 | bytes 1000 | tf_op jit(solution)/shard_map/own_first/pallas_call | solution.py:430
  10.0 1.6 collective-permute-start
  11.5 1.7 collective-permute-start.1
  13.2 2.1 %collective-permute-start.2 = (bf16[64,4096]{1,0:T(8,128)(2,1)}, bf16[64,4096]{1,0:T(8,128)(2,1)}, u32[]{:S(2)}, u32[]{:S(2)}) collective-permute-start(bf16[64,4096]{1,0:T(8,128)(2,1)} %own_first.1.refs_0_), channel_id=1, source_target_pairs={{0,1},{1,0},{2,3},{3,2},{4,5},{5,4},{6,7},{7,6},{8,9},{9,8},{10,11... | collective-permute-start | bytes 1572872 | tf_op jit(solution)/shard_map/ppermute | solution.py:381
  15.3 9.8 %collective-permute-done.refs_2_ = bf16[64,4096]{1,0:T(8,128)(2,1)S(1)} collective-permute-done((bf16[64,4096]{1,0:T(8,128)(2,1)}, bf16[64,4096]{1,0:T(8,128)(2,1)S(1)}, u32[]{:S(2)}, u32[]{:S(2)}) %collective-permute-start) | collective-permute-done | bytes 524320 | tf_op jit(solution)/shard_map/ppermute | solution.py:381
  25.1 4.8 %collective-permute-done.2.refs_1_ = bf16[64,4096]{1,0:T(8,128)(2,1)} collective-permute-done((bf16[64,4096]{1,0:T(8,128)(2,1)}, bf16[64,4096]{1,0:T(8,128)(2,1)}, u32[]{:S(2)}, u32[]{:S(2)}) %collective-permute-start.2) | collective-permute-done | bytes 524320 | tf_op jit(solution)/shard_map/ppermute | solution.py:381
  29.9 3.2 %collective-permute-start.4 = (bf16[64,4096]{1,0:T(8,128)(2,1)}, bf16[64,4096]{1,0:T(8,128)(2,1)}, u32[]{:S(2)}, u32[]{:S(2)}) collective-permute-start(bf16[64,4096]{1,0:T(8,128)(2,1)} %collective-permute-done.2.refs_1_), channel_id=1, source_target_pairs={{0,6},{2,0},{4,2},{6,4},{1,7},{3,1},{5,3},{7,5},{8,14},{10,8},{12,... | collective-permute-start | bytes 1572872 | tf_op jit(solution)/shard_map/ppermute | solution.py:381
  33.1 0.7 slice.33
  33.9 0.7 slice.34
  34.6 3.2 %collective-permute-start.6 = (bf16[32,4096]{1,0:T(8,128)(2,1)}, bf16[32,4096]{1,0:T(8,128)(2,1)}, u32[]{:S(2)}, u32[]{:S(2)}) collective-permute-start(bf16[32,4096]{1,0:T(8,128)(2,1)} %slice.34), channel_id=1, source_target_pairs={{0,6},{2,0},{4,2},{6,4},{1,7},{3,1},{5,3},{7,5},{8,14},{10,8},{12,... | collective-permute-start | bytes 786440 | tf_op jit(solution)/shard_map/ppermute | solution.py:381
  37.8 0.9 copy.19.dt_ref
  38.8 0.9 copy-done.19
  39.7 7.1 %scan_forward.1 = (f32[512,1024]{1,0:T(8,128)S(1)}, bf16[512,1024]{1,0:T(8,128)(2,1)S(1)}) custom-call(bf16[512,1024]{1,0:T(8,128)(2,1)S(1)} %copy-done.11, bf16[512,1024]{1,0:T(8,128)(2,1)S(1)} %copy-done.13, bf16[512,128]{1,0:T(8,128)(2,1)S(1)} %bitcast.37, bf16[512,128]{1,0:T(8,128)(2,1)S(1)} %bitcast.39, f32[512,16]{1,0:T(8,128)S(1)} %copy.19.dt_ref, ...), custom_call_target="tpu_custom_call" | custom-call | flops 1000 | bytes 1000 | tf_op jit(solution)/shard_map/scan_forward/pallas_call | solution.py:320
  46.8 1.3 copy-done.17
  48.2 1.0 slice.35
  49.3 1.0 slice.36
  50.3 3.3 %collective-permute-start.8 = (bf16[32,4096]{1,0:T(8,128)(2,1)S(1)}, bf16[32,4096]{1,0:T(8,128)(2,1)S(1)}, u32[]{:S(2)}, u32[]{:S(2)}) collective-permute-start(bf16[32,4096]{1,0:T(8,128)(2,1)S(1)} %slice.36), channel_id=1, source_target_pairs={{0,6},{2,0},{4,2},{6,4},{1,7},{3,1},{5,3},{7,5},{8,14},{10,8},{12,... | collective-permute-start | bytes 786440 | tf_op jit(solution)/shard_map/ppermute | solution.py:381
  53.6 0.6 pad_add_fusion
  54.2 5.0 %collective-permute-done.7.refs_8_ = bf16[32,4096]{1,0:T(8,128)(2,1)S(1)} collective-permute-done((bf16[32,4096]{1,0:T(8,128)(2,1)S(1)}, bf16[32,4096]{1,0:T(8,128)(2,1)S(1)}, u32[]{:S(2)}, u32[]{:S(2)}) %collective-permute-start.7) | collective-permute-done | bytes 262176 | tf_op jit(solution)/shard_map/ppermute | solution.py:381
  59.5 0.4 copy-done.26
  60.2 3.6 %place_tokens.2.b_ref = bf16[512,2048]{1,0:T(8,128)(2,1)} custom-call(s32[2]{0:T(128)} %get-tuple-element.139.s_ref, bf16[64,4096]{1,0:T(8,128)(2,1)} %own_first.1.refs_0_, bf16[64,4096]{1,0:T(8,128)(2,1)} %collective-permute-done.2.refs_1_, bf16[64,4096]{1,0:T(8,128)(2,1)} %copy-done.24, bf16[64,4096]{1,0:T(8,128)(2,1)} %collective-permute-done.3.refs_3_, ...), custom_call_target="tpu_custom_call" | custom-call | flops 1000 | bytes 1000 | tf_op jit(solution)/shard_map/place_tokens/pallas_call | solution.py:410
  64.1 3.7 %place_tokens.3.a_ref = bf16[512,2048]{1,0:T(8,128)(2,1)} custom-call(s32[2]{0:T(128)} %get-tuple-element.139.s_ref, bf16[64,4096]{1,0:T(8,128)(2,1)} %own_first.1.refs_0_, bf16[64,4096]{1,0:T(8,128)(2,1)} %collective-permute-done.2.refs_1_, bf16[64,4096]{1,0:T(8,128)(2,1)} %copy-done.24, bf16[64,4096]{1,0:T(8,128)(2,1)} %collective-permute-done.3.refs_3_, ...), custom_call_target="tpu_custom_call" | custom-call | flops 1000 | bytes 1000 | tf_op jit(solution)/shard_map/place_tokens/pallas_call | solution.py:410
  67.8 1.1 collective-permute-done.10.b_ref
  68.8 1.6 copy-done
  70.5 1.7 weight_blocks.3
  72.3 0.8 fusion.2
  73.1 1.3 collective-permute-start.11
  74.4 7.8 %collective-permute-start.12 = (bf16[256,512]{1,0:T(8,128)(2,1)}, bf16[256,512]{1,0:T(8,128)(2,1)}, u32[]{:S(2)}, u32[]{:S(2)}) collective-permute-start(bf16[256,512]{1,0:T(8,128)(2,1)} %get-tuple-element.134), channel_id=1, source_target_pairs={{0,224},{32,0},{64,32},{96,64},{128,96},{160,128},{192,160},{224,1... | collective-permute-start | bytes 786440 | tf_op jit(solution)/shard_map/ppermute | solution.py:381
  82.2 1.2 copy-done.4
  83.4 1.7 weight_blocks.4
  85.2 3.9 %collective-permute-done.11.up_ref = bf16[256,512]{1,0:T(8,128)(2,1)} collective-permute-done((bf16[256,512]{1,0:T(8,128)(2,1)}, bf16[256,512]{1,0:T(8,128)(2,1)}, u32[]{:S(2)}, u32[]{:S(2)}) %collective-permute-start.11) | collective-permute-done | bytes 262176 | tf_op jit(solution)/shard_map/ppermute | solution.py:381
  89.1 4.3 %ring_step.2 = (bf16[256,1024]{1,0:T(8,128)(2,1)}, bf16[256,1024]{1,0:T(8,128)(2,1)}) custom-call(s32[2]{0:T(128)S(1)} %get-tuple-element.138.at_ref, bf16[512,2048]{1,0:T(8,128)(2,1)S(1)} %copy-done.1, bf16[512,2048]{1,0:T(8,128)(2,1)} %collective-permute-done.10.b_ref, bf16[512,1024]{1,0:T(8,128)(2,1)S(1)} %get-tuple-element.72.n_ref, ...), custom_call_target="tpu_custom_call" | custom-call | flops 1000 | bytes 1000 | tf_op jit(solution)/shard_map/ring_step/pallas_call | solution.py:508
  93.4 3.2 %collective-permute-start.14 = (bf16[256,1024]{1,0:T(8,128)(2,1)}, bf16[256,1024]{1,0:T(8,128)(2,1)}, u32[]{:S(2)}, u32[]{:S(2)}) collective-permute-start(bf16[256,1024]{1,0:T(8,128)(2,1)} %get-tuple-element.91), channel_id=1, source_target_pairs={{0,224},{32,0},{64,32},{96,64},{128,96},{160,128},{192,160},{224,1... | collective-permute-start | bytes 1572872 | tf_op jit(solution)/shard_map/ppermute | solution.py:381
  96.8 1.2 copy-done.5
  98.0 3.2 %weight_blocks.5 = f32[2,256,1024]{2,1,0:T(8,128)S(1)} custom-call(s32[2]{0:T(128)S(1)} %pad_add_fusion.2.at_ref, bf16[512,2048]{1,0:T(8,128)(2,1)} %place_tokens.3.a_ref, bf16[512,2048]{1,0:T(8,128)(2,1)} %collective-permute-done.10.b_ref, bf16[512,1024]{1,0:T(8,128)(2,1)S(1)} %get-tuple-element.72.n_ref, bf16[512,1024]{1,0:T(8,128)(2,1)S(1)} %copy-done.5), custom_call_target="tpu_custom_call" | custom-call | flops 1000 | bytes 1000 | tf_op jit(solution)/shard_map/weight_blocks/pallas_call | solution.py:467
  101.2 1.3 copy-done.9
  102.5 7.9 %back_project.1.u_hbm = f32[512,1024]{1,0:T(8,128)S(1)} custom-call(s32[1]{0:T(128)} %bitcast.4.core_ref, bf16[512,2048]{1,0:T(8,128)(2,1)S(1)} %copy-done.2, bf16[512,2048]{1,0:T(8,128)(2,1)} %place_tokens.2.b_ref, bf16[16,2,128,1024]{3,2,1,0:T(8,128)(2,1)} %bitcast.47, bf16[16,2,128,1024]{3,2,1,0:T(8,128)(2,1)} %bitcast.48), custom_call_target="tpu_custom_call" | custom-call | flops 1000 | bytes 1000 | tf_op jit(solution)/shard_map/back_project/pallas_call | solution.py:528
  110.5 1.3 copy-done.7
  111.8 4.7 %ring_step.3 = (bf16[256,1024]{1,0:T(8,128)(2,1)}, bf16[256,1024]{1,0:T(8,128)(2,1)}) custom-call(s32[2]{0:T(128)S(1)} %pad_add_fusion.3.at_ref, bf16[512,2048]{1,0:T(8,128)(2,1)} %place_tokens.3.a_ref, bf16[512,2048]{1,0:T(8,128)(2,1)} %collective-permute-done.10.b_ref, bf16[512,1024]{1,0:T(8,128)(2,1)S(1)} %get-tuple-element.72.n_ref, ...), custom_call_target="tpu_custom_call" | custom-call | flops 1000 | bytes 1000 | tf_op jit(solution)/shard_map/ring_step/pallas_call | solution.py:508
  116.5 3.2 %collective-permute-start.16 = (bf16[256,1024]{1,0:T(8,128)(2,1)}, bf16[256,1024]{1,0:T(8,128)(2,1)}, u32[]{:S(2)}, u32[]{:S(2)}) collective-permute-start(bf16[256,1024]{1,0:T(8,128)(2,1)} %get-tuple-element.104), channel_id=1, source_target_pairs={{0,224},{32,0},{64,32},{96,64},{128,96},{160,128},{192,160},{224,1... | collective-permute-start | bytes 1572872 | tf_op jit(solution)/shard_map/ppermute | solution.py:381
  119.7 1.2 copy-done.12
  120.9 1.2 copy-done.14
  122.1 0.9 copy-done.20
  123.0 14.5 %scan_backward.1 = (bf16[512,1024]{1,0:T(8,128)(2,1)}, bf16[512,1024]{1,0:T(8,128)(2,1)}, bf16[512,128]{1,0:T(8,128)(2,1)}, bf16[512,128]{1,0:T(8,128)(2,1)}, f3...) custom-call(f32[512,1024]{1,0:T(8,128)S(1)} %copy-done.8, f32[512,1024]{1,0:T(8,128)} %copy-done.17, ...), custom_call_target="tpu_custom_call" | custom-call | flops 1000 | bytes 1000 | tf_op jit(solution)/shard_map/scan_backward/pallas_call | solution.py:338
  137.6 1.4 fusion
  139.0 0.6 collective-permute-start.18
  139.6 1.6 collective-permute-start.17
  141.2 1.2 collective-permute-done.19
  142.4 1.1 collective-permute-start.20
  143.5 2.6 %collective-permute-done.20 = f32[16,128]{1,0:T(8,128)S(1)} collective-permute-done((f32[16,128]{1,0:T(8,128)S(1)}, f32[16,128]{1,0:T(8,128)S(1)}, u32[]{:S(2)}, u32[]{:S(2)}) %collective-permute-start.20) | collective-permute-done | bytes 8224 | tf_op jit(solution)/shard_map/ppermute | solution.py:381
  146.2 3.6 %collective-permute-done.21 = f32[16,128]{1,0:T(8,128)S(1)} collective-permute-done((f32[16,128]{1,0:T(8,128)S(1)}, f32[16,128]{1,0:T(8,128)S(1)}, u32[]{:S(2)}, u32[]{:S(2)}) %collective-permute-start.21) | collective-permute-done | bytes 8224 | tf_op jit(solution)/shard_map/ppermute | solution.py:385
  149.7 4.5 %collective-permute-done.22 = f32[16,128]{1,0:T(8,128)S(1)} collective-permute-done((f32[16,128]{1,0:T(8,128)S(1)}, f32[16,128]{1,0:T(8,128)S(1)}, u32[]{:S(2)}, u32[]{:S(2)}) %collective-permute-start.22) | collective-permute-done | bytes 8224 | tf_op jit(solution)/shard_map/ppermute | solution.py:385
  154.5 1.4 collective-permute-start.26
  155.9 2.1 %collective-permute-start.23 = (f32[16,128]{1,0:T(8,128)S(1)}, f32[16,128]{1,0:T(8,128)S(1)}, u32[]{:S(2)}, u32[]{:S(2)}) collective-permute-start(f32[16,128]{1,0:T(8,128)S(1)} %add.138), channel_id=1, source_target_pairs={{0,128},{32,160},{64,192},{96,224},{128,0},{160,32},{192,64},{224,... | collective-permute-start | bytes 24584 | tf_op jit(solution)/shard_map/ppermute | solution.py:385
  158.0 0.7 copy.21
  158.7 1.2 collective-permute-start.25
  159.9 0.8 collective-permute-start.24
  160.7 2.9 %collective-permute-done.23 = f32[16,128]{1,0:T(8,128)S(1)} collective-permute-done((f32[16,128]{1,0:T(8,128)S(1)}, f32[16,128]{1,0:T(8,128)S(1)}, u32[]{:S(2)}, u32[]{:S(2)}) %collective-permute-start.23) | collective-permute-done | bytes 8224 | tf_op jit(solution)/shard_map/ppermute | solution.py:385
  163.6 0.5 slice_bitcast_fusion.1
  164.1 0.6 slice_bitcast_fusion
  164.7 0.4 collective-permute-done.25
  165.1 2.3 %collective-permute-done.24 = bf16[128,1024]{1,0:T(8,128)(2,1)S(1)} collective-permute-done((bf16[128,1024]{1,0:T(8,128)(2,1)S(1)}, bf16[128,1024]{1,0:T(8,128)(2,1)S(1)}, u32[]{:S(2)}, u32[]{:S(2)}) %collective-permute-start.24) | collective-permute-done | bytes 262176 | tf_op jit(solution)/shard_map/ppermute | solution.py:381
  167.5 0.9 add_add_fusion
  (83 shorter events, 1.9 us)
Async XLA Ops:
  7.2 31.5 %copy-start.23 = (f32[16]{0:T(128)S(1)}, f32[16]{0:T(128)}, u32[]{:S(2)}) copy-start(f32[16]{0:T(128)} %param.17) | copy-start | bytes 196
  7.2 31.5 %copy-start.18 = (bf16[512,1,128]{2,0,1:T(8,128)(2,1)S(1)}, bf16[512,1,128]{2,0,1:T(8,128)(2,1)}, u32[]{:S(2)}) copy-start(bf16[512,1,128]{2,0,1:T(8,128)(2,1)} %param.13) | copy-start | bytes 393220
  7.2 31.5 %copy-start.22 = (f32[16]{0:T(128)S(1)}, f32[16]{0:T(128)}, u32[]{:S(2)}) copy-start(f32[16]{0:T(128)} %param.16) | copy-start | bytes 196
  7.2 31.5 %copy-start.21 = (f32[1024]{0:T(1024)S(1)}, f32[1024]{0:T(1024)}, u32[]{:S(2)}) copy-start(f32[1024]{0:T(1024)} %param.18) | copy-start | bytes 12292
  7.2 31.5 %copy-start.11 = (bf16[512,1024]{1,0:T(8,128)(2,1)S(1)}, bf16[512,1024]{1,0:T(8,128)(2,1)}, u32[]{:S(2)}) copy-start(bf16[512,1024]{1,0:T(8,128)(2,1)} %x_hbm.1) | copy-start | bytes 3145732
  7.2 31.5 %copy-start.13 = (bf16[512,1024]{1,0:T(8,128)(2,1)S(1)}, bf16[512,1024]{1,0:T(8,128)(2,1)}, u32[]{:S(2)}) copy-start(bf16[512,1024]{1,0:T(8,128)(2,1)} %z_hbm.1) | copy-start | bytes 3145732
  7.2 95.3 %all-gather.2.cloned.1.call-start = ((), (), s32[]{:S(2)}) async-start(), calls=%async_computation | async-start | bytes 8650752 | tf_op jit(solution)/shard_map/all_gather | solution.py:552
  10.0 15.1 %collective-permute-start = (bf16[64,4096]{1,0:T(8,128)(2,1)}, bf16[64,4096]{1,0:T(8,128)(2,1)S(1)}, u32[]{:S(2)}, u32[]{:S(2)}) collective-permute-start(bf16[64,4096]{1,0:T(8,128)(2,1)} %own_first.1.refs_0_), channel_id=1, source_target_pairs={{0,2},{2,4},{4,6},{6,0},{1,3},{3,5},{5,7},{7,1},{8,10},{10,12},{12... | collective-permute-start | bytes 1572872 | tf_op jit(solution)/shard_map/ppermute | solution.py:381
  11.5 13.6 %collective-permute-start.1 = (bf16[64,4096]{1,0:T(8,128)(2,1)}, bf16[64,4096]{1,0:T(8,128)(2,1)S(1)}, u32[]{:S(2)}, u32[]{:S(2)}) collective-permute-start(bf16[64,4096]{1,0:T(8,128)(2,1)} %own_first.1.refs_0_), channel_id=1, source_target_pairs={{0,6},{2,0},{4,2},{6,4},{1,7},{3,1},{5,3},{7,5},{8,14},{10,8},{12,... | collective-permute-start | bytes 1572872 | tf_op jit(solution)/shard_map/ppermute | solution.py:381
  13.2 16.7 %collective-permute-start.2 = (bf16[64,4096]{1,0:T(8,128)(2,1)}, bf16[64,4096]{1,0:T(8,128)(2,1)}, u32[]{:S(2)}, u32[]{:S(2)}) collective-permute-start(bf16[64,4096]{1,0:T(8,128)(2,1)} %own_first.1.refs_0_), channel_id=1, source_target_pairs={{0,1},{1,0},{2,3},{3,2},{4,5},{5,4},{6,7},{7,6},{8,9},{9,8},{10,11... | collective-permute-start | bytes 1572872 | tf_op jit(solution)/shard_map/ppermute | solution.py:381
  25.1 13.6 %copy-start.24 = (bf16[64,4096]{1,0:T(8,128)(2,1)}, bf16[64,4096]{1,0:T(8,128)(2,1)S(1)}, u32[]{:S(2)}) copy-start(bf16[64,4096]{1,0:T(8,128)(2,1)S(1)} %collective-permute-done.refs_2_) | copy-start | bytes 1572868
  25.1 13.6 %copy-start.25 = (bf16[64,4096]{1,0:T(8,128)(2,1)}, bf16[64,4096]{1,0:T(8,128)(2,1)S(1)}, u32[]{:S(2)}) copy-start(bf16[64,4096]{1,0:T(8,128)(2,1)S(1)} %collective-permute-done.1.refs_4_) | copy-start | bytes 1572868
  29.9 18.2 %collective-permute-start.3 = (bf16[64,4096]{1,0:T(8,128)(2,1)}, bf16[64,4096]{1,0:T(8,128)(2,1)}, u32[]{:S(2)}, u32[]{:S(2)}) collective-permute-start(bf16[64,4096]{1,0:T(8,128)(2,1)} %collective-permute-done.2.refs_1_), channel_id=1, source_target_pairs={{0,2},{2,4},{4,6},{6,0},{1,3},{3,5},{5,7},{7,1},{8,10},{10,12},{12... | collective-permute-start | bytes 1572872 | tf_op jit(solution)/shard_map/ppermute | solution.py:381
  29.9 18.2 %collective-permute-start.4 = (bf16[64,4096]{1,0:T(8,128)(2,1)}, bf16[64,4096]{1,0:T(8,128)(2,1)}, u32[]{:S(2)}, u32[]{:S(2)}) collective-permute-start(bf16[64,4096]{1,0:T(8,128)(2,1)} %collective-permute-done.2.refs_1_), channel_id=1, source_target_pairs={{0,6},{2,0},{4,2},{6,4},{1,7},{3,1},{5,3},{7,5},{8,14},{10,8},{12,... | collective-permute-start | bytes 1572872 | tf_op jit(solution)/shard_map/ppermute | solution.py:381
  33.9 14.3 %collective-permute-start.5 = (bf16[32,4096]{1,0:T(8,128)(2,1)}, bf16[32,4096]{1,0:T(8,128)(2,1)}, u32[]{:S(2)}, u32[]{:S(2)}) collective-permute-start(bf16[32,4096]{1,0:T(8,128)(2,1)} %slice.33), channel_id=1, source_target_pairs={{0,2},{2,4},{4,6},{6,0},{1,3},{3,5},{5,7},{7,1},{8,10},{10,12},{12... | collective-permute-start | bytes 786440 | tf_op jit(solution)/shard_map/ppermute | solution.py:381
  34.6 13.5 %collective-permute-start.6 = (bf16[32,4096]{1,0:T(8,128)(2,1)}, bf16[32,4096]{1,0:T(8,128)(2,1)}, u32[]{:S(2)}, u32[]{:S(2)}) collective-permute-start(bf16[32,4096]{1,0:T(8,128)(2,1)} %slice.34), channel_id=1, source_target_pairs={{0,6},{2,0},{4,2},{6,4},{1,7},{3,1},{5,3},{7,5},{8,14},{10,8},{12,... | collective-permute-start | bytes 786440 | tf_op jit(solution)/shard_map/ppermute | solution.py:381
  38.8 0.9 copy-start.19
  46.8 1.3 copy-start.17
  48.1 11.4 %collective-permute-start.9 = (bf16[512,1024]{1,0:T(8,128)(2,1)S(1)}, bf16[512,1024]{1,0:T(8,128)(2,1)S(1)}, u32[]{:S(2)}, u32[]{:S(2)}) collective-permute-start(bf16[512,1024]{1,0:T(8,128)(2,1)S(1)} %get-tuple-element.72.n_ref), channel_id=1, source_target_pairs={{0,8},{8,0},{1,9},{9,1},{2,10},{10,2},{3,11},{11,3},{4,12},{12,4},... | collective-permute-start | bytes 3145736 | tf_op jit(solution)/shard_map/ppermute | solution.py:381
  49.2 10.0 %collective-permute-start.7 = (bf16[32,4096]{1,0:T(8,128)(2,1)S(1)}, bf16[32,4096]{1,0:T(8,128)(2,1)S(1)}, u32[]{:S(2)}, u32[]{:S(2)}) collective-permute-start(bf16[32,4096]{1,0:T(8,128)(2,1)S(1)} %slice.35), channel_id=1, source_target_pairs={{0,2},{2,4},{4,6},{6,0},{1,3},{3,5},{5,7},{7,1},{8,10},{10,12},{12... | collective-permute-start | bytes 786440 | tf_op jit(solution)/shard_map/ppermute | solution.py:381
  50.3 9.2 %collective-permute-start.8 = (bf16[32,4096]{1,0:T(8,128)(2,1)S(1)}, bf16[32,4096]{1,0:T(8,128)(2,1)S(1)}, u32[]{:S(2)}, u32[]{:S(2)}) collective-permute-start(bf16[32,4096]{1,0:T(8,128)(2,1)S(1)} %slice.36), channel_id=1, source_target_pairs={{0,6},{2,0},{4,2},{6,4},{1,7},{3,1},{5,3},{7,5},{8,14},{10,8},{12,... | collective-permute-start | bytes 786440 | tf_op jit(solution)/shard_map/ppermute | solution.py:381
  59.2 0.7 copy-start.26
  59.5 0.7 copy-start.27
  59.5 9.3 %copy-start.3 = (bf16[512,1024]{1,0:T(8,128)(2,1)}, bf16[512,1024]{1,0:T(8,128)(2,1)S(1)}, u32[]{:S(2)}) copy-start(bf16[512,1024]{1,0:T(8,128)(2,1)S(1)} %collective-permute-done.9.m_ref) | copy-start | bytes 3145732
  63.8 5.1 %collective-permute-start.10 = (bf16[512,2048]{1,0:T(8,128)(2,1)}, bf16[512,2048]{1,0:T(8,128)(2,1)}, u32[]{:S(2)}, u32[]{:S(2)}) collective-permute-start(bf16[512,2048]{1,0:T(8,128)(2,1)} %place_tokens.2.b_ref), channel_id=1, source_target_pairs={{0,8},{8,0},{1,9},{9,1},{2,10},{10,2},{3,11},{11,3},{4,12},{12,4},... | collective-permute-start | bytes 6291464 | tf_op jit(solution)/shard_map/ppermute | solution.py:381
  68.8 1.6 copy-start
  72.2 10.0 %copy-start.1 = (bf16[512,2048]{1,0:T(8,128)(2,1)S(1)}, bf16[512,2048]{1,0:T(8,128)(2,1)}, u32[]{:S(2)}) copy-start(bf16[512,2048]{1,0:T(8,128)(2,1)} %place_tokens.3.a_ref) | copy-start | bytes 6291460
  73.1 16.0 %collective-permute-start.11 = (bf16[256,512]{1,0:T(8,128)(2,1)}, bf16[256,512]{1,0:T(8,128)(2,1)}, u32[]{:S(2)}, u32[]{:S(2)}) collective-permute-start(bf16[256,512]{1,0:T(8,128)(2,1)} %get-tuple-element.135), channel_id=1, source_target_pairs={{0,32},{32,64},{64,96},{96,128},{128,160},{160,192},{192,224},{224... | collective-permute-start | bytes 786440 | tf_op jit(solution)/shard_map/ppermute | solution.py:381
  74.4 14.7 %collective-permute-start.12 = (bf16[256,512]{1,0:T(8,128)(2,1)}, bf16[256,512]{1,0:T(8,128)(2,1)}, u32[]{:S(2)}, u32[]{:S(2)}) collective-permute-start(bf16[256,512]{1,0:T(8,128)(2,1)} %get-tuple-element.134), channel_id=1, source_target_pairs={{0,224},{32,0},{64,32},{96,64},{128,96},{160,128},{192,160},{224,1... | collective-permute-start | bytes 786440 | tf_op jit(solution)/shard_map/ppermute | solution.py:381
  82.2 1.2 copy-start.4
  85.2 8.3 %copy-start.15 = (f32[1,256,1024]{2,1,0:T(8,128)}, f32[1,256,1024]{2,1,0:T(8,128)S(1)}, u32[]{:S(2)}) copy-start(f32[1,256,1024]{2,1,0:T(8,128)S(1)} %weight_blocks.4) | copy-start | bytes 3145732
  93.4 18.4 %collective-permute-start.13 = (bf16[256,1024]{1,0:T(8,128)(2,1)}, bf16[256,1024]{1,0:T(8,128)(2,1)}, u32[]{:S(2)}, u32[]{:S(2)}) collective-permute-start(bf16[256,1024]{1,0:T(8,128)(2,1)} %get-tuple-element.90), channel_id=1, source_target_pairs={{0,32},{32,64},{64,96},{96,128},{128,160},{160,192},{192,224},{224... | collective-permute-start | bytes 1572872 | tf_op jit(solution)/shard_map/ppermute | solution.py:381
  93.4 18.4 %collective-permute-start.14 = (bf16[256,1024]{1,0:T(8,128)(2,1)}, bf16[256,1024]{1,0:T(8,128)(2,1)}, u32[]{:S(2)}, u32[]{:S(2)}) collective-permute-start(bf16[256,1024]{1,0:T(8,128)(2,1)} %get-tuple-element.91), channel_id=1, source_target_pairs={{0,224},{32,0},{64,32},{96,64},{128,96},{160,128},{192,160},{224,1... | collective-permute-start | bytes 1572872 | tf_op jit(solution)/shard_map/ppermute | solution.py:381
  96.8 1.2 copy-start.5
  98.0 4.5 %copy-start.2 = (bf16[512,2048]{1,0:T(8,128)(2,1)S(1)}, bf16[512,2048]{1,0:T(8,128)(2,1)}, u32[]{:S(2)}) copy-start(bf16[512,2048]{1,0:T(8,128)(2,1)} %place_tokens.3.a_ref) | copy-start | bytes 6291460
  101.2 1.3 copy-start.9
  102.5 9.2 %copy-start.6 = (bf16[512,1024]{1,0:T(8,128)(2,1)S(1)}, bf16[512,1024]{1,0:T(8,128)(2,1)}, u32[]{:S(2)}) copy-start(bf16[512,1024]{1,0:T(8,128)(2,1)} %copy-done.3) | copy-start | bytes 3145732
  110.5 1.3 copy-start.7
  111.8 7.9 %copy-start.8 = (f32[512,1024]{1,0:T(8,128)S(1)}, f32[512,1024]{1,0:T(8,128)}, u32[]{:S(2)}) copy-start(f32[512,1024]{1,0:T(8,128)} %copy-done.7) | copy-start | bytes 6291460
  116.4 21.1 %collective-permute-start.15 = (bf16[256,1024]{1,0:T(8,128)(2,1)}, bf16[256,1024]{1,0:T(8,128)(2,1)S(1)}, u32[]{:S(2)}, u32[]{:S(2)}) collective-permute-start(bf16[256,1024]{1,0:T(8,128)(2,1)} %get-tuple-element.103), channel_id=1, source_target_pairs={{0,32},{32,64},{64,96},{96,128},{128,160},{160,192},{192,224},{224... | collective-permute-start | bytes 1572872 | tf_op jit(solution)/shard_map/ppermute | solution.py:381
  116.5 21.1 %collective-permute-start.16 = (bf16[256,1024]{1,0:T(8,128)(2,1)}, bf16[256,1024]{1,0:T(8,128)(2,1)}, u32[]{:S(2)}, u32[]{:S(2)}) collective-permute-start(bf16[256,1024]{1,0:T(8,128)(2,1)} %get-tuple-element.104), channel_id=1, source_target_pairs={{0,224},{32,0},{64,32},{96,64},{128,96},{160,128},{192,160},{224,1... | collective-permute-start | bytes 1572872 | tf_op jit(solution)/shard_map/ppermute | solution.py:381
  119.7 1.2 copy-start.12
  120.9 1.2 copy-start.14
  122.1 0.9 copy-start.20
  123.0 14.5 %copy-start.10 = (f32[2,256,1024]{2,1,0:T(8,128)S(1)}, f32[2,256,1024]{2,1,0:T(8,128)}, u32[]{:S(2)}) copy-start(f32[2,256,1024]{2,1,0:T(8,128)} %copy-done.9) | copy-start | bytes 6291460
  138.9 15.3 %copy-start.16 = (f32[1,256,1024]{2,1,0:T(8,128)S(1)}, f32[1,256,1024]{2,1,0:T(8,128)}, u32[]{:S(2)}) copy-start(f32[1,256,1024]{2,1,0:T(8,128)} %copy-done.15) | copy-start | bytes 3145732
  139.0 15.3 %collective-permute-start.18 = (bf16[128,1024]{1,0:T(8,128)(2,1)S(1)}, bf16[128,1024]{1,0:T(8,128)(2,1)S(1)}, u32[]{:S(2)}, u32[]{:S(2)}) collective-permute-start(bf16[128,1024]{1,0:T(8,128)(2,1)S(1)} %get-tuple-element.131), channel_id=1, source_target_pairs={{0,224},{32,0},{64,32},{96,64},{128,96},{160,128},{192,160},{224,1... | collective-permute-start | bytes 786440 | tf_op jit(solution)/shard_map/ppermute | solution.py:381
  139.6 14.6 %collective-permute-start.17 = (bf16[128,1024]{1,0:T(8,128)(2,1)S(1)}, bf16[128,1024]{1,0:T(8,128)(2,1)S(1)}, u32[]{:S(2)}, u32[]{:S(2)}) collective-permute-start(bf16[128,1024]{1,0:T(8,128)(2,1)S(1)} %get-tuple-element.133), channel_id=1, source_target_pairs={{0,32},{32,64},{64,96},{96,128},{128,160},{160,192},{192,224},{224... | collective-permute-start | bytes 786440 | tf_op jit(solution)/shard_map/ppermute | solution.py:381
  141.2 1.2 collective-permute-start.19
  142.4 3.7 %collective-permute-start.20 = (f32[16,128]{1,0:T(8,128)S(1)}, f32[16,128]{1,0:T(8,128)S(1)}, u32[]{:S(2)}, u32[]{:S(2)}) collective-permute-start(f32[16,128]{1,0:T(8,128)S(1)} %add.135), channel_id=1, source_target_pairs={{0,16},{16,0},{1,17},{17,1},{2,18},{18,2},{3,19},{19,3},{4,20},{20... | collective-permute-start | bytes 24584 | tf_op jit(solution)/shard_map/ppermute | solution.py:381
  146.1 3.7 %collective-permute-start.21 = (f32[16,128]{1,0:T(8,128)S(1)}, f32[16,128]{1,0:T(8,128)S(1)}, u32[]{:S(2)}, u32[]{:S(2)}) collective-permute-start(f32[16,128]{1,0:T(8,128)S(1)} %add.136), channel_id=1, source_target_pairs={{0,32},{32,0},{64,96},{96,64},{128,160},{160,128},{192,224},{224,1... | collective-permute-start | bytes 24584 | tf_op jit(solution)/shard_map/ppermute | solution.py:385
  149.7 4.5 %collective-permute-start.22 = (f32[16,128]{1,0:T(8,128)S(1)}, f32[16,128]{1,0:T(8,128)S(1)}, u32[]{:S(2)}, u32[]{:S(2)}) collective-permute-start(f32[16,128]{1,0:T(8,128)S(1)} %add.137), channel_id=1, source_target_pairs={{0,64},{32,96},{64,0},{96,32},{128,192},{160,224},{192,128},{224,1... | collective-permute-start | bytes 24584 | tf_op jit(solution)/shard_map/ppermute | solution.py:385
  154.5 13.0 %collective-permute-start.26 = (f32[128,1024]{1,0:T(8,128)S(1)}, f32[128,1024]{1,0:T(8,128)S(1)}, u32[]{:S(2)}, u32[]{:S(2)}) collective-permute-start(f32[128,1024]{1,0:T(8,128)S(1)} %get-tuple-element.129), channel_id=1, source_target_pairs={{0,16},{16,0},{1,17},{17,1},{2,18},{18,2},{3,19},{19,3},{4,20},{20... | collective-permute-start | bytes 1572872 | tf_op jit(solution)/shard_map/ppermute | solution.py:381
  155.9 7.7 %collective-permute-start.23 = (f32[16,128]{1,0:T(8,128)S(1)}, f32[16,128]{1,0:T(8,128)S(1)}, u32[]{:S(2)}, u32[]{:S(2)}) collective-permute-start(f32[16,128]{1,0:T(8,128)S(1)} %add.138), channel_id=1, source_target_pairs={{0,128},{32,160},{64,192},{96,224},{128,0},{160,32},{192,64},{224,... | collective-permute-start | bytes 24584 | tf_op jit(solution)/shard_map/ppermute | solution.py:385
  158.7 6.5 %collective-permute-start.25 = (bf16[128,1024]{1,0:T(8,128)(2,1)S(1)}, bf16[128,1024]{1,0:T(8,128)(2,1)S(1)}, u32[]{:S(2)}, u32[]{:S(2)}) collective-permute-start(bf16[128,1024]{1,0:T(8,128)(2,1)S(1)} %get-tuple-element.130), channel_id=1, source_target_pairs={{0,224},{32,0},{64,32},{96,64},{128,96},{160,128},{192,160},{224,1... | collective-permute-start | bytes 786440 | tf_op jit(solution)/shard_map/ppermute | solution.py:381
  159.9 7.6 %collective-permute-start.24 = (bf16[128,1024]{1,0:T(8,128)(2,1)S(1)}, bf16[128,1024]{1,0:T(8,128)(2,1)S(1)}, u32[]{:S(2)}, u32[]{:S(2)}) collective-permute-start(bf16[128,1024]{1,0:T(8,128)(2,1)S(1)} %get-tuple-element.132), channel_id=1, source_target_pairs={{0,32},{32,64},{64,96},{96,128},{128,160},{160,192},{192,224},{224... | collective-permute-start | bytes 786440 | tf_op jit(solution)/shard_map/ppermute | solution.py:381
Sparse Core Ops, SparseCore 0:
  9.9 77.5 all-gather.1
